TPU v7x, 32 devices: a whole 2x2x4 slice. The times are simulated.
32 devices in a mesh: fsdp: 4 (over y, x), ep: 8 (over z, core).
Axes of the slice: x: 2, y: 2, z: 4, core: 2. Of those that a mesh axis runs over, the one named last changes fastest.
Arguments:
- tokens: bfloat16 [4096, 7168], P('ep', 'fsdp'), may hold values from -6 to 6
- cotangent: bfloat16 [4096, 7168], P('ep', 'fsdp'), may hold values from -3 to 3
- gate_weight: bfloat16 [8, 7168, 2048], P('ep', None, 'fsdp'), may hold values from -0.0625 to 0.0625
- up_weight: bfloat16 [8, 7168, 2048], P('ep', None, 'fsdp'), may hold values from -0.0625 to 0.0625
- down_weight: bfloat16 [8, 2048, 7168], P('ep', 'fsdp'), may hold values from -0.125 to 0.125
- chosen: int32 [8, 8, 16], P(None, 'ep'), may hold values from 0 to 511, as said below
- counts: int32 [8, 8], P(None, 'ep'), may hold values from 1 to 16, as said below
- gate_prob: float32 [8, 8, 16], P(None, 'ep'), may hold values from 0.2 to 1
Outputs:
- mixture: bfloat16 [4096, 7168], P('ep', 'fsdp')
- grad_tokens: bfloat16 [4096, 7168], P('ep', 'fsdp')
- grad_gate: bfloat16 [8, 7168, 2048], P('ep', None, 'fsdp')
- grad_up: bfloat16 [8, 7168, 2048], P('ep', None, 'fsdp')
- grad_down: bfloat16 [8, 2048, 7168], P('ep', 'fsdp')
Inputs may be any that keep to these rules, and one draw needn't show every extreme that they name: For each expert e and group s the entries chosen[e, s, j] with j < counts[e, s] are distinct; the remaining entries are padding. `counts`: in every draw one expert takes 16 rows from every group.
All inputs are finite; a program needn't handle non-finite values.
Results may differ from a plain program's by a relative error of at most 0.017.
Values may be sent and summed in bfloat16 or wider, within the bound.
No kernel may reach another device: no remote copies, remote signals or barrier semaphores. Data moves between devices by JAX's collectives and lax.ppermute only.
A program may use at most 192 MiB of HBM per device.

v0:
```python
import jax
import jax.numpy as jnp
from jax import lax
from jax.sharding import PartitionSpec as P


def pick_rows(tokens, cotangent, row_index, live_mask, weight):
    flat_rows = row_index.reshape(-1)
    keep_rows = live_mask.reshape(-1)[:, None]
    taken_tokens = jnp.take(tokens, flat_rows, axis=0)
    picked_tokens = jnp.where(keep_rows, taken_tokens, jnp.zeros_like(taken_tokens))
    taken_grads = jnp.take(cotangent, flat_rows, axis=0).astype(jnp.float32)
    picked_grads = (weight.reshape(-1)[:, None] * taken_grads).astype(jnp.bfloat16)
    shaped = row_index.shape + (tokens.shape[1],)
    return (picked_tokens.reshape(shaped), picked_grads.reshape(shaped))


def to_slots(summed, experts, slot_count):
    return summed.astype(jnp.bfloat16).reshape(experts, slot_count, summed.shape[1])


def send_back(term, experts, slot_count):
    summed = lax.psum_scatter(
        term.astype(jnp.bfloat16), "fsdp", scatter_dimension=1, tiled=True
    ).astype(jnp.float32)
    return lax.all_to_all(
        to_slots(summed, experts, slot_count), "ep", split_axis=0, concat_axis=0, tiled=True
    )


def per_device(tokens, cotangent, gate_weight, up_weight, down_weight, chosen, counts, gate_prob):
    experts = chosen.shape[0]
    slot_count = chosen.shape[2]
    features = tokens.shape[1]
    row_index = chosen[:, 0, :]
    position = lax.broadcasted_iota(jnp.int32, (experts, slot_count), 1)
    live_mask = position < counts
    weight = jnp.where(live_mask, gate_prob[:, 0, :], 0.0)
    picked_tokens, picked_grads = pick_rows(tokens, cotangent, row_index, live_mask, weight)
    sliced_tokens, sliced_grads = (
        lax.all_to_all(picked_tokens, "ep", split_axis=0, concat_axis=0, tiled=True),
        lax.all_to_all(picked_grads, "ep", split_axis=0, concat_axis=0, tiled=True),
    )
    rows_tokens, rows_grads = (
        lax.all_gather(sliced_tokens, "fsdp", axis=2, tiled=True),
        lax.all_gather(sliced_grads, "fsdp", axis=2, tiled=True),
    )
    full_width = rows_tokens.shape[2]
    total_rows = rows_tokens.shape[0] * slot_count
    rows_tokens = rows_tokens.reshape(total_rows, full_width)
    rows_grads = rows_grads.reshape(total_rows, full_width)
    gate_local = gate_weight[0]
    up_local = up_weight[0]
    down_local = down_weight[0]
    pre_gate = jnp.dot(rows_tokens, gate_local, preferred_element_type=jnp.float32)
    pre_up = jnp.dot(rows_tokens, up_local, preferred_element_type=jnp.float32)
    sigmoid_gate = jax.nn.sigmoid(pre_gate)
    activated = pre_gate * sigmoid_gate
    hidden = (activated * pre_up).astype(jnp.bfloat16)
    output_term = jnp.dot(hidden, down_local, preferred_element_type=jnp.float32)
    output_back = send_back(output_term, experts, slot_count)
    contract_rows = (((0,), (0,)), ((), ()))
    contract_last = (((1,), (1,)), ((), ()))
    grad_hidden = lax.dot_general(
        rows_grads, down_local, contract_last, preferred_element_type=jnp.float32
    )
    grad_pre_gate = (
        grad_hidden * pre_up * sigmoid_gate * (1.0 + pre_gate * (1.0 - sigmoid_gate))
    ).astype(jnp.bfloat16)
    grad_pre_up = (grad_hidden * activated).astype(jnp.bfloat16)
    grad_down = lax.dot_general(
        hidden, rows_grads, contract_rows, preferred_element_type=jnp.float32
    ).astype(jnp.bfloat16)
    grad_gate = lax.dot_general(
        rows_tokens, grad_pre_gate, contract_rows, preferred_element_type=jnp.float32
    ).astype(jnp.bfloat16)
    grad_up = lax.dot_general(
        rows_tokens, grad_pre_up, contract_rows, preferred_element_type=jnp.float32
    ).astype(jnp.bfloat16)
    grad_term = lax.dot_general(
        grad_pre_gate, gate_local, contract_last, preferred_element_type=jnp.float32
    )
    grad_term = grad_term + lax.dot_general(
        grad_pre_up, up_local, contract_last, preferred_element_type=jnp.float32
    )
    grad_back = send_back(grad_term, experts, slot_count)
    flat_rows = row_index.reshape(-1)
    output_rows = output_back.reshape(-1, features).astype(jnp.float32)
    mixture = (
        jnp.zeros((tokens.shape[0], features), jnp.float32)
        .at[flat_rows]
        .add(weight.reshape(-1)[:, None] * output_rows)
    )
    grad_rows = jnp.where(
        live_mask.reshape(-1)[:, None], grad_back.reshape(-1, features).astype(jnp.float32), 0.0
    )
    grad_tokens = jnp.zeros((tokens.shape[0], features), jnp.float32).at[flat_rows].add(grad_rows)
    return (
        mixture.astype(jnp.bfloat16),
        grad_tokens.astype(jnp.bfloat16),
        grad_gate[None],
        grad_up[None],
        grad_down[None],
    )


def solution(mesh):
    placed = (
        P("ep", "fsdp"),
        P("ep", "fsdp"),
        P("ep", None, "fsdp"),
        P("ep", None, "fsdp"),
        P("ep", "fsdp", None),
        P(None, "ep", None),
        P(None, "ep"),
        P(None, "ep", None),
    )
    return jax.shard_map(
        per_device,
        mesh=mesh,
        in_specs=placed,
        out_specs=(
            P("ep", "fsdp"),
            P("ep", "fsdp"),
            P("ep", None, "fsdp"),
            P("ep", None, "fsdp"),
            P("ep", "fsdp", None),
        ),
        check_vma=False,
    )
```

profile of v0, /device:TPU:1, one launch (start us, length us, event | category | flops | bytes accessed | tf_op | source)
XLA Modules:
  0.0 222.3 jit_solution(8720537716635539348)
XLA Ops:
  7.2 0.0 copy-start
  7.2 0.0 copy-start.5
  7.2 0.0 all-gather.3.cloned.1.call-start
  7.2 0.9 reshape_squeeze.7
  8.1 0.7 iota_compare_fusion
  8.9 0.1 lt.41
  9.0 0.0 copy-done
  9.0 0.9 gather_fusion
  9.9 0.0 copy-start.3
  9.9 0.1 select_select_fusion
  10.1 19.4 %all_to_all.20 = bf16[8,16,1792]{2,1,0:T(8,128)(2,1)} all-to-all(bf16[8,16,1792]{2,1,0:T(8,128)(2,1)S(1)} %bitcast.58), channel_id=1, replica_groups=mesh['fsdp'=4,'ep'=8] {'ep'}, dimensions={0} | all-to-all | bytes 917504 | tf_op jit(solution)/shard_map/all_to_all | solution.py:41
  29.5 0.0 all-gather.3.cloned.1.call-update
  29.5 0.0 all-gather.5.cloned.1.call-start
  29.6 0.5 broadcast.74
  30.1 0.0 copy-done.5
  30.1 0.7 reduce.9
  30.7 0.1 squeeze.12
  30.8 0.0 copy-done.3
  30.8 0.9 gather_fusion.1
  31.8 0.3 multiply_convert_fusion
  32.0 17.0 %all_to_all.21 = bf16[8,16,1792]{2,1,0:T(8,128)(2,1)} all-to-all(bf16[8,16,1792]{2,1,0:T(8,128)(2,1)S(1)} %bitcast.57), channel_id=1, replica_groups=mesh['fsdp'=4,'ep'=8] {'ep'}, dimensions={0} | all-to-all | bytes 917504 | tf_op jit(solution)/shard_map/all_to_all | solution.py:42
  49.1 0.0 all-gather.5.cloned.1.call-update
  49.1 0.0 reduce-scatter.3.cloned.1.call-start
  49.2 12.8 %all-gather.3.cloned.1.call-done = bf16[8,16,7168]{2,1,0:T(8,128)(2,1)} async-done(((bf16[8,16,1792]{2,1,0:T(8,128)(2,1)}), bf16[8,16,7168]{2,1,0:T(8,128)(2,1)}) %all-gather.3.cloned.1.call-update) | async-done | bytes 1835024 | tf_op jit(solution)/shard_map/all_gather | solution.py:45
  62.0 0.0 copy-start.2
  62.0 4.9 %fusion.8 = f32[128,512]{1,0:T(8,128)S(1)} fusion(bf16[128,7168]{1,0:T(8,128)(2,1)} %bitcast.49, bf16[1,7168,512]{2,1,0:T(8,128)(2,1)} %param.13), kind=kOutput, calls=%fused_computation.17 | convolution fusion | flops 939524096 | bytes 9437184 | tf_op jit(solution)/shard_map/dot_general | solution.py:56
  66.9 0.0 copy-done.2
  66.9 4.2 %fusion.12 = f32[128,512]{1,0:T(8,128)S(1)} fusion(bf16[128,7168]{1,0:T(8,128)(2,1)S(1)} %bitcast.50, bf16[1,7168,512]{2,1,0:T(8,128)(2,1)} %param.12), kind=kOutput, calls=%fused_computation.21 | convolution fusion | flops 939524096 | bytes 9437184 | tf_op jit(solution)/shard_map/dot_general | solution.py:55
  71.1 25.9 %all-gather.5.cloned.1.call-done = bf16[8,16,7168]{2,1,0:T(8,128)(2,1)} async-done(((bf16[8,16,1792]{2,1,0:T(8,128)(2,1)}), bf16[8,16,7168]{2,1,0:T(8,128)(2,1)}) %all-gather.5.cloned.1.call-update) | async-done | bytes 1835024 | tf_op jit(solution)/shard_map/all_gather | solution.py:46
  97.0 6.3 %multiply_convert_fusion.1 = (bf16[128,512]{1,0:T(8,128)(2,1)S(1)}, bf16[128,512]{1,0:T(8,128)(2,1)S(1)}, bf16[128,512]{1,0:T(8,128)(2,1)S(1)}) fusion(f32[128,512]{1,0:T(8,128)S(1)} %fusion.12, f32[128,512]{1,0:T(8,128)S(1)} %fusion.8, bf16[128,7168]{1,0:T(8,128)(2,1)} %bitcast.53, bf16[1,512,7168]{2,1,0:T(8,128)(2,1)} %param.14), kind=kOutput, calls=%fused_computation.34 | convolution fusion | flops 940507136 | bytes 10092544 | tf_op jit(solution)/shard_map/dot_general | solution.py:64
  103.3 5.4 %convolution_convert_fusion.3 = bf16[128,7168]{1,0:T(8,128)(2,1)} fusion(bf16[128,512]{1,0:T(8,128)(2,1)S(1)} %get-tuple-element.8, bf16[1,512,7168]{2,1,0:T(8,128)(2,1)} %param.14), kind=kOutput, calls=%fused_computation.12 | convolution fusion | flops 940441600 | bytes 9306112 | tf_op jit(solution)/shard_map/dot_general | solution.py:60
  108.7 0.0 reduce-scatter.3.cloned.1.call-update
  108.8 0.0 reduce-scatter.5.cloned.1.call-start
  108.8 5.6 %fusion.10 = f32[128,7168]{1,0:T(8,128)S(1)} fusion(bf16[128,512]{1,0:T(8,128)(2,1)S(1)} %get-tuple-element.7, bf16[1,7168,512]{2,1,0:T(8,128)(2,1)} %param.12), kind=kOutput, calls=%fused_computation.19 | convolution fusion | flops 939524096 | bytes 11141120 | tf_op jit(solution)/shard_map/dot_general | solution.py:80
  114.4 0.0 copy-start.4
  114.4 7.1 %fusion.3 = bf16[128,7168]{1,0:T(8,128)(2,1)} fusion(f32[128,7168]{1,0:T(8,128)S(1)} %fusion.10, bf16[128,512]{1,0:T(8,128)(2,1)S(1)} %get-tuple-element.6, bf16[1,7168,512]{2,1,0:T(8,128)(2,1)} %param.13), kind=kOutput, calls=%fused_computation.11 | convolution fusion | flops 941359104 | bytes 12976128 | tf_op jit(solution)/shard_map/dot_general | solution.py:83
  121.5 0.0 reduce-scatter.5.cloned.1.call-update
  121.5 20.4 %reduce-scatter.3.cloned.1.call-done = bf16[128,1792]{1,0:T(8,128)(2,1)} async-done(((bf16[128,7168]{1,0:T(8,128)(2,1)}), bf16[128,1792]{1,0:T(8,128)(2,1)}) %reduce-scatter.3.cloned.1.call-update) | async-done | bytes 458768 | tf_op jit(solution)/shard_map/reduce_scatter | solution.py:23
  141.9 5.3 %all-to-all-start.1 = ((bf16[8,16,1792]{2,1,0:T(8,128)(2,1)}), bf16[8,16,1792]{2,1,0:T(8,128)(2,1)S(1)}, u32[]{:S(2)}, u32[]{:S(2)}) async-start(bf16[8,16,1792]{2,1,0:T(8,128)(2,1)} %bitcast.60), calls=%async_computation.2 | async-start | bytes 917504 | tf_op jit(solution)/shard_map/all_to_all | solution.py:26
  147.2 0.5 broadcast.73
  147.7 0.0 copy-done.4
  147.7 0.7 reduce.8
  148.4 0.1 reshape_squeeze.6
  148.5 30.0 %reduce-scatter.5.cloned.1.call-done = bf16[128,1792]{1,0:T(8,128)(2,1)} async-done(((bf16[128,7168]{1,0:T(8,128)(2,1)}), bf16[128,1792]{1,0:T(8,128)(2,1)}) %reduce-scatter.5.cloned.1.call-update) | async-done | bytes 458768 | tf_op jit(solution)/shard_map/reduce_scatter | solution.py:23
  178.4 0.0 all-to-all-done.1
  178.4 5.3 %all-to-all-start.3 = ((bf16[8,16,1792]{2,1,0:T(8,128)(2,1)}), bf16[8,16,1792]{2,1,0:T(8,128)(2,1)S(1)}, u32[]{:S(2)}, u32[]{:S(2)}) async-start(bf16[8,16,1792]{2,1,0:T(8,128)(2,1)} %bitcast.59), calls=%async_computation.5 | async-start | bytes 917504 | tf_op jit(solution)/shard_map/all_to_all | solution.py:26
  183.7 6.6 %fusion.2 = bf16[1,512,7168]{2,1,0:T(8,128)(2,1)} fusion(bf16[128,512]{1,0:T(8,128)(2,1)S(1)} %get-tuple-element.8, bf16[128,7168]{1,0:T(8,128)(2,1)} %bitcast.54), kind=kOutput, calls=%fused_computation.9 | convolution fusion | flops 943194112 | bytes 9306112 | tf_op jit(solution)/shard_map/dot_general | solution.py:71
  190.4 5.1 %fusion.1 = bf16[1,7168,512]{2,1,0:T(8,128)(2,1)} fusion(bf16[128,7168]{1,0:T(8,128)(2,1)S(1)} %bitcast.51, bf16[128,512]{1,0:T(8,128)(2,1)S(1)} %get-tuple-element.6), kind=kOutput, calls=%fused_computation.8 | convolution fusion | flops 943194112 | bytes 9306112 | tf_op jit(solution)/shard_map/dot_general | solution.py:77
  195.5 5.1 %fusion = bf16[1,7168,512]{2,1,0:T(8,128)(2,1)} fusion(bf16[128,7168]{1,0:T(8,128)(2,1)S(1)} %bitcast.52, bf16[128,512]{1,0:T(8,128)(2,1)S(1)} %get-tuple-element.7), kind=kOutput, calls=%fused_computation.7 | convolution fusion | flops 943194112 | bytes 9306112 | tf_op jit(solution)/shard_map/dot_general | solution.py:74
  200.6 4.1 %scatter_custom_fusion = f32[512,1792]{1,0:T(8,128)} fusion(s32[128]{0:T(128)S(1)} %fusion.22, f32[]{:T(128)} %constant.0.clone.1, bf16[128,1792]{1,0:T(8,128)(2,1)S(1)} %bitcast.55, f32[128]{0:T(128)S(1)} %broadcast_select_fusion), kind=kCustom, calls=%fused_computation.25 | custom fusion | flops 688128 | bytes 4129284 | tf_op jit(solution)/shard_map/scatter-add | solution.py:92
  204.8 3.4 %convert_element_type.56 = bf16[512,1792]{1,0:T(8,128)(2,1)} convert(f32[512,1792]{1,0:T(8,128)} %scatter_custom_fusion) | non-fusion elementwise | flops 917504 | bytes 5505024 | tf_op jit(solution)/shard_map/convert_element_type | solution.py:99
  208.2 0.0 all-to-all-done.3
  208.2 0.0 copy-start.1
  208.2 4.1 %scatter_custom_fusion.1 = f32[512,1792]{1,0:T(8,128)} fusion(s32[128]{0:T(128)S(1)} %fusion.22, f32[]{:T(128)} %constant.0.clone.1, bf16[128,1792]{1,0:T(8,128)(2,1)S(1)} %bitcast.56, pred[128]{0:T(512)(128)(4,1)S(1)} %lt.41), kind=kCustom, calls=%fused_computation.23 | custom fusion | flops 688128 | bytes 4130304 | tf_op jit(solution)/shard_map/scatter-add | solution.py:97
  212.3 3.4 %convert_element_type.64 = bf16[512,1792]{1,0:T(8,128)(2,1)} convert(f32[512,1792]{1,0:T(8,128)} %scatter_custom_fusion.1) | non-fusion elementwise | flops 917504 | bytes 5505024 | tf_op jit(solution)/shard_map/convert_element_type | solution.py:100
  215.8 0.0 copy-done.1
  (5 shorter events, 0.0 us)
Async XLA Ops:
  7.2 1.8 copy-start
  7.2 22.9 %copy-start.5 = (f32[8,1,16]{2,1,0:T(1,128)S(1)}, f32[8,1,16]{2,1,0:T(1,128)}, u32[]{:S(2)}) copy-start(f32[8,1,16]{2,1,0:T(1,128)} %param.17) | copy-start | bytes 1540
  7.2 54.8 %all-gather.3.cloned.1.call-start = ((), (), s32[]{:S(2)}) async-start(), calls=%async_computation.6 | async-start | bytes 2293760 | tf_op jit(solution)/shard_map/all_gather | solution.py:45
  9.9 20.9 %copy-start.3 = (bf16[512,1792]{1,0:T(8,128)(2,1)S(1)}, bf16[512,1792]{1,0:T(8,128)(2,1)}, u32[]{:S(2)}) copy-start(bf16[512,1792]{1,0:T(8,128)(2,1)} %param.11) | copy-start | bytes 5505028
  29.5 67.5 %all-gather.5.cloned.1.call-start = ((), (), s32[]{:S(2)}) async-start(), calls=%async_computation.8 | async-start | bytes 2293760 | tf_op jit(solution)/shard_map/all_gather | solution.py:46
  49.1 92.8 %reduce-scatter.3.cloned.1.call-start = ((), (), s32[]{:S(2)}) async-start(), calls=%async_computation.7 | async-start | bytes 2293760 | tf_op jit(solution)/shard_map/reduce_scatter | solution.py:23
  62.0 4.9 %copy-start.2 = (bf16[8,16,7168]{2,1,0:T(8,128)(2,1)S(1)}, bf16[8,16,7168]{2,1,0:T(8,128)(2,1)}, u32[]{:S(2)}) copy-start(bf16[8,16,7168]{2,1,0:T(8,128)(2,1)} %all-gather.3.cloned.1.call-done) | copy-start | bytes 5505028
  108.8 69.7 %reduce-scatter.5.cloned.1.call-start = ((), (), s32[]{:S(2)}) async-start(), calls=%async_computation.9 | async-start | bytes 2293760 | tf_op jit(solution)/shard_map/reduce_scatter | solution.py:23
  114.4 33.3 %copy-start.4 = (s32[8,1,16]{2,1,0:T(1,128)S(1)}, s32[8,1,16]{2,1,0:T(1,128)}, u32[]{:S(2)}) copy-start(s32[8,1,16]{2,1,0:T(1,128)} %param.15) | copy-start | bytes 1540
  141.9 36.5 %all-to-all-start.1 = ((bf16[8,16,1792]{2,1,0:T(8,128)(2,1)}), bf16[8,16,1792]{2,1,0:T(8,128)(2,1)S(1)}, u32[]{:S(2)}, u32[]{:S(2)}) async-start(bf16[8,16,1792]{2,1,0:T(8,128)(2,1)} %bitcast.60), calls=%async_computation.2 | async-start | bytes 917504 | tf_op jit(solution)/shard_map/all_to_all | solution.py:26
  178.4 29.8 %all-to-all-start.3 = ((bf16[8,16,1792]{2,1,0:T(8,128)(2,1)}), bf16[8,16,1792]{2,1,0:T(8,128)(2,1)S(1)}, u32[]{:S(2)}, u32[]{:S(2)}) async-start(bf16[8,16,1792]{2,1,0:T(8,128)(2,1)} %bitcast.59), calls=%async_computation.5 | async-start | bytes 917504 | tf_op jit(solution)/shard_map/all_to_all | solution.py:26
  208.2 7.6 %copy-start.1 = (bf16[512,1792]{1,0:T(8,128)(2,1)S(1)}, bf16[512,1792]{1,0:T(8,128)(2,1)}, u32[]{:S(2)}) copy-start(bf16[512,1792]{1,0:T(8,128)(2,1)} %param.10) | copy-start | bytes 5505028
Sparse Core Ops, SparseCore 0:
  29.6 32.3 all-gather.2
  63.9 33.1 all-gather.4
  108.9 32.9 reduce-scatter.2
  145.4 32.9 reduce-scatter.4
where the time goes:
time: 223 us; the launch traced here: 222 us
  waiting for transfers between devices  89.2 us (40%)
  matrix products  50.4 us (23%)
  blocking collectives  36.5 us (16%)
  other arithmetic  17.6 us (8%)
  between operations  13.9 us (6%)
  starting transfers between devices  10.7 us (5%)
  local copies, waits for them, and re-layouts  4.06 us (2%)
    reduce_scatter x2, waiting for transfers between devices, send_back(): lax.psum_scatter(term.astype(jnp.bfloat16), 'fsdp', scatter_dimension=1,...  50.3 us
    all_gather x1, waiting for transfers between devices, per_device(): lax.all_gather(sliced_grads, 'fsdp', axis=2, tiled=True)  25.9 us
    all_to_all x1, blocking collectives, per_device(): lax.all_to_all(picked_tokens, 'ep', split_axis=0, concat_axis=0, tiled=True)  19.4 us
    all_to_all x1, blocking collectives, per_device(): lax.all_to_all(picked_grads, 'ep', split_axis=0, concat_axis=0, tiled=True)  17 us
    all_gather x1, waiting for transfers between devices, per_device(): lax.all_gather(sliced_tokens, 'fsdp', axis=2, tiled=True)  12.8 us
    all_to_all x2, starting transfers between devices, send_back(): lax.all_to_all(to_slots(summed, experts, slot_count), 'ep', split_axis=0,...  10.6 us
    dot_general x1, matrix products, per_device(): lax.dot_general(grad_pre_up, up_local, contract_last, preferred_element_t...  7.13 us
    dot_general x1, matrix products, per_device(): lax.dot_general(hidden, rows_grads, contract_rows, preferred_element_type...  6.64 us
  transfers between devices with their start and end apart: 6, of which 4 were waited for; matrix products, arithmetic and copies ran while one was open for 22% of the time, Pallas kernels for 0%

commit v1 on v0

--- a/solution.py
+++ b/solution.py
@@ -1,7 +1,15 @@
+import functools
+
 import jax
 import jax.numpy as jnp
 from jax import lax
+from jax.experimental import pallas as pl
+from jax.experimental.pallas import tpu as pltpu
 from jax.sharding import PartitionSpec as P
+
+ROWS = (((0,), (0,)), ((), ()))
+LAST = (((1,), (1,)), ((), ()))
+VMEM_BYTES = 40 * 1024 * 1024
 
 
 def pick_rows(tokens, cotangent, row_index, live_mask, weight):
@@ -28,7 +36,7 @@
     )
 
 
-def per_device(tokens, cotangent, gate_weight, up_weight, down_weight, chosen, counts, gate_prob):
+def by_collectives(tokens, cotangent, gate_weight, up_weight, down_weight, chosen, counts, gate_prob):
     experts = chosen.shape[0]
     slot_count = chosen.shape[2]
     features = tokens.shape[1]
@@ -104,6 +112,459 @@
     )
 
 
+def call_kernel(body, name, grid, specs, outs, out_specs, scratch, cost, operands, prefetch=1):
+    return pl.pallas_call(
+        body,
+        name=name,
+        out_shape=outs,
+        grid_spec=pltpu.PrefetchScalarGridSpec(
+            num_scalar_prefetch=prefetch,
+            grid=grid,
+            in_specs=specs,
+            out_specs=out_specs,
+            scratch_shapes=scratch,
+        ),
+        compiler_params=pltpu.CompilerParams(vmem_limit_bytes=VMEM_BYTES),
+        cost_estimate=pl.CostEstimate(flops=cost[0], bytes_accessed=cost[1], transcendentals=0),
+    )(*operands)
+
+
+def whole(array):
+    zeros = (0,) * array.ndim
+    return pl.BlockSpec(array.shape, lambda *_: zeros)
+
+
+def exchange(array, distance, axis):
+    size = lax.axis_size(axis)
+    return lax.ppermute(array, axis, [(i, i ^ distance) for i in range(size)])
+
+
+def slot_columns(me, chosen_ref, counts_ref, prob_ref):
+    experts, _, slots = chosen_ref.shape
+    diagonal = lax.broadcasted_iota(jnp.int32, (slots, slots), 0) == lax.broadcasted_iota(
+        jnp.int32, (slots, slots), 1
+    )
+    position = lax.broadcasted_iota(jnp.int32, (slots, 1), 0)
+    rows, weights = [], []
+    for step in range(experts):
+        expert = me ^ step
+        live = position < counts_ref[expert, 0]
+        row = jnp.broadcast_to(chosen_ref[expert].astype(jnp.float32), (slots, slots))
+        row = jnp.sum(jnp.where(diagonal, row, 0.0), axis=1, keepdims=True)
+        prob = jnp.broadcast_to(prob_ref[expert], (slots, slots))
+        prob = jnp.sum(jnp.where(diagonal, prob, 0.0), axis=1, keepdims=True)
+        rows.append(jnp.where(live, row, -1.0))
+        weights.append(jnp.where(live, prob, 0.0))
+    return jnp.concatenate(rows, axis=0), jnp.concatenate(weights, axis=0)
+
+
+def token_mask(rows, tokens):
+    place = lax.broadcasted_iota(jnp.int32, (rows.shape[0], tokens), 1).astype(jnp.float32)
+    return place == rows
+
+
+def pick_body(me_ref, counts_ref, chosen_ref, prob_ref, tokens_ref, cotangent_ref, *outs):
+    experts, _, slots = chosen_ref.shape
+    rows, weights = slot_columns(me_ref[0], chosen_ref, counts_ref, prob_ref)
+    select = token_mask(rows, tokens_ref.shape[0]).astype(jnp.bfloat16)
+    picked = jnp.dot(select, tokens_ref[...], preferred_element_type=jnp.float32)
+    grads = weights * jnp.dot(select, cotangent_ref[...], preferred_element_type=jnp.float32)
+    for value, (even_ref, odd_ref) in zip((picked, grads), (outs[:2], outs[2:])):
+        value = value.astype(jnp.bfloat16)
+        for step in range(experts):
+            target = (even_ref, odd_ref)[step % 2]
+            target[pl.ds(step // 2 * slots, slots), :] = value[step * slots : (step + 1) * slots]
+
+
+def pick_slots(ep_index, chosen, counts, gate_prob, tokens, cotangent):
+    experts, _, slots = chosen.shape
+    length, width = tokens.shape
+    block = width // 2 if width % 256 == 0 else width
+    half = experts // 2 * slots
+    small = [pl.BlockSpec(memory_space=pltpu.SMEM), whole(chosen), whole(gate_prob)]
+    long_spec = pl.BlockSpec((length, block), lambda i, *_: (0, i))
+    out = jax.ShapeDtypeStruct((half, width), jnp.bfloat16)
+    return call_kernel(
+        pick_body,
+        "pick_slots",
+        (width // block,),
+        small + [long_spec] * 2,
+        [out] * 4,
+        [pl.BlockSpec((half, block), lambda i, *_: (0, i))] * 4,
+        [],
+        (8 * half * length * width, 6 * length * width),
+        (ep_index, counts, chosen, gate_prob, tokens, cotangent),
+    )
+
+
+def spread_body(weighted, layout, me_ref, counts_ref, chosen_ref, prob_ref, *refs):
+    pieces, out_ref = refs[:-1], refs[-1]
+    slots = chosen_ref.shape[2]
+    rows, weights = slot_columns(me_ref[0], chosen_ref, counts_ref, prob_ref)
+    blocks = [pieces[p][pl.ds(q * slots, slots), :] for p, q in layout]
+    values = jnp.concatenate(blocks, axis=0)
+    mask = token_mask(rows, out_ref.shape[0])
+    if weighted:
+        high = weights.astype(jnp.bfloat16).astype(jnp.float32)
+        parts = [jnp.where(mask, high, 0.0), jnp.where(mask, weights - high, 0.0)]
+        spread = jnp.concatenate([part.astype(jnp.bfloat16) for part in parts], axis=0)
+        values = jnp.concatenate([values, values], axis=0)
+    else:
+        spread = mask.astype(jnp.bfloat16)
+    total = lax.dot_general(spread, values, ROWS, preferred_element_type=jnp.float32)
+    out_ref[...] = total.astype(jnp.bfloat16)
+
+
+def spread_rows(ep_index, chosen, counts, gate_prob, pieces, layout, weighted, length):
+    width = pieces[0].shape[1]
+    block = width // 2 if width % 256 == 0 else width
+    small = [pl.BlockSpec(memory_space=pltpu.SMEM), whole(chosen), whole(gate_prob)]
+    piece_specs = [pl.BlockSpec((piece.shape[0], block), lambda i, *_: (0, i)) for piece in pieces]
+    return call_kernel(
+        functools.partial(spread_body, weighted, layout),
+        "spread_rows",
+        (width // block,),
+        small + piece_specs,
+        jax.ShapeDtypeStruct((length, width), jnp.bfloat16),
+        pl.BlockSpec((length, block), lambda i, *_: (0, i)),
+        [],
+        (4 * 128 * length * width, 3 * length * width),
+        (ep_index, counts, chosen, gate_prob, *pieces),
+    )
+
+
+def stacked(refs, start, size):
+    blocks = [ref[:, start : start + size] for ref in refs]
+    return blocks[0] if len(blocks) == 1 else jnp.concatenate(blocks, axis=0)
+
+
+def per_step(step, count, function):
+    for index in range(count):
+
+        @pl.when(step == index)
+        def _(index=index):
+            function(index)
+
+
+def pre_body(counts, splits, me_ref, *refs):
+    total = sum(counts)
+    pieces, (gate_ref, up_ref) = refs[:total], refs[total : total + 2]
+    hidden_ref, slope_ref, silu_ref, gate_sum, up_sum = refs[total + 2 :]
+    step = pl.program_id(0)
+    size = gate_ref.shape[0]
+
+    def add(index):
+        slice_index, part = divmod(index, splits)
+        first = sum(counts[:slice_index])
+        rows = stacked(pieces[first : first + counts[slice_index]], part * size, size)
+        gate = jnp.dot(rows, gate_ref[...], preferred_element_type=jnp.float32)
+        up = jnp.dot(rows, up_ref[...], preferred_element_type=jnp.float32)
+        if index == 0:
+            gate_sum[...] = gate
+            up_sum[...] = up
+        else:
+            gate_sum[...] += gate
+            up_sum[...] += up
+
+    per_step(step, splits * len(counts), add)
+
+    @pl.when(step == pl.num_programs(0) - 1)
+    def _():
+        gate = gate_sum[...]
+        up = up_sum[...]
+        sigmoid = jax.nn.sigmoid(gate)
+        silu = gate * sigmoid
+        hidden_ref[...] = (silu * up).astype(jnp.bfloat16)
+        slope_ref[...] = up * sigmoid * (1.0 + gate * (1.0 - sigmoid))
+        silu_ref[...] = silu
+
+
+def pre_activations(fsdp_index, slices, gate, up, splits=2):
+    counts = [len(pieces) for pieces in slices]
+    flat = [piece for pieces in slices for piece in pieces]
+    rows = sum(piece.shape[0] for piece in slices[0])
+    width = slices[0][0].shape[1]
+    hidden = gate.shape[1]
+    size = width // splits
+    weight_spec = pl.BlockSpec(
+        (size, hidden), lambda i, me: ((me[0] ^ (i // splits)) * splits + i % splits, 0)
+    )
+    outs = [jax.ShapeDtypeStruct((rows, hidden), t) for t in (jnp.bfloat16, jnp.float32, jnp.float32)]
+    return call_kernel(
+        functools.partial(pre_body, counts, splits),
+        "pre_activations",
+        (splits * len(slices),),
+        [whole(piece) for piece in flat] + [weight_spec] * 2,
+        outs,
+        [whole(out) for out in outs],
+        [pltpu.VMEM((rows, hidden), jnp.float32)] * 2,
+        (4 * rows * hidden * gate.shape[0], 4 * hidden * gate.shape[0]),
+        (fsdp_index, *flat, gate, up),
+    )
+
+
+def hidden_grad_body(counts, me_ref, *refs):
+    total = sum(counts)
+    pieces, (down_ref, slope_ref, silu_ref) = refs[:total], refs[total : total + 3]
+    gate_ref, up_ref, grad_sum = refs[total + 3 :]
+    step = pl.program_id(0)
+
+    def add(index):
+        first = sum(counts[:index])
+        rows = stacked(pieces[first : first + counts[index]], 0, down_ref.shape[1])
+        grad = lax.dot_general(rows, down_ref[...], LAST, preferred_element_type=jnp.float32)
+        if index == 0:
+            grad_sum[...] = grad
+        else:
+            grad_sum[...] += grad
+
+    per_step(step, len(counts), add)
+
+    @pl.when(step == pl.num_programs(0) - 1)
+    def _():
+        grad = grad_sum[...]
+        gate_ref[...] = (grad * slope_ref[...]).astype(jnp.bfloat16)
+        up_ref[...] = (grad * silu_ref[...]).astype(jnp.bfloat16)
+
+
+def hidden_grads(fsdp_index, slices, down, slope, silu):
+    counts = [len(pieces) for pieces in slices]
+    flat = [piece for pieces in slices for piece in pieces]
+    rows, hidden = slope.shape
+    width = slices[0][0].shape[1]
+    out = jax.ShapeDtypeStruct((rows, hidden), jnp.bfloat16)
+    return call_kernel(
+        functools.partial(hidden_grad_body, counts),
+        "hidden_grads",
+        (len(slices),),
+        [whole(piece) for piece in flat]
+        + [pl.BlockSpec((hidden, width), lambda i, me: (0, me[0] ^ i)), whole(slope), whole(silu)],
+        [out] * 2,
+        [whole(out)] * 2,
+        [pltpu.VMEM((rows, hidden), jnp.float32)],
+        (2 * rows * down.size, 2 * down.size),
+        (fsdp_index, *flat, down, slope, silu),
+    )
+
+
+def store_pieces(index, order, pieces, refs, value):
+    start = 0
+    for piece, size in enumerate(pieces):
+        refs[order[index] * len(pieces) + piece][...] = value[start : start + size]
+        start += size
+
+
+def output_body(order, pieces, me_ref, hidden_ref, down_ref, *refs):
+    value = jnp.dot(hidden_ref[...], down_ref[...], preferred_element_type=jnp.float32)
+    value = value.astype(jnp.bfloat16)
+    per_step(
+        pl.program_id(0), len(order), lambda index: store_pieces(index, order, pieces, refs, value)
+    )
+
+
+def output_terms(fsdp_index, hidden, down, order, pieces):
+    rows, units = hidden.shape
+    width = down.shape[1] // len(order)
+    outs = [jax.ShapeDtypeStruct((size, width), jnp.bfloat16) for _ in order for size in pieces]
+    flip = order[0]
+    assert all(order[i] == i ^ flip for i in range(len(order)))
+    flat = call_kernel(
+        functools.partial(output_body, order, pieces),
+        "output_terms",
+        (len(order),),
+        [whole(hidden), pl.BlockSpec((units, width), lambda i, me: (0, me[0] ^ flip ^ i))],
+        outs,
+        [whole(out) for out in outs],
+        [],
+        (2 * rows * down.size, 2 * down.size + 2 * rows * down.shape[1]),
+        (fsdp_index, hidden, down),
+    )
+    return [flat[i * len(pieces) : (i + 1) * len(pieces)] for i in range(len(order))]
+
+
+def grad_term_body(order, pieces, me_ref, gate_grad_ref, up_grad_ref, gate_ref, up_ref, *refs):
+    value = lax.dot_general(
+        gate_grad_ref[...], gate_ref[...], LAST, preferred_element_type=jnp.float32
+    )
+    value = value + lax.dot_general(
+        up_grad_ref[...], up_ref[...], LAST, preferred_element_type=jnp.float32
+    )
+    value = value.astype(jnp.bfloat16)
+    per_step(
+        pl.program_id(0), len(order), lambda index: store_pieces(index, order, pieces, refs, value)
+    )
+
+
+def grad_terms(fsdp_index, gate_grad, up_grad, gate, up, order, pieces):
+    rows, units = gate_grad.shape
+    width = gate.shape[0] // len(order)
+    outs = [jax.ShapeDtypeStruct((size, width), jnp.bfloat16) for _ in order for size in pieces]
+    flip = order[0]
+    assert all(order[i] == i ^ flip for i in range(len(order)))
+    weight_spec = pl.BlockSpec((width, units), lambda i, me: (me[0] ^ flip ^ i, 0))
+    flat = call_kernel(
+        functools.partial(grad_term_body, order, pieces),
+        "grad_terms",
+        (len(order),),
+        [whole(gate_grad), whole(up_grad), weight_spec, weight_spec],
+        outs,
+        [whole(out) for out in outs],
+        [],
+        (4 * rows * gate.size, 4 * gate.size + 2 * rows * gate.shape[0]),
+        (fsdp_index, gate_grad, up_grad, gate, up),
+    )
+    return [flat[i * len(pieces) : (i + 1) * len(pieces)] for i in range(len(order))]
+
+
+def down_grad_body(counts, me_ref, hidden_ref, *refs):
+    pieces, out_ref = refs[:-1], refs[-1]
+
+    def multiply(index):
+        first = sum(counts[:index])
+        rows = stacked(pieces[first : first + counts[index]], 0, out_ref.shape[1])
+        out_ref[...] = lax.dot_general(
+            hidden_ref[...], rows, ROWS, preferred_element_type=jnp.float32
+        ).astype(jnp.bfloat16)
+
+    per_step(pl.program_id(0), len(counts), multiply)
+
+
+def down_grads(fsdp_index, hidden, slices):
+    counts = [len(pieces) for pieces in slices]
+    flat = [piece for pieces in slices for piece in pieces]
+    rows, units = hidden.shape
+    width = slices[0][0].shape[1]
+    full = width * len(slices)
+    return call_kernel(
+        functools.partial(down_grad_body, counts),
+        "down_grads",
+        (len(slices),),
+        [whole(hidden)] + [whole(piece) for piece in flat],
+        jax.ShapeDtypeStruct((units, full), jnp.bfloat16),
+        pl.BlockSpec((units, width), lambda i, me: (0, me[0] ^ i)),
+        [],
+        (2 * rows * units * full, 2 * (units + rows) * full),
+        (fsdp_index, hidden, *flat),
+    )
+
+
+def weight_grad_body(counts, me_ref, gate_grad_ref, up_grad_ref, *refs):
+    pieces, (gate_ref, up_ref) = refs[:-2], refs[-2:]
+
+    def multiply(index):
+        first = sum(counts[:index])
+        rows = stacked(pieces[first : first + counts[index]], 0, gate_ref.shape[0])
+        for grad_ref, out_ref in ((gate_grad_ref, gate_ref), (up_grad_ref, up_ref)):
+            out_ref[...] = lax.dot_general(
+                rows, grad_ref[...], ROWS, preferred_element_type=jnp.float32
+            ).astype(jnp.bfloat16)
+
+    per_step(pl.program_id(0), len(counts), multiply)
+
+
+def weight_grads(fsdp_index, slices, gate_grad, up_grad):
+    counts = [len(pieces) for pieces in slices]
+    flat = [piece for pieces in slices for piece in pieces]
+    rows, units = gate_grad.shape
+    width = slices[0][0].shape[1]
+    full = width * len(slices)
+    out = jax.ShapeDtypeStruct((full, units), jnp.bfloat16)
+    return call_kernel(
+        functools.partial(weight_grad_body, counts),
+        "weight_grads",
+        (len(slices),),
+        [whole(gate_grad), whole(up_grad)] + [whole(piece) for piece in flat],
+        [out] * 2,
+        [pl.BlockSpec((width, units), lambda i, me: (me[0] ^ i, 0))] * 2,
+        [],
+        (4 * rows * units * full, 2 * (2 * units + rows) * full),
+        (fsdp_index, gate_grad, up_grad, *flat),
+    )
+
+
+def gather_pair(first, second):
+    first_x = exchange(first, 1, "fsdp")
+    second_y = exchange(second, 2, "fsdp")
+    first_y = exchange(first, 2, "fsdp")
+    second_x = exchange(second, 1, "fsdp")
+    first_d = exchange(first_x, 2, "fsdp")
+    second_d = exchange(second_y, 1, "fsdp")
+    return [[first, second], [first_x, second_x], [first_y, second_y], [first_d, second_d]]
+
+
+def added(*terms):
+    return sum(term.astype(jnp.float32) for term in terms).astype(jnp.bfloat16)
+
+
+def reduce_pair(terms):
+    first_d = exchange(terms[3][0], 1, "fsdp")
+    second_d = exchange(terms[3][1], 2, "fsdp")
+    first_x = exchange(terms[1][0], 1, "fsdp")
+    second_y = exchange(terms[2][1], 2, "fsdp")
+    first_y = exchange(added(terms[2][0], first_d), 2, "fsdp")
+    second_x = exchange(added(terms[1][1], second_d), 1, "fsdp")
+    return added(terms[0][0], first_x, first_y), added(terms[0][1], second_y, second_x)
+
+
+def to_experts(even, odd, slots):
+    count = even.shape[0] // slots
+    other = exchange(odd, 1, "ep")
+    pairs = []
+    for step in range(count):
+        part = slice(step * slots, (step + 1) * slots)
+        pairs.append(jnp.concatenate([even[part], other[part]], axis=0))
+    return [pairs[0]] + [exchange(pairs[step], 2 * step, "ep") for step in range(1, count)]
+
+
+def to_groups(pairs, slots):
+    back = [pairs[0]] + [exchange(pair, 2 * step, "ep") for step, pair in enumerate(pairs) if step]
+    odd = jnp.concatenate([pair[slots:] for pair in back], axis=0)
+    other = exchange(odd, 1, "ep")
+    layout = []
+    for step in range(len(pairs)):
+        layout += [(step, 0), (len(pairs), step)]
+    return back + [other], layout
+
+
+def by_links(tokens, cotangent, gate_weight, up_weight, down_weight, chosen, counts, gate_prob):
+    experts, _, slots = chosen.shape
+    length = tokens.shape[0]
+    ep_index = lax.axis_index("ep").reshape(1)
+    fsdp_index = lax.axis_index("fsdp").reshape(1)
+    gate, up, down = gate_weight[0], up_weight[0], down_weight[0]
+    token_even, token_odd, grad_even, grad_odd = pick_slots(
+        ep_index, chosen, counts, gate_prob, tokens, cotangent
+    )
+    pairs = to_experts(token_even, token_odd, slots)
+    near = gather_pair(pairs[0], pairs[1])
+    far = gather_pair(pairs[2], pairs[3])
+    token_slices = [a + b for a, b in zip(near, far)]
+    grad_pairs = to_experts(grad_even, grad_odd, slots)
+    grad_slices = gather_pair(
+        jnp.concatenate(grad_pairs[:2], axis=0), jnp.concatenate(grad_pairs[2:], axis=0)
+    )
+    hidden, slope, silu = pre_activations(fsdp_index, token_slices, gate, up)
+    half = experts // 2 * slots
+    order = (3, 2, 1, 0)
+    terms = output_terms(fsdp_index, hidden, down, order, (half, half))
+    near_rows, far_rows = reduce_pair(terms)
+    two = 2 * slots
+    pieces, layout = to_groups(
+        [near_rows[:two], near_rows[two:], far_rows[:two], far_rows[two:]], slots
+    )
+    mixture = spread_rows(ep_index, chosen, counts, gate_prob, pieces, layout, True, length)
+    gate_grad, up_grad = hidden_grads(fsdp_index, grad_slices, down, slope, silu)
+    terms = grad_terms(fsdp_index, gate_grad, up_grad, gate, up, order, (half, half))
+    near_rows, far_rows = reduce_pair(terms)
+    pieces, layout = to_groups(
+        [near_rows[:two], near_rows[two:], far_rows[:two], far_rows[two:]], slots
+    )
+    grad_tokens = spread_rows(ep_index, chosen, counts, gate_prob, pieces, layout, False, length)
+    grad_down = down_grads(fsdp_index, hidden, grad_slices)
+    grad_gate, grad_up = weight_grads(fsdp_index, token_slices, gate_grad, up_grad)
+    return mixture, grad_tokens, grad_gate[None], grad_up[None], grad_down[None]
+
+
 def solution(mesh):
     placed = (
         P("ep", "fsdp"),
@@ -115,8 +576,13 @@
         P(None, "ep"),
         P(None, "ep", None),
     )
+
+    def per_part(*arrays):
+        fits = mesh.shape["fsdp"] == 4 and mesh.shape["ep"] == 8 and arrays[0].shape[1] % 128 == 0
+        return (by_links if fits else by_collectives)(*arrays)
+
     return jax.shard_map(
-        per_device,
+        per_part,
         mesh=mesh,
         in_specs=placed,
         out_specs=(

time: 223 us -> 171 us (0.77)
  waiting for transfers between devices: 89.2 us -> 32.1 us
  matrix products: 50.4 us -> 0 us
  starting transfers between devices: 10.7 us -> 58.9 us
  Pallas kernels: 0 us -> 44 us
  blocking collectives: 36.5 us -> 0 us
  local copies, waits for them, and re-layouts: 4.06 us -> 33 us
  other arithmetic: 17.6 us -> 0.7 us
  between operations: 13.9 us -> 1.26 us
    ppermute x0 -> x46, starting transfers between devices: none -> 58.9 us  [exchange(): return lax.ppermute(array, axis, [(i, i ^ distance) for i in range(size)])]
    dot_general x9 -> x0, matrix products: 50.4 us -> none  [the longest x1 7.13 us: per_device(): lax.dot_general(grad_pre_up, up_local, contract_last, preferred_element_t...]
    reduce_scatter x2 -> x0, waiting for transfers between devices: 50.3 us -> none  [send_back(): lax.psum_scatter(term.astype(jnp.bfloat16), 'fsdp', scatter_dimension=1,...]
    pallas_call x0 -> x9, Pallas kernels: none -> 44 us  [call_kernel(): pl.pallas_call(body, name=name, out_shape=outs, grid_spec=pltpu.PrefetchS...]
    all_gather x2 -> x0, waiting for transfers between devices: 38.8 us -> none  [the longest x1 25.9 us: per_device(): lax.all_gather(sliced_grads, 'fsdp', axis=2, tiled=True)]
    all_to_all x2 -> x0, blocking collectives: 36.5 us -> none  [the longest x1 19.4 us: per_device(): lax.all_to_all(picked_tokens, 'ep', split_axis=0, concat_axis=0, tiled=True)]
    ppermute x0 -> x46, waiting for transfers between devices: none -> 32.1 us  [exchange(): return lax.ppermute(array, axis, [(i, i ^ distance) for i in range(size)])]
    unnamed x14 -> x120, local copies, waits for them, and re-layouts: 1.06 us -> 32.2 us
  transfers between devices with their start and end apart: 6 -> 46, of which waited for: 4 -> 16; matrix products, arithmetic and copies ran while one was open for 22% -> 1% of each run, Pallas kernels for 0% -> 23%
where the time goes in v1:
time: 171 us; the launch traced here: 170 us
  starting transfers between devices  58.9 us (34%)
  Pallas kernels  44 us (26%)
  local copies, waits for them, and re-layouts  33 us (19%)
  waiting for transfers between devices  32.1 us (19%)
    ppermute x46, starting transfers between devices, exchange(): return lax.ppermute(array, axis, [(i, i ^ distance) for i in range(size)])  58.9 us
    pallas_call x9, Pallas kernels, call_kernel(): pl.pallas_call(body, name=name, out_shape=outs, grid_spec=pltpu.PrefetchS...  44 us
    unnamed x120, local copies, waits for them, and re-layouts  32.2 us
    ppermute x46, waiting for transfers between devices, exchange(): return lax.ppermute(array, axis, [(i, i ^ distance) for i in range(size)])  32.1 us
  transfers between devices with their start and end apart: 46, of which 16 were waited for; matrix products, arithmetic and copies ran while one was open for 1% of the time, Pallas kernels for 23%

profile of v1, /device:TPU:1, one launch (start us, length us, event | category | flops | bytes accessed | tf_op | source)
XLA Modules:
  0.0 170.0 jit_solution(14500966984917295944)
XLA Ops:
  1.4 1.5 copy-done.1
  2.9 1.5 copy-done.2
  5.7 2.0 %pick_slots.1 = (bf16[64,1792]{1,0:T(8,128)(2,1)S(1)}, bf16[64,1792]{1,0:T(8,128)(2,1)S(1)}, bf16[64,1792]{1,0:T(8,128)(2,1)S(1)}, bf16[64,1792]{1,0:T(8,128)(2,1)S(1)}) custom-call(s32[1]{0:T(128)} %bitcast.me_ref, s32[8,1]{1,0:T(8,128)S(1)} %copy.14.counts_ref, s32[8,1,16]{2,1,0:T(1,128)S(1)} %copy-done.51, f32[8,1,16]{2,1,0:T(1,128)S(1)} %copy-done.53, ...), custom_call_target="tpu_custom_call" | custom-call | flops 469762048 | bytes 5505024 | tf_op jit(solution)/shard_map/pick_slots/pallas_call | solution.py:116
  8.4 0.9 collective-permute-done
  9.4 4.5 %collective-permute-start.3 = (bf16[32,1792]{1,0:T(8,128)(2,1)S(1)}, bf16[32,1792]{1,0:T(8,128)(2,1)S(1)}, u32[]{:S(2)}, u32[]{:S(2)}) collective-permute-start(bf16[32,1792]{1,0:T(8,128)(2,1)S(1)} %pad_maximum_fusion.6), channel_id=1, source_target_pairs={{0,6},{1,7},{2,4},{3,5},{4,2},{5,3},{6,0},{7,1},{8,14},{9,15},{10,... | collective-permute-start | bytes 344072 | tf_op jit(solution)/shard_map/ppermute | solution.py:139
  14.4 1.3 collective-permute-start.4
  15.7 1.2 collective-permute-start.27
  17.0 7.8 %collective-permute-done.27 = bf16[32,1792]{1,0:T(8,128)(2,1)S(1)} collective-permute-done((bf16[32,1792]{1,0:T(8,128)(2,1)S(1)}, bf16[32,1792]{1,0:T(8,128)(2,1)S(1)}, u32[]{:S(2)}, u32[]{:S(2)}) %collective-permute-start.27) | collective-permute-done | bytes 114720 | tf_op jit(solution)/shard_map/ppermute | solution.py:139
  24.7 1.4 collective-permute-start.28
  26.1 6.0 %collective-permute-done.28 = bf16[32,1792]{1,0:T(8,128)(2,1)S(1)} collective-permute-done((bf16[32,1792]{1,0:T(8,128)(2,1)S(1)}, bf16[32,1792]{1,0:T(8,128)(2,1)S(1)}, u32[]{:S(2)}, u32[]{:S(2)}) %collective-permute-start.28) | collective-permute-done | bytes 114720 | tf_op jit(solution)/shard_map/ppermute | solution.py:139
  32.2 3.3 %collective-permute-start.29 = (bf16[32,1792]{1,0:T(8,128)(2,1)S(1)}, bf16[32,1792]{1,0:T(8,128)(2,1)S(1)}, u32[]{:S(2)}, u32[]{:S(2)}) collective-permute-start(bf16[32,1792]{1,0:T(8,128)(2,1)S(1)} %pad_maximum_fusion.9), channel_id=1, source_target_pairs={{0,6},{1,7},{2,4},{3,5},{4,2},{5,3},{6,0},{7,1},{8,14},{9,15},{10,... | collective-permute-start | bytes 344072 | tf_op jit(solution)/shard_map/ppermute | solution.py:139
  36.1 1.2 collective-permute-start.8
  37.6 1.2 collective-permute-start.6
  38.8 1.2 collective-permute-start.9
  42.6 1.2 collective-permute-start.10
  44.1 1.0 collective-permute-done.9.refs_9_
  45.1 1.2 collective-permute-start.30
  46.3 1.2 collective-permute-done.12.refs_12_
  48.1 1.2 collective-permute-start.5
  52.2 1.2 collective-permute-start.14
  54.6 0.7 collective-permute-start.13
  55.3 1.1 collective-permute-done.15.refs_15_
  57.3 1.2 collective-permute-start.32
  58.5 1.3 collective-permute-start.35
  60.1 3.1 %copy-done = bf16[1,7168,512]{2,1,0:T(8,128)(2,1)S(1)} copy-done((bf16[1,7168,512]{2,1,0:T(8,128)(2,1)S(1)}, bf16[1,7168,512]{2,1,0:T(8,128)(2,1)}, u32[]{:S(2)}) %copy-start) | copy-done | bytes 7340056
  63.2 0.9 copy-done.15
  64.1 0.9 copy-done.22
  65.0 0.9 copy-done.25
  65.9 0.9 copy-done.28
  66.8 0.9 copy-done.31
  67.7 0.9 copy-done.34
  68.6 0.9 copy-done.37
  69.5 0.9 copy-done.40
  70.4 0.9 copy-done.43
  71.3 0.9 copy-done.46
  72.2 0.9 copy-done.49
  73.1 7.7 %pre_activations.1 = (bf16[128,512]{1,0:T(8,128)(2,1)S(1)}, f32[128,512]{1,0:T(8,128)S(1)}, f32[128,512]{1,0:T(8,128)S(1)}) custom-call(s32[1]{0:T(128)} %bitcast.1.me_ref, bf16[32,1792]{1,0:T(8,128)(2,1)S(1)} %copy-done.15, bf16[32,1792]{1,0:T(8,128)(2,1)S(1)} %copy-done.28, bf16[32,1792]{1,0:T(8,128)(2,1)S(1)} %copy-done.25, ...), custom_call_target="tpu_custom_call" | custom-call | flops 1879048192 | bytes 14680064 | tf_op jit(solution)/shard_map/pre_activations/pallas_call | solution.py:116
  81.5 2.4 %output_terms.1 = (bf16[64,1792]{1,0:T(8,128)(2,1)S(1)}, bf16[64,1792]{1,0:T(8,128)(2,1)S(1)}, bf16[64,1792]{1,0:T(8,128)(2,1)S(1)}, bf16[64,1792]{1,0:T(8,128)(...) custom-call(s32[1]{0:T(128)} %bitcast.1.me_ref, ...), custom_call_target="tpu_custom_call" | custom-call | flops 939524096 | bytes 9175040 | tf_op jit(solution)/shard_map/output_terms/pallas_call | solution.py:116
  84.0 1.3 collective-permute-start.21
  88.3 0.7 collective-permute-start.16
  89.8 0.9 copy-done.4
  90.7 0.9 copy-done.7
  91.6 0.9 copy-done.10
  92.6 0.9 copy-done.12
  93.5 0.9 copy-done.20
  94.5 4.7 %hidden_grads.1 = (bf16[128,512]{1,0:T(8,128)(2,1)S(1)}, bf16[128,512]{1,0:T(8,128)(2,1)S(1)}) custom-call(s32[1]{0:T(128)} %bitcast.1.me_ref, bf16[64,1792]{1,0:T(8,128)(2,1)S(1)} %pad_maximum_fusion.1.refs_0_, bf16[64,1792]{1,0:T(8,128)(2,1)} %constant_dynamic-update-slice_fusion.refs_1_, bf16[64,1792]{1,0:T(8,128)(2,1)} %collective-permute-done.30.refs_2_, ...), custom_call_target="tpu_custom_call" | custom-call | flops 939524096 | bytes 7340032 | tf_op jit(solution)/shard_map/hidden_grads/pallas_call | solution.py:116
  99.2 7.2 %grad_terms.1 = (bf16[64,1792]{1,0:T(8,128)(2,1)S(1)}, bf16[64,1792]{1,0:T(8,128)(2,1)S(1)}, bf16[64,1792]{1,0:T(8,128)(2,1)S(1)}, bf16[64,1792]{1,0:T(8,128)(2,...) custom-call(s32[1]{0:T(128)} %bitcast.1.me_ref, ...), custom_call_target="tpu_custom_call" | custom-call | flops 1879048192 | bytes 16515072 | tf_op jit(solution)/shard_map/grad_terms/pallas_call | solution.py:116
  106.4 1.3 collective-permute-start.41
  108.0 0.8 collective-permute-start.37
  108.9 2.5 %collective-permute-done.41 = bf16[64,1792]{1,0:T(8,128)(2,1)S(1)} collective-permute-done((bf16[64,1792]{1,0:T(8,128)(2,1)S(1)}, bf16[64,1792]{1,0:T(8,128)(2,1)S(1)}, u32[]{:S(2)}, u32[]{:S(2)}) %collective-permute-start.41) | collective-permute-done | bytes 229408 | tf_op jit(solution)/shard_map/ppermute | solution.py:139
  112.2 1.1 collective-permute-start.18
  113.2 3.3 %collective-permute-done.22 = bf16[64,1792]{1,0:T(8,128)(2,1)S(1)} collective-permute-done((bf16[64,1792]{1,0:T(8,128)(2,1)S(1)}, bf16[64,1792]{1,0:T(8,128)(2,1)S(1)}, u32[]{:S(2)}, u32[]{:S(2)}) %collective-permute-start.22) | collective-permute-done | bytes 229408 | tf_op jit(solution)/shard_map/ppermute | solution.py:139
  117.5 1.8 %collective-permute-done.18 = bf16[64,1792]{1,0:T(8,128)(2,1)S(1)} collective-permute-done((bf16[64,1792]{1,0:T(8,128)(2,1)S(1)}, bf16[64,1792]{1,0:T(8,128)(2,1)S(1)}, u32[]{:S(2)}, u32[]{:S(2)}) %collective-permute-start.18) | collective-permute-done | bytes 229408 | tf_op jit(solution)/shard_map/ppermute | solution.py:139
  119.3 1.8 %collective-permute-start.24 = (bf16[32,1792]{1,0:T(8,128)(2,1)S(1)}, bf16[32,1792]{1,0:T(8,128)(2,1)S(1)}, u32[]{:S(2)}, u32[]{:S(2)}) collective-permute-start(bf16[32,1792]{1,0:T(8,128)(2,1)S(1)} %get-tuple-element.71), channel_id=1, source_target_pairs={{0,6},{1,7},{2,4},{3,5},{4,2},{5,3},{6,0},{7,1},{8,14},{9,15},{10,... | collective-permute-start | bytes 344072 | tf_op jit(solution)/shard_map/ppermute | solution.py:139
  121.5 1.2 collective-permute-done.23.refs_2_
  123.1 1.8 %collective-permute-done.24.refs_3_ = bf16[32,1792]{1,0:T(8,128)(2,1)S(1)} collective-permute-done((bf16[32,1792]{1,0:T(8,128)(2,1)S(1)}, bf16[32,1792]{1,0:T(8,128)(2,1)S(1)}, u32[]{:S(2)}, u32[]{:S(2)}) %collective-permute-start.24) | collective-permute-done | bytes 114720 | tf_op jit(solution)/shard_map/ppermute | solution.py:139
  126.9 1.4 collective-permute-start.44
  128.3 1.8 %collective-permute-done.38 = bf16[64,1792]{1,0:T(8,128)(2,1)S(1)} collective-permute-done((bf16[64,1792]{1,0:T(8,128)(2,1)S(1)}, bf16[64,1792]{1,0:T(8,128)(2,1)S(1)}, u32[]{:S(2)}, u32[]{:S(2)}) %collective-permute-start.38) | collective-permute-done | bytes 229408 | tf_op jit(solution)/shard_map/ppermute | solution.py:139
  130.8 15.8 %collective-permute-start.25 = (bf16[64,1792]{1,0:T(8,128)(2,1)S(1)}, bf16[64,1792]{1,0:T(8,128)(2,1)S(1)}, u32[]{:S(2)}, u32[]{:S(2)}) collective-permute-start(bf16[64,1792]{1,0:T(8,128)(2,1)S(1)} %pad_maximum_fusion), channel_id=1, source_target_pairs={{0,1},{1,0},{2,3},{3,2},{4,5},{5,4},{6,7},{7,6},{8,9},{9,8},{10,11... | collective-permute-start | bytes 688136 | tf_op jit(solution)/shard_map/ppermute | solution.py:139
  146.8 3.2 %collective-permute-start.45 = (bf16[64,1792]{1,0:T(8,128)(2,1)S(1)}, bf16[64,1792]{1,0:T(8,128)(2,1)S(1)}, u32[]{:S(2)}, u32[]{:S(2)}) collective-permute-start(bf16[64,1792]{1,0:T(8,128)(2,1)S(1)} %pad_maximum_fusion.2), channel_id=1, source_target_pairs={{0,1},{1,0},{2,3},{3,2},{4,5},{5,4},{6,7},{7,6},{8,9},{9,8},{10,11... | collective-permute-start | bytes 688136 | tf_op jit(solution)/shard_map/ppermute | solution.py:139
  150.0 5.9 %down_grads.1 = bf16[512,7168]{1,0:T(8,128)(2,1)} custom-call(s32[1]{0:T(128)} %bitcast.1.me_ref, bf16[128,512]{1,0:T(8,128)(2,1)S(1)} %get-tuple-element.34.hidden_ref, bf16[64,1792]{1,0:T(8,128)(2,1)S(1)} %pad_maximum_fusion.1.refs_0_, bf16[64,1792]{1,0:T(8,128)(2,1)} %constant_dynamic-update-slice_fusion.refs_1_, ...), custom_call_target="tpu_custom_call" | custom-call | flops 939524096 | bytes 9175040 | tf_op jit(solution)/shard_map/down_grads/pallas_call | solution.py:116
  155.9 8.3 %weight_grads.1 = (bf16[7168,512]{1,0:T(8,128)(2,1)}, bf16[7168,512]{1,0:T(8,128)(2,1)}) custom-call(s32[1]{0:T(128)} %bitcast.1.me_ref, bf16[128,512]{1,0:T(8,128)(2,1)S(1)} %get-tuple-element.47.gate_grad_ref, bf16[128,512]{1,0:T(8,128)(2,1)S(1)} %get-tuple-element.48.up_grad_ref, bf16[32,1792]{1,0:T(8,128)(2,1)S(1)} %copy-done.16, ...), custom_call_target="tpu_custom_call" | custom-call | flops 1879048192 | bytes 16515072 | tf_op jit(solution)/shard_map/weight_grads/pallas_call | solution.py:116
  164.2 3.0 %spread_rows.2 = bf16[512,1792]{1,0:T(8,128)(2,1)} custom-call(s32[1]{0:T(128)} %bitcast.me_ref, s32[8,1]{1,0:T(8,128)S(1)} %copy.14.counts_ref, s32[8,1,16]{2,1,0:T(1,128)S(1)} %copy-done.52, f32[8,1,16]{2,1,0:T(1,128)S(1)} %copy-done.54, bf16[32,1792]{1,0:T(8,128)(2,1)S(1)} %get-tuple-element.74.refs_0_, ...), custom_call_target="tpu_custom_call" | custom-call | flops 469762048 | bytes 2752512 | tf_op jit(solution)/shard_map/spread_rows/pallas_call | solution.py:116
  167.2 2.8 %spread_rows.3 = bf16[512,1792]{1,0:T(8,128)(2,1)} custom-call(s32[1]{0:T(128)} %bitcast.me_ref, s32[8,1]{1,0:T(8,128)S(1)} %copy.14.counts_ref, s32[8,1,16]{2,1,0:T(1,128)S(1)} %copy-done.52, f32[8,1,16]{2,1,0:T(1,128)S(1)} %copy-done.54, bf16[32,1792]{1,0:T(8,128)(2,1)S(1)} %get-tuple-element.62.refs_0_, ...), custom_call_target="tpu_custom_call" | custom-call | flops 469762048 | bytes 2752512 | tf_op jit(solution)/shard_map/spread_rows/pallas_call | solution.py:116
  (193 shorter events, 22.7 us)
Async XLA Ops:
  5.7 75.8 %slice-start.2 = ((s8[7340032]{0:T(1024)(128)(4,1)}), s8[3145728]{0:T(1024)(128)(4,1)S(1)}, s32[]{:S(2)}) async-start(s8[7340032]{0:T(1024)(128)(4,1)} %bitcast.12), calls=%async_computation.2 | async-start | bytes 6291456
  7.8 1.6 collective-permute-start
  7.9 7.8 %collective-permute-start.26 = (bf16[64,1792]{1,0:T(8,128)(2,1)S(1)}, bf16[64,1792]{1,0:T(8,128)(2,1)S(1)}, u32[]{:S(2)}, u32[]{:S(2)}) collective-permute-start(bf16[64,1792]{1,0:T(8,128)(2,1)S(1)} %get-tuple-element.44), channel_id=1, source_target_pairs={{0,1},{1,0},{2,3},{3,2},{4,5},{5,4},{6,7},{7,6},{8,9},{9,8},{10,11... | collective-permute-start | bytes 688136 | tf_op jit(solution)/shard_map/ppermute | solution.py:139
  9.4 26.7 %collective-permute-start.3 = (bf16[32,1792]{1,0:T(8,128)(2,1)S(1)}, bf16[32,1792]{1,0:T(8,128)(2,1)S(1)}, u32[]{:S(2)}, u32[]{:S(2)}) collective-permute-start(bf16[32,1792]{1,0:T(8,128)(2,1)S(1)} %pad_maximum_fusion.6), channel_id=1, source_target_pairs={{0,6},{1,7},{2,4},{3,5},{4,2},{5,3},{6,0},{7,1},{8,14},{9,15},{10,... | collective-permute-start | bytes 344072 | tf_op jit(solution)/shard_map/ppermute | solution.py:139
  13.9 23.5 %collective-permute-start.2 = (bf16[32,1792]{1,0:T(8,128)(2,1)S(1)}, bf16[32,1792]{1,0:T(8,128)(2,1)S(1)}, u32[]{:S(2)}, u32[]{:S(2)}) collective-permute-start(bf16[32,1792]{1,0:T(8,128)(2,1)S(1)} %pad_maximum_fusion.5), channel_id=1, source_target_pairs={{0,4},{1,5},{2,6},{3,7},{4,0},{5,1},{6,2},{7,3},{8,12},{9,13},{10,... | collective-permute-start | bytes 344072 | tf_op jit(solution)/shard_map/ppermute | solution.py:139
  14.0 23.6 %collective-permute-start.1 = (bf16[32,1792]{1,0:T(8,128)(2,1)S(1)}, bf16[32,1792]{1,0:T(8,128)(2,1)S(1)}, u32[]{:S(2)}, u32[]{:S(2)}) collective-permute-start(bf16[32,1792]{1,0:T(8,128)(2,1)S(1)} %pad_maximum_fusion.4), channel_id=1, source_target_pairs={{0,2},{1,3},{2,0},{3,1},{4,6},{5,7},{6,4},{7,5},{8,10},{9,11},{10,... | collective-permute-start | bytes 344072 | tf_op jit(solution)/shard_map/ppermute | solution.py:139
  14.4 29.8 %copy-start.14 = (bf16[32,1792]{1,0:T(8,128)(2,1)}, bf16[32,1792]{1,0:T(8,128)(2,1)S(1)}, u32[]{:S(2)}) copy-start(bf16[32,1792]{1,0:T(8,128)(2,1)S(1)} %pad_maximum_fusion.3.refs_0_) | copy-start | bytes 344068
  14.4 24.5 %collective-permute-start.4 = (bf16[32,1792]{1,0:T(8,128)(2,1)S(1)}, bf16[32,1792]{1,0:T(8,128)(2,1)S(1)}, u32[]{:S(2)}, u32[]{:S(2)}) collective-permute-start(bf16[32,1792]{1,0:T(8,128)(2,1)S(1)} %pad_maximum_fusion.3.refs_0_), channel_id=1, source_target_pairs={{0,8},{8,0},{16,24},{24,16},{1,9},{9,1},{17,25},{25,17},{2,10},{10... | collective-permute-start | bytes 344072 | tf_op jit(solution)/shard_map/ppermute | solution.py:139
  15.7 9.0 %collective-permute-start.27 = (bf16[32,1792]{1,0:T(8,128)(2,1)S(1)}, bf16[32,1792]{1,0:T(8,128)(2,1)S(1)}, u32[]{:S(2)}, u32[]{:S(2)}) collective-permute-start(bf16[32,1792]{1,0:T(8,128)(2,1)S(1)} %pad_maximum_fusion.7), channel_id=1, source_target_pairs={{0,2},{1,3},{2,0},{3,1},{4,6},{5,7},{6,4},{7,5},{8,10},{9,11},{10,... | collective-permute-start | bytes 344072 | tf_op jit(solution)/shard_map/ppermute | solution.py:139
  24.7 7.4 %collective-permute-start.28 = (bf16[32,1792]{1,0:T(8,128)(2,1)S(1)}, bf16[32,1792]{1,0:T(8,128)(2,1)S(1)}, u32[]{:S(2)}, u32[]{:S(2)}) collective-permute-start(bf16[32,1792]{1,0:T(8,128)(2,1)S(1)} %pad_maximum_fusion.8), channel_id=1, source_target_pairs={{0,4},{1,5},{2,6},{3,7},{4,0},{5,1},{6,2},{7,3},{8,12},{9,13},{10,... | collective-permute-start | bytes 344072 | tf_op jit(solution)/shard_map/ppermute | solution.py:139
  32.2 7.9 %collective-permute-start.29 = (bf16[32,1792]{1,0:T(8,128)(2,1)S(1)}, bf16[32,1792]{1,0:T(8,128)(2,1)S(1)}, u32[]{:S(2)}, u32[]{:S(2)}) collective-permute-start(bf16[32,1792]{1,0:T(8,128)(2,1)S(1)} %pad_maximum_fusion.9), channel_id=1, source_target_pairs={{0,6},{1,7},{2,4},{3,5},{4,2},{5,3},{6,0},{7,1},{8,14},{9,15},{10,... | collective-permute-start | bytes 344072 | tf_op jit(solution)/shard_map/ppermute | solution.py:139
  36.1 5.5 %collective-permute-start.8 = (bf16[32,1792]{1,0:T(8,128)(2,1)S(1)}, bf16[32,1792]{1,0:T(8,128)(2,1)S(1)}, u32[]{:S(2)}, u32[]{:S(2)}) collective-permute-start(bf16[32,1792]{1,0:T(8,128)(2,1)S(1)} %pad_maximum_fusion.3.refs_0_), channel_id=1, source_target_pairs={{0,16},{8,24},{16,0},{24,8},{1,17},{9,25},{17,1},{25,9},{2,18},{10... | collective-permute-start | bytes 344072 | tf_op jit(solution)/shard_map/ppermute | solution.py:139
  37.4 5.3 %collective-permute-start.11 = (bf16[32,1792]{1,0:T(8,128)(2,1)S(1)}, bf16[32,1792]{1,0:T(8,128)(2,1)S(1)}, u32[]{:S(2)}, u32[]{:S(2)}) collective-permute-start(bf16[32,1792]{1,0:T(8,128)(2,1)S(1)} %collective-permute-done.3.refs_3_), channel_id=1, source_target_pairs={{0,16},{8,24},{16,0},{24,8},{1,17},{9,25},{17,1},{25,9},{2,18},{10... | collective-permute-start | bytes 344072 | tf_op jit(solution)/shard_map/ppermute | solution.py:139
  37.6 6.2 %collective-permute-start.6 = (bf16[32,1792]{1,0:T(8,128)(2,1)S(1)}, bf16[32,1792]{1,0:T(8,128)(2,1)}, u32[]{:S(2)}, u32[]{:S(2)}) collective-permute-start(bf16[32,1792]{1,0:T(8,128)(2,1)S(1)} %collective-permute-done.2.refs_2_), channel_id=1, source_target_pairs={{0,8},{8,0},{16,24},{24,16},{1,9},{9,1},{17,25},{25,17},{2,10},{10... | collective-permute-start | bytes 344072 | tf_op jit(solution)/shard_map/ppermute | solution.py:139
  38.8 6.3 %collective-permute-start.9 = (bf16[32,1792]{1,0:T(8,128)(2,1)S(1)}, bf16[32,1792]{1,0:T(8,128)(2,1)}, u32[]{:S(2)}, u32[]{:S(2)}) collective-permute-start(bf16[32,1792]{1,0:T(8,128)(2,1)S(1)} %collective-permute-done.1.refs_1_), channel_id=1, source_target_pairs={{0,16},{8,24},{16,0},{24,8},{1,17},{9,25},{17,1},{25,9},{2,18},{10... | collective-permute-start | bytes 344072 | tf_op jit(solution)/shard_map/ppermute | solution.py:139
  40.1 7.5 %collective-permute-start.12 = (bf16[32,1792]{1,0:T(8,128)(2,1)S(1)}, bf16[32,1792]{1,0:T(8,128)(2,1)S(1)}, u32[]{:S(2)}, u32[]{:S(2)}) collective-permute-start(bf16[32,1792]{1,0:T(8,128)(2,1)S(1)} %collective-permute-done.4.refs_4_), channel_id=1, source_target_pairs={{0,16},{8,24},{16,0},{24,8},{1,17},{9,25},{17,1},{25,9},{2,18},{10... | collective-permute-start | bytes 344072 | tf_op jit(solution)/shard_map/ppermute | solution.py:139
  42.2 7.8 %collective-permute-start.7 = (bf16[32,1792]{1,0:T(8,128)(2,1)S(1)}, bf16[32,1792]{1,0:T(8,128)(2,1)S(1)}, u32[]{:S(2)}, u32[]{:S(2)}) collective-permute-start(bf16[32,1792]{1,0:T(8,128)(2,1)S(1)} %collective-permute-done.3.refs_3_), channel_id=1, source_target_pairs={{0,8},{8,0},{16,24},{24,16},{1,9},{9,1},{17,25},{25,17},{2,10},{10... | collective-permute-start | bytes 344072 | tf_op jit(solution)/shard_map/ppermute | solution.py:139
  42.6 8.9 %collective-permute-start.10 = (bf16[32,1792]{1,0:T(8,128)(2,1)S(1)}, bf16[32,1792]{1,0:T(8,128)(2,1)S(1)}, u32[]{:S(2)}, u32[]{:S(2)}) collective-permute-start(bf16[32,1792]{1,0:T(8,128)(2,1)S(1)} %collective-permute-done.2.refs_2_), channel_id=1, source_target_pairs={{0,16},{8,24},{16,0},{24,8},{1,17},{9,25},{17,1},{25,9},{2,18},{10... | collective-permute-start | bytes 344072 | tf_op jit(solution)/shard_map/ppermute | solution.py:139
  43.8 14.7 %collective-permute-start.33 = (bf16[64,1792]{1,0:T(8,128)(2,1)}, bf16[64,1792]{1,0:T(8,128)(2,1)}, u32[]{:S(2)}, u32[]{:S(2)}) collective-permute-start(bf16[64,1792]{1,0:T(8,128)(2,1)} %constant_dynamic-update-slice_fusion.refs_1_), channel_id=1, source_target_pairs={{0,16},{8,24},{16,0},{24,8},{1,17},{9,25},{17,1},{25,9},{2,18},{10... | collective-permute-start | bytes 688136 | tf_op jit(solution)/shard_map/ppermute | solution.py:139
  45.1 14.7 %collective-permute-start.30 = (bf16[64,1792]{1,0:T(8,128)(2,1)S(1)}, bf16[64,1792]{1,0:T(8,128)(2,1)}, u32[]{:S(2)}, u32[]{:S(2)}) collective-permute-start(bf16[64,1792]{1,0:T(8,128)(2,1)S(1)} %pad_maximum_fusion.1.refs_0_), channel_id=1, source_target_pairs={{0,8},{8,0},{16,24},{24,16},{1,9},{9,1},{17,25},{25,17},{2,10},{10... | collective-permute-start | bytes 688136 | tf_op jit(solution)/shard_map/ppermute | solution.py:139
  48.1 5.8 %collective-permute-start.5 = (bf16[32,1792]{1,0:T(8,128)(2,1)S(1)}, bf16[32,1792]{1,0:T(8,128)(2,1)S(1)}, u32[]{:S(2)}, u32[]{:S(2)}) collective-permute-start(bf16[32,1792]{1,0:T(8,128)(2,1)S(1)} %collective-permute-done.1.refs_1_), channel_id=1, source_target_pairs={{0,8},{8,0},{16,24},{24,16},{1,9},{9,1},{17,25},{25,17},{2,10},{10... | collective-permute-start | bytes 344072 | tf_op jit(solution)/shard_map/ppermute | solution.py:139
  50.7 5.7 %collective-permute-start.15 = (bf16[32,1792]{1,0:T(8,128)(2,1)S(1)}, bf16[32,1792]{1,0:T(8,128)(2,1)}, u32[]{:S(2)}, u32[]{:S(2)}) collective-permute-start(bf16[32,1792]{1,0:T(8,128)(2,1)S(1)} %collective-permute-done.11.refs_11_), channel_id=1, source_target_pairs={{0,8},{8,0},{16,24},{24,16},{1,9},{9,1},{17,25},{25,17},{2,10},{10... | collective-permute-start | bytes 344072 | tf_op jit(solution)/shard_map/ppermute | solution.py:139
  52.2 5.0 %collective-permute-start.14 = (bf16[32,1792]{1,0:T(8,128)(2,1)}, bf16[32,1792]{1,0:T(8,128)(2,1)}, u32[]{:S(2)}, u32[]{:S(2)}) collective-permute-start(bf16[32,1792]{1,0:T(8,128)(2,1)} %collective-permute-done.6.refs_6_), channel_id=1, source_target_pairs={{0,16},{8,24},{16,0},{24,8},{1,17},{9,25},{17,1},{25,9},{2,18},{10... | collective-permute-start | bytes 344072 | tf_op jit(solution)/shard_map/ppermute | solution.py:139
  54.6 5.5 %collective-permute-start.13 = (bf16[32,1792]{1,0:T(8,128)(2,1)}, bf16[32,1792]{1,0:T(8,128)(2,1)}, u32[]{:S(2)}, u32[]{:S(2)}) collective-permute-start(bf16[32,1792]{1,0:T(8,128)(2,1)} %collective-permute-done.9.refs_9_), channel_id=1, source_target_pairs={{0,8},{8,0},{16,24},{24,16},{1,9},{9,1},{17,25},{25,17},{2,10},{10... | collective-permute-start | bytes 344072 | tf_op jit(solution)/shard_map/ppermute | solution.py:139
  56.4 28.9 %collective-permute-start.31 = (bf16[64,1792]{1,0:T(8,128)(2,1)}, bf16[64,1792]{1,0:T(8,128)(2,1)S(1)}, u32[]{:S(2)}, u32[]{:S(2)}) collective-permute-start(bf16[64,1792]{1,0:T(8,128)(2,1)} %constant_dynamic-update-slice_fusion.refs_1_), channel_id=1, source_target_pairs={{0,8},{8,0},{16,24},{24,16},{1,9},{9,1},{17,25},{25,17},{2,10},{10... | collective-permute-start | bytes 688136 | tf_op jit(solution)/shard_map/ppermute | solution.py:139
  57.3 29.0 %collective-permute-start.32 = (bf16[64,1792]{1,0:T(8,128)(2,1)S(1)}, bf16[64,1792]{1,0:T(8,128)(2,1)S(1)}, u32[]{:S(2)}, u32[]{:S(2)}) collective-permute-start(bf16[64,1792]{1,0:T(8,128)(2,1)S(1)} %pad_maximum_fusion.1.refs_0_), channel_id=1, source_target_pairs={{0,16},{8,24},{16,0},{24,8},{1,17},{9,25},{17,1},{25,9},{2,18},{10... | collective-permute-start | bytes 688136 | tf_op jit(solution)/shard_map/ppermute | solution.py:139
  58.5 29.1 %collective-permute-start.35 = (bf16[64,1792]{1,0:T(8,128)(2,1)}, bf16[64,1792]{1,0:T(8,128)(2,1)S(1)}, u32[]{:S(2)}, u32[]{:S(2)}) collective-permute-start(bf16[64,1792]{1,0:T(8,128)(2,1)} %collective-permute-done.33.refs_5_), channel_id=1, source_target_pairs={{0,8},{8,0},{16,24},{24,16},{1,9},{9,1},{17,25},{25,17},{2,10},{10... | collective-permute-start | bytes 688136 | tf_op jit(solution)/shard_map/ppermute | solution.py:139
  59.8 29.2 %collective-permute-start.34 = (bf16[64,1792]{1,0:T(8,128)(2,1)}, bf16[64,1792]{1,0:T(8,128)(2,1)S(1)}, u32[]{:S(2)}, u32[]{:S(2)}) collective-permute-start(bf16[64,1792]{1,0:T(8,128)(2,1)} %collective-permute-done.30.refs_2_), channel_id=1, source_target_pairs={{0,16},{8,24},{16,0},{24,8},{1,17},{9,25},{17,1},{25,9},{2,18},{10... | collective-permute-start | bytes 688136 | tf_op jit(solution)/shard_map/ppermute | solution.py:139
  81.5 17.7 %slice-start = ((s8[7340032]{0:T(1024)(128)(4,1)}), s8[4194304]{0:T(1024)(128)(4,1)S(1)}, s32[]{:S(2)}) async-start(s8[7340032]{0:T(1024)(128)(4,1)} %bitcast.9), calls=%async_computation | async-start | bytes 8388608
  84.0 23.7 %collective-permute-start.21 = (bf16[64,1792]{1,0:T(8,128)(2,1)S(1)}, bf16[64,1792]{1,0:T(8,128)(2,1)S(1)}, u32[]{:S(2)}, u32[]{:S(2)}) collective-permute-start(bf16[64,1792]{1,0:T(8,128)(2,1)S(1)} %get-tuple-element.42), channel_id=1, source_target_pairs={{0,16},{8,24},{16,0},{24,8},{1,17},{9,25},{17,1},{25,9},{2,18},{10... | collective-permute-start | bytes 688136 | tf_op jit(solution)/shard_map/ppermute | solution.py:139
  86.0 26.2 %collective-permute-start.20 = (bf16[64,1792]{1,0:T(8,128)(2,1)S(1)}, bf16[64,1792]{1,0:T(8,128)(2,1)S(1)}, u32[]{:S(2)}, u32[]{:S(2)}) collective-permute-start(bf16[64,1792]{1,0:T(8,128)(2,1)S(1)} %get-tuple-element.40), channel_id=1, source_target_pairs={{0,16},{8,24},{16,0},{24,8},{1,17},{9,25},{17,1},{25,9},{2,18},{10... | collective-permute-start | bytes 688136 | tf_op jit(solution)/shard_map/ppermute | solution.py:139
  86.9 21.1 %collective-permute-start.17 = (bf16[64,1792]{1,0:T(8,128)(2,1)S(1)}, bf16[64,1792]{1,0:T(8,128)(2,1)S(1)}, u32[]{:S(2)}, u32[]{:S(2)}) collective-permute-start(bf16[64,1792]{1,0:T(8,128)(2,1)S(1)} %get-tuple-element.38), channel_id=1, source_target_pairs={{0,8},{8,0},{16,24},{24,16},{1,9},{9,1},{17,25},{25,17},{2,10},{10... | collective-permute-start | bytes 688136 | tf_op jit(solution)/shard_map/ppermute | solution.py:139
  88.3 29.0 %collective-permute-start.16 = (bf16[64,1792]{1,0:T(8,128)(2,1)S(1)}, bf16[64,1792]{1,0:T(8,128)(2,1)S(1)}, u32[]{:S(2)}, u32[]{:S(2)}) collective-permute-start(bf16[64,1792]{1,0:T(8,128)(2,1)S(1)} %get-tuple-element.36), channel_id=1, source_target_pairs={{0,8},{8,0},{16,24},{24,16},{1,9},{9,1},{17,25},{25,17},{2,10},{10... | collective-permute-start | bytes 688136 | tf_op jit(solution)/shard_map/ppermute | solution.py:139
  106.4 43.6 %copy-start.5 = (bf16[64,1792]{1,0:T(8,128)(2,1)S(1)}, bf16[64,1792]{1,0:T(8,128)(2,1)}, u32[]{:S(2)}) copy-start(bf16[64,1792]{1,0:T(8,128)(2,1)} %copy-done.3) | copy-start | bytes 688132
  106.4 43.6 %copy-start.8 = (bf16[64,1792]{1,0:T(8,128)(2,1)S(1)}, bf16[64,1792]{1,0:T(8,128)(2,1)}, u32[]{:S(2)}) copy-start(bf16[64,1792]{1,0:T(8,128)(2,1)} %copy-done.6) | copy-start | bytes 688132
  106.4 43.5 %copy-start.13 = (bf16[64,1792]{1,0:T(8,128)(2,1)S(1)}, bf16[64,1792]{1,0:T(8,128)(2,1)}, u32[]{:S(2)}) copy-start(bf16[64,1792]{1,0:T(8,128)(2,1)} %copy-done.11) | copy-start | bytes 688132
  106.4 4.9 %collective-permute-start.41 = (bf16[64,1792]{1,0:T(8,128)(2,1)S(1)}, bf16[64,1792]{1,0:T(8,128)(2,1)S(1)}, u32[]{:S(2)}, u32[]{:S(2)}) collective-permute-start(bf16[64,1792]{1,0:T(8,128)(2,1)S(1)} %get-tuple-element.56), channel_id=1, source_target_pairs={{0,16},{8,24},{16,0},{24,8},{1,17},{9,25},{17,1},{25,9},{2,18},{10... | collective-permute-start | bytes 688136 | tf_op jit(solution)/shard_map/ppermute | solution.py:139
  107.7 18.6 %collective-permute-start.40 = (bf16[64,1792]{1,0:T(8,128)(2,1)S(1)}, bf16[64,1792]{1,0:T(8,128)(2,1)S(1)}, u32[]{:S(2)}, u32[]{:S(2)}) collective-permute-start(bf16[64,1792]{1,0:T(8,128)(2,1)S(1)} %get-tuple-element.54), channel_id=1, source_target_pairs={{0,16},{8,24},{16,0},{24,8},{1,17},{9,25},{17,1},{25,9},{2,18},{10... | collective-permute-start | bytes 688136 | tf_op jit(solution)/shard_map/ppermute | solution.py:139
  108.0 13.3 %collective-permute-start.37 = (bf16[64,1792]{1,0:T(8,128)(2,1)S(1)}, bf16[64,1792]{1,0:T(8,128)(2,1)S(1)}, u32[]{:S(2)}, u32[]{:S(2)}) collective-permute-start(bf16[64,1792]{1,0:T(8,128)(2,1)S(1)} %get-tuple-element.52), channel_id=1, source_target_pairs={{0,8},{8,0},{16,24},{24,16},{1,9},{9,1},{17,25},{25,17},{2,10},{10... | collective-permute-start | bytes 688136 | tf_op jit(solution)/shard_map/ppermute | solution.py:139
  111.4 5.2 %collective-permute-start.22 = (bf16[64,1792]{1,0:T(8,128)(2,1)S(1)}, bf16[64,1792]{1,0:T(8,128)(2,1)S(1)}, u32[]{:S(2)}, u32[]{:S(2)}) collective-permute-start(bf16[64,1792]{1,0:T(8,128)(2,1)S(1)} %add_convert_fusion.5), channel_id=1, source_target_pairs={{0,8},{8,0},{16,24},{24,16},{1,9},{9,1},{17,25},{25,17},{2,10},{10... | collective-permute-start | bytes 688136 | tf_op jit(solution)/shard_map/ppermute | solution.py:139
  112.2 7.1 %collective-permute-start.18 = (bf16[64,1792]{1,0:T(8,128)(2,1)S(1)}, bf16[64,1792]{1,0:T(8,128)(2,1)S(1)}, u32[]{:S(2)}, u32[]{:S(2)}) collective-permute-start(bf16[64,1792]{1,0:T(8,128)(2,1)S(1)} %add_convert_fusion.7), channel_id=1, source_target_pairs={{0,16},{8,24},{16,0},{24,8},{1,17},{9,25},{17,1},{25,9},{2,18},{10... | collective-permute-start | bytes 688136 | tf_op jit(solution)/shard_map/ppermute | solution.py:139
  116.5 9.8 %collective-permute-start.42 = (bf16[64,1792]{1,0:T(8,128)(2,1)S(1)}, bf16[64,1792]{1,0:T(8,128)(2,1)S(1)}, u32[]{:S(2)}, u32[]{:S(2)}) collective-permute-start(bf16[64,1792]{1,0:T(8,128)(2,1)S(1)} %add_convert_fusion.1), channel_id=1, source_target_pairs={{0,8},{8,0},{16,24},{24,16},{1,9},{9,1},{17,25},{25,17},{2,10},{10... | collective-permute-start | bytes 688136 | tf_op jit(solution)/shard_map/ppermute | solution.py:139
  117.4 5.3 %collective-permute-start.23 = (bf16[32,1792]{1,0:T(8,128)(2,1)S(1)}, bf16[32,1792]{1,0:T(8,128)(2,1)S(1)}, u32[]{:S(2)}, u32[]{:S(2)}) collective-permute-start(bf16[32,1792]{1,0:T(8,128)(2,1)S(1)} %get-tuple-element.72), channel_id=1, source_target_pairs={{0,4},{1,5},{2,6},{3,7},{4,0},{5,1},{6,2},{7,3},{8,12},{9,13},{10,... | collective-permute-start | bytes 344072 | tf_op jit(solution)/shard_map/ppermute | solution.py:139
  119.3 5.6 %collective-permute-start.24 = (bf16[32,1792]{1,0:T(8,128)(2,1)S(1)}, bf16[32,1792]{1,0:T(8,128)(2,1)S(1)}, u32[]{:S(2)}, u32[]{:S(2)}) collective-permute-start(bf16[32,1792]{1,0:T(8,128)(2,1)S(1)} %get-tuple-element.71), channel_id=1, source_target_pairs={{0,6},{1,7},{2,4},{3,5},{4,2},{5,3},{6,0},{7,1},{8,14},{9,15},{10,... | collective-permute-start | bytes 344072 | tf_op jit(solution)/shard_map/ppermute | solution.py:139
  121.2 34.6 %copy-start.16 = (bf16[32,1792]{1,0:T(8,128)(2,1)S(1)}, bf16[32,1792]{1,0:T(8,128)(2,1)}, u32[]{:S(2)}) copy-start(bf16[32,1792]{1,0:T(8,128)(2,1)} %copy-done.14) | copy-start | bytes 344068
  121.2 34.6 %copy-start.23 = (bf16[32,1792]{1,0:T(8,128)(2,1)S(1)}, bf16[32,1792]{1,0:T(8,128)(2,1)}, u32[]{:S(2)}) copy-start(bf16[32,1792]{1,0:T(8,128)(2,1)} %copy-done.21) | copy-start | bytes 344068
  121.2 34.6 %copy-start.26 = (bf16[32,1792]{1,0:T(8,128)(2,1)S(1)}, bf16[32,1792]{1,0:T(8,128)(2,1)}, u32[]{:S(2)}) copy-start(bf16[32,1792]{1,0:T(8,128)(2,1)} %copy-done.24) | copy-start | bytes 344068
  121.3 34.6 %copy-start.29 = (bf16[32,1792]{1,0:T(8,128)(2,1)S(1)}, bf16[32,1792]{1,0:T(8,128)(2,1)}, u32[]{:S(2)}) copy-start(bf16[32,1792]{1,0:T(8,128)(2,1)} %copy-done.27) | copy-start | bytes 344068
  121.3 34.6 %copy-start.32 = (bf16[32,1792]{1,0:T(8,128)(2,1)S(1)}, bf16[32,1792]{1,0:T(8,128)(2,1)}, u32[]{:S(2)}) copy-start(bf16[32,1792]{1,0:T(8,128)(2,1)} %copy-done.30) | copy-start | bytes 344068
  121.3 34.6 %copy-start.35 = (bf16[32,1792]{1,0:T(8,128)(2,1)S(1)}, bf16[32,1792]{1,0:T(8,128)(2,1)}, u32[]{:S(2)}) copy-start(bf16[32,1792]{1,0:T(8,128)(2,1)} %copy-done.33) | copy-start | bytes 344068
  121.3 34.6 %copy-start.38 = (bf16[32,1792]{1,0:T(8,128)(2,1)S(1)}, bf16[32,1792]{1,0:T(8,128)(2,1)}, u32[]{:S(2)}) copy-start(bf16[32,1792]{1,0:T(8,128)(2,1)} %copy-done.36) | copy-start | bytes 344068
  121.3 34.6 %copy-start.41 = (bf16[32,1792]{1,0:T(8,128)(2,1)S(1)}, bf16[32,1792]{1,0:T(8,128)(2,1)}, u32[]{:S(2)}) copy-start(bf16[32,1792]{1,0:T(8,128)(2,1)} %copy-done.39) | copy-start | bytes 344068
  121.3 34.6 %copy-start.44 = (bf16[32,1792]{1,0:T(8,128)(2,1)S(1)}, bf16[32,1792]{1,0:T(8,128)(2,1)}, u32[]{:S(2)}) copy-start(bf16[32,1792]{1,0:T(8,128)(2,1)} %copy-done.42) | copy-start | bytes 344068
  121.3 34.6 %copy-start.47 = (bf16[32,1792]{1,0:T(8,128)(2,1)S(1)}, bf16[32,1792]{1,0:T(8,128)(2,1)}, u32[]{:S(2)}) copy-start(bf16[32,1792]{1,0:T(8,128)(2,1)} %copy-done.45) | copy-start | bytes 344068
  121.3 34.6 %copy-start.50 = (bf16[32,1792]{1,0:T(8,128)(2,1)S(1)}, bf16[32,1792]{1,0:T(8,128)(2,1)}, u32[]{:S(2)}) copy-start(bf16[32,1792]{1,0:T(8,128)(2,1)} %copy-done.48) | copy-start | bytes 344068
  121.4 5.0 %collective-permute-start.19 = (bf16[32,1792]{1,0:T(8,128)(2,1)S(1)}, bf16[32,1792]{1,0:T(8,128)(2,1)S(1)}, u32[]{:S(2)}, u32[]{:S(2)}) collective-permute-start(bf16[32,1792]{1,0:T(8,128)(2,1)S(1)} %get-tuple-element.73), channel_id=1, source_target_pairs={{0,2},{1,3},{2,0},{3,1},{4,6},{5,7},{6,4},{7,5},{8,10},{9,11},{10,... | collective-permute-start | bytes 344072 | tf_op jit(solution)/shard_map/ppermute | solution.py:139
  122.7 5.6 %collective-permute-start.36 = (bf16[64,1792]{1,0:T(8,128)(2,1)S(1)}, bf16[64,1792]{1,0:T(8,128)(2,1)S(1)}, u32[]{:S(2)}, u32[]{:S(2)}) collective-permute-start(bf16[64,1792]{1,0:T(8,128)(2,1)S(1)} %get-tuple-element.50), channel_id=1, source_target_pairs={{0,8},{8,0},{16,24},{24,16},{1,9},{9,1},{17,25},{25,17},{2,10},{10... | collective-permute-start | bytes 688136 | tf_op jit(solution)/shard_map/ppermute | solution.py:139
  124.9 5.2 %collective-permute-start.38 = (bf16[64,1792]{1,0:T(8,128)(2,1)S(1)}, bf16[64,1792]{1,0:T(8,128)(2,1)S(1)}, u32[]{:S(2)}, u32[]{:S(2)}) collective-permute-start(bf16[64,1792]{1,0:T(8,128)(2,1)S(1)} %add_convert_fusion.3), channel_id=1, source_target_pairs={{0,16},{8,24},{16,0},{24,8},{1,17},{9,25},{17,1},{25,9},{2,18},{10... | collective-permute-start | bytes 688136 | tf_op jit(solution)/shard_map/ppermute | solution.py:139
  126.5 20.2 %collective-permute-start.43 = (bf16[32,1792]{1,0:T(8,128)(2,1)S(1)}, bf16[32,1792]{1,0:T(8,128)(2,1)S(1)}, u32[]{:S(2)}, u32[]{:S(2)}) collective-permute-start(bf16[32,1792]{1,0:T(8,128)(2,1)S(1)} %get-tuple-element.60), channel_id=1, source_target_pairs={{0,4},{1,5},{2,6},{3,7},{4,0},{5,1},{6,2},{7,3},{8,12},{9,13},{10,... | collective-permute-start | bytes 344072 | tf_op jit(solution)/shard_map/ppermute | solution.py:139
  126.9 19.8 %collective-permute-start.44 = (bf16[32,1792]{1,0:T(8,128)(2,1)S(1)}, bf16[32,1792]{1,0:T(8,128)(2,1)S(1)}, u32[]{:S(2)}, u32[]{:S(2)}) collective-permute-start(bf16[32,1792]{1,0:T(8,128)(2,1)S(1)} %get-tuple-element.59), channel_id=1, source_target_pairs={{0,6},{1,7},{2,4},{3,5},{4,2},{5,3},{6,0},{7,1},{8,14},{9,15},{10,... | collective-permute-start | bytes 344072 | tf_op jit(solution)/shard_map/ppermute | solution.py:139
  130.2 16.5 %collective-permute-start.39 = (bf16[32,1792]{1,0:T(8,128)(2,1)S(1)}, bf16[32,1792]{1,0:T(8,128)(2,1)S(1)}, u32[]{:S(2)}, u32[]{:S(2)}) collective-permute-start(bf16[32,1792]{1,0:T(8,128)(2,1)S(1)} %get-tuple-element.61), channel_id=1, source_target_pairs={{0,2},{1,3},{2,0},{3,1},{4,6},{5,7},{6,4},{7,5},{8,10},{9,11},{10,... | collective-permute-start | bytes 344072 | tf_op jit(solution)/shard_map/ppermute | solution.py:139
  130.8 33.4 %collective-permute-start.25 = (bf16[64,1792]{1,0:T(8,128)(2,1)S(1)}, bf16[64,1792]{1,0:T(8,128)(2,1)S(1)}, u32[]{:S(2)}, u32[]{:S(2)}) collective-permute-start(bf16[64,1792]{1,0:T(8,128)(2,1)S(1)} %pad_maximum_fusion), channel_id=1, source_target_pairs={{0,1},{1,0},{2,3},{3,2},{4,5},{5,4},{6,7},{7,6},{8,9},{9,8},{10,11... | collective-permute-start | bytes 688136 | tf_op jit(solution)/shard_map/ppermute | solution.py:139
  146.7 17.5 %copy-start.52 = (s32[8,1,16]{2,1,0:T(1,128)S(1)}, s32[8,1,16]{2,1,0:T(1,128)}, u32[]{:S(2)}) copy-start(s32[8,1,16]{2,1,0:T(1,128)} %chosen_ref.5) | copy-start | bytes 1540
  146.8 20.5 %collective-permute-start.45 = (bf16[64,1792]{1,0:T(8,128)(2,1)S(1)}, bf16[64,1792]{1,0:T(8,128)(2,1)S(1)}, u32[]{:S(2)}, u32[]{:S(2)}) collective-permute-start(bf16[64,1792]{1,0:T(8,128)(2,1)S(1)} %pad_maximum_fusion.2), channel_id=1, source_target_pairs={{0,1},{1,0},{2,3},{3,2},{4,5},{5,4},{6,7},{7,6},{8,9},{9,8},{10,11... | collective-permute-start | bytes 688136 | tf_op jit(solution)/shard_map/ppermute | solution.py:139
  (41 other events, 99.5 us)

commit v2 on v0

--- a/solution.py
+++ b/solution.py
@@ -1,7 +1,458 @@
+import functools
+
 import jax
 import jax.numpy as jnp
 from jax import lax
+from jax.experimental import pallas as pl
+from jax.experimental.pallas import tpu as pltpu
 from jax.sharding import PartitionSpec as P
+
+ROWS = (((0,), (0,)), ((), ()))
+LAST = (((1,), (1,)), ((), ()))
+IN_VMEM = pl.BlockSpec(memory_space=pltpu.VMEM)
+IN_SMEM = pl.BlockSpec(memory_space=pltpu.SMEM)
+ANYWHERE = pl.BlockSpec(memory_space=pl.ANY)
+MIB = 1024 * 1024
+
+
+def run_kernel(body, name, operands, specs, outs, out_specs, scratch, mib, later=(), mark=False, cost=1024):
+    used = len(operands)
+    outs, out_specs = list(outs), list(out_specs)
+    results = len(outs)
+    if mark:
+        outs.append(jax.ShapeDtypeStruct((8, 128), jnp.float32))
+        out_specs.append(IN_VMEM)
+
+    def run(*refs):
+        refs = [*refs[:used], *refs[used + len(later) :]]
+        if mark:
+            mark_ref = refs.pop(used + results)
+            mark_ref[...] = jnp.zeros_like(mark_ref)
+        body(*refs)
+
+    out = pl.pallas_call(
+        run,
+        name=name,
+        in_specs=[*specs, *[ANYWHERE] * len(later)],
+        out_shape=outs,
+        out_specs=out_specs,
+        scratch_shapes=scratch,
+        compiler_params=pltpu.CompilerParams(vmem_limit_bytes=mib * MIB),
+        cost_estimate=pl.CostEstimate(flops=1024, bytes_accessed=cost, transcendentals=0),
+    )(*operands, *later)
+    return out if len(out) > 1 else out[0]
+
+
+def in_hbm(array):
+    return pltpu.with_memory_space_constraint(array, pltpu.HBM)
+
+
+def like(rows, width, kind=jnp.bfloat16):
+    return jax.ShapeDtypeStruct((rows, width), kind)
+
+
+def slot_columns(me, chosen_ref, counts_ref, prob_ref):
+    experts, _, slots = chosen_ref.shape
+    diagonal = lax.broadcasted_iota(jnp.int32, (slots, slots), 0) == lax.broadcasted_iota(
+        jnp.int32, (slots, slots), 1
+    )
+    position = lax.broadcasted_iota(jnp.int32, (slots, 1), 0)
+    rows, weights = [], []
+    for step in range(experts):
+        expert = me ^ step
+        live = position < counts_ref[0, expert]
+        row = jnp.broadcast_to(chosen_ref[expert].astype(jnp.float32), (slots, slots))
+        row = jnp.sum(jnp.where(diagonal, row, 0.0), axis=1, keepdims=True)
+        prob = jnp.broadcast_to(prob_ref[expert], (slots, slots))
+        prob = jnp.sum(jnp.where(diagonal, prob, 0.0), axis=1, keepdims=True)
+        rows.append(jnp.where(live, row, -1.0))
+        weights.append(jnp.where(live, prob, 0.0))
+    return jnp.concatenate(rows, axis=0), jnp.concatenate(weights, axis=0)
+
+
+def pick_body(me_ref, counts_hbm, chosen_hbm, prob_hbm, tokens_hbm, cotangent_hbm, *refs):
+    *outs, mask_ref, weights_ref = refs[:-6]
+    counts_ref, chosen_ref, prob_ref, tokens_ref, cotangent_ref, sems = refs[-6:]
+    experts, _, slots = chosen_ref.shape
+    pairs = (
+        (counts_hbm, counts_ref),
+        (chosen_hbm, chosen_ref),
+        (prob_hbm, prob_ref),
+        (tokens_hbm, tokens_ref),
+        (cotangent_hbm, cotangent_ref),
+    )
+    copies = [pltpu.make_async_copy(*pair, sems.at[index]) for index, pair in enumerate(pairs)]
+    for copy in copies:
+        copy.start()
+    for copy in copies[:3]:
+        copy.wait()
+    rows, weights = slot_columns(me_ref[0], chosen_ref, counts_ref, prob_ref)
+    length = tokens_ref.shape[0]
+    place = lax.broadcasted_iota(jnp.int32, (rows.shape[0], length), 1).astype(jnp.float32)
+    mask = (place == rows).astype(jnp.bfloat16)
+    mask_ref[...] = mask
+    weights_ref[...] = jnp.broadcast_to(weights, weights_ref.shape)
+    for which, source_ref in enumerate((tokens_ref, cotangent_ref)):
+        copies[3 + which].wait()
+        value = jnp.dot(mask, source_ref[...], preferred_element_type=jnp.float32)
+        if which:
+            value = weights * value
+        value = value.astype(jnp.bfloat16)
+        step = 0
+        for out_ref in outs:
+            for start in range(which * slots, out_ref.shape[0], 2 * slots):
+                out_ref[pl.ds(start, slots), :] = value[step * slots : (step + 1) * slots]
+                step += 1
+
+
+def pick_slots(me, chosen, counts, gate_prob, tokens, cotangent, split):
+    experts, _, slots = chosen.shape
+    length, width = tokens.shape
+    total = experts * slots
+    operands = (counts, chosen, gate_prob, tokens, cotangent)
+    return run_kernel(
+        pick_body,
+        "pick_slots",
+        (me, *[in_hbm(array) for array in operands]),
+        [IN_SMEM] + [ANYWHERE] * 5,
+        [like(2 * slots * part, width) for part in split]
+        + [like(total, length), like(total, 128, jnp.float32)],
+        [IN_VMEM] * (len(split) + 2),
+        [pltpu.SMEM(counts.shape, counts.dtype)]
+        + [pltpu.VMEM(array.shape, array.dtype) for array in operands[1:]]
+        + [pltpu.SemaphoreType.DMA((5,))],
+        16,
+    )
+
+
+def spread_matrix_body(mask_ref, weights_ref, weighted_ref, plain_ref):
+    mask = mask_ref[...].astype(jnp.float32)
+    weights = weights_ref[...][:, :1]
+    high = weights.astype(jnp.bfloat16).astype(jnp.float32)
+    count = mask.shape[0]
+    plain_ref[...] = mask.T.astype(jnp.bfloat16)
+    weighted_ref[:, :count] = (mask * high).T.astype(jnp.bfloat16)
+    weighted_ref[:, count:] = (mask * (weights - high)).T.astype(jnp.bfloat16)
+
+
+def spread_matrices(mask, weights, later=()):
+    count, length = mask.shape
+    return run_kernel(
+        spread_matrix_body,
+        "spread_matrices",
+        (mask, weights),
+        [IN_VMEM] * 2,
+        [like(length, 2 * count), like(length, count)],
+        [IN_VMEM] * 2,
+        [],
+        8,
+        later,
+    )
+
+
+def spread_body(layout, slots, spread_ref, *refs):
+    pieces, (out_hbm, block, sems) = refs[:-3], refs[-3:]
+    values = jnp.concatenate([pieces[p][pl.ds(q * slots, slots), :] for p, q in layout], axis=0)
+    if spread_ref.shape[1] > values.shape[0]:
+        values = jnp.concatenate([values, values], axis=0)
+    parts = sems.shape[0]
+    size = block.shape[0] // parts
+    copies = []
+    for part in range(parts):
+        rows = pl.ds(part * size, size)
+        total = jnp.dot(spread_ref[rows, :], values, preferred_element_type=jnp.float32)
+        block[rows, :] = total.astype(jnp.bfloat16)
+        copies.append(pltpu.make_async_copy(block.at[rows], out_hbm.at[rows], sems.at[part]))
+        copies[-1].start()
+    for copy in copies:
+        copy.wait()
+
+
+def spread_rows(spread, pieces, layout, slots, later=(), mark=False, parts=4):
+    length, width = spread.shape[0], pieces[0].shape[1]
+    return run_kernel(
+        functools.partial(spread_body, layout, slots),
+        "spread_rows",
+        (spread, *pieces),
+        [IN_VMEM] * (1 + len(pieces)),
+        [like(length, width)],
+        [ANYWHERE],
+        [pltpu.VMEM((length, width), jnp.bfloat16), pltpu.SemaphoreType.DMA((parts,))],
+        16,
+        later,
+        mark,
+    )
+
+
+def load_body(by_rows, count, me_ref, source_ref, target_ref, sems):
+    width = target_ref.shape[1 if by_rows else 2]
+    copies = []
+    for index in range(count):
+        part = pl.ds(pl.multiple_of((me_ref[0] ^ index) * width, width), width)
+        source = source_ref.at[part, :] if by_rows else source_ref.at[:, part]
+        copies.append(pltpu.make_async_copy(source, target_ref.at[index], sems.at[index]))
+        copies[-1].start()
+    for copy in copies:
+        copy.wait()
+
+
+def load_weight(me, weight, by_rows, count, later=()):
+    first, second = weight.shape
+    shape = (count, first // count, second) if by_rows else (count, first, second // count)
+    return run_kernel(
+        functools.partial(load_body, by_rows, count),
+        "load_weight",
+        (me, in_hbm(weight)),
+        [IN_SMEM, ANYWHERE],
+        [jax.ShapeDtypeStruct(shape, weight.dtype)],
+        [IN_VMEM],
+        [pltpu.SemaphoreType.DMA((count,))],
+        4,
+        later,
+    )
+
+
+def arrange_body(plan, used, *refs):
+    for rows, out_ref in zip(plan, refs[used:]):
+        start = 0
+        for source, first, size in rows:
+            out_ref[pl.ds(start, size), :] = refs[source][pl.ds(first, size), :]
+            start += size
+
+
+def arrange(sources, plan, later=(), cost=1024):
+    width = sources[0].shape[1]
+    sizes = [sum(size for _, _, size in rows) for rows in plan]
+    return run_kernel(
+        functools.partial(arrange_body, plan, len(sources)),
+        "arrange",
+        tuple(sources),
+        [IN_VMEM] * len(sources),
+        [like(size, width) for size in sizes],
+        [IN_VMEM] * len(plan),
+        [],
+        8,
+        later,
+        cost=cost,
+    )
+
+
+def add_body(used, *refs):
+    total = refs[0][...].astype(jnp.float32)
+    for ref in refs[1:used]:
+        total += ref[...].astype(jnp.float32)
+    start = 0
+    for out_ref in refs[used:]:
+        out_ref[...] = total[start : start + out_ref.shape[0]].astype(out_ref.dtype)
+        start += out_ref.shape[0]
+
+
+def add_up(terms, parts=1, later=(), cost=1024):
+    rows, width = terms[0].shape
+    return run_kernel(
+        functools.partial(add_body, len(terms)),
+        "add_up",
+        tuple(terms),
+        [IN_VMEM] * len(terms),
+        [like(rows // parts, width)] * parts,
+        [IN_VMEM] * parts,
+        [],
+        8,
+        later,
+        cost=cost,
+    )
+
+
+class Slices:
+    def __init__(self, pieces, part, slots):
+        self.pieces, self.part, self.slots = pieces, part, slots
+        self.flat = [piece for row in pieces for piece in row]
+        self.rows = sum(piece.shape[0] for piece in pieces[0]) // 2
+        self.width = self.flat[0].shape[1]
+
+    def read(self, refs, index):
+        first = sum(len(pieces) for pieces in self.pieces[:index])
+        blocks = []
+        for ref in refs[first : first + len(self.pieces[index])]:
+            for start in range(self.part * self.slots, ref.shape[0], 2 * self.slots):
+                blocks.append(ref[pl.ds(start, self.slots), :])
+        return jnp.concatenate(blocks, axis=0)
+
+
+def store_halves(refs, index, term):
+    size = term.shape[0] // 2
+    refs[2 * index][...] = term[:size].astype(jnp.bfloat16)
+    refs[2 * index + 1][...] = term[size:].astype(jnp.bfloat16)
+
+
+def forward_body(slices, *refs):
+    gate_ref, up_ref, down_ref, hidden_ref, slope_ref, silu_ref, *terms = refs[len(slices.flat) :]
+    count = gate_ref.shape[0]
+    gate = up = None
+    for index in range(count):
+        rows = slices.read(refs, index)
+        more_gate = jnp.dot(rows, gate_ref[index], preferred_element_type=jnp.float32)
+        more_up = jnp.dot(rows, up_ref[index], preferred_element_type=jnp.float32)
+        gate = more_gate if gate is None else gate + more_gate
+        up = more_up if up is None else up + more_up
+    sigmoid = jax.nn.sigmoid(gate)
+    silu = gate * sigmoid
+    hidden = (silu * up).astype(jnp.bfloat16)
+    hidden_ref[...] = hidden
+    slope_ref[...] = up * sigmoid * (1.0 + gate * (1.0 - sigmoid))
+    silu_ref[...] = silu
+    for index in reversed(range(count)):
+        term = jnp.dot(hidden, down_ref[index], preferred_element_type=jnp.float32)
+        store_halves(terms, index, term)
+
+
+def forward_terms(slices, gate, up, down, later=()):
+    count, width, units = gate.shape
+    rows = slices.rows
+    outs = [like(rows, units), like(rows, units, jnp.float32), like(rows, units, jnp.float32)]
+    outs += [like(rows // 2, width)] * (2 * count)
+    out = run_kernel(
+        functools.partial(forward_body, slices),
+        "forward_terms",
+        (*slices.flat, gate, up, down),
+        [IN_VMEM] * (len(slices.flat) + 3),
+        outs,
+        [IN_VMEM] * len(outs),
+        [],
+        8,
+        later,
+    )
+    return out[:3], [out[3 + 2 * i : 5 + 2 * i] for i in range(count)]
+
+
+def hidden_grad_body(slices, *refs):
+    down_ref, slope_ref, silu_ref, gate_grad_ref, up_grad_ref = refs[len(slices.flat) :]
+    grad = None
+    for index in range(down_ref.shape[0]):
+        rows = slices.read(refs, index)
+        more = lax.dot_general(rows, down_ref[index], LAST, preferred_element_type=jnp.float32)
+        grad = more if grad is None else grad + more
+    gate_grad_ref[...] = (grad * slope_ref[...]).astype(jnp.bfloat16)
+    up_grad_ref[...] = (grad * silu_ref[...]).astype(jnp.bfloat16)
+
+
+def hidden_grads(slices, down, slope, silu, later=()):
+    return run_kernel(
+        functools.partial(hidden_grad_body, slices),
+        "hidden_grads",
+        (*slices.flat, down, slope, silu),
+        [IN_VMEM] * (len(slices.flat) + 3),
+        [like(*slope.shape)] * 2,
+        [IN_VMEM] * 2,
+        [],
+        8,
+        later,
+    )
+
+
+def grad_term_body(wanted, gate_grad_ref, up_grad_ref, gate_ref, up_ref, *terms):
+    for place, index in enumerate(wanted):
+        term = lax.dot_general(
+            gate_grad_ref[...], gate_ref[index], LAST, preferred_element_type=jnp.float32
+        )
+        term += lax.dot_general(
+            up_grad_ref[...], up_ref[index], LAST, preferred_element_type=jnp.float32
+        )
+        store_halves(terms, place, term)
+
+
+def grad_terms(wanted, gate_grad, up_grad, gate, up, later=()):
+    _, width, _ = gate.shape
+    rows = gate_grad.shape[0]
+    terms = run_kernel(
+        functools.partial(grad_term_body, wanted),
+        "grad_terms",
+        (gate_grad, up_grad, gate, up),
+        [IN_VMEM] * 4,
+        [like(rows // 2, width)] * (2 * len(wanted)),
+        [IN_VMEM] * (2 * len(wanted)),
+        [],
+        8,
+        later,
+    )
+    return [terms[2 * i : 2 * i + 2] for i in range(len(wanted))]
+
+
+def down_grad_body(slices, me_ref, hidden_ref, *refs):
+    out_ref, block, sems = refs[-3:]
+    count, _, width = block.shape
+    hidden = hidden_ref[...]
+    copies = []
+    for index in range(count):
+        rows = slices.read(refs, index)
+        block[index] = lax.dot_general(
+            hidden, rows, ROWS, preferred_element_type=jnp.float32
+        ).astype(jnp.bfloat16)
+        start = pl.multiple_of((me_ref[0] ^ index) * width, width)
+        target = out_ref.at[:, pl.ds(start, width)]
+        copies.append(pltpu.make_async_copy(block.at[index], target, sems.at[index]))
+        copies[-1].start()
+    for copy in copies:
+        copy.wait()
+
+
+def down_grads(me, hidden, slices, later=()):
+    count = len(slices.pieces)
+    units = hidden.shape[1]
+    return run_kernel(
+        functools.partial(down_grad_body, slices),
+        "down_grads",
+        (me, hidden, *slices.flat),
+        [IN_SMEM] + [IN_VMEM] * (1 + len(slices.flat)),
+        [like(units, slices.width * count)],
+        [ANYWHERE],
+        [
+            pltpu.VMEM((count, units, slices.width), jnp.bfloat16),
+            pltpu.SemaphoreType.DMA((count,)),
+        ],
+        16,
+        later,
+        True,
+    )
+
+
+def weight_grad_body(slices, me_ref, *refs):
+    grad_refs, (gate_hbm, up_hbm, block, sems) = refs[:2], refs[-4:]
+    _, count, width, _ = block.shape
+    copies = []
+    for index in range(count):
+        rows = slices.read(refs[2:], index)
+        start = pl.multiple_of((me_ref[0] ^ index) * width, width)
+        for which, out_ref in enumerate((gate_hbm, up_hbm)):
+            block[which, index] = lax.dot_general(
+                rows, grad_refs[which][...], ROWS, preferred_element_type=jnp.float32
+            ).astype(jnp.bfloat16)
+            target = out_ref.at[pl.ds(start, width), :]
+            sem = sems.at[2 * index + which]
+            copies.append(pltpu.make_async_copy(block.at[which, index], target, sem))
+            copies[-1].start()
+    for copy in copies:
+        copy.wait()
+
+
+def weight_grads(me, slices, gate_grad, up_grad, later=()):
+    count = len(slices.pieces)
+    units = gate_grad.shape[1]
+    return run_kernel(
+        functools.partial(weight_grad_body, slices),
+        "weight_grads",
+        (me, gate_grad, up_grad, *slices.flat),
+        [IN_SMEM] + [IN_VMEM] * (2 + len(slices.flat)),
+        [like(slices.width * count, units)] * 2,
+        [ANYWHERE] * 2,
+        [
+            pltpu.VMEM((2, count, slices.width, units), jnp.bfloat16),
+            pltpu.SemaphoreType.DMA((2 * count,)),
+        ],
+        20,
+        later,
+        True,
+    )
 
 
 def pick_rows(tokens, cotangent, row_index, live_mask, weight):
@@ -28,7 +479,7 @@
     )
 
 
-def per_device(tokens, cotangent, gate_weight, up_weight, down_weight, chosen, counts, gate_prob):
+def by_collectives(tokens, cotangent, gate_weight, up_weight, down_weight, chosen, counts, gate_prob):
     experts = chosen.shape[0]
     slot_count = chosen.shape[2]
     features = tokens.shape[1]
@@ -104,6 +555,107 @@
     )
 
 
+LONG = 64 * MIB
+
+
+def swap(array, distance, axis):
+    size = lax.axis_size(axis)
+    return lax.ppermute(array, axis, [(i, i ^ distance) for i in range(size)])
+
+
+def joined(*arrays):
+    return jnp.concatenate(arrays, axis=0)
+
+
+def by_links(tokens, cotangent, gate_weight, up_weight, down_weight, chosen, counts, gate_prob):
+    experts, _, slots = chosen.shape
+    count = lax.axis_size("fsdp")
+    ep_index = lax.axis_index("ep").reshape(1)
+    me = lax.axis_index("fsdp").reshape(1)
+    two = 2 * slots
+    half = 2 * two
+    own, core, even1, odd1, pair2, pair3, mask, weights = pick_slots(
+        ep_index,
+        chosen,
+        counts.reshape(1, experts),
+        gate_prob,
+        tokens,
+        cotangent,
+        (1, 1, 1, 1, 2, 2),
+    )
+
+    pair2 = swap(pair2, 4, "ep")
+    pair3 = swap(pair3, 6, "ep")
+    even1 = swap(even1, 2, "ep")
+    odd1 = swap(odd1, 3, "ep")
+    core = swap(core, 1, "ep")
+
+    gate = load_weight(me, gate_weight[0], True, count, (own,))
+    up = load_weight(me, up_weight[0], True, count, (gate,))
+    weighted, plain = spread_matrices(mask, weights, (up,))
+    near = joined(arrange((own,), [[(0, 0, two)]], (weighted,)), core, even1, odd1)
+    near_x = swap(near, 1, "fsdp")
+    near_y = swap(near, 2, "fsdp")
+    near_d = [swap(near_x[:half], 2, "fsdp"), swap(near_y[half:], 1, "fsdp")]
+    odd = swap(joined(pair2[two:], pair3[two:]), 1, "ep")
+    far = arrange(
+        (pair2, pair3, odd), [[(0, 0, two), (2, 0, two), (1, 0, two), (2, two, two)]], tuple(near_d)
+    )
+    far_x = swap(far, 1, "fsdp")
+    far_y = swap(far, 2, "fsdp")
+    down = load_weight(me, down_weight[0], False, count, (far,))
+    far_d = [swap(far_x[:half], 2, "fsdp"), swap(far_y[half:], 1, "fsdp")]
+    pieces = [[near, far], [near_x, far_x], [near_y, far_y], near_d + far_d]
+    tokens, grads = Slices(pieces, 0, slots), Slices(pieces, 1, slots)
+
+    (hidden, slope, silu), terms = forward_terms(tokens, gate, up, down)
+    far_sum_d = swap(terms[3][1], 1, "fsdp")
+    near_sum_d = swap(terms[3][0], 2, "fsdp")
+    far_sum_x = swap(terms[1][1], 1, "fsdp")
+    near_sum_y = swap(terms[2][0], 2, "fsdp")
+    gate_grad, up_grad = hidden_grads(grads, down, slope, silu, (terms[0][0],))
+    back_d = grad_terms((3,), gate_grad, up_grad, gate, up)[0]
+    far_back_d = swap(back_d[1], 1, "fsdp")
+    near_back_d = swap(back_d[0], 2, "fsdp")
+    far_sum_y = add_up([terms[2][1], far_sum_d], 1, (back_d[0],))
+    near_sum_x = add_up([terms[1][0], near_sum_d], 1, (back_d[0],))
+    back = grad_terms((0, 1, 2), gate_grad, up_grad, gate, up, (far_sum_y, near_sum_x))
+    far_sum_y = swap(far_sum_y, 2, "fsdp")
+    near_sum_x = swap(near_sum_x, 1, "fsdp")
+    far_back_x = swap(back[1][1], 1, "fsdp")
+    near_back_y = swap(back[2][0], 2, "fsdp")
+    far_back_y = add_up([back[2][1], far_back_d])
+    near_back_x = add_up([back[1][0], near_back_d])
+    sent = (far_back_y, near_back_x)
+    far_back_y = swap(far_back_y, 2, "fsdp")
+    near_back_x = swap(near_back_x, 1, "fsdp")
+    out2, out3 = add_up([terms[0][1], far_sum_x, far_sum_y], 2, sent)
+    near_sum_y = add_up([terms[0][0], near_sum_y], 1, sent, LONG)
+    out0, out1 = add_up([near_sum_y, near_sum_x], 2)
+    grad_down, down_mark = down_grads(me, hidden, grads, (out0, out2))
+    out3 = swap(out3, 6, "ep")
+    out2 = swap(out2, 4, "ep")
+    out1 = swap(out1, 2, "ep")
+    back2, back3 = add_up([back[0][1], far_back_x, far_back_y], 2, (down_mark,))
+    near_back_y = add_up([back[0][0], near_back_y], 1, (down_mark,), LONG)
+    back0, back1 = add_up([near_back_y, near_back_x], 2)
+    back3 = swap(back3, 6, "ep")
+    back2 = swap(back2, 4, "ep")
+    back1 = swap(back1, 2, "ep")
+    layout = []
+    for step in range(experts // 2):
+        layout += [(step, 0), (experts // 2, step)]
+    outs = [out0, out1, out2, out3]
+    outs.append(swap(joined(*[piece[slots:] for piece in outs]), 1, "ep"))
+    grad_gate, grad_up, mark = weight_grads(me, tokens, gate_grad, up_grad, (back0, back2))
+    mixture = spread_rows(weighted, outs, layout, slots)
+    backs = [back0, back1, back2, back3]
+    odd = arrange(backs, [[(piece, slots, slots) for piece in range(4)]], (mark,))
+    backs.append(swap(odd, 1, "ep"))
+    grad_tokens = spread_rows(plain, backs, layout, slots)
+    return mixture, grad_tokens, grad_gate[None], grad_up[None], grad_down[None]
+
+
 def solution(mesh):
     placed = (
         P("ep", "fsdp"),
@@ -115,8 +667,13 @@
         P(None, "ep"),
         P(None, "ep", None),
     )
+
+    def per_part(*arrays):
+        fits = mesh.shape["fsdp"] == 4 and mesh.shape["ep"] == 8 and arrays[0].shape[1] % 128 == 0
+        return (by_links if fits else by_collectives)(*arrays)
+
     return jax.shard_map(
-        per_device,
+        per_part,
         mesh=mesh,
         in_specs=placed,
         out_specs=(

time: 223 us -> 115 us (0.52)
  waiting for transfers between devices: 89.2 us -> 29.1 us
  matrix products: 50.4 us -> 0 us
  starting transfers between devices: 10.7 us -> 48.2 us
  Pallas kernels: 0 us -> 36.5 us
  blocking collectives: 36.5 us -> 0 us
  other arithmetic: 17.6 us -> 0.07 us
  between operations: 13.9 us -> 1.14 us
  local copies, waits for them, and re-layouts: 4.06 us -> 0.1 us
    dot_general x9 -> x0, matrix products: 50.4 us -> none  [the longest x1 7.13 us: per_device(): lax.dot_general(grad_pre_up, up_local, contract_last, preferred_element_t...]
    reduce_scatter x2 -> x0, waiting for transfers between devices: 50.3 us -> none  [send_back(): lax.psum_scatter(term.astype(jnp.bfloat16), 'fsdp', scatter_dimension=1,...]
    ppermute x0 -> x34, starting transfers between devices: none -> 48.2 us  [swap(): return lax.ppermute(array, axis, [(i, i ^ distance) for i in range(size)])]
    all_gather x2 -> x0, waiting for transfers between devices: 38.8 us -> none  [the longest x1 25.9 us: per_device(): lax.all_gather(sliced_grads, 'fsdp', axis=2, tiled=True)]
    pallas_call x0 -> x26, Pallas kernels: none -> 36.5 us  [run_kernel(): pl.pallas_call(run, name=name, in_specs=[*specs, *[ANYWHERE] * len(later)...]
    all_to_all x2 -> x0, blocking collectives: 36.5 us -> none  [the longest x1 19.4 us: per_device(): lax.all_to_all(picked_tokens, 'ep', split_axis=0, concat_axis=0, tiled=True)]
    ppermute x0 -> x34, waiting for transfers between devices: none -> 29.1 us  [swap(): return lax.ppermute(array, axis, [(i, i ^ distance) for i in range(size)])]
    all_to_all x2 -> x0, starting transfers between devices: 10.6 us -> none  [send_back(): lax.all_to_all(to_slots(summed, experts, slot_count), 'ep', split_axis=0,...]
  transfers between devices with their start and end apart: 6 -> 34, of which waited for: 4 -> 12; matrix products, arithmetic and copies ran while one was open for 22% -> 0% of each run, Pallas kernels for 0% -> 25%
where the time goes in v2:
time: 115 us
  starting transfers between devices  48.2 us (42%)
  Pallas kernels  36.5 us (32%)
  waiting for transfers between devices  29.1 us (25%)
    ppermute x34, starting transfers between devices, swap(): return lax.ppermute(array, axis, [(i, i ^ distance) for i in range(size)])  48.2 us
    pallas_call x26, Pallas kernels, run_kernel(): pl.pallas_call(run, name=name, in_specs=[*specs, *[ANYWHERE] * len(later)...  36.5 us
    ppermute x34, waiting for transfers between devices, swap(): return lax.ppermute(array, axis, [(i, i ^ distance) for i in range(size)])  29.1 us
  transfers between devices with their start and end apart: 34, of which 12 were waited for; matrix products, arithmetic and copies ran while one was open for 0% of the time, Pallas kernels for 25%

profile of v2, /device:TPU:1, one launch (start us, length us, event | category | flops | bytes accessed | tf_op | source)
XLA Modules:
  0.0 115.2 jit_solution(3515886200782947500)
XLA Ops:
  0.6 2.6 %pick_slots.1 = (bf16[32,1792]{1,0:T(8,128)(2,1)S(1)}, bf16[32,1792]{1,0:T(8,128)(2,1)S(1)}, bf16[32,1792]{1,0:T(8,128)(2,1)S(1)}, bf16[32,1792]{1,0:T(8,128)(2,...) custom-call(s32[1]{0:T(128)} %bitcast.refs_0_, ...), custom_call_target="tpu_custom_call" | custom-call | flops 1024 | bytes 1024 | tf_op jit(solution)/shard_map/pick_slots/pallas_call | solution.py:33
  3.2 0.1 collective-permute-start
  3.3 2.8 %collective-permute-start.1 = (bf16[32,1792]{1,0:T(8,128)(2,1)S(1)}, bf16[32,1792]{1,0:T(8,128)(2,1)S(1)}, u32[]{:S(2)}, u32[]{:S(2)}) collective-permute-start(bf16[32,1792]{1,0:T(8,128)(2,1)S(1)} %get-tuple-element.54), channel_id=1, source_target_pairs={{0,2},{1,3},{2,0},{3,1},{4,6},{5,7},{6,4},{7,5},{8,10},{9,11},{10,... | collective-permute-start | bytes 344072 | tf_op jit(solution)/shard_map/ppermute | solution.py:563
  6.1 2.7 %collective-permute-start.3 = (bf16[64,1792]{1,0:T(8,128)(2,1)S(1)}, bf16[64,1792]{1,0:T(8,128)(2,1)S(1)}, u32[]{:S(2)}, u32[]{:S(2)}) collective-permute-start(bf16[64,1792]{1,0:T(8,128)(2,1)S(1)} %get-tuple-element.56), channel_id=1, source_target_pairs={{0,4},{1,5},{2,6},{3,7},{4,0},{5,1},{6,2},{7,3},{8,12},{9,13},{10,... | collective-permute-start | bytes 688136 | tf_op jit(solution)/shard_map/ppermute | solution.py:563
  8.8 1.1 collective-permute-start.4
  9.9 3.2 %load_weight.3.refs_2_.refs_10_ = bf16[4,1792,512]{2,1,0:T(8,128)(2,1)S(1)} custom-call(s32[1]{0:T(128)} %bitcast.2.refs_0_, bf16[7168,512]{1,0:T(8,128)(2,1)} %bitcast.9, bf16[32,1792]{1,0:T(8,128)(2,1)S(1)} %get-tuple-element.51.refs_2_.refs_0_), custom_call_target="tpu_custom_call" | custom-call | flops 1024 | bytes 1024 | tf_op jit(solution)/shard_map/load_weight/pallas_call | solution.py:33
  13.1 3.2 %load_weight.4.refs_2_.refs_11_.refs_3_ = bf16[4,1792,512]{2,1,0:T(8,128)(2,1)S(1)} custom-call(s32[1]{0:T(128)} %bitcast.2.refs_0_, bf16[7168,512]{1,0:T(8,128)(2,1)} %bitcast.11, bf16[4,1792,512]{2,1,0:T(8,128)(2,1)S(1)} %load_weight.3.refs_2_.refs_10_), custom_call_target="tpu_custom_call" | custom-call | flops 1024 | bytes 1024 | tf_op jit(solution)/shard_map/load_weight/pallas_call | solution.py:33
  16.3 0.2 spread_matrices.1
  16.5 0.2 collective-permute-done.2
  16.7 1.4 %collective-permute-start.8 = (bf16[128,1792]{1,0:T(8,128)(2,1)S(1)}, bf16[128,1792]{1,0:T(8,128)(2,1)S(1)}, u32[]{:S(2)}, u32[]{:S(2)}) collective-permute-start(bf16[128,1792]{1,0:T(8,128)(2,1)S(1)} %pad_maximum_fusion.refs_0_.refs_2_.refs_3_), channel_id=1, source_target_pairs={{0,16},{8,24},{16,0},{24,8},{1,17},{9,25},{17,1},{25,9},{2,18},{10... | collective-permute-start | bytes 1376264 | tf_op jit(solution)/shard_map/ppermute | solution.py:563
  18.1 1.2 %collective-permute-start.6 = (bf16[128,1792]{1,0:T(8,128)(2,1)S(1)}, bf16[128,1792]{1,0:T(8,128)(2,1)S(1)}, u32[]{:S(2)}, u32[]{:S(2)}) collective-permute-start(bf16[128,1792]{1,0:T(8,128)(2,1)S(1)} %pad_maximum_fusion.refs_0_.refs_2_.refs_3_), channel_id=1, source_target_pairs={{0,8},{8,0},{16,24},{24,16},{1,9},{9,1},{17,25},{25,17},{2,10},{10... | collective-permute-start | bytes 1376264 | tf_op jit(solution)/shard_map/ppermute | solution.py:563
  19.4 4.5 %collective-permute-done.4.refs_1_ = bf16[64,1792]{1,0:T(8,128)(2,1)S(1)} collective-permute-done((bf16[64,1792]{1,0:T(8,128)(2,1)S(1)}, bf16[64,1792]{1,0:T(8,128)(2,1)S(1)}, u32[]{:S(2)}, u32[]{:S(2)}) %collective-permute-start.4) | collective-permute-done | bytes 229408 | tf_op jit(solution)/shard_map/ppermute | solution.py:563
  23.9 1.9 %collective-permute-start.5 = (bf16[64,1792]{1,0:T(8,128)(2,1)S(1)}, bf16[64,1792]{1,0:T(8,128)(2,1)S(1)}, u32[]{:S(2)}, u32[]{:S(2)}) collective-permute-start(bf16[64,1792]{1,0:T(8,128)(2,1)S(1)} %pad_maximum_fusion.1), channel_id=1, source_target_pairs={{0,1},{1,0},{2,3},{3,2},{4,5},{5,4},{6,7},{7,6},{8,9},{9,8},{10,11... | collective-permute-start | bytes 688136 | tf_op jit(solution)/shard_map/ppermute | solution.py:563
  25.8 2.5 %collective-permute-done.8.refs_4_.refs_6_.refs_7_ = bf16[128,1792]{1,0:T(8,128)(2,1)S(1)} collective-permute-done((bf16[128,1792]{1,0:T(8,128)(2,1)S(1)}, bf16[128,1792]{1,0:T(8,128)(2,1)S(1)}, u32[]{:S(2)}, u32[]{:S(2)}) %collective-permute-start.8) | collective-permute-done | bytes 458784 | tf_op jit(solution)/shard_map/ppermute | solution.py:563
  28.3 1.5 %collective-permute-start.9 = (bf16[64,1792]{1,0:T(8,128)(2,1)S(1)}, bf16[64,1792]{1,0:T(8,128)(2,1)S(1)}, u32[]{:S(2)}, u32[]{:S(2)}) collective-permute-start(bf16[64,1792]{1,0:T(8,128)(2,1)S(1)} %slice.43), channel_id=1, source_target_pairs={{0,8},{8,0},{16,24},{24,16},{1,9},{9,1},{17,25},{25,17},{2,10},{10... | collective-permute-start | bytes 688136 | tf_op jit(solution)/shard_map/ppermute | solution.py:563
  29.8 1.3 %collective-permute-start.7 = (bf16[64,1792]{1,0:T(8,128)(2,1)S(1)}, bf16[64,1792]{1,0:T(8,128)(2,1)S(1)}, u32[]{:S(2)}, u32[]{:S(2)}) collective-permute-start(bf16[64,1792]{1,0:T(8,128)(2,1)S(1)} %slice.42), channel_id=1, source_target_pairs={{0,16},{8,24},{16,0},{24,8},{1,17},{9,25},{17,1},{25,9},{2,18},{10... | collective-permute-start | bytes 688136 | tf_op jit(solution)/shard_map/ppermute | solution.py:563
  31.1 2.9 %collective-permute-done.9.refs_4_.refs_7_.refs_9_.refs_10_ = bf16[64,1792]{1,0:T(8,128)(2,1)S(1)} collective-permute-done((bf16[64,1792]{1,0:T(8,128)(2,1)S(1)}, bf16[64,1792]{1,0:T(8,128)(2,1)S(1)}, u32[]{:S(2)}, u32[]{:S(2)}) %collective-permute-start.9) | collective-permute-done | bytes 229408 | tf_op jit(solution)/shard_map/ppermute | solution.py:563
  34.1 1.3 %collective-permute-done.7.refs_3_.refs_6_.refs_8_.refs_9_ = bf16[64,1792]{1,0:T(8,128)(2,1)S(1)} collective-permute-done((bf16[64,1792]{1,0:T(8,128)(2,1)S(1)}, bf16[64,1792]{1,0:T(8,128)(2,1)S(1)}, u32[]{:S(2)}, u32[]{:S(2)}) %collective-permute-start.7) | collective-permute-done | bytes 229408 | tf_op jit(solution)/shard_map/ppermute | solution.py:563
  35.4 1.3 %collective-permute-start.11 = (bf16[128,1792]{1,0:T(8,128)(2,1)S(1)}, bf16[128,1792]{1,0:T(8,128)(2,1)S(1)}, u32[]{:S(2)}, u32[]{:S(2)}) collective-permute-start(bf16[128,1792]{1,0:T(8,128)(2,1)S(1)} %arrange.4.refs_2_.refs_1_.refs_3_.refs_4_), channel_id=1, source_target_pairs={{0,16},{8,24},{16,0},{24,8},{1,17},{9,25},{17,1},{25,9},{2,18},{10... | collective-permute-start | bytes 1376264 | tf_op jit(solution)/shard_map/ppermute | solution.py:563
  36.7 0.2 collective-permute-start.10
  37.0 8.0 %collective-permute-done.11.refs_5_.refs_7_.refs_8_ = bf16[128,1792]{1,0:T(8,128)(2,1)S(1)} collective-permute-done((bf16[128,1792]{1,0:T(8,128)(2,1)S(1)}, bf16[128,1792]{1,0:T(8,128)(2,1)S(1)}, u32[]{:S(2)}, u32[]{:S(2)}) %collective-permute-start.11) | collective-permute-done | bytes 458784 | tf_op jit(solution)/shard_map/ppermute | solution.py:563
  45.0 0.8 collective-permute-start.13
  45.8 0.1 collective-permute-done.10.refs_3_.refs_5_.refs_6_
  46.0 0.7 collective-permute-start.12
  46.7 3.2 %load_weight.5.refs_12_.refs_10_ = bf16[4,512,1792]{2,1,0:T(8,128)(2,1)S(1)} custom-call(s32[1]{0:T(128)} %bitcast.2.refs_0_, bf16[512,7168]{1,0:T(8,128)(2,1)} %bitcast.10, bf16[128,1792]{1,0:T(8,128)(2,1)S(1)} %arrange.4.refs_2_.refs_1_.refs_3_.refs_4_), custom_call_target="tpu_custom_call" | custom-call | flops 1024 | bytes 1024 | tf_op jit(solution)/shard_map/load_weight/pallas_call | solution.py:33
  49.9 1.6 %collective-permute-done.13.refs_9_.refs_11_.refs_12_ = bf16[64,1792]{1,0:T(8,128)(2,1)S(1)} collective-permute-done((bf16[64,1792]{1,0:T(8,128)(2,1)S(1)}, bf16[64,1792]{1,0:T(8,128)(2,1)S(1)}, u32[]{:S(2)}, u32[]{:S(2)}) %collective-permute-start.13) | collective-permute-done | bytes 229408 | tf_op jit(solution)/shard_map/ppermute | solution.py:563
  51.4 3.2 %forward_terms.1 = (bf16[128,512]{1,0:T(8,128)(2,1)S(1)}, f32[128,512]{1,0:T(8,128)S(1)}, f32[128,512]{1,0:T(8,128)S(1)}, bf16[64,1792]{1,0:T(8,128)(2,1)S(1)}, ...) custom-call(bf16[128,1792]{1,0:T(8,128)(2,1)S(1)} %pad_maximum_fusio, ...), custom_call_target="tpu_custom_call" | custom-call | flops 1024 | bytes 1024 | tf_op jit(solution)/shard_map/forward_terms/pallas_call | solution.py:33
  54.6 0.3 collective-permute-start.15
  54.9 1.0 collective-permute-start.16
  56.0 0.4 collective-permute-start.14
  56.4 2.4 %hidden_grads.1 = (bf16[128,512]{1,0:T(8,128)(2,1)S(1)}, bf16[128,512]{1,0:T(8,128)(2,1)S(1)}) custom-call(bf16[128,1792]{1,0:T(8,128)(2,1)S(1)} %pad_maximum_fusion.refs_0_.refs_2_.refs_3_, bf16[128,1792]{1,0:T(8,128)(2,1)S(1)} %arrange.4.refs_2_.refs_1_.refs_3_.refs_4_, bf16[128,1792]{1,0:T(8,128)(2,1)S(1)} %collective-permute-done.6.refs_2_.refs_4_.refs_5_, ...), custom_call_target="tpu_custom_call" | custom-call | flops 1024 | bytes 1024 | tf_op jit(solution)/shard_map/hidden_grads/pallas_call | solution.py:33
  58.8 1.3 %grad_terms.2 = (bf16[64,1792]{1,0:T(8,128)(2,1)S(1)}, bf16[64,1792]{1,0:T(8,128)(2,1)S(1)}) custom-call(bf16[128,512]{1,0:T(8,128)(2,1)S(1)} %get-tuple-element.62.refs_0_.refs_1_, bf16[128,512]{1,0:T(8,128)(2,1)S(1)} %get-tuple-element.63.refs_1_.refs_2_, bf16[4,1792,512]{2,1,0:T(8,128)(2,1)S(1)} %load_weight.3.refs_2_.refs_10_, ...), custom_call_target="tpu_custom_call" | custom-call | flops 1024 | bytes 1024 | tf_op jit(solution)/shard_map/grad_terms/pallas_call | solution.py:33
  60.2 1.3 %collective-permute-start.17 = (bf16[64,1792]{1,0:T(8,128)(2,1)S(1)}, bf16[64,1792]{1,0:T(8,128)(2,1)S(1)}, u32[]{:S(2)}, u32[]{:S(2)}) collective-permute-start(bf16[64,1792]{1,0:T(8,128)(2,1)S(1)} %get-tuple-element.70), channel_id=1, source_target_pairs={{0,8},{8,0},{16,24},{24,16},{1,9},{9,1},{17,25},{25,17},{2,10},{10... | collective-permute-start | bytes 688136 | tf_op jit(solution)/shard_map/ppermute | solution.py:563
  61.5 0.2 collective-permute-start.21
  61.7 1.1 collective-permute-start.18
  62.8 0.1 add_up.10.refs_4_
  62.8 0.5 collective-permute-start.22
  63.3 0.1 add_up.11.refs_5_
  63.4 3.7 %grad_terms.3 = (bf16[64,1792]{1,0:T(8,128)(2,1)S(1)}, bf16[64,1792]{1,0:T(8,128)(2,1)S(1)}, bf16[64,1792]{1,0:T(8,128)(2,1)S(1)}, bf16[64,1792]{1,0:T(8,128)(2,...) custom-call(bf16[128,512]{1,0:T(8,128)(2,1)S(1)} %get-tuple-element.62.refs_0_.refs_1_, ...), custom_call_target="tpu_custom_call" | custom-call | flops 1024 | bytes 1024 | tf_op jit(solution)/shard_map/grad_terms/pallas_call | solution.py:33
  67.0 1.3 %collective-permute-start.19 = (bf16[64,1792]{1,0:T(8,128)(2,1)S(1)}, bf16[64,1792]{1,0:T(8,128)(2,1)S(1)}, u32[]{:S(2)}, u32[]{:S(2)}) collective-permute-start(bf16[64,1792]{1,0:T(8,128)(2,1)S(1)} %add_up.11.refs_5_), channel_id=1, source_target_pairs={{0,8},{8,0},{16,24},{24,16},{1,9},{9,1},{17,25},{25,17},{2,10},{10... | collective-permute-start | bytes 688136 | tf_op jit(solution)/shard_map/ppermute | solution.py:563
  68.3 0.2 collective-permute-start.29
  68.6 0.1 add_up.12.refs_2_.refs_3_
  68.6 2.3 %collective-permute-done.21.refs_1_ = bf16[64,1792]{1,0:T(8,128)(2,1)S(1)} collective-permute-done((bf16[64,1792]{1,0:T(8,128)(2,1)S(1)}, bf16[64,1792]{1,0:T(8,128)(2,1)S(1)}, u32[]{:S(2)}, u32[]{:S(2)}) %collective-permute-start.21) | collective-permute-done | bytes 229408 | tf_op jit(solution)/shard_map/ppermute | solution.py:563
  71.0 0.1 collective-permute-start.30
  71.1 1.4 %collective-permute-start.26 = (bf16[64,1792]{1,0:T(8,128)(2,1)S(1)}, bf16[64,1792]{1,0:T(8,128)(2,1)S(1)}, u32[]{:S(2)}, u32[]{:S(2)}) collective-permute-start(bf16[64,1792]{1,0:T(8,128)(2,1)S(1)} %get-tuple-element.80), channel_id=1, source_target_pairs={{0,16},{8,24},{16,0},{24,8},{1,17},{9,25},{17,1},{25,9},{2,18},{10... | collective-permute-start | bytes 688136 | tf_op jit(solution)/shard_map/ppermute | solution.py:563
  72.5 1.7 %collective-permute-done.22.refs_2_ = bf16[64,1792]{1,0:T(8,128)(2,1)S(1)} collective-permute-done((bf16[64,1792]{1,0:T(8,128)(2,1)S(1)}, bf16[64,1792]{1,0:T(8,128)(2,1)S(1)}, u32[]{:S(2)}, u32[]{:S(2)}) %collective-permute-start.22) | collective-permute-done | bytes 229408 | tf_op jit(solution)/shard_map/ppermute | solution.py:563
  74.2 1.3 %collective-permute-start.27 = (bf16[64,1792]{1,0:T(8,128)(2,1)S(1)}, bf16[64,1792]{1,0:T(8,128)(2,1)S(1)}, u32[]{:S(2)}, u32[]{:S(2)}) collective-permute-start(bf16[64,1792]{1,0:T(8,128)(2,1)S(1)} %add_up.13.refs_3_.refs_4_), channel_id=1, source_target_pairs={{0,8},{8,0},{16,24},{24,16},{1,9},{9,1},{17,25},{25,17},{2,10},{10... | collective-permute-start | bytes 688136 | tf_op jit(solution)/shard_map/ppermute | solution.py:563
  75.5 0.1 add_up.14.refs_0_
  75.5 0.1 add_up.16
  75.6 0.3 collective-permute-done.19.refs_1_
  75.9 1.1 collective-permute-start.24
  77.1 3.7 %collective-permute-done.29.refs_1_ = bf16[64,1792]{1,0:T(8,128)(2,1)S(1)} collective-permute-done((bf16[64,1792]{1,0:T(8,128)(2,1)S(1)}, bf16[64,1792]{1,0:T(8,128)(2,1)S(1)}, u32[]{:S(2)}, u32[]{:S(2)}) %collective-permute-start.29) | collective-permute-done | bytes 229408 | tf_op jit(solution)/shard_map/ppermute | solution.py:563
  80.8 6.0 %collective-permute-start.23 = (bf16[32,1792]{1,0:T(8,128)(2,1)S(1)}, bf16[32,1792]{1,0:T(8,128)(2,1)S(1)}, u32[]{:S(2)}, u32[]{:S(2)}) collective-permute-start(bf16[32,1792]{1,0:T(8,128)(2,1)S(1)} %get-tuple-element.76.refs_13_), channel_id=1, source_target_pairs={{0,4},{1,5},{2,6},{3,7},{4,0},{5,1},{6,2},{7,3},{8,12},{9,13},{10,... | collective-permute-start | bytes 344072 | tf_op jit(solution)/shard_map/ppermute | solution.py:563
  86.8 3.8 %down_grads.1 = (bf16[512,7168]{1,0:T(8,128)(2,1)}, f32[8,128]{1,0:T(8,128)S(1)}) custom-call(s32[1]{0:T(128)} %bitcast.2.refs_0_, bf16[128,512]{1,0:T(8,128)(2,1)S(1)} %get-tuple-element.81.refs_1_, bf16[128,1792]{1,0:T(8,128)(2,1)S(1)} %pad_maximum_fusion.refs_0_.refs_2_.refs_3_, bf16[128,1792]{1,0:T(8,128)(2,1)S(1)} %arrange.4.refs_2_.refs_1_.refs_3_.refs_4_, ...), custom_call_target="tpu_custom_call" | custom-call | flops 1024 | bytes 1024 | tf_op jit(solution)/shard_map/down_grads/pallas_call | solution.py:33
  90.7 0.1 add_up.19
  90.8 0.5 collective-permute-start.31
  91.3 0.1 add_up.17.refs_0_
  91.3 3.2 %collective-permute-start.32 = (bf16[32,1792]{1,0:T(8,128)(2,1)S(1)}, bf16[32,1792]{1,0:T(8,128)(2,1)S(1)}, u32[]{:S(2)}, u32[]{:S(2)}) collective-permute-start(bf16[32,1792]{1,0:T(8,128)(2,1)S(1)} %get-tuple-element.88), channel_id=1, source_target_pairs={{0,6},{1,7},{2,4},{3,5},{4,2},{5,3},{6,0},{7,1},{8,14},{9,15},{10,... | collective-permute-start | bytes 344072 | tf_op jit(solution)/shard_map/ppermute | solution.py:563
  94.6 0.1 collective-permute-start.28
  94.7 7.2 %collective-permute-start.25 = (bf16[64,1792]{1,0:T(8,128)(2,1)S(1)}, bf16[64,1792]{1,0:T(8,128)(2,1)S(1)}, u32[]{:S(2)}, u32[]{:S(2)}) collective-permute-start(bf16[64,1792]{1,0:T(8,128)(2,1)S(1)} %pad_maximum_fusion.2), channel_id=1, source_target_pairs={{0,1},{1,0},{2,3},{3,2},{4,5},{5,4},{6,7},{7,6},{8,9},{9,8},{10,11... | collective-permute-start | bytes 688136 | tf_op jit(solution)/shard_map/ppermute | solution.py:563
  101.9 6.0 %weight_grads.1 = (bf16[7168,512]{1,0:T(8,128)(2,1)}, bf16[7168,512]{1,0:T(8,128)(2,1)}, f32[8,128]{1,0:T(8,128)S(1)}) custom-call(s32[1]{0:T(128)} %bitcast.2.refs_0_, bf16[128,512]{1,0:T(8,128)(2,1)S(1)} %get-tuple-element.62.refs_0_.refs_1_, bf16[128,512]{1,0:T(8,128)(2,1)S(1)} %get-tuple-element.63.refs_1_.refs_2_, ...), custom_call_target="tpu_custom_call" | custom-call | flops 1024 | bytes 1024 | tf_op jit(solution)/shard_map/weight_grads/pallas_call | solution.py:33
  107.9 3.9 %collective-permute-start.33 = (bf16[64,1792]{1,0:T(8,128)(2,1)S(1)}, bf16[64,1792]{1,0:T(8,128)(2,1)S(1)}, u32[]{:S(2)}, u32[]{:S(2)}) collective-permute-start(bf16[64,1792]{1,0:T(8,128)(2,1)S(1)} %arrange.5), channel_id=1, source_target_pairs={{0,1},{1,0},{2,3},{3,2},{4,5},{5,4},{6,7},{7,6},{8,9},{9,8},{10,11... | collective-permute-start | bytes 688136 | tf_op jit(solution)/shard_map/ppermute | solution.py:563
  111.9 1.6 %spread_rows.2 = bf16[512,1792]{1,0:T(8,128)(2,1)} custom-call(bf16[512,256]{1,0:T(8,128)(2,1)S(1)} %get-tuple-element.52.refs_1_.refs_0_, bf16[32,1792]{1,0:T(8,128)(2,1)S(1)} %get-tuple-element.72.refs_1_.refs_12_, bf16[32,1792]{1,0:T(8,128)(2,1)S(1)} %collective-permute-done.20.refs_2_, bf16[32,1792]{1,0:T(8,128)(2,1)S(1)} %collective-permute-done.23.refs_3_, ...), custom_call_target="tpu_custom_call" | custom-call | flops 1024 | bytes 1024 | tf_op jit(solution)/shard_map/spread_rows/pallas_call | solution.py:33
  113.5 1.5 %spread_rows.3 = bf16[512,1792]{1,0:T(8,128)(2,1)} custom-call(bf16[512,128]{1,0:T(8,128)(2,1)S(1)} %get-tuple-element.78.refs_0_, bf16[32,1792]{1,0:T(8,128)(2,1)S(1)} %get-tuple-element.83.refs_13_.refs_0_.refs_1_, bf16[32,1792]{1,0:T(8,128)(2,1)S(1)} %collective-permute-done.28.refs_1_.refs_2_, ...), custom_call_target="tpu_custom_call" | custom-call | flops 1024 | bytes 1024 | tf_op jit(solution)/shard_map/spread_rows/pallas_call | solution.py:33
  (43 shorter events, 0.5 us)
Async XLA Ops:
  3.2 13.3 %collective-permute-start = (bf16[32,1792]{1,0:T(8,128)(2,1)S(1)}, bf16[32,1792]{1,0:T(8,128)(2,1)S(1)}, u32[]{:S(2)}, u32[]{:S(2)}) collective-permute-start(bf16[32,1792]{1,0:T(8,128)(2,1)S(1)} %get-tuple-element.53), channel_id=1, source_target_pairs={{0,1},{1,0},{2,3},{3,2},{4,5},{5,4},{6,7},{7,6},{8,9},{9,8},{10,11... | collective-permute-start | bytes 344072 | tf_op jit(solution)/shard_map/ppermute | solution.py:563
  3.3 13.2 %collective-permute-start.1 = (bf16[32,1792]{1,0:T(8,128)(2,1)S(1)}, bf16[32,1792]{1,0:T(8,128)(2,1)S(1)}, u32[]{:S(2)}, u32[]{:S(2)}) collective-permute-start(bf16[32,1792]{1,0:T(8,128)(2,1)S(1)} %get-tuple-element.54), channel_id=1, source_target_pairs={{0,2},{1,3},{2,0},{3,1},{4,6},{5,7},{6,4},{7,5},{8,10},{9,11},{10,... | collective-permute-start | bytes 344072 | tf_op jit(solution)/shard_map/ppermute | solution.py:563
  6.1 10.6 %collective-permute-start.2 = (bf16[32,1792]{1,0:T(8,128)(2,1)S(1)}, bf16[32,1792]{1,0:T(8,128)(2,1)S(1)}, u32[]{:S(2)}, u32[]{:S(2)}) collective-permute-start(bf16[32,1792]{1,0:T(8,128)(2,1)S(1)} %get-tuple-element.55), channel_id=1, source_target_pairs={{0,3},{1,2},{2,1},{3,0},{4,7},{5,6},{6,5},{7,4},{8,11},{9,10},{10,... | collective-permute-start | bytes 344072 | tf_op jit(solution)/shard_map/ppermute | solution.py:563
  6.1 13.2 %collective-permute-start.3 = (bf16[64,1792]{1,0:T(8,128)(2,1)S(1)}, bf16[64,1792]{1,0:T(8,128)(2,1)S(1)}, u32[]{:S(2)}, u32[]{:S(2)}) collective-permute-start(bf16[64,1792]{1,0:T(8,128)(2,1)S(1)} %get-tuple-element.56), channel_id=1, source_target_pairs={{0,4},{1,5},{2,6},{3,7},{4,0},{5,1},{6,2},{7,3},{8,12},{9,13},{10,... | collective-permute-start | bytes 688136 | tf_op jit(solution)/shard_map/ppermute | solution.py:563
  8.8 15.1 %collective-permute-start.4 = (bf16[64,1792]{1,0:T(8,128)(2,1)S(1)}, bf16[64,1792]{1,0:T(8,128)(2,1)S(1)}, u32[]{:S(2)}, u32[]{:S(2)}) collective-permute-start(bf16[64,1792]{1,0:T(8,128)(2,1)S(1)} %get-tuple-element.57), channel_id=1, source_target_pairs={{0,6},{1,7},{2,4},{3,5},{4,2},{5,3},{6,0},{7,1},{8,14},{9,15},{10,... | collective-permute-start | bytes 688136 | tf_op jit(solution)/shard_map/ppermute | solution.py:563
  16.7 11.6 %collective-permute-start.8 = (bf16[128,1792]{1,0:T(8,128)(2,1)S(1)}, bf16[128,1792]{1,0:T(8,128)(2,1)S(1)}, u32[]{:S(2)}, u32[]{:S(2)}) collective-permute-start(bf16[128,1792]{1,0:T(8,128)(2,1)S(1)} %pad_maximum_fusion.refs_0_.refs_2_.refs_3_), channel_id=1, source_target_pairs={{0,16},{8,24},{16,0},{24,8},{1,17},{9,25},{17,1},{25,9},{2,18},{10... | collective-permute-start | bytes 1376264 | tf_op jit(solution)/shard_map/ppermute | solution.py:563
  18.1 11.7 %collective-permute-start.6 = (bf16[128,1792]{1,0:T(8,128)(2,1)S(1)}, bf16[128,1792]{1,0:T(8,128)(2,1)S(1)}, u32[]{:S(2)}, u32[]{:S(2)}) collective-permute-start(bf16[128,1792]{1,0:T(8,128)(2,1)S(1)} %pad_maximum_fusion.refs_0_.refs_2_.refs_3_), channel_id=1, source_target_pairs={{0,8},{8,0},{16,24},{24,16},{1,9},{9,1},{17,25},{25,17},{2,10},{10... | collective-permute-start | bytes 1376264 | tf_op jit(solution)/shard_map/ppermute | solution.py:563
  23.9 7.2 %collective-permute-start.5 = (bf16[64,1792]{1,0:T(8,128)(2,1)S(1)}, bf16[64,1792]{1,0:T(8,128)(2,1)S(1)}, u32[]{:S(2)}, u32[]{:S(2)}) collective-permute-start(bf16[64,1792]{1,0:T(8,128)(2,1)S(1)} %pad_maximum_fusion.1), channel_id=1, source_target_pairs={{0,1},{1,0},{2,3},{3,2},{4,5},{5,4},{6,7},{7,6},{8,9},{9,8},{10,11... | collective-permute-start | bytes 688136 | tf_op jit(solution)/shard_map/ppermute | solution.py:563
  28.3 5.7 %collective-permute-start.9 = (bf16[64,1792]{1,0:T(8,128)(2,1)S(1)}, bf16[64,1792]{1,0:T(8,128)(2,1)S(1)}, u32[]{:S(2)}, u32[]{:S(2)}) collective-permute-start(bf16[64,1792]{1,0:T(8,128)(2,1)S(1)} %slice.43), channel_id=1, source_target_pairs={{0,8},{8,0},{16,24},{24,16},{1,9},{9,1},{17,25},{25,17},{2,10},{10... | collective-permute-start | bytes 688136 | tf_op jit(solution)/shard_map/ppermute | solution.py:563
  29.8 5.6 %collective-permute-start.7 = (bf16[64,1792]{1,0:T(8,128)(2,1)S(1)}, bf16[64,1792]{1,0:T(8,128)(2,1)S(1)}, u32[]{:S(2)}, u32[]{:S(2)}) collective-permute-start(bf16[64,1792]{1,0:T(8,128)(2,1)S(1)} %slice.42), channel_id=1, source_target_pairs={{0,16},{8,24},{16,0},{24,8},{1,17},{9,25},{17,1},{25,9},{2,18},{10... | collective-permute-start | bytes 688136 | tf_op jit(solution)/shard_map/ppermute | solution.py:563
  35.4 9.5 %collective-permute-start.11 = (bf16[128,1792]{1,0:T(8,128)(2,1)S(1)}, bf16[128,1792]{1,0:T(8,128)(2,1)S(1)}, u32[]{:S(2)}, u32[]{:S(2)}) collective-permute-start(bf16[128,1792]{1,0:T(8,128)(2,1)S(1)} %arrange.4.refs_2_.refs_1_.refs_3_.refs_4_), channel_id=1, source_target_pairs={{0,16},{8,24},{16,0},{24,8},{1,17},{9,25},{17,1},{25,9},{2,18},{10... | collective-permute-start | bytes 1376264 | tf_op jit(solution)/shard_map/ppermute | solution.py:563
  36.7 9.2 %collective-permute-start.10 = (bf16[128,1792]{1,0:T(8,128)(2,1)S(1)}, bf16[128,1792]{1,0:T(8,128)(2,1)S(1)}, u32[]{:S(2)}, u32[]{:S(2)}) collective-permute-start(bf16[128,1792]{1,0:T(8,128)(2,1)S(1)} %arrange.4.refs_2_.refs_1_.refs_3_.refs_4_), channel_id=1, source_target_pairs={{0,8},{8,0},{16,24},{24,16},{1,9},{9,1},{17,25},{25,17},{2,10},{10... | collective-permute-start | bytes 1376264 | tf_op jit(solution)/shard_map/ppermute | solution.py:563
  45.0 6.5 %collective-permute-start.13 = (bf16[64,1792]{1,0:T(8,128)(2,1)S(1)}, bf16[64,1792]{1,0:T(8,128)(2,1)S(1)}, u32[]{:S(2)}, u32[]{:S(2)}) collective-permute-start(bf16[64,1792]{1,0:T(8,128)(2,1)S(1)} %slice.45), channel_id=1, source_target_pairs={{0,8},{8,0},{16,24},{24,16},{1,9},{9,1},{17,25},{25,17},{2,10},{10... | collective-permute-start | bytes 688136 | tf_op jit(solution)/shard_map/ppermute | solution.py:563
  46.0 5.5 %collective-permute-start.12 = (bf16[64,1792]{1,0:T(8,128)(2,1)S(1)}, bf16[64,1792]{1,0:T(8,128)(2,1)S(1)}, u32[]{:S(2)}, u32[]{:S(2)}) collective-permute-start(bf16[64,1792]{1,0:T(8,128)(2,1)S(1)} %slice.44), channel_id=1, source_target_pairs={{0,16},{8,24},{16,0},{24,8},{1,17},{9,25},{17,1},{25,9},{2,18},{10... | collective-permute-start | bytes 688136 | tf_op jit(solution)/shard_map/ppermute | solution.py:563
  54.6 7.1 %collective-permute-start.15 = (bf16[64,1792]{1,0:T(8,128)(2,1)S(1)}, bf16[64,1792]{1,0:T(8,128)(2,1)S(1)}, u32[]{:S(2)}, u32[]{:S(2)}) collective-permute-start(bf16[64,1792]{1,0:T(8,128)(2,1)S(1)} %get-tuple-element.65), channel_id=1, source_target_pairs={{0,8},{8,0},{16,24},{24,16},{1,9},{9,1},{17,25},{25,17},{2,10},{10... | collective-permute-start | bytes 688136 | tf_op jit(solution)/shard_map/ppermute | solution.py:563
  54.9 7.9 %collective-permute-start.16 = (bf16[64,1792]{1,0:T(8,128)(2,1)S(1)}, bf16[64,1792]{1,0:T(8,128)(2,1)S(1)}, u32[]{:S(2)}, u32[]{:S(2)}) collective-permute-start(bf16[64,1792]{1,0:T(8,128)(2,1)S(1)} %get-tuple-element.68), channel_id=1, source_target_pairs={{0,16},{8,24},{16,0},{24,8},{1,17},{9,25},{17,1},{25,9},{2,18},{10... | collective-permute-start | bytes 688136 | tf_op jit(solution)/shard_map/ppermute | solution.py:563
  56.0 11.1 %collective-permute-start.14 = (bf16[64,1792]{1,0:T(8,128)(2,1)S(1)}, bf16[64,1792]{1,0:T(8,128)(2,1)S(1)}, u32[]{:S(2)}, u32[]{:S(2)}) collective-permute-start(bf16[64,1792]{1,0:T(8,128)(2,1)S(1)} %get-tuple-element.59), channel_id=1, source_target_pairs={{0,16},{8,24},{16,0},{24,8},{1,17},{9,25},{17,1},{25,9},{2,18},{10... | collective-permute-start | bytes 688136 | tf_op jit(solution)/shard_map/ppermute | solution.py:563
  60.2 8.2 %collective-permute-start.17 = (bf16[64,1792]{1,0:T(8,128)(2,1)S(1)}, bf16[64,1792]{1,0:T(8,128)(2,1)S(1)}, u32[]{:S(2)}, u32[]{:S(2)}) collective-permute-start(bf16[64,1792]{1,0:T(8,128)(2,1)S(1)} %get-tuple-element.70), channel_id=1, source_target_pairs={{0,8},{8,0},{16,24},{24,16},{1,9},{9,1},{17,25},{25,17},{2,10},{10... | collective-permute-start | bytes 688136 | tf_op jit(solution)/shard_map/ppermute | solution.py:563
  61.5 9.5 %collective-permute-start.21 = (bf16[64,1792]{1,0:T(8,128)(2,1)S(1)}, bf16[64,1792]{1,0:T(8,128)(2,1)S(1)}, u32[]{:S(2)}, u32[]{:S(2)}) collective-permute-start(bf16[64,1792]{1,0:T(8,128)(2,1)S(1)} %get-tuple-element.75), channel_id=1, source_target_pairs={{0,8},{8,0},{16,24},{24,16},{1,9},{9,1},{17,25},{25,17},{2,10},{10... | collective-permute-start | bytes 688136 | tf_op jit(solution)/shard_map/ppermute | solution.py:563
  61.7 9.4 %collective-permute-start.18 = (bf16[64,1792]{1,0:T(8,128)(2,1)S(1)}, bf16[64,1792]{1,0:T(8,128)(2,1)S(1)}, u32[]{:S(2)}, u32[]{:S(2)}) collective-permute-start(bf16[64,1792]{1,0:T(8,128)(2,1)S(1)} %get-tuple-element.66.refs_2_), channel_id=1, source_target_pairs={{0,16},{8,24},{16,0},{24,8},{1,17},{9,25},{17,1},{25,9},{2,18},{10... | collective-permute-start | bytes 688136 | tf_op jit(solution)/shard_map/ppermute | solution.py:563
  62.8 11.4 %collective-permute-start.22 = (bf16[64,1792]{1,0:T(8,128)(2,1)S(1)}, bf16[64,1792]{1,0:T(8,128)(2,1)S(1)}, u32[]{:S(2)}, u32[]{:S(2)}) collective-permute-start(bf16[64,1792]{1,0:T(8,128)(2,1)S(1)} %add_up.10.refs_4_), channel_id=1, source_target_pairs={{0,16},{8,24},{16,0},{24,8},{1,17},{9,25},{17,1},{25,9},{2,18},{10... | collective-permute-start | bytes 688136 | tf_op jit(solution)/shard_map/ppermute | solution.py:563
  67.0 8.9 %collective-permute-start.19 = (bf16[64,1792]{1,0:T(8,128)(2,1)S(1)}, bf16[64,1792]{1,0:T(8,128)(2,1)S(1)}, u32[]{:S(2)}, u32[]{:S(2)}) collective-permute-start(bf16[64,1792]{1,0:T(8,128)(2,1)S(1)} %add_up.11.refs_5_), channel_id=1, source_target_pairs={{0,8},{8,0},{16,24},{24,16},{1,9},{9,1},{17,25},{25,17},{2,10},{10... | collective-permute-start | bytes 688136 | tf_op jit(solution)/shard_map/ppermute | solution.py:563
  68.3 12.5 %collective-permute-start.29 = (bf16[64,1792]{1,0:T(8,128)(2,1)S(1)}, bf16[64,1792]{1,0:T(8,128)(2,1)S(1)}, u32[]{:S(2)}, u32[]{:S(2)}) collective-permute-start(bf16[64,1792]{1,0:T(8,128)(2,1)S(1)} %get-tuple-element.86), channel_id=1, source_target_pairs={{0,8},{8,0},{16,24},{24,16},{1,9},{9,1},{17,25},{25,17},{2,10},{10... | collective-permute-start | bytes 688136 | tf_op jit(solution)/shard_map/ppermute | solution.py:563
  71.0 15.9 %collective-permute-start.30 = (bf16[64,1792]{1,0:T(8,128)(2,1)S(1)}, bf16[64,1792]{1,0:T(8,128)(2,1)S(1)}, u32[]{:S(2)}, u32[]{:S(2)}) collective-permute-start(bf16[64,1792]{1,0:T(8,128)(2,1)S(1)} %add_up.12.refs_2_.refs_3_), channel_id=1, source_target_pairs={{0,16},{8,24},{16,0},{24,8},{1,17},{9,25},{17,1},{25,9},{2,18},{10... | collective-permute-start | bytes 688136 | tf_op jit(solution)/shard_map/ppermute | solution.py:563
  71.1 19.7 %collective-permute-start.26 = (bf16[64,1792]{1,0:T(8,128)(2,1)S(1)}, bf16[64,1792]{1,0:T(8,128)(2,1)S(1)}, u32[]{:S(2)}, u32[]{:S(2)}) collective-permute-start(bf16[64,1792]{1,0:T(8,128)(2,1)S(1)} %get-tuple-element.80), channel_id=1, source_target_pairs={{0,16},{8,24},{16,0},{24,8},{1,17},{9,25},{17,1},{25,9},{2,18},{10... | collective-permute-start | bytes 688136 | tf_op jit(solution)/shard_map/ppermute | solution.py:563
  74.2 17.1 %collective-permute-start.27 = (bf16[64,1792]{1,0:T(8,128)(2,1)S(1)}, bf16[64,1792]{1,0:T(8,128)(2,1)S(1)}, u32[]{:S(2)}, u32[]{:S(2)}) collective-permute-start(bf16[64,1792]{1,0:T(8,128)(2,1)S(1)} %add_up.13.refs_3_.refs_4_), channel_id=1, source_target_pairs={{0,8},{8,0},{16,24},{24,16},{1,9},{9,1},{17,25},{25,17},{2,10},{10... | collective-permute-start | bytes 688136 | tf_op jit(solution)/shard_map/ppermute | solution.py:563
  75.9 18.7 %collective-permute-start.24 = (bf16[32,1792]{1,0:T(8,128)(2,1)S(1)}, bf16[32,1792]{1,0:T(8,128)(2,1)S(1)}, u32[]{:S(2)}, u32[]{:S(2)}) collective-permute-start(bf16[32,1792]{1,0:T(8,128)(2,1)S(1)} %get-tuple-element.77), channel_id=1, source_target_pairs={{0,6},{1,7},{2,4},{3,5},{4,2},{5,3},{6,0},{7,1},{8,14},{9,15},{10,... | collective-permute-start | bytes 344072 | tf_op jit(solution)/shard_map/ppermute | solution.py:563
  80.8 13.9 %collective-permute-start.23 = (bf16[32,1792]{1,0:T(8,128)(2,1)S(1)}, bf16[32,1792]{1,0:T(8,128)(2,1)S(1)}, u32[]{:S(2)}, u32[]{:S(2)}) collective-permute-start(bf16[32,1792]{1,0:T(8,128)(2,1)S(1)} %get-tuple-element.76.refs_13_), channel_id=1, source_target_pairs={{0,4},{1,5},{2,6},{3,7},{4,0},{5,1},{6,2},{7,3},{8,12},{9,13},{10,... | collective-permute-start | bytes 344072 | tf_op jit(solution)/shard_map/ppermute | solution.py:563
  86.8 7.9 %collective-permute-start.20 = (bf16[32,1792]{1,0:T(8,128)(2,1)S(1)}, bf16[32,1792]{1,0:T(8,128)(2,1)S(1)}, u32[]{:S(2)}, u32[]{:S(2)}) collective-permute-start(bf16[32,1792]{1,0:T(8,128)(2,1)S(1)} %get-tuple-element.73), channel_id=1, source_target_pairs={{0,2},{1,3},{2,0},{3,1},{4,6},{5,7},{6,4},{7,5},{8,10},{9,11},{10,... | collective-permute-start | bytes 344072 | tf_op jit(solution)/shard_map/ppermute | solution.py:563
  90.8 11.2 %collective-permute-start.31 = (bf16[32,1792]{1,0:T(8,128)(2,1)S(1)}, bf16[32,1792]{1,0:T(8,128)(2,1)S(1)}, u32[]{:S(2)}, u32[]{:S(2)}) collective-permute-start(bf16[32,1792]{1,0:T(8,128)(2,1)S(1)} %get-tuple-element.87), channel_id=1, source_target_pairs={{0,4},{1,5},{2,6},{3,7},{4,0},{5,1},{6,2},{7,3},{8,12},{9,13},{10,... | collective-permute-start | bytes 344072 | tf_op jit(solution)/shard_map/ppermute | solution.py:563
  91.3 16.6 %collective-permute-start.32 = (bf16[32,1792]{1,0:T(8,128)(2,1)S(1)}, bf16[32,1792]{1,0:T(8,128)(2,1)S(1)}, u32[]{:S(2)}, u32[]{:S(2)}) collective-permute-start(bf16[32,1792]{1,0:T(8,128)(2,1)S(1)} %get-tuple-element.88), channel_id=1, source_target_pairs={{0,6},{1,7},{2,4},{3,5},{4,2},{5,3},{6,0},{7,1},{8,14},{9,15},{10,... | collective-permute-start | bytes 344072 | tf_op jit(solution)/shard_map/ppermute | solution.py:563
  94.6 13.3 %collective-permute-start.28 = (bf16[32,1792]{1,0:T(8,128)(2,1)S(1)}, bf16[32,1792]{1,0:T(8,128)(2,1)S(1)}, u32[]{:S(2)}, u32[]{:S(2)}) collective-permute-start(bf16[32,1792]{1,0:T(8,128)(2,1)S(1)} %get-tuple-element.84), channel_id=1, source_target_pairs={{0,2},{1,3},{2,0},{3,1},{4,6},{5,7},{6,4},{7,5},{8,10},{9,11},{10,... | collective-permute-start | bytes 344072 | tf_op jit(solution)/shard_map/ppermute | solution.py:563
  94.7 17.1 %collective-permute-start.25 = (bf16[64,1792]{1,0:T(8,128)(2,1)S(1)}, bf16[64,1792]{1,0:T(8,128)(2,1)S(1)}, u32[]{:S(2)}, u32[]{:S(2)}) collective-permute-start(bf16[64,1792]{1,0:T(8,128)(2,1)S(1)} %pad_maximum_fusion.2), channel_id=1, source_target_pairs={{0,1},{1,0},{2,3},{3,2},{4,5},{5,4},{6,7},{7,6},{8,9},{9,8},{10,11... | collective-permute-start | bytes 688136 | tf_op jit(solution)/shard_map/ppermute | solution.py:563
  107.9 5.5 %collective-permute-start.33 = (bf16[64,1792]{1,0:T(8,128)(2,1)S(1)}, bf16[64,1792]{1,0:T(8,128)(2,1)S(1)}, u32[]{:S(2)}, u32[]{:S(2)}) collective-permute-start(bf16[64,1792]{1,0:T(8,128)(2,1)S(1)} %arrange.5), channel_id=1, source_target_pairs={{0,1},{1,0},{2,3},{3,2},{4,5},{5,4},{6,7},{7,6},{8,9},{9,8},{10,11... | collective-permute-start | bytes 688136 | tf_op jit(solution)/shard_map/ppermute | solution.py:563

commit v3 on v2

--- a/solution.py
+++ b/solution.py
@@ -24,7 +24,7 @@
         out_specs.append(IN_VMEM)
 
     def run(*refs):
-        refs = [*refs[:used], *refs[used + len(later) :]]
+        refs = list(refs[len(later) :])
         if mark:
             mark_ref = refs.pop(used + results)
             mark_ref[...] = jnp.zeros_like(mark_ref)
@@ -33,13 +33,13 @@
     out = pl.pallas_call(
         run,
         name=name,
-        in_specs=[*specs, *[ANYWHERE] * len(later)],
+        in_specs=[*[ANYWHERE] * len(later), *specs],
         out_shape=outs,
         out_specs=out_specs,
         scratch_shapes=scratch,
         compiler_params=pltpu.CompilerParams(vmem_limit_bytes=mib * MIB),
         cost_estimate=pl.CostEstimate(flops=1024, bytes_accessed=cost, transcendentals=0),
-    )(*operands, *later)
+    )(*later, *operands)
     return out if len(out) > 1 else out[0]
 
 
@@ -279,70 +279,123 @@
         return jnp.concatenate(blocks, axis=0)
 
 
-def store_halves(refs, index, term):
-    size = term.shape[0] // 2
-    refs[2 * index][...] = term[:size].astype(jnp.bfloat16)
-    refs[2 * index + 1][...] = term[size:].astype(jnp.bfloat16)
-
-
-def forward_body(slices, *refs):
-    gate_ref, up_ref, down_ref, hidden_ref, slope_ref, silu_ref, *terms = refs[len(slices.flat) :]
-    count = gate_ref.shape[0]
-    gate = up = None
-    for index in range(count):
-        rows = slices.read(refs, index)
-        more_gate = jnp.dot(rows, gate_ref[index], preferred_element_type=jnp.float32)
-        more_up = jnp.dot(rows, up_ref[index], preferred_element_type=jnp.float32)
-        gate = more_gate if gate is None else gate + more_gate
-        up = more_up if up is None else up + more_up
+def gather_slices(pieces, slots):
+    parts = []
+    for part in range(2):
+        blocks = []
+        for ref in pieces:
+            for start in range(part * slots, ref.shape[0], 2 * slots):
+                blocks.append(ref[pl.ds(start, slots), :])
+        parts.append(jnp.concatenate(blocks, axis=0))
+    return parts
+
+
+def products(pieces, slots, index, gate_ref, up_ref, down_ref):
+    tokens, grads = gather_slices(pieces, slots)
+    return (
+        jnp.dot(tokens, gate_ref[index], preferred_element_type=jnp.float32),
+        jnp.dot(tokens, up_ref[index], preferred_element_type=jnp.float32),
+        lax.dot_general(grads, down_ref[index], LAST, preferred_element_type=jnp.float32),
+    )
+
+
+def partial_body(counts, slots, *refs):
+    gate_ref, up_ref, down_ref, *sums = refs[sum(counts) :]
+    for index in range(len(counts)):
+        first = sum(counts[:index])
+        pieces = refs[first : first + counts[index]]
+        more = products(pieces, slots, index, gate_ref, up_ref, down_ref)
+        for sum_ref, value in zip(sums, more):
+            if index == 0:
+                sum_ref[...] = value
+            else:
+                sum_ref[...] += value
+
+
+def partial_products(slices, slots, gate, up, down, later=()):
+    counts = [len(pieces) for pieces in slices]
+    flat = [piece for pieces in slices for piece in pieces]
+    rows = sum(piece.shape[0] for piece in slices[0]) // 2
+    return run_kernel(
+        functools.partial(partial_body, counts, slots),
+        "partial_products",
+        (*flat, gate, up, down),
+        [IN_VMEM] * (len(flat) + 3),
+        [like(rows, gate.shape[2], jnp.float32)] * 3,
+        [IN_VMEM] * 3,
+        [],
+        8,
+        later,
+    )
+
+
+def hidden_body(used, slots, *refs):
+    sums, gate_ref, up_ref, down_ref = refs[used : used + 3], *refs[used + 3 : used + 6]
+    hidden_ref, gate_grad_ref, up_grad_ref, *terms = refs[used + 6 :]
+    last = gate_ref.shape[0] - 1
+    more = products(refs[:used], slots, last, gate_ref, up_ref, down_ref)
+    gate, up, grad = [sum_ref[...] + value for sum_ref, value in zip(sums, more)]
     sigmoid = jax.nn.sigmoid(gate)
     silu = gate * sigmoid
     hidden = (silu * up).astype(jnp.bfloat16)
     hidden_ref[...] = hidden
-    slope_ref[...] = up * sigmoid * (1.0 + gate * (1.0 - sigmoid))
-    silu_ref[...] = silu
-    for index in reversed(range(count)):
+    gate_grad_ref[...] = (grad * (up * sigmoid * (1.0 + gate * (1.0 - sigmoid)))).astype(
+        jnp.bfloat16
+    )
+    up_grad_ref[...] = (grad * silu).astype(jnp.bfloat16)
+    for index in reversed(range(last + 1)):
         term = jnp.dot(hidden, down_ref[index], preferred_element_type=jnp.float32)
-        store_halves(terms, index, term)
-
-
-def forward_terms(slices, gate, up, down, later=()):
+        store_term(terms, index, term)
+
+
+def store_term(refs, index, term):
+    term = term.astype(jnp.bfloat16)
+    if index < len(refs) - 2:
+        refs[index][...] = term
+    else:
+        size = term.shape[0] // 2
+        refs[index][...] = term[:size]
+        refs[index + 1][...] = term[size:]
+
+
+def hidden_units(pieces, slots, sums, gate, up, down, later=()):
     count, width, units = gate.shape
-    rows = slices.rows
-    outs = [like(rows, units), like(rows, units, jnp.float32), like(rows, units, jnp.float32)]
-    outs += [like(rows // 2, width)] * (2 * count)
+    rows = sums[0].shape[0]
     out = run_kernel(
-        functools.partial(forward_body, slices),
-        "forward_terms",
-        (*slices.flat, gate, up, down),
-        [IN_VMEM] * (len(slices.flat) + 3),
-        outs,
-        [IN_VMEM] * len(outs),
+        functools.partial(hidden_body, len(pieces), slots),
+        "hidden_units",
+        (*pieces, *sums, gate, up, down),
+        [IN_VMEM] * (len(pieces) + 6),
+        [like(rows, units)] * 3
+        + [like(rows, width)] * (count - 1)
+        + [like(rows // 2, width)] * 2,
+        [IN_VMEM] * (4 + count),
         [],
         8,
         later,
     )
-    return out[:3], [out[3 + 2 * i : 5 + 2 * i] for i in range(count)]
-
-
-def hidden_grad_body(slices, *refs):
-    down_ref, slope_ref, silu_ref, gate_grad_ref, up_grad_ref = refs[len(slices.flat) :]
-    grad = None
-    for index in range(down_ref.shape[0]):
-        rows = slices.read(refs, index)
-        more = lax.dot_general(rows, down_ref[index], LAST, preferred_element_type=jnp.float32)
-        grad = more if grad is None else grad + more
-    gate_grad_ref[...] = (grad * slope_ref[...]).astype(jnp.bfloat16)
-    up_grad_ref[...] = (grad * silu_ref[...]).astype(jnp.bfloat16)
-
-
-def hidden_grads(slices, down, slope, silu, later=()):
-    return run_kernel(
-        functools.partial(hidden_grad_body, slices),
-        "hidden_grads",
-        (*slices.flat, down, slope, silu),
-        [IN_VMEM] * (len(slices.flat) + 3),
-        [like(*slope.shape)] * 2,
+    return out[:3], out[3:]
+
+
+def merge_body(first_ref, second_ref, top_ref, bottom_ref, first_out, second_out):
+    size = top_ref.shape[0]
+    top, bottom = pl.ds(0, size), pl.ds(size, size)
+    for rows, part, source, other, out, other_out in (
+        (top, top_ref, first_ref, second_ref, first_out, second_out),
+        (bottom, bottom_ref, second_ref, first_ref, second_out, first_out),
+    ):
+        total = source[rows, :].astype(jnp.float32) + part[...].astype(jnp.float32)
+        out[rows, :] = total.astype(out.dtype)
+        other_out[rows, :] = other[rows, :]
+
+
+def merge(first, second, top, bottom, later=()):
+    return run_kernel(
+        merge_body,
+        "merge",
+        (first, second, top, bottom),
+        [IN_VMEM] * 4,
+        [like(*first.shape)] * 2,
         [IN_VMEM] * 2,
         [],
         8,
@@ -358,7 +411,9 @@
         term += lax.dot_general(
             up_grad_ref[...], up_ref[index], LAST, preferred_element_type=jnp.float32
         )
-        store_halves(terms, place, term)
+        size = term.shape[0] // 2
+        terms[2 * place][...] = term[:size].astype(jnp.bfloat16)
+        terms[2 * place + 1][...] = term[size:].astype(jnp.bfloat16)
 
 
 def grad_terms(wanted, gate_grad, up_grad, gate, up, later=()):
@@ -599,7 +654,9 @@
     near_d = [swap(near_x[:half], 2, "fsdp"), swap(near_y[half:], 1, "fsdp")]
     odd = swap(joined(pair2[two:], pair3[two:]), 1, "ep")
     far = arrange(
-        (pair2, pair3, odd), [[(0, 0, two), (2, 0, two), (1, 0, two), (2, two, two)]], tuple(near_d)
+        (pair2, pair3, odd),
+        [[(0, 0, two), (2, 0, two), (1, 0, two), (2, two, two)]],
+        (near_x, near_y),
     )
     far_x = swap(far, 1, "fsdp")
     far_y = swap(far, 2, "fsdp")
@@ -608,37 +665,32 @@
     pieces = [[near, far], [near_x, far_x], [near_y, far_y], near_d + far_d]
     tokens, grads = Slices(pieces, 0, slots), Slices(pieces, 1, slots)
 
-    (hidden, slope, silu), terms = forward_terms(tokens, gate, up, down)
-    far_sum_d = swap(terms[3][1], 1, "fsdp")
-    near_sum_d = swap(terms[3][0], 2, "fsdp")
-    far_sum_x = swap(terms[1][1], 1, "fsdp")
-    near_sum_y = swap(terms[2][0], 2, "fsdp")
-    gate_grad, up_grad = hidden_grads(grads, down, slope, silu, (terms[0][0],))
-    back_d = grad_terms((3,), gate_grad, up_grad, gate, up)[0]
+    sums = partial_products(pieces[:3], slots, gate, up, down)
+    (hidden, gate_grad, up_grad), terms = hidden_units(pieces[3], slots, sums, gate, up, down)
+    top = swap(terms[3], 2, "fsdp")
+    bottom = swap(terms[4], 1, "fsdp")
+    back = grad_terms((3, 1, 2, 0), gate_grad, up_grad, gate, up, (terms[0],))
+    back_d, back_x, back_y, back_own = back
     far_back_d = swap(back_d[1], 1, "fsdp")
     near_back_d = swap(back_d[0], 2, "fsdp")
-    far_sum_y = add_up([terms[2][1], far_sum_d], 1, (back_d[0],))
-    near_sum_x = add_up([terms[1][0], near_sum_d], 1, (back_d[0],))
-    back = grad_terms((0, 1, 2), gate_grad, up_grad, gate, up, (far_sum_y, near_sum_x))
-    far_sum_y = swap(far_sum_y, 2, "fsdp")
-    near_sum_x = swap(near_sum_x, 1, "fsdp")
-    far_back_x = swap(back[1][1], 1, "fsdp")
-    near_back_y = swap(back[2][0], 2, "fsdp")
-    far_back_y = add_up([back[2][1], far_back_d])
-    near_back_x = add_up([back[1][0], near_back_d])
+    far_back_x = swap(back_x[1], 1, "fsdp")
+    sum_x, sum_y = merge(terms[1], terms[2], top, bottom, (back_own[0],))
+    sum_x = swap(sum_x, 1, "fsdp")
+    sum_y = swap(sum_y, 2, "fsdp")
+
+    far_back_y = add_up([back_y[1], far_back_d])
+    near_back_x = add_up([back_x[0], near_back_d])
     sent = (far_back_y, near_back_x)
     far_back_y = swap(far_back_y, 2, "fsdp")
     near_back_x = swap(near_back_x, 1, "fsdp")
-    out2, out3 = add_up([terms[0][1], far_sum_x, far_sum_y], 2, sent)
-    near_sum_y = add_up([terms[0][0], near_sum_y], 1, sent, LONG)
-    out0, out1 = add_up([near_sum_y, near_sum_x], 2)
-    grad_down, down_mark = down_grads(me, hidden, grads, (out0, out2))
+    near_back_y = swap(back_y[0], 2, "fsdp")
+    grad_down, down_mark = down_grads(me, hidden, grads, sent)
+    out0, out1, out2, out3 = add_up([terms[0], sum_x, sum_y], 4, (down_mark,))
     out3 = swap(out3, 6, "ep")
     out2 = swap(out2, 4, "ep")
     out1 = swap(out1, 2, "ep")
-    back2, back3 = add_up([back[0][1], far_back_x, far_back_y], 2, (down_mark,))
-    near_back_y = add_up([back[0][0], near_back_y], 1, (down_mark,), LONG)
-    back0, back1 = add_up([near_back_y, near_back_x], 2)
+    back2, back3 = add_up([back_own[1], far_back_x, far_back_y], 2, (down_mark,))
+    back0, back1 = add_up([back_own[0], near_back_x, near_back_y], 2, (down_mark,))
     back3 = swap(back3, 6, "ep")
     back2 = swap(back2, 4, "ep")
     back1 = swap(back1, 2, "ep")

time: 115 us -> 111 us (0.965)
  waiting for transfers between devices: 29.1 us -> 26 us
  starting transfers between devices: 48.2 us -> 46.9 us
    ppermute x34 -> x32, waiting for transfers between devices: 29.1 us -> 26 us  [swap(): return lax.ppermute(array, axis, [(i, i ^ distance) for i in range(size)])]
    ppermute x34 -> x32, starting transfers between devices: 48.2 us -> 46.9 us  [swap(): return lax.ppermute(array, axis, [(i, i ^ distance) for i in range(size)])]
    pallas_call x26 -> x21, Pallas kernels: 36.5 us -> 36.3 us  [run_kernel(): pl.pallas_call(run, name=name, in_specs=[*[ANYWHERE] * len(later), *specs...]
  transfers between devices with their start and end apart: 34 -> 32, of which waited for: 12 -> 10; matrix products, arithmetic and copies ran while one was open for 0% -> 0% of each run, Pallas kernels for 25% -> 27%
where the time goes in v3:
time: 111 us; the launch traced here: 110 us
  starting transfers between devices  46.9 us (42%)
  Pallas kernels  36.3 us (33%)
  waiting for transfers between devices  26 us (23%)
    ppermute x32, starting transfers between devices, swap(): return lax.ppermute(array, axis, [(i, i ^ distance) for i in range(size)])  46.9 us
    pallas_call x21, Pallas kernels, run_kernel(): pl.pallas_call(run, name=name, in_specs=[*[ANYWHERE] * len(later), *specs...  36.3 us
    ppermute x32, waiting for transfers between devices, swap(): return lax.ppermute(array, axis, [(i, i ^ distance) for i in range(size)])  26 us
  transfers between devices with their start and end apart: 32, of which 10 were waited for; matrix products, arithmetic and copies ran while one was open for 0% of the time, Pallas kernels for 27%

profile of v3, /device:TPU:1, one launch (start us, length us, event | category | flops | bytes accessed | tf_op | source)
XLA Modules:
  0.0 110.4 jit_solution(16292453094059350504)
XLA Ops:
  0.6 2.6 %pick_slots.1 = (bf16[32,1792]{1,0:T(8,128)(2,1)S(1)}, bf16[32,1792]{1,0:T(8,128)(2,1)S(1)}, bf16[32,1792]{1,0:T(8,128)(2,1)S(1)}, bf16[32,1792]{1,0:T(8,128)(2,...) custom-call(s32[1]{0:T(128)} %bitcast.refs_0_, ...), custom_call_target="tpu_custom_call" | custom-call | flops 1024 | bytes 1024 | tf_op jit(solution)/shard_map/pick_slots/pallas_call | solution.py:33
  3.2 0.1 collective-permute-start
  3.3 2.8 %collective-permute-start.1 = (bf16[32,1792]{1,0:T(8,128)(2,1)S(1)}, bf16[32,1792]{1,0:T(8,128)(2,1)S(1)}, u32[]{:S(2)}, u32[]{:S(2)}) collective-permute-start(bf16[32,1792]{1,0:T(8,128)(2,1)S(1)} %get-tuple-element.54), channel_id=1, source_target_pairs={{0,2},{1,3},{2,0},{3,1},{4,6},{5,7},{6,4},{7,5},{8,10},{9,11},{10,... | collective-permute-start | bytes 344072 | tf_op jit(solution)/shard_map/ppermute | solution.py:618
  6.1 0.0 collective-permute-start.2
  6.1 2.7 %collective-permute-start.7 = (bf16[64,1792]{1,0:T(8,128)(2,1)S(1)}, bf16[64,1792]{1,0:T(8,128)(2,1)S(1)}, u32[]{:S(2)}, u32[]{:S(2)}) collective-permute-start(bf16[64,1792]{1,0:T(8,128)(2,1)S(1)} %get-tuple-element.56), channel_id=1, source_target_pairs={{0,4},{1,5},{2,6},{3,7},{4,0},{5,1},{6,2},{7,3},{8,12},{9,13},{10,... | collective-permute-start | bytes 688136 | tf_op jit(solution)/shard_map/ppermute | solution.py:618
  8.8 1.1 collective-permute-start.8
  9.9 3.2 %load_weight.3.refs_0_.refs_6_.refs_7_.refs_3_ = bf16[4,1792,512]{2,1,0:T(8,128)(2,1)S(1)} custom-call(bf16[32,1792]{1,0:T(8,128)(2,1)S(1)} %get-tuple-element.49.refs_0_.refs_1_, s32[1]{0:T(128)} %bitcast.2.refs_1_.refs_2_, bf16[7168,512]{1,0:T(8,128)(2,1)} %bitcast.9), custom_call_target="tpu_custom_call" | custom-call | flops 1024 | bytes 1024 | tf_op jit(solution)/shard_map/load_weight/pallas_call | solution.py:33
  13.1 3.2 %load_weight.4.refs_0_.refs_7_.refs_8_.refs_4_ = bf16[4,1792,512]{2,1,0:T(8,128)(2,1)S(1)} custom-call(bf16[4,1792,512]{2,1,0:T(8,128)(2,1)S(1)} %load_weight.3.refs_0_.refs_6_.refs_7_.refs_3_, s32[1]{0:T(128)} %bitcast.2.refs_1_.refs_2_, bf16[7168,512]{1,0:T(8,128)(2,1)} %bitcast.11), custom_call_target="tpu_custom_call" | custom-call | flops 1024 | bytes 1024 | tf_op jit(solution)/shard_map/load_weight/pallas_call | solution.py:33
  16.3 0.2 spread_matrices.1
  16.5 0.0 collective-permute-done
  16.5 0.2 collective-permute-done.2
  16.7 1.4 %collective-permute-start.5 = (bf16[128,1792]{1,0:T(8,128)(2,1)S(1)}, bf16[128,1792]{1,0:T(8,128)(2,1)S(1)}, u32[]{:S(2)}, u32[]{:S(2)}) collective-permute-start(bf16[128,1792]{1,0:T(8,128)(2,1)S(1)} %pad_maximum_fusion.refs_0_.refs_4_.refs_5_), channel_id=1, source_target_pairs={{0,16},{8,24},{16,0},{24,8},{1,17},{9,25},{17,1},{25,9},{2,18},{10... | collective-permute-start | bytes 1376264 | tf_op jit(solution)/shard_map/ppermute | solution.py:618
  18.1 1.2 %collective-permute-start.3 = (bf16[128,1792]{1,0:T(8,128)(2,1)S(1)}, bf16[128,1792]{1,0:T(8,128)(2,1)S(1)}, u32[]{:S(2)}, u32[]{:S(2)}) collective-permute-start(bf16[128,1792]{1,0:T(8,128)(2,1)S(1)} %pad_maximum_fusion.refs_0_.refs_4_.refs_5_), channel_id=1, source_target_pairs={{0,8},{8,0},{16,24},{24,16},{1,9},{9,1},{17,25},{25,17},{2,10},{10... | collective-permute-start | bytes 1376264 | tf_op jit(solution)/shard_map/ppermute | solution.py:618
  19.4 4.5 %collective-permute-done.8.refs_3_ = bf16[64,1792]{1,0:T(8,128)(2,1)S(1)} collective-permute-done((bf16[64,1792]{1,0:T(8,128)(2,1)S(1)}, bf16[64,1792]{1,0:T(8,128)(2,1)S(1)}, u32[]{:S(2)}, u32[]{:S(2)}) %collective-permute-start.8) | collective-permute-done | bytes 229408 | tf_op jit(solution)/shard_map/ppermute | solution.py:618
  23.9 1.9 %collective-permute-start.9 = (bf16[64,1792]{1,0:T(8,128)(2,1)S(1)}, bf16[64,1792]{1,0:T(8,128)(2,1)S(1)}, u32[]{:S(2)}, u32[]{:S(2)}) collective-permute-start(bf16[64,1792]{1,0:T(8,128)(2,1)S(1)} %pad_maximum_fusion.1), channel_id=1, source_target_pairs={{0,1},{1,0},{2,3},{3,2},{4,5},{5,4},{6,7},{7,6},{8,9},{9,8},{10,11... | collective-permute-start | bytes 688136 | tf_op jit(solution)/shard_map/ppermute | solution.py:618
  25.8 1.1 %collective-permute-done.9.refs_4_ = bf16[64,1792]{1,0:T(8,128)(2,1)S(1)} collective-permute-done((bf16[64,1792]{1,0:T(8,128)(2,1)S(1)}, bf16[64,1792]{1,0:T(8,128)(2,1)S(1)}, u32[]{:S(2)}, u32[]{:S(2)}) %collective-permute-start.9) | collective-permute-done | bytes 229408 | tf_op jit(solution)/shard_map/ppermute | solution.py:618
  26.9 1.4 %collective-permute-done.5.refs_1_.refs_4_.refs_8_.refs_9_ = bf16[128,1792]{1,0:T(8,128)(2,1)S(1)} collective-permute-done((bf16[128,1792]{1,0:T(8,128)(2,1)S(1)}, bf16[128,1792]{1,0:T(8,128)(2,1)S(1)}, u32[]{:S(2)}, u32[]{:S(2)}) %collective-permute-start.5) | collective-permute-done | bytes 458784 | tf_op jit(solution)/shard_map/ppermute | solution.py:618
  28.3 1.1 %collective-permute-done.3.refs_0_.refs_2_.refs_6_.refs_7_ = bf16[128,1792]{1,0:T(8,128)(2,1)S(1)} collective-permute-done((bf16[128,1792]{1,0:T(8,128)(2,1)S(1)}, bf16[128,1792]{1,0:T(8,128)(2,1)S(1)}, u32[]{:S(2)}, u32[]{:S(2)}) %collective-permute-start.3) | collective-permute-done | bytes 458784 | tf_op jit(solution)/shard_map/ppermute | solution.py:618
  29.5 0.4 collective-permute-start.12
  29.9 1.2 %collective-permute-start.10 = (bf16[128,1792]{1,0:T(8,128)(2,1)S(1)}, bf16[128,1792]{1,0:T(8,128)(2,1)S(1)}, u32[]{:S(2)}, u32[]{:S(2)}) collective-permute-start(bf16[128,1792]{1,0:T(8,128)(2,1)S(1)} %arrange.4.refs_0_.refs_1_.refs_5_.refs_6_), channel_id=1, source_target_pairs={{0,8},{8,0},{16,24},{24,16},{1,9},{9,1},{17,25},{25,17},{2,10},{10... | collective-permute-start | bytes 1376264 | tf_op jit(solution)/shard_map/ppermute | solution.py:618
  31.1 0.3 collective-permute-start.6
  31.4 1.2 %collective-permute-start.4 = (bf16[64,1792]{1,0:T(8,128)(2,1)S(1)}, bf16[64,1792]{1,0:T(8,128)(2,1)S(1)}, u32[]{:S(2)}, u32[]{:S(2)}) collective-permute-start(bf16[64,1792]{1,0:T(8,128)(2,1)S(1)} %slice.40), channel_id=1, source_target_pairs={{0,16},{8,24},{16,0},{24,8},{1,17},{9,25},{17,1},{25,9},{2,18},{10... | collective-permute-start | bytes 688136 | tf_op jit(solution)/shard_map/ppermute | solution.py:618
  32.6 7.3 %collective-permute-done.12.refs_5_.refs_9_.refs_10_ = bf16[128,1792]{1,0:T(8,128)(2,1)S(1)} collective-permute-done((bf16[128,1792]{1,0:T(8,128)(2,1)S(1)}, bf16[128,1792]{1,0:T(8,128)(2,1)S(1)}, u32[]{:S(2)}, u32[]{:S(2)}) %collective-permute-start.12) | collective-permute-done | bytes 458784 | tf_op jit(solution)/shard_map/ppermute | solution.py:618
  39.9 1.3 %collective-permute-start.13 = (bf16[64,1792]{1,0:T(8,128)(2,1)S(1)}, bf16[64,1792]{1,0:T(8,128)(2,1)S(1)}, u32[]{:S(2)}, u32[]{:S(2)}) collective-permute-start(bf16[64,1792]{1,0:T(8,128)(2,1)S(1)} %slice.45), channel_id=1, source_target_pairs={{0,8},{8,0},{16,24},{24,16},{1,9},{9,1},{17,25},{25,17},{2,10},{10... | collective-permute-start | bytes 688136 | tf_op jit(solution)/shard_map/ppermute | solution.py:618
  41.2 0.5 collective-permute-start.11
  41.7 3.2 %load_weight.5.refs_8_.refs_9_ = bf16[4,512,1792]{2,1,0:T(8,128)(2,1)S(1)} custom-call(bf16[128,1792]{1,0:T(8,128)(2,1)S(1)} %arrange.4.refs_0_.refs_1_.refs_5_.refs_6_, s32[1]{0:T(128)} %bitcast.2.refs_1_.refs_2_, bf16[512,7168]{1,0:T(8,128)(2,1)} %bitcast.10), custom_call_target="tpu_custom_call" | custom-call | flops 1024 | bytes 1024 | tf_op jit(solution)/shard_map/load_weight/pallas_call | solution.py:33
  44.9 3.3 %partial_products.1 = (f32[128,512]{1,0:T(8,128)S(1)}, f32[128,512]{1,0:T(8,128)S(1)}, f32[128,512]{1,0:T(8,128)S(1)}) custom-call(bf16[128,1792]{1,0:T(8,128)(2,1)S(1)} %pad_maximum_fusion.refs_0_.refs_4_.refs_5_, bf16[128,1792]{1,0:T(8,128)(2,1)S(1)} %arrange.4.refs_0_.refs_1_.refs_5_.refs_6_, ...), custom_call_target="tpu_custom_call" | custom-call | flops 1024 | bytes 1024 | tf_op jit(solution)/shard_map/partial_products/pallas_call | solution.py:33
  48.3 1.7 %collective-permute-done.13.refs_3_.refs_13_.refs_14_ = bf16[64,1792]{1,0:T(8,128)(2,1)S(1)} collective-permute-done((bf16[64,1792]{1,0:T(8,128)(2,1)S(1)}, bf16[64,1792]{1,0:T(8,128)(2,1)S(1)}, u32[]{:S(2)}, u32[]{:S(2)}) %collective-permute-start.13) | collective-permute-done | bytes 229408 | tf_op jit(solution)/shard_map/ppermute | solution.py:618
  50.0 2.3 %hidden_units.1 = (bf16[128,512]{1,0:T(8,128)(2,1)S(1)}, bf16[128,512]{1,0:T(8,128)(2,1)S(1)}, bf16[128,512]{1,0:T(8,128)(2,1)S(1)}, bf16[128,1792]{1,0:T(8,128)...) custom-call(bf16[64,1792]{1,0:T(8,128)(2,1)S(1)} %collective-permute, ...), custom_call_target="tpu_custom_call" | custom-call | flops 1024 | bytes 1024 | tf_op jit(solution)/shard_map/hidden_units/pallas_call | solution.py:33
  52.3 1.0 collective-permute-start.16
  53.3 1.2 %collective-permute-start.17 = (bf16[64,1792]{1,0:T(8,128)(2,1)S(1)}, bf16[64,1792]{1,0:T(8,128)(2,1)S(1)}, u32[]{:S(2)}, u32[]{:S(2)}) collective-permute-start(bf16[64,1792]{1,0:T(8,128)(2,1)S(1)} %get-tuple-element.74), channel_id=1, source_target_pairs={{0,8},{8,0},{16,24},{24,16},{1,9},{9,1},{17,25},{25,17},{2,10},{10... | collective-permute-start | bytes 688136 | tf_op jit(solution)/shard_map/ppermute | solution.py:618
  54.5 4.8 %grad_terms.1 = (bf16[64,1792]{1,0:T(8,128)(2,1)S(1)}, bf16[64,1792]{1,0:T(8,128)(2,1)S(1)}, bf16[64,1792]{1,0:T(8,128)(2,1)S(1)}, bf16[64,1792]{1,0:T(8,128)(2,...) custom-call(bf16[128,1792]{1,0:T(8,128)(2,1)S(1)} %get-tuple-element, ...), custom_call_target="tpu_custom_call" | custom-call | flops 1024 | bytes 1024 | tf_op jit(solution)/shard_map/grad_terms/pallas_call | solution.py:33
  59.3 0.3 collective-permute-start.14
  59.6 0.5 collective-permute-start.15
  60.1 1.1 %collective-permute-start.27 = (bf16[64,1792]{1,0:T(8,128)(2,1)S(1)}, bf16[64,1792]{1,0:T(8,128)(2,1)S(1)}, u32[]{:S(2)}, u32[]{:S(2)}) collective-permute-start(bf16[64,1792]{1,0:T(8,128)(2,1)S(1)} %get-tuple-element.86), channel_id=1, source_target_pairs={{0,8},{8,0},{16,24},{24,16},{1,9},{9,1},{17,25},{25,17},{2,10},{10... | collective-permute-start | bytes 688136 | tf_op jit(solution)/shard_map/ppermute | solution.py:618
  61.2 0.1 merge.1
  61.4 0.4 collective-permute-start.18
  61.8 1.0 collective-permute-start.19
  62.7 2.3 %collective-permute-done.14.refs_1_ = bf16[64,1792]{1,0:T(8,128)(2,1)S(1)} collective-permute-done((bf16[64,1792]{1,0:T(8,128)(2,1)S(1)}, bf16[64,1792]{1,0:T(8,128)(2,1)S(1)}, u32[]{:S(2)}, u32[]{:S(2)}) %collective-permute-start.14) | collective-permute-done | bytes 229408 | tf_op jit(solution)/shard_map/ppermute | solution.py:618
  65.0 0.1 add_up.5.refs_0_
  65.1 0.3 collective-permute-start.28
  65.4 1.2 %collective-permute-start.25 = (bf16[64,1792]{1,0:T(8,128)(2,1)S(1)}, bf16[64,1792]{1,0:T(8,128)(2,1)S(1)}, u32[]{:S(2)}, u32[]{:S(2)}) collective-permute-start(bf16[64,1792]{1,0:T(8,128)(2,1)S(1)} %get-tuple-element.82), channel_id=1, source_target_pairs={{0,16},{8,24},{16,0},{24,8},{1,17},{9,25},{17,1},{25,9},{2,18},{10... | collective-permute-start | bytes 688136 | tf_op jit(solution)/shard_map/ppermute | solution.py:618
  66.6 0.1 add_up.6.refs_1_
  66.7 2.9 %collective-permute-done.27.refs_2_ = bf16[64,1792]{1,0:T(8,128)(2,1)S(1)} collective-permute-done((bf16[64,1792]{1,0:T(8,128)(2,1)S(1)}, bf16[64,1792]{1,0:T(8,128)(2,1)S(1)}, u32[]{:S(2)}, u32[]{:S(2)}) %collective-permute-start.27) | collective-permute-done | bytes 229408 | tf_op jit(solution)/shard_map/ppermute | solution.py:618
  69.6 0.0 collective-permute-start.24
  69.6 3.8 %down_grads.1 = (bf16[512,7168]{1,0:T(8,128)(2,1)}, f32[8,128]{1,0:T(8,128)S(1)}) custom-call(bf16[64,1792]{1,0:T(8,128)(2,1)S(1)} %add_up.5.refs_0_, bf16[64,1792]{1,0:T(8,128)(2,1)S(1)} %add_up.6.refs_1_, s32[1]{0:T(128)} %bitcast.2.refs_1_.refs_2_, bf16[128,512]{1,0:T(8,128)(2,1)S(1)} %get-tuple-element.68.refs_3_, ...), custom_call_target="tpu_custom_call" | custom-call | flops 1024 | bytes 1024 | tf_op jit(solution)/shard_map/down_grads/pallas_call | solution.py:33
  73.4 3.5 %collective-permute-done.28.refs_3_ = bf16[64,1792]{1,0:T(8,128)(2,1)S(1)} collective-permute-done((bf16[64,1792]{1,0:T(8,128)(2,1)S(1)}, bf16[64,1792]{1,0:T(8,128)(2,1)S(1)}, u32[]{:S(2)}, u32[]{:S(2)}) %collective-permute-start.28) | collective-permute-done | bytes 229408 | tf_op jit(solution)/shard_map/ppermute | solution.py:618
  76.9 0.1 add_up.9
  77.0 8.9 %collective-permute-start.29 = (bf16[32,1792]{1,0:T(8,128)(2,1)S(1)}, bf16[32,1792]{1,0:T(8,128)(2,1)S(1)}, u32[]{:S(2)}, u32[]{:S(2)}) collective-permute-start(bf16[32,1792]{1,0:T(8,128)(2,1)S(1)} %get-tuple-element.87), channel_id=1, source_target_pairs={{0,4},{1,5},{2,6},{3,7},{4,0},{5,1},{6,2},{7,3},{8,12},{9,13},{10,... | collective-permute-start | bytes 344072 | tf_op jit(solution)/shard_map/ppermute | solution.py:618
  85.8 0.0 collective-permute-done.25.refs_3_
  85.8 0.2 collective-permute-start.30
  86.0 0.1 add_up.8
  86.1 4.9 %collective-permute-start.26 = (bf16[32,1792]{1,0:T(8,128)(2,1)S(1)}, bf16[32,1792]{1,0:T(8,128)(2,1)S(1)}, u32[]{:S(2)}, u32[]{:S(2)}) collective-permute-start(bf16[32,1792]{1,0:T(8,128)(2,1)S(1)} %get-tuple-element.84), channel_id=1, source_target_pairs={{0,2},{1,3},{2,0},{3,1},{4,6},{5,7},{6,4},{7,5},{8,10},{9,11},{10,... | collective-permute-start | bytes 344072 | tf_op jit(solution)/shard_map/ppermute | solution.py:618
  91.1 0.0 collective-permute-done.18.refs_2_
  91.1 0.2 add_up.7
  91.2 0.3 collective-permute-start.20
  91.5 1.2 %collective-permute-start.21 = (bf16[32,1792]{1,0:T(8,128)(2,1)S(1)}, bf16[32,1792]{1,0:T(8,128)(2,1)S(1)}, u32[]{:S(2)}, u32[]{:S(2)}) collective-permute-start(bf16[32,1792]{1,0:T(8,128)(2,1)S(1)} %get-tuple-element.79), channel_id=1, source_target_pairs={{0,4},{1,5},{2,6},{3,7},{4,0},{5,1},{6,2},{7,3},{8,12},{9,13},{10,... | collective-permute-start | bytes 344072 | tf_op jit(solution)/shard_map/ppermute | solution.py:618
  92.7 0.0 collective-permute-done.29.refs_1_.refs_3_
  92.7 2.4 %collective-permute-start.22 = (bf16[32,1792]{1,0:T(8,128)(2,1)S(1)}, bf16[32,1792]{1,0:T(8,128)(2,1)S(1)}, u32[]{:S(2)}, u32[]{:S(2)}) collective-permute-start(bf16[32,1792]{1,0:T(8,128)(2,1)S(1)} %get-tuple-element.80), channel_id=1, source_target_pairs={{0,6},{1,7},{2,4},{3,5},{4,2},{5,3},{6,0},{7,1},{8,14},{9,15},{10,... | collective-permute-start | bytes 344072 | tf_op jit(solution)/shard_map/ppermute | solution.py:618
  95.0 6.0 %weight_grads.1 = (bf16[7168,512]{1,0:T(8,128)(2,1)}, bf16[7168,512]{1,0:T(8,128)(2,1)}, f32[8,128]{1,0:T(8,128)S(1)}) custom-call(bf16[32,1792]{1,0:T(8,128)(2,1)S(1)} %get-tuple-element.83.refs_0_.refs_1_, bf16[32,1792]{1,0:T(8,128)(2,1)S(1)} %collective-permute-done.29.refs_1_.refs_3_, s32[1]{0:T(128)} %bitcast.2.refs_1_.refs_2_, ...), custom_call_target="tpu_custom_call" | custom-call | flops 1024 | bytes 1024 | tf_op jit(solution)/shard_map/weight_grads/pallas_call | solution.py:33
  101.1 4.2 %collective-permute-start.31 = (bf16[64,1792]{1,0:T(8,128)(2,1)S(1)}, bf16[64,1792]{1,0:T(8,128)(2,1)S(1)}, u32[]{:S(2)}, u32[]{:S(2)}) collective-permute-start(bf16[64,1792]{1,0:T(8,128)(2,1)S(1)} %arrange.5), channel_id=1, source_target_pairs={{0,1},{1,0},{2,3},{3,2},{4,5},{5,4},{6,7},{7,6},{8,9},{9,8},{10,11... | collective-permute-start | bytes 688136 | tf_op jit(solution)/shard_map/ppermute | solution.py:618
  105.4 1.7 %collective-permute-start.23 = (bf16[64,1792]{1,0:T(8,128)(2,1)S(1)}, bf16[64,1792]{1,0:T(8,128)(2,1)S(1)}, u32[]{:S(2)}, u32[]{:S(2)}) collective-permute-start(bf16[64,1792]{1,0:T(8,128)(2,1)S(1)} %pad_maximum_fusion.2), channel_id=1, source_target_pairs={{0,1},{1,0},{2,3},{3,2},{4,5},{5,4},{6,7},{7,6},{8,9},{9,8},{10,11... | collective-permute-start | bytes 688136 | tf_op jit(solution)/shard_map/ppermute | solution.py:618
  107.1 1.5 %spread_rows.3 = bf16[512,1792]{1,0:T(8,128)(2,1)} custom-call(bf16[512,128]{1,0:T(8,128)(2,1)S(1)} %get-tuple-element.81.refs_0_, bf16[32,1792]{1,0:T(8,128)(2,1)S(1)} %get-tuple-element.83.refs_0_.refs_1_, bf16[32,1792]{1,0:T(8,128)(2,1)S(1)} %collective-permute-done.26.refs_2_, bf16[32,1792]{1,0:T(8,128)(2,1)S(1)} %collective-permute-done.29.refs_1_.refs_3_, ...), custom_call_target="tpu_custom_call" | custom-call | flops 1024 | bytes 1024 | tf_op jit(solution)/shard_map/spread_rows/pallas_call | solution.py:33
  108.7 1.6 %spread_rows.2 = bf16[512,1792]{1,0:T(8,128)(2,1)} custom-call(bf16[512,256]{1,0:T(8,128)(2,1)S(1)} %get-tuple-element.52.refs_0_, bf16[32,1792]{1,0:T(8,128)(2,1)S(1)} %get-tuple-element.77.refs_1_, bf16[32,1792]{1,0:T(8,128)(2,1)S(1)} %collective-permute-done.20.refs_2_, bf16[32,1792]{1,0:T(8,128)(2,1)S(1)} %collective-permute-done.21.refs_3_, ...), custom_call_target="tpu_custom_call" | custom-call | flops 1024 | bytes 1024 | tf_op jit(solution)/shard_map/spread_rows/pallas_call | solution.py:33
  (34 shorter events, 0.3 us)
Async XLA Ops:
  3.2 13.3 %collective-permute-start = (bf16[32,1792]{1,0:T(8,128)(2,1)S(1)}, bf16[32,1792]{1,0:T(8,128)(2,1)S(1)}, u32[]{:S(2)}, u32[]{:S(2)}) collective-permute-start(bf16[32,1792]{1,0:T(8,128)(2,1)S(1)} %get-tuple-element.53), channel_id=1, source_target_pairs={{0,1},{1,0},{2,3},{3,2},{4,5},{5,4},{6,7},{7,6},{8,9},{9,8},{10,11... | collective-permute-start | bytes 344072 | tf_op jit(solution)/shard_map/ppermute | solution.py:618
  3.3 13.2 %collective-permute-start.1 = (bf16[32,1792]{1,0:T(8,128)(2,1)S(1)}, bf16[32,1792]{1,0:T(8,128)(2,1)S(1)}, u32[]{:S(2)}, u32[]{:S(2)}) collective-permute-start(bf16[32,1792]{1,0:T(8,128)(2,1)S(1)} %get-tuple-element.54), channel_id=1, source_target_pairs={{0,2},{1,3},{2,0},{3,1},{4,6},{5,7},{6,4},{7,5},{8,10},{9,11},{10,... | collective-permute-start | bytes 344072 | tf_op jit(solution)/shard_map/ppermute | solution.py:618
  6.1 10.6 %collective-permute-start.2 = (bf16[32,1792]{1,0:T(8,128)(2,1)S(1)}, bf16[32,1792]{1,0:T(8,128)(2,1)S(1)}, u32[]{:S(2)}, u32[]{:S(2)}) collective-permute-start(bf16[32,1792]{1,0:T(8,128)(2,1)S(1)} %get-tuple-element.55), channel_id=1, source_target_pairs={{0,3},{1,2},{2,1},{3,0},{4,7},{5,6},{6,5},{7,4},{8,11},{9,10},{10,... | collective-permute-start | bytes 344072 | tf_op jit(solution)/shard_map/ppermute | solution.py:618
  6.1 13.2 %collective-permute-start.7 = (bf16[64,1792]{1,0:T(8,128)(2,1)S(1)}, bf16[64,1792]{1,0:T(8,128)(2,1)S(1)}, u32[]{:S(2)}, u32[]{:S(2)}) collective-permute-start(bf16[64,1792]{1,0:T(8,128)(2,1)S(1)} %get-tuple-element.56), channel_id=1, source_target_pairs={{0,4},{1,5},{2,6},{3,7},{4,0},{5,1},{6,2},{7,3},{8,12},{9,13},{10,... | collective-permute-start | bytes 688136 | tf_op jit(solution)/shard_map/ppermute | solution.py:618
  8.8 15.1 %collective-permute-start.8 = (bf16[64,1792]{1,0:T(8,128)(2,1)S(1)}, bf16[64,1792]{1,0:T(8,128)(2,1)S(1)}, u32[]{:S(2)}, u32[]{:S(2)}) collective-permute-start(bf16[64,1792]{1,0:T(8,128)(2,1)S(1)} %get-tuple-element.57), channel_id=1, source_target_pairs={{0,6},{1,7},{2,4},{3,5},{4,2},{5,3},{6,0},{7,1},{8,14},{9,15},{10,... | collective-permute-start | bytes 688136 | tf_op jit(solution)/shard_map/ppermute | solution.py:618
  16.7 11.6 %collective-permute-start.5 = (bf16[128,1792]{1,0:T(8,128)(2,1)S(1)}, bf16[128,1792]{1,0:T(8,128)(2,1)S(1)}, u32[]{:S(2)}, u32[]{:S(2)}) collective-permute-start(bf16[128,1792]{1,0:T(8,128)(2,1)S(1)} %pad_maximum_fusion.refs_0_.refs_4_.refs_5_), channel_id=1, source_target_pairs={{0,16},{8,24},{16,0},{24,8},{1,17},{9,25},{17,1},{25,9},{2,18},{10... | collective-permute-start | bytes 1376264 | tf_op jit(solution)/shard_map/ppermute | solution.py:618
  18.1 11.3 %collective-permute-start.3 = (bf16[128,1792]{1,0:T(8,128)(2,1)S(1)}, bf16[128,1792]{1,0:T(8,128)(2,1)S(1)}, u32[]{:S(2)}, u32[]{:S(2)}) collective-permute-start(bf16[128,1792]{1,0:T(8,128)(2,1)S(1)} %pad_maximum_fusion.refs_0_.refs_4_.refs_5_), channel_id=1, source_target_pairs={{0,8},{8,0},{16,24},{24,16},{1,9},{9,1},{17,25},{25,17},{2,10},{10... | collective-permute-start | bytes 1376264 | tf_op jit(solution)/shard_map/ppermute | solution.py:618
  23.9 3.0 %collective-permute-start.9 = (bf16[64,1792]{1,0:T(8,128)(2,1)S(1)}, bf16[64,1792]{1,0:T(8,128)(2,1)S(1)}, u32[]{:S(2)}, u32[]{:S(2)}) collective-permute-start(bf16[64,1792]{1,0:T(8,128)(2,1)S(1)} %pad_maximum_fusion.1), channel_id=1, source_target_pairs={{0,1},{1,0},{2,3},{3,2},{4,5},{5,4},{6,7},{7,6},{8,9},{9,8},{10,11... | collective-permute-start | bytes 688136 | tf_op jit(solution)/shard_map/ppermute | solution.py:618
  29.5 10.4 %collective-permute-start.12 = (bf16[128,1792]{1,0:T(8,128)(2,1)S(1)}, bf16[128,1792]{1,0:T(8,128)(2,1)S(1)}, u32[]{:S(2)}, u32[]{:S(2)}) collective-permute-start(bf16[128,1792]{1,0:T(8,128)(2,1)S(1)} %arrange.4.refs_0_.refs_1_.refs_5_.refs_6_), channel_id=1, source_target_pairs={{0,16},{8,24},{16,0},{24,8},{1,17},{9,25},{17,1},{25,9},{2,18},{10... | collective-permute-start | bytes 1376264 | tf_op jit(solution)/shard_map/ppermute | solution.py:618
  29.9 11.4 %collective-permute-start.10 = (bf16[128,1792]{1,0:T(8,128)(2,1)S(1)}, bf16[128,1792]{1,0:T(8,128)(2,1)S(1)}, u32[]{:S(2)}, u32[]{:S(2)}) collective-permute-start(bf16[128,1792]{1,0:T(8,128)(2,1)S(1)} %arrange.4.refs_0_.refs_1_.refs_5_.refs_6_), channel_id=1, source_target_pairs={{0,8},{8,0},{16,24},{24,16},{1,9},{9,1},{17,25},{25,17},{2,10},{10... | collective-permute-start | bytes 1376264 | tf_op jit(solution)/shard_map/ppermute | solution.py:618
  31.1 17.2 %collective-permute-start.6 = (bf16[64,1792]{1,0:T(8,128)(2,1)S(1)}, bf16[64,1792]{1,0:T(8,128)(2,1)S(1)}, u32[]{:S(2)}, u32[]{:S(2)}) collective-permute-start(bf16[64,1792]{1,0:T(8,128)(2,1)S(1)} %slice.41), channel_id=1, source_target_pairs={{0,8},{8,0},{16,24},{24,16},{1,9},{9,1},{17,25},{25,17},{2,10},{10... | collective-permute-start | bytes 688136 | tf_op jit(solution)/shard_map/ppermute | solution.py:618
  31.4 16.8 %collective-permute-start.4 = (bf16[64,1792]{1,0:T(8,128)(2,1)S(1)}, bf16[64,1792]{1,0:T(8,128)(2,1)S(1)}, u32[]{:S(2)}, u32[]{:S(2)}) collective-permute-start(bf16[64,1792]{1,0:T(8,128)(2,1)S(1)} %slice.40), channel_id=1, source_target_pairs={{0,16},{8,24},{16,0},{24,8},{1,17},{9,25},{17,1},{25,9},{2,18},{10... | collective-permute-start | bytes 688136 | tf_op jit(solution)/shard_map/ppermute | solution.py:618
  39.9 10.0 %collective-permute-start.13 = (bf16[64,1792]{1,0:T(8,128)(2,1)S(1)}, bf16[64,1792]{1,0:T(8,128)(2,1)S(1)}, u32[]{:S(2)}, u32[]{:S(2)}) collective-permute-start(bf16[64,1792]{1,0:T(8,128)(2,1)S(1)} %slice.45), channel_id=1, source_target_pairs={{0,8},{8,0},{16,24},{24,16},{1,9},{9,1},{17,25},{25,17},{2,10},{10... | collective-permute-start | bytes 688136 | tf_op jit(solution)/shard_map/ppermute | solution.py:618
  41.2 8.7 %collective-permute-start.11 = (bf16[64,1792]{1,0:T(8,128)(2,1)S(1)}, bf16[64,1792]{1,0:T(8,128)(2,1)S(1)}, u32[]{:S(2)}, u32[]{:S(2)}) collective-permute-start(bf16[64,1792]{1,0:T(8,128)(2,1)S(1)} %slice.44), channel_id=1, source_target_pairs={{0,16},{8,24},{16,0},{24,8},{1,17},{9,25},{17,1},{25,9},{2,18},{10... | collective-permute-start | bytes 688136 | tf_op jit(solution)/shard_map/ppermute | solution.py:618
  52.3 9.0 %collective-permute-start.16 = (bf16[64,1792]{1,0:T(8,128)(2,1)S(1)}, bf16[64,1792]{1,0:T(8,128)(2,1)S(1)}, u32[]{:S(2)}, u32[]{:S(2)}) collective-permute-start(bf16[64,1792]{1,0:T(8,128)(2,1)S(1)} %get-tuple-element.73), channel_id=1, source_target_pairs={{0,16},{8,24},{16,0},{24,8},{1,17},{9,25},{17,1},{25,9},{2,18},{10... | collective-permute-start | bytes 688136 | tf_op jit(solution)/shard_map/ppermute | solution.py:618
  53.3 8.0 %collective-permute-start.17 = (bf16[64,1792]{1,0:T(8,128)(2,1)S(1)}, bf16[64,1792]{1,0:T(8,128)(2,1)S(1)}, u32[]{:S(2)}, u32[]{:S(2)}) collective-permute-start(bf16[64,1792]{1,0:T(8,128)(2,1)S(1)} %get-tuple-element.74), channel_id=1, source_target_pairs={{0,8},{8,0},{16,24},{24,16},{1,9},{9,1},{17,25},{25,17},{2,10},{10... | collective-permute-start | bytes 688136 | tf_op jit(solution)/shard_map/ppermute | solution.py:618
  59.3 5.8 %collective-permute-start.14 = (bf16[64,1792]{1,0:T(8,128)(2,1)S(1)}, bf16[64,1792]{1,0:T(8,128)(2,1)S(1)}, u32[]{:S(2)}, u32[]{:S(2)}) collective-permute-start(bf16[64,1792]{1,0:T(8,128)(2,1)S(1)} %get-tuple-element.65), channel_id=1, source_target_pairs={{0,8},{8,0},{16,24},{24,16},{1,9},{9,1},{17,25},{25,17},{2,10},{10... | collective-permute-start | bytes 688136 | tf_op jit(solution)/shard_map/ppermute | solution.py:618
  59.6 5.8 %collective-permute-start.15 = (bf16[64,1792]{1,0:T(8,128)(2,1)S(1)}, bf16[64,1792]{1,0:T(8,128)(2,1)S(1)}, u32[]{:S(2)}, u32[]{:S(2)}) collective-permute-start(bf16[64,1792]{1,0:T(8,128)(2,1)S(1)} %get-tuple-element.67), channel_id=1, source_target_pairs={{0,16},{8,24},{16,0},{24,8},{1,17},{9,25},{17,1},{25,9},{2,18},{10... | collective-permute-start | bytes 688136 | tf_op jit(solution)/shard_map/ppermute | solution.py:618
  60.1 9.5 %collective-permute-start.27 = (bf16[64,1792]{1,0:T(8,128)(2,1)S(1)}, bf16[64,1792]{1,0:T(8,128)(2,1)S(1)}, u32[]{:S(2)}, u32[]{:S(2)}) collective-permute-start(bf16[64,1792]{1,0:T(8,128)(2,1)S(1)} %get-tuple-element.86), channel_id=1, source_target_pairs={{0,8},{8,0},{16,24},{24,16},{1,9},{9,1},{17,25},{25,17},{2,10},{10... | collective-permute-start | bytes 688136 | tf_op jit(solution)/shard_map/ppermute | solution.py:618
  61.4 29.7 %collective-permute-start.18 = (bf16[128,1792]{1,0:T(8,128)(2,1)S(1)}, bf16[128,1792]{1,0:T(8,128)(2,1)S(1)}, u32[]{:S(2)}, u32[]{:S(2)}) collective-permute-start(bf16[128,1792]{1,0:T(8,128)(2,1)S(1)} %get-tuple-element.75), channel_id=1, source_target_pairs={{0,8},{8,0},{16,24},{24,16},{1,9},{9,1},{17,25},{25,17},{2,10},{10... | collective-permute-start | bytes 1376264 | tf_op jit(solution)/shard_map/ppermute | solution.py:618
  61.8 29.3 %collective-permute-start.19 = (bf16[128,1792]{1,0:T(8,128)(2,1)S(1)}, bf16[128,1792]{1,0:T(8,128)(2,1)S(1)}, u32[]{:S(2)}, u32[]{:S(2)}) collective-permute-start(bf16[128,1792]{1,0:T(8,128)(2,1)S(1)} %get-tuple-element.76), channel_id=1, source_target_pairs={{0,16},{8,24},{16,0},{24,8},{1,17},{9,25},{17,1},{25,9},{2,18},{10... | collective-permute-start | bytes 1376264 | tf_op jit(solution)/shard_map/ppermute | solution.py:618
  65.1 11.8 %collective-permute-start.28 = (bf16[64,1792]{1,0:T(8,128)(2,1)S(1)}, bf16[64,1792]{1,0:T(8,128)(2,1)S(1)}, u32[]{:S(2)}, u32[]{:S(2)}) collective-permute-start(bf16[64,1792]{1,0:T(8,128)(2,1)S(1)} %add_up.5.refs_0_), channel_id=1, source_target_pairs={{0,16},{8,24},{16,0},{24,8},{1,17},{9,25},{17,1},{25,9},{2,18},{10... | collective-permute-start | bytes 688136 | tf_op jit(solution)/shard_map/ppermute | solution.py:618
  65.4 20.5 %collective-permute-start.25 = (bf16[64,1792]{1,0:T(8,128)(2,1)S(1)}, bf16[64,1792]{1,0:T(8,128)(2,1)S(1)}, u32[]{:S(2)}, u32[]{:S(2)}) collective-permute-start(bf16[64,1792]{1,0:T(8,128)(2,1)S(1)} %get-tuple-element.82), channel_id=1, source_target_pairs={{0,16},{8,24},{16,0},{24,8},{1,17},{9,25},{17,1},{25,9},{2,18},{10... | collective-permute-start | bytes 688136 | tf_op jit(solution)/shard_map/ppermute | solution.py:618
  69.6 16.4 %collective-permute-start.24 = (bf16[64,1792]{1,0:T(8,128)(2,1)S(1)}, bf16[64,1792]{1,0:T(8,128)(2,1)S(1)}, u32[]{:S(2)}, u32[]{:S(2)}) collective-permute-start(bf16[64,1792]{1,0:T(8,128)(2,1)S(1)} %add_up.6.refs_1_), channel_id=1, source_target_pairs={{0,8},{8,0},{16,24},{24,16},{1,9},{9,1},{17,25},{25,17},{2,10},{10... | collective-permute-start | bytes 688136 | tf_op jit(solution)/shard_map/ppermute | solution.py:618
  77.0 15.7 %collective-permute-start.29 = (bf16[32,1792]{1,0:T(8,128)(2,1)S(1)}, bf16[32,1792]{1,0:T(8,128)(2,1)S(1)}, u32[]{:S(2)}, u32[]{:S(2)}) collective-permute-start(bf16[32,1792]{1,0:T(8,128)(2,1)S(1)} %get-tuple-element.87), channel_id=1, source_target_pairs={{0,4},{1,5},{2,6},{3,7},{4,0},{5,1},{6,2},{7,3},{8,12},{9,13},{10,... | collective-permute-start | bytes 344072 | tf_op jit(solution)/shard_map/ppermute | solution.py:618
  85.8 15.2 %collective-permute-start.30 = (bf16[32,1792]{1,0:T(8,128)(2,1)S(1)}, bf16[32,1792]{1,0:T(8,128)(2,1)S(1)}, u32[]{:S(2)}, u32[]{:S(2)}) collective-permute-start(bf16[32,1792]{1,0:T(8,128)(2,1)S(1)} %get-tuple-element.88), channel_id=1, source_target_pairs={{0,6},{1,7},{2,4},{3,5},{4,2},{5,3},{6,0},{7,1},{8,14},{9,15},{10,... | collective-permute-start | bytes 344072 | tf_op jit(solution)/shard_map/ppermute | solution.py:618
  86.1 14.9 %collective-permute-start.26 = (bf16[32,1792]{1,0:T(8,128)(2,1)S(1)}, bf16[32,1792]{1,0:T(8,128)(2,1)S(1)}, u32[]{:S(2)}, u32[]{:S(2)}) collective-permute-start(bf16[32,1792]{1,0:T(8,128)(2,1)S(1)} %get-tuple-element.84), channel_id=1, source_target_pairs={{0,2},{1,3},{2,0},{3,1},{4,6},{5,7},{6,4},{7,5},{8,10},{9,11},{10,... | collective-permute-start | bytes 344072 | tf_op jit(solution)/shard_map/ppermute | solution.py:618
  91.2 14.1 %collective-permute-start.20 = (bf16[32,1792]{1,0:T(8,128)(2,1)S(1)}, bf16[32,1792]{1,0:T(8,128)(2,1)S(1)}, u32[]{:S(2)}, u32[]{:S(2)}) collective-permute-start(bf16[32,1792]{1,0:T(8,128)(2,1)S(1)} %get-tuple-element.78), channel_id=1, source_target_pairs={{0,2},{1,3},{2,0},{3,1},{4,6},{5,7},{6,4},{7,5},{8,10},{9,11},{10,... | collective-permute-start | bytes 344072 | tf_op jit(solution)/shard_map/ppermute | solution.py:618
  91.5 13.8 %collective-permute-start.21 = (bf16[32,1792]{1,0:T(8,128)(2,1)S(1)}, bf16[32,1792]{1,0:T(8,128)(2,1)S(1)}, u32[]{:S(2)}, u32[]{:S(2)}) collective-permute-start(bf16[32,1792]{1,0:T(8,128)(2,1)S(1)} %get-tuple-element.79), channel_id=1, source_target_pairs={{0,4},{1,5},{2,6},{3,7},{4,0},{5,1},{6,2},{7,3},{8,12},{9,13},{10,... | collective-permute-start | bytes 344072 | tf_op jit(solution)/shard_map/ppermute | solution.py:618
  92.7 12.7 %collective-permute-start.22 = (bf16[32,1792]{1,0:T(8,128)(2,1)S(1)}, bf16[32,1792]{1,0:T(8,128)(2,1)S(1)}, u32[]{:S(2)}, u32[]{:S(2)}) collective-permute-start(bf16[32,1792]{1,0:T(8,128)(2,1)S(1)} %get-tuple-element.80), channel_id=1, source_target_pairs={{0,6},{1,7},{2,4},{3,5},{4,2},{5,3},{6,0},{7,1},{8,14},{9,15},{10,... | collective-permute-start | bytes 344072 | tf_op jit(solution)/shard_map/ppermute | solution.py:618
  101.1 6.1 %collective-permute-start.31 = (bf16[64,1792]{1,0:T(8,128)(2,1)S(1)}, bf16[64,1792]{1,0:T(8,128)(2,1)S(1)}, u32[]{:S(2)}, u32[]{:S(2)}) collective-permute-start(bf16[64,1792]{1,0:T(8,128)(2,1)S(1)} %arrange.5), channel_id=1, source_target_pairs={{0,1},{1,0},{2,3},{3,2},{4,5},{5,4},{6,7},{7,6},{8,9},{9,8},{10,11... | collective-permute-start | bytes 688136 | tf_op jit(solution)/shard_map/ppermute | solution.py:618
  105.4 3.3 %collective-permute-start.23 = (bf16[64,1792]{1,0:T(8,128)(2,1)S(1)}, bf16[64,1792]{1,0:T(8,128)(2,1)S(1)}, u32[]{:S(2)}, u32[]{:S(2)}) collective-permute-start(bf16[64,1792]{1,0:T(8,128)(2,1)S(1)} %pad_maximum_fusion.2), channel_id=1, source_target_pairs={{0,1},{1,0},{2,3},{3,2},{4,5},{5,4},{6,7},{7,6},{8,9},{9,8},{10,11... | collective-permute-start | bytes 688136 | tf_op jit(solution)/shard_map/ppermute | solution.py:618

commit v4 on v2

--- a/solution.py
+++ b/solution.py
@@ -8,6 +8,7 @@
 from jax.sharding import PartitionSpec as P
 
 ROWS = (((0,), (0,)), ((), ()))
+PLAIN = (((1,), (0,)), ((), ()))
 LAST = (((1,), (1,)), ((), ()))
 IN_VMEM = pl.BlockSpec(memory_space=pltpu.VMEM)
 IN_SMEM = pl.BlockSpec(memory_space=pltpu.SMEM)
@@ -24,7 +25,7 @@
         out_specs.append(IN_VMEM)
 
     def run(*refs):
-        refs = [*refs[:used], *refs[used + len(later) :]]
+        refs = list(refs[len(later) :])
         if mark:
             mark_ref = refs.pop(used + results)
             mark_ref[...] = jnp.zeros_like(mark_ref)
@@ -33,13 +34,13 @@
     out = pl.pallas_call(
         run,
         name=name,
-        in_specs=[*specs, *[ANYWHERE] * len(later)],
+        in_specs=[*[ANYWHERE] * len(later), *specs],
         out_shape=outs,
         out_specs=out_specs,
         scratch_shapes=scratch,
         compiler_params=pltpu.CompilerParams(vmem_limit_bytes=mib * MIB),
         cost_estimate=pl.CostEstimate(flops=1024, bytes_accessed=cost, transcendentals=0),
-    )(*operands, *later)
+    )(*later, *operands)
     return out if len(out) > 1 else out[0]
 
 
@@ -70,7 +71,7 @@
     return jnp.concatenate(rows, axis=0), jnp.concatenate(weights, axis=0)
 
 
-def pick_body(me_ref, counts_hbm, chosen_hbm, prob_hbm, tokens_hbm, cotangent_hbm, *refs):
+def pick_body(plan, me_ref, counts_hbm, chosen_hbm, prob_hbm, tokens_hbm, cotangent_hbm, *refs):
     *outs, mask_ref, weights_ref = refs[:-6]
     counts_ref, chosen_ref, prob_ref, tokens_ref, cotangent_ref, sems = refs[-6:]
     experts, _, slots = chosen_ref.shape
@@ -98,26 +99,26 @@
         if which:
             value = weights * value
         value = value.astype(jnp.bfloat16)
-        step = 0
-        for out_ref in outs:
-            for start in range(which * slots, out_ref.shape[0], 2 * slots):
-                out_ref[pl.ds(start, slots), :] = value[step * slots : (step + 1) * slots]
-                step += 1
-
-
-def pick_slots(me, chosen, counts, gate_prob, tokens, cotangent, split):
+        for out_ref, blocks in zip(outs, plan):
+            for place, (part, step) in enumerate(blocks):
+                if part == which:
+                    target = pl.ds(place * slots, slots)
+                    out_ref[target, :] = value[step * slots : (step + 1) * slots]
+
+
+def pick_slots(me, chosen, counts, gate_prob, tokens, cotangent, plan):
     experts, _, slots = chosen.shape
     length, width = tokens.shape
     total = experts * slots
     operands = (counts, chosen, gate_prob, tokens, cotangent)
     return run_kernel(
-        pick_body,
+        functools.partial(pick_body, plan),
         "pick_slots",
         (me, *[in_hbm(array) for array in operands]),
         [IN_SMEM] + [ANYWHERE] * 5,
-        [like(2 * slots * part, width) for part in split]
+        [like(slots * len(blocks), width) for blocks in plan]
         + [like(total, length), like(total, 128, jnp.float32)],
-        [IN_VMEM] * (len(split) + 2),
+        [IN_VMEM] * (len(plan) + 2),
         [pltpu.SMEM(counts.shape, counts.dtype)]
         + [pltpu.VMEM(array.shape, array.dtype) for array in operands[1:]]
         + [pltpu.SemaphoreType.DMA((5,))],
@@ -263,61 +264,114 @@
     )
 
 
+def add_pairs_body(*refs):
+    for first_ref, second_ref, out_ref in zip(refs[0:4:2], refs[1:4:2], refs[4:]):
+        total = first_ref[...].astype(jnp.float32) + second_ref[...].astype(jnp.float32)
+        out_ref[...] = total.astype(out_ref.dtype)
+
+
+def add_pairs(first, second, later=()):
+    return run_kernel(
+        add_pairs_body,
+        "add_pairs",
+        (*first, *second),
+        [IN_VMEM] * 4,
+        [like(*first[0].shape), like(*second[0].shape)],
+        [IN_VMEM] * 2,
+        [],
+        8,
+        later,
+    )
+
+
 class Slices:
-    def __init__(self, pieces, part, slots):
-        self.pieces, self.part, self.slots = pieces, part, slots
-        self.flat = [piece for row in pieces for piece in row]
-        self.rows = sum(piece.shape[0] for piece in pieces[0]) // 2
-        self.width = self.flat[0].shape[1]
+    def __init__(self, slices, part, slots):
+        self.mixed = [[mixed for _, mixed in pieces] for pieces in slices]
+        self.flat = [array for pieces in slices for array, _ in pieces]
+        self.part, self.slots = part, slots
+        self.count, self.width = len(slices), self.flat[0].shape[1]
+        self.rows = sum(array.shape[0] // (2 if mixed else 1) for array, mixed in slices[0])
 
     def read(self, refs, index):
-        first = sum(len(pieces) for pieces in self.pieces[:index])
+        first = sum(len(mixed) for mixed in self.mixed[:index])
         blocks = []
-        for ref in refs[first : first + len(self.pieces[index])]:
-            for start in range(self.part * self.slots, ref.shape[0], 2 * self.slots):
-                blocks.append(ref[pl.ds(start, self.slots), :])
-        return jnp.concatenate(blocks, axis=0)
-
-
-def store_halves(refs, index, term):
+        for place, mixed in enumerate(self.mixed[index]):
+            ref = refs[first + place]
+            if mixed:
+                for start in range(self.part * self.slots, ref.shape[0], 2 * self.slots):
+                    blocks.append(ref[pl.ds(start, self.slots), :])
+            else:
+                blocks.append(ref[...])
+        return blocks[0] if len(blocks) == 1 else jnp.concatenate(blocks, axis=0)
+
+
+def partial_body(slices, dims, *refs):
+    used = len(slices.flat)
+    weights, sums = refs[used:][: len(dims)], refs[used + len(dims) :]
+    for index in range(slices.count):
+        rows = slices.read(refs, index)
+        for weight_ref, dim, sum_ref in zip(weights, dims, sums):
+            value = lax.dot_general(
+                rows, weight_ref[index], dim, preferred_element_type=jnp.float32
+            )
+            if index == 0:
+                sum_ref[...] = value
+            else:
+                sum_ref[...] += value
+
+
+def partial_products(slices, weights, dims, units, later=()):
+    return run_kernel(
+        functools.partial(partial_body, slices, dims),
+        "partial_products",
+        (*slices.flat, *weights),
+        [IN_VMEM] * (len(slices.flat) + len(weights)),
+        [like(slices.rows, units, jnp.float32)] * len(weights),
+        [IN_VMEM] * len(weights),
+        [],
+        8,
+        later,
+    )
+
+
+def store_term(refs, index, term):
+    term = term.astype(jnp.bfloat16)
     size = term.shape[0] // 2
-    refs[2 * index][...] = term[:size].astype(jnp.bfloat16)
-    refs[2 * index + 1][...] = term[size:].astype(jnp.bfloat16)
+    refs[2 * index][...] = term[:size]
+    refs[2 * index + 1][...] = term[size:]
 
 
 def forward_body(slices, *refs):
-    gate_ref, up_ref, down_ref, hidden_ref, slope_ref, silu_ref, *terms = refs[len(slices.flat) :]
-    count = gate_ref.shape[0]
-    gate = up = None
-    for index in range(count):
-        rows = slices.read(refs, index)
-        more_gate = jnp.dot(rows, gate_ref[index], preferred_element_type=jnp.float32)
-        more_up = jnp.dot(rows, up_ref[index], preferred_element_type=jnp.float32)
-        gate = more_gate if gate is None else gate + more_gate
-        up = more_up if up is None else up + more_up
+    used = len(slices.flat)
+    gate_sum, up_sum, gate_ref, up_ref, down_ref = refs[used : used + 5]
+    hidden_ref, slope_ref, silu_ref, *terms = refs[used + 5 :]
+    last = gate_ref.shape[0] - 1
+    rows = slices.read(refs, 0)
+    gate = gate_sum[...] + jnp.dot(rows, gate_ref[last], preferred_element_type=jnp.float32)
+    up = up_sum[...] + jnp.dot(rows, up_ref[last], preferred_element_type=jnp.float32)
     sigmoid = jax.nn.sigmoid(gate)
     silu = gate * sigmoid
     hidden = (silu * up).astype(jnp.bfloat16)
     hidden_ref[...] = hidden
     slope_ref[...] = up * sigmoid * (1.0 + gate * (1.0 - sigmoid))
     silu_ref[...] = silu
-    for index in reversed(range(count)):
+    for index in reversed(range(last + 1)):
         term = jnp.dot(hidden, down_ref[index], preferred_element_type=jnp.float32)
-        store_halves(terms, index, term)
-
-
-def forward_terms(slices, gate, up, down, later=()):
+        store_term(terms, index, term)
+
+
+def forward_terms(slices, sums, gate, up, down, later=()):
     count, width, units = gate.shape
-    rows = slices.rows
-    outs = [like(rows, units), like(rows, units, jnp.float32), like(rows, units, jnp.float32)]
-    outs += [like(rows // 2, width)] * (2 * count)
+    rows = sums[0].shape[0]
+    f32 = jnp.float32
     out = run_kernel(
         functools.partial(forward_body, slices),
         "forward_terms",
-        (*slices.flat, gate, up, down),
-        [IN_VMEM] * (len(slices.flat) + 3),
-        outs,
-        [IN_VMEM] * len(outs),
+        (*slices.flat, *sums, gate, up, down),
+        [IN_VMEM] * (len(slices.flat) + 5),
+        [like(rows, units), like(rows, units, f32), like(rows, units, f32)]
+        + [like(rows // 2, width)] * (2 * count),
+        [IN_VMEM] * (3 + 2 * count),
         [],
         8,
         later,
@@ -325,57 +379,90 @@
     return out[:3], [out[3 + 2 * i : 5 + 2 * i] for i in range(count)]
 
 
-def hidden_grad_body(slices, *refs):
-    down_ref, slope_ref, silu_ref, gate_grad_ref, up_grad_ref = refs[len(slices.flat) :]
-    grad = None
-    for index in range(down_ref.shape[0]):
-        rows = slices.read(refs, index)
-        more = lax.dot_general(rows, down_ref[index], LAST, preferred_element_type=jnp.float32)
-        grad = more if grad is None else grad + more
-    gate_grad_ref[...] = (grad * slope_ref[...]).astype(jnp.bfloat16)
-    up_grad_ref[...] = (grad * silu_ref[...]).astype(jnp.bfloat16)
-
-
-def hidden_grads(slices, down, slope, silu, later=()):
-    return run_kernel(
-        functools.partial(hidden_grad_body, slices),
-        "hidden_grads",
-        (*slices.flat, down, slope, silu),
-        [IN_VMEM] * (len(slices.flat) + 3),
-        [like(*slope.shape)] * 2,
-        [IN_VMEM] * 2,
-        [],
-        8,
-        later,
-    )
-
-
-def grad_term_body(wanted, gate_grad_ref, up_grad_ref, gate_ref, up_ref, *terms):
-    for place, index in enumerate(wanted):
-        term = lax.dot_general(
-            gate_grad_ref[...], gate_ref[index], LAST, preferred_element_type=jnp.float32
-        )
-        term += lax.dot_general(
-            up_grad_ref[...], up_ref[index], LAST, preferred_element_type=jnp.float32
-        )
-        store_halves(terms, place, term)
-
-
-def grad_terms(wanted, gate_grad, up_grad, gate, up, later=()):
-    _, width, _ = gate.shape
+def backward_body(slices, *refs):
+    used = len(slices.flat)
+    grad_sum, slope_ref, silu_ref, gate_ref, up_ref, down_ref = refs[used : used + 6]
+    gate_grad_ref, up_grad_ref, *terms = refs[used + 6 :]
+    last = gate_ref.shape[0] - 1
+    rows = slices.read(refs, 0)
+    grad = lax.dot_general(rows, down_ref[last], LAST, preferred_element_type=jnp.float32)
+    grad += grad_sum[...]
+    gate_grad = (grad * slope_ref[...]).astype(jnp.bfloat16)
+    up_grad = (grad * silu_ref[...]).astype(jnp.bfloat16)
+    gate_grad_ref[...] = gate_grad
+    up_grad_ref[...] = up_grad
+    store_term(terms, 0, back_term(gate_grad, up_grad, gate_ref, up_ref, last))
+
+
+def back_term(gate_grad, up_grad, gate_ref, up_ref, index):
+    term = lax.dot_general(gate_grad, gate_ref[index], LAST, preferred_element_type=jnp.float32)
+    return term + lax.dot_general(up_grad, up_ref[index], LAST, preferred_element_type=jnp.float32)
+
+
+def backward_rest_body(gate_grad_ref, up_grad_ref, gate_ref, up_ref, *terms):
+    for index in reversed(range(len(terms) // 2)):
+        term = back_term(gate_grad_ref[...], up_grad_ref[...], gate_ref, up_ref, index)
+        store_term(terms, index, term)
+
+
+def backward_rest(gate_grad, up_grad, gate, up, later=()):
+    count, width, _ = gate.shape
     rows = gate_grad.shape[0]
-    terms = run_kernel(
-        functools.partial(grad_term_body, wanted),
-        "grad_terms",
+    out = run_kernel(
+        backward_rest_body,
+        "backward_rest",
         (gate_grad, up_grad, gate, up),
         [IN_VMEM] * 4,
-        [like(rows // 2, width)] * (2 * len(wanted)),
-        [IN_VMEM] * (2 * len(wanted)),
-        [],
-        8,
-        later,
-    )
-    return [terms[2 * i : 2 * i + 2] for i in range(len(wanted))]
+        [like(rows // 2, width)] * (2 * count - 2),
+        [IN_VMEM] * (2 * count - 2),
+        [],
+        8,
+        later,
+    )
+    return [out[2 * i : 2 * i + 2] for i in range(count - 1)]
+
+
+def backward_terms(slices, grad_sum, slope, silu, gate, up, down, later=()):
+    _, width, units = gate.shape
+    rows = slope.shape[0]
+    out = run_kernel(
+        functools.partial(backward_body, slices),
+        "backward_terms",
+        (*slices.flat, grad_sum, slope, silu, gate, up, down),
+        [IN_VMEM] * (len(slices.flat) + 6),
+        [like(rows, units)] * 2 + [like(rows // 2, width)] * 2,
+        [IN_VMEM] * 4,
+        [],
+        8,
+        later,
+    )
+    return out[:2], out[2:]
+
+
+def merge_body(first_top, first_bottom, second_top, second_bottom, top, bottom, first, second):
+    size = top.shape[0]
+    upper, lower = pl.ds(0, size), pl.ds(size, size)
+    total = first_top[...].astype(jnp.float32) + top[...].astype(jnp.float32)
+    first[upper, :] = total.astype(first.dtype)
+    first[lower, :] = first_bottom[...]
+    total = second_bottom[...].astype(jnp.float32) + bottom[...].astype(jnp.float32)
+    second[lower, :] = total.astype(second.dtype)
+    second[upper, :] = second_top[...]
+
+
+def merge(first, second, top, bottom, later=()):
+    rows, width = first[0].shape
+    return run_kernel(
+        merge_body,
+        "merge",
+        (*first, *second, top, bottom),
+        [IN_VMEM] * 6,
+        [like(2 * rows, width)] * 2,
+        [IN_VMEM] * 2,
+        [],
+        8,
+        later,
+    )
 
 
 def down_grad_body(slices, me_ref, hidden_ref, *refs):
@@ -397,17 +484,16 @@
 
 
 def down_grads(me, hidden, slices, later=()):
-    count = len(slices.pieces)
-    units = hidden.shape[1]
+    count, width, units = slices.count, slices.width, hidden.shape[1]
     return run_kernel(
         functools.partial(down_grad_body, slices),
         "down_grads",
         (me, hidden, *slices.flat),
         [IN_SMEM] + [IN_VMEM] * (1 + len(slices.flat)),
-        [like(units, slices.width * count)],
+        [like(units, width * count)],
         [ANYWHERE],
         [
-            pltpu.VMEM((count, units, slices.width), jnp.bfloat16),
+            pltpu.VMEM((count, units, width), jnp.bfloat16),
             pltpu.SemaphoreType.DMA((count,)),
         ],
         16,
@@ -436,17 +522,16 @@
 
 
 def weight_grads(me, slices, gate_grad, up_grad, later=()):
-    count = len(slices.pieces)
-    units = gate_grad.shape[1]
+    count, width, units = slices.count, slices.width, gate_grad.shape[1]
     return run_kernel(
         functools.partial(weight_grad_body, slices),
         "weight_grads",
         (me, gate_grad, up_grad, *slices.flat),
         [IN_SMEM] + [IN_VMEM] * (2 + len(slices.flat)),
-        [like(slices.width * count, units)] * 2,
+        [like(width * count, units)] * 2,
         [ANYWHERE] * 2,
         [
-            pltpu.VMEM((2, count, slices.width, units), jnp.bfloat16),
+            pltpu.VMEM((2, count, width, units), jnp.bfloat16),
             pltpu.SemaphoreType.DMA((2 * count,)),
         ],
         20,
@@ -555,9 +640,6 @@
     )
 
 
-LONG = 64 * MIB
-
-
 def swap(array, distance, axis):
     size = lax.axis_size(axis)
     return lax.ppermute(array, axis, [(i, i ^ distance) for i in range(size)])
@@ -565,6 +647,22 @@
 
 def joined(*arrays):
     return jnp.concatenate(arrays, axis=0)
+
+
+def gathered(whole, first, second):
+    from_first = swap(whole, first, "fsdp")
+    from_second = swap(whole, second, "fsdp")
+    passed = arrange((from_first,), [[(0, 0, whole.shape[0])]], (from_second,))
+    slices = [[whole], [None], [None], [swap(passed, second, "fsdp")]]
+    slices[first], slices[second] = [from_first], [from_second]
+    return slices
+
+
+def pieces_of(mixed, plain):
+    return [
+        [(piece, True) for piece in some] + [(piece, False) for piece in others]
+        for some, others in zip(mixed, plain)
+    ]
 
 
 def by_links(tokens, cotangent, gate_weight, up_weight, down_weight, chosen, counts, gate_prob):
@@ -572,86 +670,84 @@
     count = lax.axis_size("fsdp")
     ep_index = lax.axis_index("ep").reshape(1)
     me = lax.axis_index("fsdp").reshape(1)
+    units = gate_weight.shape[2]
     two = 2 * slots
-    half = 2 * two
-    own, core, even1, odd1, pair2, pair3, mask, weights = pick_slots(
-        ep_index,
-        chosen,
-        counts.reshape(1, experts),
-        gate_prob,
-        tokens,
-        cotangent,
-        (1, 1, 1, 1, 2, 2),
-    )
-
-    pair2 = swap(pair2, 4, "ep")
-    pair3 = swap(pair3, 6, "ep")
+    plan = [[(part, step) for part in range(2)] for step in range(4)]
+    plan += [[(part, step), (part, step + 1)] for part in range(2) for step in (4, 6)]
+    own, core, even1, odd1, token2, token3, grad2, grad3, mask, weights = pick_slots(
+        ep_index, chosen, counts.reshape(1, experts), gate_prob, tokens, cotangent, plan
+    )
+
+    token2 = swap(token2, 4, "ep")
+    token3 = swap(token3, 6, "ep")
     even1 = swap(even1, 2, "ep")
     odd1 = swap(odd1, 3, "ep")
     core = swap(core, 1, "ep")
-
     gate = load_weight(me, gate_weight[0], True, count, (own,))
-    up = load_weight(me, up_weight[0], True, count, (gate,))
-    weighted, plain = spread_matrices(mask, weights, (up,))
-    near = joined(arrange((own,), [[(0, 0, two)]], (weighted,)), core, even1, odd1)
-    near_x = swap(near, 1, "fsdp")
-    near_y = swap(near, 2, "fsdp")
-    near_d = [swap(near_x[:half], 2, "fsdp"), swap(near_y[half:], 1, "fsdp")]
-    odd = swap(joined(pair2[two:], pair3[two:]), 1, "ep")
-    far = arrange(
-        (pair2, pair3, odd), [[(0, 0, two), (2, 0, two), (1, 0, two), (2, two, two)]], tuple(near_d)
-    )
-    far_x = swap(far, 1, "fsdp")
-    far_y = swap(far, 2, "fsdp")
-    down = load_weight(me, down_weight[0], False, count, (far,))
-    far_d = [swap(far_x[:half], 2, "fsdp"), swap(far_y[half:], 1, "fsdp")]
-    pieces = [[near, far], [near_x, far_x], [near_y, far_y], near_d + far_d]
-    tokens, grads = Slices(pieces, 0, slots), Slices(pieces, 1, slots)
-
-    (hidden, slope, silu), terms = forward_terms(tokens, gate, up, down)
-    far_sum_d = swap(terms[3][1], 1, "fsdp")
-    near_sum_d = swap(terms[3][0], 2, "fsdp")
-    far_sum_x = swap(terms[1][1], 1, "fsdp")
-    near_sum_y = swap(terms[2][0], 2, "fsdp")
-    gate_grad, up_grad = hidden_grads(grads, down, slope, silu, (terms[0][0],))
-    back_d = grad_terms((3,), gate_grad, up_grad, gate, up)[0]
-    far_back_d = swap(back_d[1], 1, "fsdp")
-    near_back_d = swap(back_d[0], 2, "fsdp")
-    far_sum_y = add_up([terms[2][1], far_sum_d], 1, (back_d[0],))
-    near_sum_x = add_up([terms[1][0], near_sum_d], 1, (back_d[0],))
-    back = grad_terms((0, 1, 2), gate_grad, up_grad, gate, up, (far_sum_y, near_sum_x))
-    far_sum_y = swap(far_sum_y, 2, "fsdp")
-    near_sum_x = swap(near_sum_x, 1, "fsdp")
-    far_back_x = swap(back[1][1], 1, "fsdp")
-    near_back_y = swap(back[2][0], 2, "fsdp")
-    far_back_y = add_up([back[2][1], far_back_d])
-    near_back_x = add_up([back[1][0], near_back_d])
-    sent = (far_back_y, near_back_x)
-    far_back_y = swap(far_back_y, 2, "fsdp")
-    near_back_x = swap(near_back_x, 1, "fsdp")
-    out2, out3 = add_up([terms[0][1], far_sum_x, far_sum_y], 2, sent)
-    near_sum_y = add_up([terms[0][0], near_sum_y], 1, sent, LONG)
-    out0, out1 = add_up([near_sum_y, near_sum_x], 2)
-    grad_down, down_mark = down_grads(me, hidden, grads, (out0, out2))
+    near = joined(arrange((own,), [[(0, 0, two)]], (gate,)), core, even1, odd1)
+    mixed = gathered(near, 1, 2)
+    odd = swap(joined(token2[slots:], token3[slots:], token2, token3), 1, "ep")
+    ends = [(0, 0, slots), (2, 0, slots), (1, 0, slots), (2, slots, slots)]
+    up = load_weight(me, up_weight[0], True, count, (near,))
+    far = arrange((token2, token3, odd), [ends], (mixed[1][0], mixed[2][0], up))
+    far_tokens = gathered(far, 2, 1)
+    grad2 = swap(grad2, 4, "ep")
+    grad3 = swap(grad3, 6, "ep")
+    down = load_weight(me, down_weight[0], False, count, (up,))
+    weighted, plain = spread_matrices(mask, weights, (down,))
+    odd = arrange(
+        (grad2, grad3),
+        [[(0, slots, slots), (1, slots, slots), (0, 0, two), (1, 0, two)]],
+    )
+    odd = swap(odd, 1, "ep")
+    far_grads = gathered(arrange((grad2, grad3, odd), [ends]), 2, 1)
+    picked = pieces_of(mixed, far_tokens)
+    grads = pieces_of(mixed, far_grads)
+    first = Slices(picked[:3], 0, slots)
+    last = Slices(picked[3:], 0, slots)
+
+    sums = partial_products(first, (gate, up), (PLAIN, PLAIN), units)
+    (hidden, slope, silu), terms = forward_terms(last, sums, gate, up, down)
+    bottom = swap(terms[3][1], 1, "fsdp")
+    top = swap(terms[3][0], 2, "fsdp")
+
+    first = Slices(grads[:3], 1, slots)
+    last = Slices(grads[3:], 1, slots)
+    (grad_sum,) = [partial_products(first, (down,), (LAST,), units, (hidden,))]
+    sum_x, sum_y = merge(terms[1], terms[2], top, bottom, (grad_sum,))
+    (gate_grad, up_grad), back_d = backward_terms(
+        last, grad_sum, slope, silu, gate, up, down, (sum_x,)
+    )
+    sum_x = swap(sum_x, 1, "fsdp")
+    sum_y = swap(sum_y, 2, "fsdp")
+    bottom = swap(back_d[1], 1, "fsdp")
+    top = swap(back_d[0], 2, "fsdp")
+    back = backward_rest(gate_grad, up_grad, gate, up)
+    out0, out1, out2, out3 = add_up([joined(*terms[0]), sum_x, sum_y], 4, (back[0][0],))
     out3 = swap(out3, 6, "ep")
     out2 = swap(out2, 4, "ep")
     out1 = swap(out1, 2, "ep")
-    back2, back3 = add_up([back[0][1], far_back_x, far_back_y], 2, (down_mark,))
-    near_back_y = add_up([back[0][0], near_back_y], 1, (down_mark,), LONG)
-    back0, back1 = add_up([near_back_y, near_back_x], 2)
-    back3 = swap(back3, 6, "ep")
-    back2 = swap(back2, 4, "ep")
-    back1 = swap(back1, 2, "ep")
+
+    back_x, back_y = merge(back[1], back[2], top, bottom, (out0,))
+    grad_down, mark = down_grads(me, hidden, Slices(grads, 1, slots), (back_x,))
+    back_x = swap(back_x, 1, "fsdp")
+    back_y = swap(back_y, 2, "fsdp")
     layout = []
     for step in range(experts // 2):
         layout += [(step, 0), (experts // 2, step)]
     outs = [out0, out1, out2, out3]
     outs.append(swap(joined(*[piece[slots:] for piece in outs]), 1, "ep"))
-    grad_gate, grad_up, mark = weight_grads(me, tokens, gate_grad, up_grad, (back0, back2))
+    back0, back1, back2, back3 = add_up([joined(*back[0]), back_x, back_y], 4, (outs[-1], mark))
+    back3 = swap(back3, 6, "ep")
+    back2 = swap(back2, 4, "ep")
+    back1 = swap(back1, 2, "ep")
+    grad_gate, grad_up, mark = weight_grads(
+        me, Slices(picked, 0, slots), gate_grad, up_grad, (back0,)
+    )
     mixture = spread_rows(weighted, outs, layout, slots)
     backs = [back0, back1, back2, back3]
-    odd = arrange(backs, [[(piece, slots, slots) for piece in range(4)]], (mark,))
-    backs.append(swap(odd, 1, "ep"))
+    other = arrange(backs, [[(piece, slots, slots) for piece in range(4)]], (mark,))
+    backs.append(swap(other, 1, "ep"))
     grad_tokens = spread_rows(plain, backs, layout, slots)
     return mixture, grad_tokens, grad_gate[None], grad_up[None], grad_down[None]
 

time: 115 us -> 103 us (0.90)
  waiting for transfers between devices: 29.1 us -> 16 us
    ppermute x34, waiting for transfers between devices: 29.1 us -> 16 us  [swap(): return lax.ppermute(array, axis, [(i, i ^ distance) for i in range(size)])]
  transfers between devices with their start and end apart: 34 -> 34, of which waited for: 12 -> 13; matrix products, arithmetic and copies ran while one was open for 0% -> 0% of each run, Pallas kernels for 25% -> 31%
where the time goes in v4:
time: 103 us
  starting transfers between devices  49.1 us (48%)
  Pallas kernels  36.8 us (36%)
  waiting for transfers between devices  16 us (16%)
  between operations  1.13 us (1%)
    ppermute x34, starting transfers between devices, swap(): return lax.ppermute(array, axis, [(i, i ^ distance) for i in range(size)])  49.1 us
    pallas_call x26, Pallas kernels, run_kernel(): pl.pallas_call(run, name=name, in_specs=[*[ANYWHERE] * len(later), *specs...  36.8 us
    ppermute x34, waiting for transfers between devices, swap(): return lax.ppermute(array, axis, [(i, i ^ distance) for i in range(size)])  16 us
  transfers between devices with their start and end apart: 34, of which 13 were waited for; matrix products, arithmetic and copies ran while one was open for 0% of the time, Pallas kernels for 31%

profile of v4, /device:TPU:1, one launch (start us, length us, event | category | flops | bytes accessed | tf_op | source)
XLA Modules:
  0.0 103.2 jit_solution(2477942246581035719)
XLA Ops:
  0.6 2.6 %pick_slots.1 = (bf16[32,1792]{1,0:T(8,128)(2,1)S(1)}, bf16[32,1792]{1,0:T(8,128)(2,1)S(1)}, bf16[32,1792]{1,0:T(8,128)(2,1)S(1)}, bf16[32,1792]{1,0:T(8,128)(2,...) custom-call(s32[1]{0:T(128)} %bitcast.refs_0_, ...), custom_call_target="tpu_custom_call" | custom-call | flops 1024 | bytes 1024 | tf_op jit(solution)/shard_map/pick_slots/pallas_call | solution.py:34
  3.2 2.7 %collective-permute-start.2 = (bf16[32,1792]{1,0:T(8,128)(2,1)S(1)}, bf16[32,1792]{1,0:T(8,128)(2,1)S(1)}, u32[]{:S(2)}, u32[]{:S(2)}) collective-permute-start(bf16[32,1792]{1,0:T(8,128)(2,1)S(1)} %get-tuple-element.60), channel_id=1, source_target_pairs={{0,3},{1,2},{2,1},{3,0},{4,7},{5,6},{6,5},{7,4},{8,11},{9,10},{10,... | collective-permute-start | bytes 344072 | tf_op jit(solution)/shard_map/ppermute | solution.py:645
  6.0 0.0 collective-permute-start.1
  6.0 0.5 collective-permute-start
  6.4 2.3 %collective-permute-start.6 = (bf16[32,1792]{1,0:T(8,128)(2,1)S(1)}, bf16[32,1792]{1,0:T(8,128)(2,1)S(1)}, u32[]{:S(2)}, u32[]{:S(2)}) collective-permute-start(bf16[32,1792]{1,0:T(8,128)(2,1)S(1)} %get-tuple-element.64), channel_id=1, source_target_pairs={{0,4},{1,5},{2,6},{3,7},{4,0},{5,1},{6,2},{7,3},{8,12},{9,13},{10,... | collective-permute-start | bytes 344072 | tf_op jit(solution)/shard_map/ppermute | solution.py:645
  8.8 3.2 %load_weight.3.refs_0_.refs_6_.refs_4_.refs_2_ = bf16[4,1792,512]{2,1,0:T(8,128)(2,1)S(1)} custom-call(bf16[32,1792]{1,0:T(8,128)(2,1)S(1)} %get-tuple-element.57.refs_0_.refs_1_, s32[1]{0:T(128)} %bitcast.2.refs_1_, bf16[7168,512]{1,0:T(8,128)(2,1)} %bitcast.9), custom_call_target="tpu_custom_call" | custom-call | flops 1024 | bytes 1024 | tf_op jit(solution)/shard_map/load_weight/pallas_call | solution.py:34
  11.9 0.9 collective-permute-start.7
  12.9 0.7 collective-permute-done.1
  13.7 2.3 %collective-permute-start.3 = (bf16[128,1792]{1,0:T(8,128)(2,1)S(1)}, bf16[128,1792]{1,0:T(8,128)(2,1)S(1)}, u32[]{:S(2)}, u32[]{:S(2)}) collective-permute-start(bf16[128,1792]{1,0:T(8,128)(2,1)S(1)} %pad_maximum_fusion.refs_0_.refs_1_.refs_3_.refs_4_), channel_id=1, source_target_pairs={{0,16},{8,24},{16,0},{24,8},{1,17},{9,25},{17,1},{25,9},{2,18},{10... | collective-permute-start | bytes 1376264 | tf_op jit(solution)/shard_map/ppermute | solution.py:645
  16.0 1.2 %collective-permute-start.4 = (bf16[128,1792]{1,0:T(8,128)(2,1)S(1)}, bf16[128,1792]{1,0:T(8,128)(2,1)S(1)}, u32[]{:S(2)}, u32[]{:S(2)}) collective-permute-start(bf16[128,1792]{1,0:T(8,128)(2,1)S(1)} %pad_maximum_fusion.refs_0_.refs_1_.refs_3_.refs_4_), channel_id=1, source_target_pairs={{0,8},{8,0},{16,24},{24,16},{1,9},{9,1},{17,25},{25,17},{2,10},{10... | collective-permute-start | bytes 1376264 | tf_op jit(solution)/shard_map/ppermute | solution.py:645
  17.2 1.4 %collective-permute-done.7.refs_4_ = bf16[32,1792]{1,0:T(8,128)(2,1)S(1)} collective-permute-done((bf16[32,1792]{1,0:T(8,128)(2,1)S(1)}, bf16[32,1792]{1,0:T(8,128)(2,1)S(1)}, u32[]{:S(2)}, u32[]{:S(2)}) %collective-permute-start.7) | collective-permute-done | bytes 114720 | tf_op jit(solution)/shard_map/ppermute | solution.py:645
  18.6 1.2 %collective-permute-start.8 = (bf16[96,1792]{1,0:T(8,128)(2,1)S(1)}, bf16[96,1792]{1,0:T(8,128)(2,1)S(1)}, u32[]{:S(2)}, u32[]{:S(2)}) collective-permute-start(bf16[96,1792]{1,0:T(8,128)(2,1)S(1)} %pad_maximum_fusion.3), channel_id=1, source_target_pairs={{0,1},{1,0},{2,3},{3,2},{4,5},{5,4},{6,7},{7,6},{8,9},{9,8},{10,11... | collective-permute-start | bytes 1032200 | tf_op jit(solution)/shard_map/ppermute | solution.py:645
  19.9 2.8 %collective-permute-start.12 = (bf16[32,1792]{1,0:T(8,128)(2,1)S(1)}, bf16[32,1792]{1,0:T(8,128)(2,1)S(1)}, u32[]{:S(2)}, u32[]{:S(2)}) collective-permute-start(bf16[32,1792]{1,0:T(8,128)(2,1)S(1)} %get-tuple-element.69), channel_id=1, source_target_pairs={{0,4},{1,5},{2,6},{3,7},{4,0},{5,1},{6,2},{7,3},{8,12},{9,13},{10,... | collective-permute-start | bytes 344072 | tf_op jit(solution)/shard_map/ppermute | solution.py:645
  22.7 1.9 %collective-permute-start.13 = (bf16[32,1792]{1,0:T(8,128)(2,1)S(1)}, bf16[32,1792]{1,0:T(8,128)(2,1)S(1)}, u32[]{:S(2)}, u32[]{:S(2)}) collective-permute-start(bf16[32,1792]{1,0:T(8,128)(2,1)S(1)} %get-tuple-element.70), channel_id=1, source_target_pairs={{0,6},{1,7},{2,4},{3,5},{4,2},{5,3},{6,0},{7,1},{8,14},{9,15},{10,... | collective-permute-start | bytes 344072 | tf_op jit(solution)/shard_map/ppermute | solution.py:645
  24.6 3.2 %load_weight.4.refs_0_.refs_2_.refs_7_.refs_5_.refs_3_ = bf16[4,1792,512]{2,1,0:T(8,128)(2,1)S(1)} custom-call(bf16[128,1792]{1,0:T(8,128)(2,1)S(1)} %pad_maximum_fusion.refs_0_.refs_1_.refs_3_.refs_4_, s32[1]{0:T(128)} %bitcast.2.refs_1_, bf16[7168,512]{1,0:T(8,128)(2,1)} %bitcast.10), custom_call_target="tpu_custom_call" | custom-call | flops 1024 | bytes 1024 | tf_op jit(solution)/shard_map/load_weight/pallas_call | solution.py:34
  27.8 1.3 %collective-permute-start.9 = (bf16[64,1792]{1,0:T(8,128)(2,1)S(1)}, bf16[64,1792]{1,0:T(8,128)(2,1)S(1)}, u32[]{:S(2)}, u32[]{:S(2)}) collective-permute-start(bf16[64,1792]{1,0:T(8,128)(2,1)S(1)} %arrange.10.refs_1_.refs_5_), channel_id=1, source_target_pairs={{0,8},{8,0},{16,24},{24,16},{1,9},{9,1},{17,25},{25,17},{2,10},{10... | collective-permute-start | bytes 688136 | tf_op jit(solution)/shard_map/ppermute | solution.py:645
  29.1 1.2 %collective-permute-start.10 = (bf16[64,1792]{1,0:T(8,128)(2,1)S(1)}, bf16[64,1792]{1,0:T(8,128)(2,1)S(1)}, u32[]{:S(2)}, u32[]{:S(2)}) collective-permute-start(bf16[64,1792]{1,0:T(8,128)(2,1)S(1)} %arrange.10.refs_1_.refs_5_), channel_id=1, source_target_pairs={{0,16},{8,24},{16,0},{24,8},{1,17},{9,25},{17,1},{25,9},{2,18},{10... | collective-permute-start | bytes 688136 | tf_op jit(solution)/shard_map/ppermute | solution.py:645
  30.4 0.3 collective-permute-start.5
  30.7 0.3 collective-permute-done.12.refs_0_
  31.1 1.6 %collective-permute-start.14 = (bf16[96,1792]{1,0:T(8,128)(2,1)S(1)}, bf16[96,1792]{1,0:T(8,128)(2,1)S(1)}, u32[]{:S(2)}, u32[]{:S(2)}) collective-permute-start(bf16[96,1792]{1,0:T(8,128)(2,1)S(1)} %arrange.12), channel_id=1, source_target_pairs={{0,1},{1,0},{2,3},{3,2},{4,5},{5,4},{6,7},{7,6},{8,9},{9,8},{10,11... | collective-permute-start | bytes 1032200 | tf_op jit(solution)/shard_map/ppermute | solution.py:645
  32.7 1.2 %collective-permute-done.9.refs_0_.refs_3_.refs_7_ = bf16[64,1792]{1,0:T(8,128)(2,1)S(1)} collective-permute-done((bf16[64,1792]{1,0:T(8,128)(2,1)S(1)}, bf16[64,1792]{1,0:T(8,128)(2,1)S(1)}, u32[]{:S(2)}, u32[]{:S(2)}) %collective-permute-start.9) | collective-permute-done | bytes 229408 | tf_op jit(solution)/shard_map/ppermute | solution.py:645
  33.9 0.9 collective-permute-done.10.refs_1_.refs_5_.refs_9_
  34.9 0.3 collective-permute-start.11
  35.3 1.2 %collective-permute-start.15 = (bf16[64,1792]{1,0:T(8,128)(2,1)S(1)}, bf16[64,1792]{1,0:T(8,128)(2,1)S(1)}, u32[]{:S(2)}, u32[]{:S(2)}) collective-permute-start(bf16[64,1792]{1,0:T(8,128)(2,1)S(1)} %arrange.13.refs_2_.refs_4_), channel_id=1, source_target_pairs={{0,8},{8,0},{16,24},{24,16},{1,9},{9,1},{17,25},{25,17},{2,10},{10... | collective-permute-start | bytes 688136 | tf_op jit(solution)/shard_map/ppermute | solution.py:645
  36.5 1.7 %collective-permute-start.16 = (bf16[64,1792]{1,0:T(8,128)(2,1)S(1)}, bf16[64,1792]{1,0:T(8,128)(2,1)S(1)}, u32[]{:S(2)}, u32[]{:S(2)}) collective-permute-start(bf16[64,1792]{1,0:T(8,128)(2,1)S(1)} %arrange.13.refs_2_.refs_4_), channel_id=1, source_target_pairs={{0,16},{8,24},{16,0},{24,8},{1,17},{9,25},{17,1},{25,9},{2,18},{10... | collective-permute-start | bytes 688136 | tf_op jit(solution)/shard_map/ppermute | solution.py:645
  38.2 3.2 %load_weight.5.refs_0_.refs_6_.refs_7_.refs_8_ = bf16[4,512,1792]{2,1,0:T(8,128)(2,1)S(1)} custom-call(bf16[4,1792,512]{2,1,0:T(8,128)(2,1)S(1)} %load_weight.4.refs_0_.refs_2_.refs_7_.refs_5_.refs_3_, s32[1]{0:T(128)} %bitcast.2.refs_1_, bf16[512,7168]{1,0:T(8,128)(2,1)} %bitcast.11), custom_call_target="tpu_custom_call" | custom-call | flops 1024 | bytes 1024 | tf_op jit(solution)/shard_map/load_weight/pallas_call | solution.py:34
  41.4 1.6 %partial_products.2 = (f32[128,512]{1,0:T(8,128)S(1)}, f32[128,512]{1,0:T(8,128)S(1)}) custom-call(bf16[128,1792]{1,0:T(8,128)(2,1)S(1)} %pad_maximum_fusion.refs_0_.refs_1_.refs_3_.refs_4_, bf16[64,1792]{1,0:T(8,128)(2,1)S(1)} %arrange.10.refs_1_.refs_5_, bf16[128,1792]{1,0:T(8,128)(2,1)S(1)} %collective-permute-done.4.refs_1_.refs_0_.refs_2_.refs_3_.refs_5_.refs_6_, ...), custom_call_target="tpu_custom_call" | custom-call | flops 1024 | bytes 1024 | tf_op jit(solution)/shard_map/partial_products/pallas_call | solution.py:34
  43.0 1.7 %collective-permute-done.5.refs_0_.refs_1_.refs_9_.refs_10_ = bf16[128,1792]{1,0:T(8,128)(2,1)S(1)} collective-permute-done((bf16[128,1792]{1,0:T(8,128)(2,1)S(1)}, bf16[128,1792]{1,0:T(8,128)(2,1)S(1)}, u32[]{:S(2)}, u32[]{:S(2)}) %collective-permute-start.5) | collective-permute-done | bytes 458784 | tf_op jit(solution)/shard_map/ppermute | solution.py:645
  44.7 1.8 %forward_terms.1 = (bf16[128,512]{1,0:T(8,128)(2,1)S(1)}, f32[128,512]{1,0:T(8,128)S(1)}, f32[128,512]{1,0:T(8,128)S(1)}, bf16[64,1792]{1,0:T(8,128)(2,1)S(1)}, ...) custom-call(bf16[128,1792]{1,0:T(8,128)(2,1)S(1)} %collective-permut, ...), custom_call_target="tpu_custom_call" | custom-call | flops 1024 | bytes 1024 | tf_op jit(solution)/shard_map/forward_terms/pallas_call | solution.py:34
  46.5 1.8 %collective-permute-start.17 = (bf16[64,1792]{1,0:T(8,128)(2,1)S(1)}, bf16[64,1792]{1,0:T(8,128)(2,1)S(1)}, u32[]{:S(2)}, u32[]{:S(2)}) collective-permute-start(bf16[64,1792]{1,0:T(8,128)(2,1)S(1)} %get-tuple-element.75), channel_id=1, source_target_pairs={{0,16},{8,24},{16,0},{24,8},{1,17},{9,25},{17,1},{25,9},{2,18},{10... | collective-permute-start | bytes 688136 | tf_op jit(solution)/shard_map/ppermute | solution.py:645
  48.3 0.3 collective-permute-start.18
  48.5 1.1 %collective-permute-done.16.refs_6_.refs_1_.refs_8_ = bf16[64,1792]{1,0:T(8,128)(2,1)S(1)} collective-permute-done((bf16[64,1792]{1,0:T(8,128)(2,1)S(1)}, bf16[64,1792]{1,0:T(8,128)(2,1)S(1)}, u32[]{:S(2)}, u32[]{:S(2)}) %collective-permute-start.16) | collective-permute-done | bytes 229408 | tf_op jit(solution)/shard_map/ppermute | solution.py:645
  49.6 0.3 collective-permute-start.19
  49.9 1.9 %partial_products.3.refs_0_.refs_3_ = f32[128,512]{1,0:T(8,128)S(1)} custom-call(bf16[128,512]{1,0:T(8,128)(2,1)S(1)} %get-tuple-element.68.refs_0_.refs_2_, bf16[128,1792]{1,0:T(8,128)(2,1)S(1)} %pad_maximum_fusion.refs_0_.refs_1_.refs_3_.refs_4_, bf16[64,1792]{1,0:T(8,128)(2,1)S(1)} %arrange.13.refs_2_.refs_4_, ...), custom_call_target="tpu_custom_call" | custom-call | flops 1024 | bytes 1024 | tf_op jit(solution)/shard_map/partial_products/pallas_call | solution.py:34
  51.8 2.2 %collective-permute-done.17.refs_5_ = bf16[64,1792]{1,0:T(8,128)(2,1)S(1)} collective-permute-done((bf16[64,1792]{1,0:T(8,128)(2,1)S(1)}, bf16[64,1792]{1,0:T(8,128)(2,1)S(1)}, u32[]{:S(2)}, u32[]{:S(2)}) %collective-permute-start.17) | collective-permute-done | bytes 229408 | tf_op jit(solution)/shard_map/ppermute | solution.py:645
  54.0 0.1 merge.2
  54.1 0.1 collective-permute-start.20
  54.2 1.9 %collective-permute-start.21 = (bf16[128,1792]{1,0:T(8,128)(2,1)S(1)}, bf16[128,1792]{1,0:T(8,128)(2,1)S(1)}, u32[]{:S(2)}, u32[]{:S(2)}) collective-permute-start(bf16[128,1792]{1,0:T(8,128)(2,1)S(1)} %get-tuple-element.85), channel_id=1, source_target_pairs={{0,16},{8,24},{16,0},{24,8},{1,17},{9,25},{17,1},{25,9},{2,18},{10... | collective-permute-start | bytes 1376264 | tf_op jit(solution)/shard_map/ppermute | solution.py:645
  56.1 0.7 collective-permute-done.19.refs_2_.refs_10_
  56.8 1.9 %backward_terms.1 = (bf16[128,512]{1,0:T(8,128)(2,1)S(1)}, bf16[128,512]{1,0:T(8,128)(2,1)S(1)}, bf16[64,1792]{1,0:T(8,128)(2,1)S(1)}, bf16[64,1792]{1,0:T(8,128)(2,1)S(1)}) custom-call(bf16[128,1792]{1,0:T(8,128)(2,1)S(1)} %get-tuple-element.77.refs_0_, bf16[128,1792]{1,0:T(8,128)(2,1)S(1)} %collective-permute-done.5.refs_0_.refs_1_.refs_9_.refs_10_, ...), custom_call_target="tpu_custom_call" | custom-call | flops 1024 | bytes 1024 | tf_op jit(solution)/shard_map/backward_terms/pallas_call | solution.py:34
  58.7 0.7 collective-permute-start.26
  59.5 0.2 collective-permute-start.27
  59.8 3.6 %backward_rest.1 = (bf16[64,1792]{1,0:T(8,128)(2,1)S(1)}, bf16[64,1792]{1,0:T(8,128)(2,1)S(1)}, bf16[64,1792]{1,0:T(8,128)(2,1)S(1)}, bf16[64,1792]{1,0:T(8,128)...) custom-call(bf16[128,512]{1,0:T(8,128)(2,1)S(1)} %get-tuple-element.80.refs_0_.refs_2_, ...), custom_call_target="tpu_custom_call" | custom-call | flops 1024 | bytes 1024 | tf_op jit(solution)/shard_map/backward_rest/pallas_call | solution.py:34
  63.4 3.4 %collective-permute-done.20.refs_2_ = bf16[128,1792]{1,0:T(8,128)(2,1)S(1)} collective-permute-done((bf16[128,1792]{1,0:T(8,128)(2,1)S(1)}, bf16[128,1792]{1,0:T(8,128)(2,1)S(1)}, u32[]{:S(2)}, u32[]{:S(2)}) %collective-permute-start.20) | collective-permute-done | bytes 458784 | tf_op jit(solution)/shard_map/ppermute | solution.py:645
  66.8 0.2 add_up.2
  66.9 2.7 %collective-permute-start.24 = (bf16[32,1792]{1,0:T(8,128)(2,1)S(1)}, bf16[32,1792]{1,0:T(8,128)(2,1)S(1)}, u32[]{:S(2)}, u32[]{:S(2)}) collective-permute-start(bf16[32,1792]{1,0:T(8,128)(2,1)S(1)} %get-tuple-element.89), channel_id=1, source_target_pairs={{0,6},{1,7},{2,4},{3,5},{4,2},{5,3},{6,0},{7,1},{8,14},{9,15},{10,... | collective-permute-start | bytes 344072 | tf_op jit(solution)/shard_map/ppermute | solution.py:645
  69.7 0.9 collective-permute-start.22
  70.6 1.1 %collective-permute-done.27.refs_6_ = bf16[64,1792]{1,0:T(8,128)(2,1)S(1)} collective-permute-done((bf16[64,1792]{1,0:T(8,128)(2,1)S(1)}, bf16[64,1792]{1,0:T(8,128)(2,1)S(1)}, u32[]{:S(2)}, u32[]{:S(2)}) %collective-permute-start.27) | collective-permute-done | bytes 229408 | tf_op jit(solution)/shard_map/ppermute | solution.py:645
  71.7 0.1 merge.3
  71.8 0.2 collective-permute-start.28
  72.0 1.8 %collective-permute-start.29 = (bf16[128,1792]{1,0:T(8,128)(2,1)S(1)}, bf16[128,1792]{1,0:T(8,128)(2,1)S(1)}, u32[]{:S(2)}, u32[]{:S(2)}) collective-permute-start(bf16[128,1792]{1,0:T(8,128)(2,1)S(1)} %get-tuple-element.100), channel_id=1, source_target_pairs={{0,16},{8,24},{16,0},{24,8},{1,17},{9,25},{17,1},{25,9},{2,18},{10... | collective-permute-start | bytes 1376264 | tf_op jit(solution)/shard_map/ppermute | solution.py:645
  73.9 1.2 %collective-permute-done.23.refs_3_ = bf16[32,1792]{1,0:T(8,128)(2,1)S(1)} collective-permute-done((bf16[32,1792]{1,0:T(8,128)(2,1)S(1)}, bf16[32,1792]{1,0:T(8,128)(2,1)S(1)}, u32[]{:S(2)}, u32[]{:S(2)}) %collective-permute-start.23) | collective-permute-done | bytes 114720 | tf_op jit(solution)/shard_map/ppermute | solution.py:645
  75.1 7.8 %collective-permute-start.25 = (bf16[64,1792]{1,0:T(8,128)(2,1)S(1)}, bf16[64,1792]{1,0:T(8,128)(2,1)S(1)}, u32[]{:S(2)}, u32[]{:S(2)}) collective-permute-start(bf16[64,1792]{1,0:T(8,128)(2,1)S(1)} %pad_maximum_fusion.4), channel_id=1, source_target_pairs={{0,1},{1,0},{2,3},{3,2},{4,5},{5,4},{6,7},{7,6},{8,9},{9,8},{10,11... | collective-permute-start | bytes 688136 | tf_op jit(solution)/shard_map/ppermute | solution.py:645
  82.9 3.8 %down_grads.1 = (bf16[512,7168]{1,0:T(8,128)(2,1)}, f32[8,128]{1,0:T(8,128)S(1)}) custom-call(bf16[128,1792]{1,0:T(8,128)(2,1)S(1)} %get-tuple-element.97.refs_0_, s32[1]{0:T(128)} %bitcast.2.refs_1_, bf16[128,512]{1,0:T(8,128)(2,1)S(1)} %get-tuple-element.68.refs_0_.refs_2_, bf16[128,1792]{1,0:T(8,128)(2,1)S(1)} %pad_maximum_fusion.refs_0_.refs_1_.refs_3_.refs_4_, ...), custom_call_target="tpu_custom_call" | custom-call | flops 1024 | bytes 1024 | tf_op jit(solution)/shard_map/down_grads/pallas_call | solution.py:34
  86.8 0.2 add_up.3
  87.0 0.1 collective-permute-start.30
  87.0 2.0 %collective-permute-start.31 = (bf16[32,1792]{1,0:T(8,128)(2,1)S(1)}, bf16[32,1792]{1,0:T(8,128)(2,1)S(1)}, u32[]{:S(2)}, u32[]{:S(2)}) collective-permute-start(bf16[32,1792]{1,0:T(8,128)(2,1)S(1)} %get-tuple-element.103), channel_id=1, source_target_pairs={{0,4},{1,5},{2,6},{3,7},{4,0},{5,1},{6,2},{7,3},{8,12},{9,13},{10,... | collective-permute-start | bytes 344072 | tf_op jit(solution)/shard_map/ppermute | solution.py:645
  89.1 1.5 %collective-permute-start.32 = (bf16[32,1792]{1,0:T(8,128)(2,1)S(1)}, bf16[32,1792]{1,0:T(8,128)(2,1)S(1)}, u32[]{:S(2)}, u32[]{:S(2)}) collective-permute-start(bf16[32,1792]{1,0:T(8,128)(2,1)S(1)} %get-tuple-element.104), channel_id=1, source_target_pairs={{0,6},{1,7},{2,4},{3,5},{4,2},{5,3},{6,0},{7,1},{8,14},{9,15},{10,... | collective-permute-start | bytes 344072 | tf_op jit(solution)/shard_map/ppermute | solution.py:645
  90.6 6.0 %weight_grads.1 = (bf16[7168,512]{1,0:T(8,128)(2,1)}, bf16[7168,512]{1,0:T(8,128)(2,1)}, f32[8,128]{1,0:T(8,128)S(1)}) custom-call(bf16[32,1792]{1,0:T(8,128)(2,1)S(1)} %get-tuple-element.101.refs_0_.refs_1_, s32[1]{0:T(128)} %bitcast.2.refs_1_, bf16[128,512]{1,0:T(8,128)(2,1)S(1)} %get-tuple-element.80.refs_0_.refs_2_, ...), custom_call_target="tpu_custom_call" | custom-call | flops 1024 | bytes 1024 | tf_op jit(solution)/shard_map/weight_grads/pallas_call | solution.py:34
  96.6 0.1 collective-permute-done.32.refs_4_
  96.7 3.0 %collective-permute-start.33 = (bf16[64,1792]{1,0:T(8,128)(2,1)S(1)}, bf16[64,1792]{1,0:T(8,128)(2,1)S(1)}, u32[]{:S(2)}, u32[]{:S(2)}) collective-permute-start(bf16[64,1792]{1,0:T(8,128)(2,1)S(1)} %arrange.15), channel_id=1, source_target_pairs={{0,1},{1,0},{2,3},{3,2},{4,5},{5,4},{6,7},{7,6},{8,9},{9,8},{10,11... | collective-permute-start | bytes 688136 | tf_op jit(solution)/shard_map/ppermute | solution.py:645
  99.7 0.2 spread_matrices.1
  99.9 1.6 %spread_rows.2 = bf16[512,1792]{1,0:T(8,128)(2,1)} custom-call(bf16[512,256]{1,0:T(8,128)(2,1)S(1)} %get-tuple-element.63.refs_0_, bf16[32,1792]{1,0:T(8,128)(2,1)S(1)} %get-tuple-element.86.refs_1_.refs_0_, bf16[32,1792]{1,0:T(8,128)(2,1)S(1)} %collective-permute-done.22.refs_2_, bf16[32,1792]{1,0:T(8,128)(2,1)S(1)} %collective-permute-done.23.refs_3_, ...), custom_call_target="tpu_custom_call" | custom-call | flops 1024 | bytes 1024 | tf_op jit(solution)/shard_map/spread_rows/pallas_call | solution.py:34
  101.5 1.5 %spread_rows.3 = bf16[512,1792]{1,0:T(8,128)(2,1)} custom-call(bf16[512,128]{1,0:T(8,128)(2,1)S(1)} %get-tuple-element.90.refs_0_, bf16[32,1792]{1,0:T(8,128)(2,1)S(1)} %get-tuple-element.101.refs_0_.refs_1_, bf16[32,1792]{1,0:T(8,128)(2,1)S(1)} %collective-permute-done.30.refs_2_, bf16[32,1792]{1,0:T(8,128)(2,1)S(1)} %collective-permute-done.31.refs_3_, ...), custom_call_target="tpu_custom_call" | custom-call | flops 1024 | bytes 1024 | tf_op jit(solution)/shard_map/spread_rows/pallas_call | solution.py:34
  (41 shorter events, 0.4 us)
Async XLA Ops:
  3.2 9.7 %collective-permute-start.2 = (bf16[32,1792]{1,0:T(8,128)(2,1)S(1)}, bf16[32,1792]{1,0:T(8,128)(2,1)S(1)}, u32[]{:S(2)}, u32[]{:S(2)}) collective-permute-start(bf16[32,1792]{1,0:T(8,128)(2,1)S(1)} %get-tuple-element.60), channel_id=1, source_target_pairs={{0,3},{1,2},{2,1},{3,0},{4,7},{5,6},{6,5},{7,4},{8,11},{9,10},{10,... | collective-permute-start | bytes 344072 | tf_op jit(solution)/shard_map/ppermute | solution.py:645
  6.0 7.6 %collective-permute-start.1 = (bf16[32,1792]{1,0:T(8,128)(2,1)S(1)}, bf16[32,1792]{1,0:T(8,128)(2,1)S(1)}, u32[]{:S(2)}, u32[]{:S(2)}) collective-permute-start(bf16[32,1792]{1,0:T(8,128)(2,1)S(1)} %get-tuple-element.59), channel_id=1, source_target_pairs={{0,2},{1,3},{2,0},{3,1},{4,6},{5,7},{6,4},{7,5},{8,10},{9,11},{10,... | collective-permute-start | bytes 344072 | tf_op jit(solution)/shard_map/ppermute | solution.py:645
  6.0 7.6 %collective-permute-start = (bf16[32,1792]{1,0:T(8,128)(2,1)S(1)}, bf16[32,1792]{1,0:T(8,128)(2,1)S(1)}, u32[]{:S(2)}, u32[]{:S(2)}) collective-permute-start(bf16[32,1792]{1,0:T(8,128)(2,1)S(1)} %get-tuple-element.58), channel_id=1, source_target_pairs={{0,1},{1,0},{2,3},{3,2},{4,5},{5,4},{6,7},{7,6},{8,9},{9,8},{10,11... | collective-permute-start | bytes 344072 | tf_op jit(solution)/shard_map/ppermute | solution.py:645
  6.4 12.1 %collective-permute-start.6 = (bf16[32,1792]{1,0:T(8,128)(2,1)S(1)}, bf16[32,1792]{1,0:T(8,128)(2,1)S(1)}, u32[]{:S(2)}, u32[]{:S(2)}) collective-permute-start(bf16[32,1792]{1,0:T(8,128)(2,1)S(1)} %get-tuple-element.64), channel_id=1, source_target_pairs={{0,4},{1,5},{2,6},{3,7},{4,0},{5,1},{6,2},{7,3},{8,12},{9,13},{10,... | collective-permute-start | bytes 344072 | tf_op jit(solution)/shard_map/ppermute | solution.py:645
  11.9 6.6 %collective-permute-start.7 = (bf16[32,1792]{1,0:T(8,128)(2,1)S(1)}, bf16[32,1792]{1,0:T(8,128)(2,1)S(1)}, u32[]{:S(2)}, u32[]{:S(2)}) collective-permute-start(bf16[32,1792]{1,0:T(8,128)(2,1)S(1)} %get-tuple-element.65), channel_id=1, source_target_pairs={{0,6},{1,7},{2,4},{3,5},{4,2},{5,3},{6,0},{7,1},{8,14},{9,15},{10,... | collective-permute-start | bytes 344072 | tf_op jit(solution)/shard_map/ppermute | solution.py:645
  13.7 14.1 %collective-permute-start.3 = (bf16[128,1792]{1,0:T(8,128)(2,1)S(1)}, bf16[128,1792]{1,0:T(8,128)(2,1)S(1)}, u32[]{:S(2)}, u32[]{:S(2)}) collective-permute-start(bf16[128,1792]{1,0:T(8,128)(2,1)S(1)} %pad_maximum_fusion.refs_0_.refs_1_.refs_3_.refs_4_), channel_id=1, source_target_pairs={{0,16},{8,24},{16,0},{24,8},{1,17},{9,25},{17,1},{25,9},{2,18},{10... | collective-permute-start | bytes 1376264 | tf_op jit(solution)/shard_map/ppermute | solution.py:645
  16.0 11.8 %collective-permute-start.4 = (bf16[128,1792]{1,0:T(8,128)(2,1)S(1)}, bf16[128,1792]{1,0:T(8,128)(2,1)S(1)}, u32[]{:S(2)}, u32[]{:S(2)}) collective-permute-start(bf16[128,1792]{1,0:T(8,128)(2,1)S(1)} %pad_maximum_fusion.refs_0_.refs_1_.refs_3_.refs_4_), channel_id=1, source_target_pairs={{0,8},{8,0},{16,24},{24,16},{1,9},{9,1},{17,25},{25,17},{2,10},{10... | collective-permute-start | bytes 1376264 | tf_op jit(solution)/shard_map/ppermute | solution.py:645
  18.6 9.2 %collective-permute-start.8 = (bf16[96,1792]{1,0:T(8,128)(2,1)S(1)}, bf16[96,1792]{1,0:T(8,128)(2,1)S(1)}, u32[]{:S(2)}, u32[]{:S(2)}) collective-permute-start(bf16[96,1792]{1,0:T(8,128)(2,1)S(1)} %pad_maximum_fusion.3), channel_id=1, source_target_pairs={{0,1},{1,0},{2,3},{3,2},{4,5},{5,4},{6,7},{7,6},{8,9},{9,8},{10,11... | collective-permute-start | bytes 1032200 | tf_op jit(solution)/shard_map/ppermute | solution.py:645
  19.9 11.2 %collective-permute-start.12 = (bf16[32,1792]{1,0:T(8,128)(2,1)S(1)}, bf16[32,1792]{1,0:T(8,128)(2,1)S(1)}, u32[]{:S(2)}, u32[]{:S(2)}) collective-permute-start(bf16[32,1792]{1,0:T(8,128)(2,1)S(1)} %get-tuple-element.69), channel_id=1, source_target_pairs={{0,4},{1,5},{2,6},{3,7},{4,0},{5,1},{6,2},{7,3},{8,12},{9,13},{10,... | collective-permute-start | bytes 344072 | tf_op jit(solution)/shard_map/ppermute | solution.py:645
  22.7 8.3 %collective-permute-start.13 = (bf16[32,1792]{1,0:T(8,128)(2,1)S(1)}, bf16[32,1792]{1,0:T(8,128)(2,1)S(1)}, u32[]{:S(2)}, u32[]{:S(2)}) collective-permute-start(bf16[32,1792]{1,0:T(8,128)(2,1)S(1)} %get-tuple-element.70), channel_id=1, source_target_pairs={{0,6},{1,7},{2,4},{3,5},{4,2},{5,3},{6,0},{7,1},{8,14},{9,15},{10,... | collective-permute-start | bytes 344072 | tf_op jit(solution)/shard_map/ppermute | solution.py:645
  27.8 6.1 %collective-permute-start.9 = (bf16[64,1792]{1,0:T(8,128)(2,1)S(1)}, bf16[64,1792]{1,0:T(8,128)(2,1)S(1)}, u32[]{:S(2)}, u32[]{:S(2)}) collective-permute-start(bf16[64,1792]{1,0:T(8,128)(2,1)S(1)} %arrange.10.refs_1_.refs_5_), channel_id=1, source_target_pairs={{0,8},{8,0},{16,24},{24,16},{1,9},{9,1},{17,25},{25,17},{2,10},{10... | collective-permute-start | bytes 688136 | tf_op jit(solution)/shard_map/ppermute | solution.py:645
  29.1 5.7 %collective-permute-start.10 = (bf16[64,1792]{1,0:T(8,128)(2,1)S(1)}, bf16[64,1792]{1,0:T(8,128)(2,1)S(1)}, u32[]{:S(2)}, u32[]{:S(2)}) collective-permute-start(bf16[64,1792]{1,0:T(8,128)(2,1)S(1)} %arrange.10.refs_1_.refs_5_), channel_id=1, source_target_pairs={{0,16},{8,24},{16,0},{24,8},{1,17},{9,25},{17,1},{25,9},{2,18},{10... | collective-permute-start | bytes 688136 | tf_op jit(solution)/shard_map/ppermute | solution.py:645
  30.4 14.3 %collective-permute-start.5 = (bf16[128,1792]{1,0:T(8,128)(2,1)S(1)}, bf16[128,1792]{1,0:T(8,128)(2,1)S(1)}, u32[]{:S(2)}, u32[]{:S(2)}) collective-permute-start(bf16[128,1792]{1,0:T(8,128)(2,1)S(1)} %arrange.9), channel_id=1, source_target_pairs={{0,16},{8,24},{16,0},{24,8},{1,17},{9,25},{17,1},{25,9},{2,18},{10... | collective-permute-start | bytes 1376264 | tf_op jit(solution)/shard_map/ppermute | solution.py:645
  31.1 4.2 %collective-permute-start.14 = (bf16[96,1792]{1,0:T(8,128)(2,1)S(1)}, bf16[96,1792]{1,0:T(8,128)(2,1)S(1)}, u32[]{:S(2)}, u32[]{:S(2)}) collective-permute-start(bf16[96,1792]{1,0:T(8,128)(2,1)S(1)} %arrange.12), channel_id=1, source_target_pairs={{0,1},{1,0},{2,3},{3,2},{4,5},{5,4},{6,7},{7,6},{8,9},{9,8},{10,11... | collective-permute-start | bytes 1032200 | tf_op jit(solution)/shard_map/ppermute | solution.py:645
  34.9 9.8 %collective-permute-start.11 = (bf16[64,1792]{1,0:T(8,128)(2,1)S(1)}, bf16[64,1792]{1,0:T(8,128)(2,1)S(1)}, u32[]{:S(2)}, u32[]{:S(2)}) collective-permute-start(bf16[64,1792]{1,0:T(8,128)(2,1)S(1)} %arrange.11), channel_id=1, source_target_pairs={{0,8},{8,0},{16,24},{24,16},{1,9},{9,1},{17,25},{25,17},{2,10},{10... | collective-permute-start | bytes 688136 | tf_op jit(solution)/shard_map/ppermute | solution.py:645
  35.3 13.3 %collective-permute-start.15 = (bf16[64,1792]{1,0:T(8,128)(2,1)S(1)}, bf16[64,1792]{1,0:T(8,128)(2,1)S(1)}, u32[]{:S(2)}, u32[]{:S(2)}) collective-permute-start(bf16[64,1792]{1,0:T(8,128)(2,1)S(1)} %arrange.13.refs_2_.refs_4_), channel_id=1, source_target_pairs={{0,8},{8,0},{16,24},{24,16},{1,9},{9,1},{17,25},{25,17},{2,10},{10... | collective-permute-start | bytes 688136 | tf_op jit(solution)/shard_map/ppermute | solution.py:645
  36.5 13.1 %collective-permute-start.16 = (bf16[64,1792]{1,0:T(8,128)(2,1)S(1)}, bf16[64,1792]{1,0:T(8,128)(2,1)S(1)}, u32[]{:S(2)}, u32[]{:S(2)}) collective-permute-start(bf16[64,1792]{1,0:T(8,128)(2,1)S(1)} %arrange.13.refs_2_.refs_4_), channel_id=1, source_target_pairs={{0,16},{8,24},{16,0},{24,8},{1,17},{9,25},{17,1},{25,9},{2,18},{10... | collective-permute-start | bytes 688136 | tf_op jit(solution)/shard_map/ppermute | solution.py:645
  46.5 7.5 %collective-permute-start.17 = (bf16[64,1792]{1,0:T(8,128)(2,1)S(1)}, bf16[64,1792]{1,0:T(8,128)(2,1)S(1)}, u32[]{:S(2)}, u32[]{:S(2)}) collective-permute-start(bf16[64,1792]{1,0:T(8,128)(2,1)S(1)} %get-tuple-element.75), channel_id=1, source_target_pairs={{0,16},{8,24},{16,0},{24,8},{1,17},{9,25},{17,1},{25,9},{2,18},{10... | collective-permute-start | bytes 688136 | tf_op jit(solution)/shard_map/ppermute | solution.py:645
  48.3 5.7 %collective-permute-start.18 = (bf16[64,1792]{1,0:T(8,128)(2,1)S(1)}, bf16[64,1792]{1,0:T(8,128)(2,1)S(1)}, u32[]{:S(2)}, u32[]{:S(2)}) collective-permute-start(bf16[64,1792]{1,0:T(8,128)(2,1)S(1)} %get-tuple-element.76), channel_id=1, source_target_pairs={{0,8},{8,0},{16,24},{24,16},{1,9},{9,1},{17,25},{25,17},{2,10},{10... | collective-permute-start | bytes 688136 | tf_op jit(solution)/shard_map/ppermute | solution.py:645
  49.6 7.1 %collective-permute-start.19 = (bf16[64,1792]{1,0:T(8,128)(2,1)S(1)}, bf16[64,1792]{1,0:T(8,128)(2,1)S(1)}, u32[]{:S(2)}, u32[]{:S(2)}) collective-permute-start(bf16[64,1792]{1,0:T(8,128)(2,1)S(1)} %arrange.14), channel_id=1, source_target_pairs={{0,8},{8,0},{16,24},{24,16},{1,9},{9,1},{17,25},{25,17},{2,10},{10... | collective-permute-start | bytes 688136 | tf_op jit(solution)/shard_map/ppermute | solution.py:645
  54.1 12.7 %collective-permute-start.20 = (bf16[128,1792]{1,0:T(8,128)(2,1)S(1)}, bf16[128,1792]{1,0:T(8,128)(2,1)S(1)}, u32[]{:S(2)}, u32[]{:S(2)}) collective-permute-start(bf16[128,1792]{1,0:T(8,128)(2,1)S(1)} %get-tuple-element.77.refs_0_), channel_id=1, source_target_pairs={{0,8},{8,0},{16,24},{24,16},{1,9},{9,1},{17,25},{25,17},{2,10},{10... | collective-permute-start | bytes 1376264 | tf_op jit(solution)/shard_map/ppermute | solution.py:645
  54.2 12.6 %collective-permute-start.21 = (bf16[128,1792]{1,0:T(8,128)(2,1)S(1)}, bf16[128,1792]{1,0:T(8,128)(2,1)S(1)}, u32[]{:S(2)}, u32[]{:S(2)}) collective-permute-start(bf16[128,1792]{1,0:T(8,128)(2,1)S(1)} %get-tuple-element.85), channel_id=1, source_target_pairs={{0,16},{8,24},{16,0},{24,8},{1,17},{9,25},{17,1},{25,9},{2,18},{10... | collective-permute-start | bytes 1376264 | tf_op jit(solution)/shard_map/ppermute | solution.py:645
  58.7 11.8 %collective-permute-start.26 = (bf16[64,1792]{1,0:T(8,128)(2,1)S(1)}, bf16[64,1792]{1,0:T(8,128)(2,1)S(1)}, u32[]{:S(2)}, u32[]{:S(2)}) collective-permute-start(bf16[64,1792]{1,0:T(8,128)(2,1)S(1)} %get-tuple-element.95), channel_id=1, source_target_pairs={{0,16},{8,24},{16,0},{24,8},{1,17},{9,25},{17,1},{25,9},{2,18},{10... | collective-permute-start | bytes 688136 | tf_op jit(solution)/shard_map/ppermute | solution.py:645
  59.5 12.2 %collective-permute-start.27 = (bf16[64,1792]{1,0:T(8,128)(2,1)S(1)}, bf16[64,1792]{1,0:T(8,128)(2,1)S(1)}, u32[]{:S(2)}, u32[]{:S(2)}) collective-permute-start(bf16[64,1792]{1,0:T(8,128)(2,1)S(1)} %get-tuple-element.96), channel_id=1, source_target_pairs={{0,8},{8,0},{16,24},{24,16},{1,9},{9,1},{17,25},{25,17},{2,10},{10... | collective-permute-start | bytes 688136 | tf_op jit(solution)/shard_map/ppermute | solution.py:645
  66.9 6.9 %collective-permute-start.24 = (bf16[32,1792]{1,0:T(8,128)(2,1)S(1)}, bf16[32,1792]{1,0:T(8,128)(2,1)S(1)}, u32[]{:S(2)}, u32[]{:S(2)}) collective-permute-start(bf16[32,1792]{1,0:T(8,128)(2,1)S(1)} %get-tuple-element.89), channel_id=1, source_target_pairs={{0,6},{1,7},{2,4},{3,5},{4,2},{5,3},{6,0},{7,1},{8,14},{9,15},{10,... | collective-permute-start | bytes 344072 | tf_op jit(solution)/shard_map/ppermute | solution.py:645
  69.7 5.4 %collective-permute-start.23 = (bf16[32,1792]{1,0:T(8,128)(2,1)S(1)}, bf16[32,1792]{1,0:T(8,128)(2,1)S(1)}, u32[]{:S(2)}, u32[]{:S(2)}) collective-permute-start(bf16[32,1792]{1,0:T(8,128)(2,1)S(1)} %get-tuple-element.88), channel_id=1, source_target_pairs={{0,4},{1,5},{2,6},{3,7},{4,0},{5,1},{6,2},{7,3},{8,12},{9,13},{10,... | collective-permute-start | bytes 344072 | tf_op jit(solution)/shard_map/ppermute | solution.py:645
  69.7 5.4 %collective-permute-start.22 = (bf16[32,1792]{1,0:T(8,128)(2,1)S(1)}, bf16[32,1792]{1,0:T(8,128)(2,1)S(1)}, u32[]{:S(2)}, u32[]{:S(2)}) collective-permute-start(bf16[32,1792]{1,0:T(8,128)(2,1)S(1)} %get-tuple-element.87), channel_id=1, source_target_pairs={{0,2},{1,3},{2,0},{3,1},{4,6},{5,7},{6,4},{7,5},{8,10},{9,11},{10,... | collective-permute-start | bytes 344072 | tf_op jit(solution)/shard_map/ppermute | solution.py:645
  71.8 14.9 %collective-permute-start.28 = (bf16[128,1792]{1,0:T(8,128)(2,1)S(1)}, bf16[128,1792]{1,0:T(8,128)(2,1)S(1)}, u32[]{:S(2)}, u32[]{:S(2)}) collective-permute-start(bf16[128,1792]{1,0:T(8,128)(2,1)S(1)} %get-tuple-element.97.refs_0_), channel_id=1, source_target_pairs={{0,8},{8,0},{16,24},{24,16},{1,9},{9,1},{17,25},{25,17},{2,10},{10... | collective-permute-start | bytes 1376264 | tf_op jit(solution)/shard_map/ppermute | solution.py:645
  72.0 14.8 %collective-permute-start.29 = (bf16[128,1792]{1,0:T(8,128)(2,1)S(1)}, bf16[128,1792]{1,0:T(8,128)(2,1)S(1)}, u32[]{:S(2)}, u32[]{:S(2)}) collective-permute-start(bf16[128,1792]{1,0:T(8,128)(2,1)S(1)} %get-tuple-element.100), channel_id=1, source_target_pairs={{0,16},{8,24},{16,0},{24,8},{1,17},{9,25},{17,1},{25,9},{2,18},{10... | collective-permute-start | bytes 1376264 | tf_op jit(solution)/shard_map/ppermute | solution.py:645
  75.1 11.7 %collective-permute-start.25 = (bf16[64,1792]{1,0:T(8,128)(2,1)S(1)}, bf16[64,1792]{1,0:T(8,128)(2,1)S(1)}, u32[]{:S(2)}, u32[]{:S(2)}) collective-permute-start(bf16[64,1792]{1,0:T(8,128)(2,1)S(1)} %pad_maximum_fusion.4), channel_id=1, source_target_pairs={{0,1},{1,0},{2,3},{3,2},{4,5},{5,4},{6,7},{7,6},{8,9},{9,8},{10,11... | collective-permute-start | bytes 688136 | tf_op jit(solution)/shard_map/ppermute | solution.py:645
  87.0 9.6 %collective-permute-start.30 = (bf16[32,1792]{1,0:T(8,128)(2,1)S(1)}, bf16[32,1792]{1,0:T(8,128)(2,1)S(1)}, u32[]{:S(2)}, u32[]{:S(2)}) collective-permute-start(bf16[32,1792]{1,0:T(8,128)(2,1)S(1)} %get-tuple-element.102), channel_id=1, source_target_pairs={{0,2},{1,3},{2,0},{3,1},{4,6},{5,7},{6,4},{7,5},{8,10},{9,11},{10,... | collective-permute-start | bytes 344072 | tf_op jit(solution)/shard_map/ppermute | solution.py:645
  87.0 9.5 %collective-permute-start.31 = (bf16[32,1792]{1,0:T(8,128)(2,1)S(1)}, bf16[32,1792]{1,0:T(8,128)(2,1)S(1)}, u32[]{:S(2)}, u32[]{:S(2)}) collective-permute-start(bf16[32,1792]{1,0:T(8,128)(2,1)S(1)} %get-tuple-element.103), channel_id=1, source_target_pairs={{0,4},{1,5},{2,6},{3,7},{4,0},{5,1},{6,2},{7,3},{8,12},{9,13},{10,... | collective-permute-start | bytes 344072 | tf_op jit(solution)/shard_map/ppermute | solution.py:645
  89.1 7.6 %collective-permute-start.32 = (bf16[32,1792]{1,0:T(8,128)(2,1)S(1)}, bf16[32,1792]{1,0:T(8,128)(2,1)S(1)}, u32[]{:S(2)}, u32[]{:S(2)}) collective-permute-start(bf16[32,1792]{1,0:T(8,128)(2,1)S(1)} %get-tuple-element.104), channel_id=1, source_target_pairs={{0,6},{1,7},{2,4},{3,5},{4,2},{5,3},{6,0},{7,1},{8,14},{9,15},{10,... | collective-permute-start | bytes 344072 | tf_op jit(solution)/shard_map/ppermute | solution.py:645
  96.7 4.8 %collective-permute-start.33 = (bf16[64,1792]{1,0:T(8,128)(2,1)S(1)}, bf16[64,1792]{1,0:T(8,128)(2,1)S(1)}, u32[]{:S(2)}, u32[]{:S(2)}) collective-permute-start(bf16[64,1792]{1,0:T(8,128)(2,1)S(1)} %arrange.15), channel_id=1, source_target_pairs={{0,1},{1,0},{2,3},{3,2},{4,5},{5,4},{6,7},{7,6},{8,9},{9,8},{10,11... | collective-permute-start | bytes 688136 | tf_op jit(solution)/shard_map/ppermute | solution.py:645

commit v5 on v4

--- a/solution.py
+++ b/solution.py
@@ -16,7 +16,7 @@
 MIB = 1024 * 1024
 
 
-def run_kernel(body, name, operands, specs, outs, out_specs, scratch, mib, later=(), mark=False, cost=1024):
+def run_kernel(body, name, operands, specs, outs, out_specs, scratch, mib, later=(), mark=False, aliases=None):
     used = len(operands)
     outs, out_specs = list(outs), list(out_specs)
     results = len(outs)
@@ -38,8 +38,9 @@
         out_shape=outs,
         out_specs=out_specs,
         scratch_shapes=scratch,
+        input_output_aliases={len(later) + i: o for i, o in (aliases or {}).items()},
         compiler_params=pltpu.CompilerParams(vmem_limit_bytes=mib * MIB),
-        cost_estimate=pl.CostEstimate(flops=1024, bytes_accessed=cost, transcendentals=0),
+        cost_estimate=pl.CostEstimate(flops=1024, bytes_accessed=1024, transcendentals=0),
     )(*later, *operands)
     return out if len(out) > 1 else out[0]
 
@@ -221,7 +222,7 @@
             start += size
 
 
-def arrange(sources, plan, later=(), cost=1024):
+def arrange(sources, plan, later=()):
     width = sources[0].shape[1]
     sizes = [sum(size for _, _, size in rows) for rows in plan]
     return run_kernel(
@@ -234,7 +235,6 @@
         [],
         8,
         later,
-        cost=cost,
     )
 
 
@@ -248,7 +248,7 @@
         start += out_ref.shape[0]
 
 
-def add_up(terms, parts=1, later=(), cost=1024):
+def add_up(terms, parts=1, later=()):
     rows, width = terms[0].shape
     return run_kernel(
         functools.partial(add_body, len(terms)),
@@ -260,7 +260,6 @@
         [],
         8,
         later,
-        cost=cost,
     )
 
 
@@ -465,54 +464,55 @@
     )
 
 
-def down_grad_body(slices, me_ref, hidden_ref, *refs):
+def down_grad_body(slices, start, filled, me_ref, hidden_ref, *refs):
     out_ref, block, sems = refs[-3:]
-    count, _, width = block.shape
+    _, _, width = block.shape
     hidden = hidden_ref[...]
     copies = []
-    for index in range(count):
-        rows = slices.read(refs, index)
+    for index in range(slices.count):
         block[index] = lax.dot_general(
-            hidden, rows, ROWS, preferred_element_type=jnp.float32
+            hidden, slices.read(refs[filled:], index), ROWS, preferred_element_type=jnp.float32
         ).astype(jnp.bfloat16)
-        start = pl.multiple_of((me_ref[0] ^ index) * width, width)
-        target = out_ref.at[:, pl.ds(start, width)]
+        first = pl.multiple_of((me_ref[0] ^ (start + index)) * width, width)
+        target = out_ref.at[:, pl.ds(first, width)]
         copies.append(pltpu.make_async_copy(block.at[index], target, sems.at[index]))
         copies[-1].start()
     for copy in copies:
         copy.wait()
 
 
-def down_grads(me, hidden, slices, later=()):
-    count, width, units = slices.count, slices.width, hidden.shape[1]
-    return run_kernel(
-        functools.partial(down_grad_body, slices),
+def down_grads(me, hidden, slices, start, total, filled=(), later=()):
+    width, units = slices.width, hidden.shape[1]
+    return run_kernel(
+        functools.partial(down_grad_body, slices, start, len(filled)),
         "down_grads",
-        (me, hidden, *slices.flat),
-        [IN_SMEM] + [IN_VMEM] * (1 + len(slices.flat)),
-        [like(units, width * count)],
+        (me, hidden, *filled, *slices.flat),
+        [IN_SMEM, IN_VMEM] + [ANYWHERE] * len(filled) + [IN_VMEM] * len(slices.flat),
+        [like(units, width * total)],
         [ANYWHERE],
         [
-            pltpu.VMEM((count, units, width), jnp.bfloat16),
-            pltpu.SemaphoreType.DMA((count,)),
+            pltpu.VMEM((slices.count, units, width), jnp.bfloat16),
+            pltpu.SemaphoreType.DMA((slices.count,)),
         ],
         16,
         later,
         True,
+        {2: 0} if filled else None,
     )
 
 
 def weight_grad_body(slices, me_ref, *refs):
     grad_refs, (gate_hbm, up_hbm, block, sems) = refs[:2], refs[-4:]
-    _, count, width, _ = block.shape
+    _, count, width, units = block.shape
+    grads = jnp.concatenate([ref[...] for ref in grad_refs], axis=1)
     copies = []
     for index in range(count):
         rows = slices.read(refs[2:], index)
         start = pl.multiple_of((me_ref[0] ^ index) * width, width)
+        both = lax.dot_general(rows, grads, ROWS, preferred_element_type=jnp.float32)
+        both = both.astype(jnp.bfloat16)
         for which, out_ref in enumerate((gate_hbm, up_hbm)):
-            block[which, index] = lax.dot_general(
-                rows, grad_refs[which][...], ROWS, preferred_element_type=jnp.float32
-            ).astype(jnp.bfloat16)
+            block[which, index] = both[:, which * units : (which + 1) * units]
             target = out_ref.at[pl.ds(start, width), :]
             sem = sems.at[2 * index + which]
             copies.append(pltpu.make_async_copy(block.at[which, index], target, sem))
@@ -685,11 +685,12 @@
     core = swap(core, 1, "ep")
     gate = load_weight(me, gate_weight[0], True, count, (own,))
     near = joined(arrange((own,), [[(0, 0, two)]], (gate,)), core, even1, odd1)
-    mixed = gathered(near, 1, 2)
+    near_x = swap(near, 1, "fsdp")
+    near_y = swap(near, 2, "fsdp")
     odd = swap(joined(token2[slots:], token3[slots:], token2, token3), 1, "ep")
     ends = [(0, 0, slots), (2, 0, slots), (1, 0, slots), (2, slots, slots)]
     up = load_weight(me, up_weight[0], True, count, (near,))
-    far = arrange((token2, token3, odd), [ends], (mixed[1][0], mixed[2][0], up))
+    far = arrange((token2, token3, odd), [ends], (near_x, near_y, up))
     far_tokens = gathered(far, 2, 1)
     grad2 = swap(grad2, 4, "ep")
     grad3 = swap(grad3, 6, "ep")
@@ -700,9 +701,15 @@
         [[(0, slots, slots), (1, slots, slots), (0, 0, two), (1, 0, two)]],
     )
     odd = swap(odd, 1, "ep")
-    far_grads = gathered(arrange((grad2, grad3, odd), [ends]), 2, 1)
+    far_grads = gathered(arrange((grad2, grad3, odd), [ends]), 1, 2)
+    halves = [[(0, first, slots) for first in range(part * slots, 4 * two, two)] for part in range(2)]
+    near_d = swap(arrange((near_x,), halves[:1]), 2, "fsdp")
+    near_grad_d = swap(arrange((near_y,), halves[1:]), 1, "fsdp")
+    mixed = [[near], [near_x], [near_y], []]
     picked = pieces_of(mixed, far_tokens)
     grads = pieces_of(mixed, far_grads)
+    picked[3].insert(0, (near_d, False))
+    grads[3].insert(0, (near_grad_d, False))
     first = Slices(picked[:3], 0, slots)
     last = Slices(picked[3:], 0, slots)
 
@@ -714,7 +721,8 @@
     first = Slices(grads[:3], 1, slots)
     last = Slices(grads[3:], 1, slots)
     (grad_sum,) = [partial_products(first, (down,), (LAST,), units, (hidden,))]
-    sum_x, sum_y = merge(terms[1], terms[2], top, bottom, (grad_sum,))
+    grad_down, mark = down_grads(me, hidden, first, 0, count, (), (grad_sum,))
+    sum_x, sum_y = merge(terms[1], terms[2], top, bottom, (mark,))
     (gate_grad, up_grad), back_d = backward_terms(
         last, grad_sum, slope, silu, gate, up, down, (sum_x,)
     )
@@ -728,16 +736,20 @@
     out2 = swap(out2, 4, "ep")
     out1 = swap(out1, 2, "ep")
 
-    back_x, back_y = merge(back[1], back[2], top, bottom, (out0,))
-    grad_down, mark = down_grads(me, hidden, Slices(grads, 1, slots), (back_x,))
-    back_x = swap(back_x, 1, "fsdp")
-    back_y = swap(back_y, 2, "fsdp")
+    y_far, x_near = add_pairs((back[2][1], bottom), (back[1][0], top), (out0,))
+    x_far = swap(back[1][1], 1, "fsdp")
+    y_far = swap(y_far, 2, "fsdp")
+    x_near = swap(x_near, 1, "fsdp")
+    y_near = swap(back[2][0], 2, "fsdp")
     layout = []
     for step in range(experts // 2):
         layout += [(step, 0), (experts // 2, step)]
     outs = [out0, out1, out2, out3]
     outs.append(swap(joined(*[piece[slots:] for piece in outs]), 1, "ep"))
-    back0, back1, back2, back3 = add_up([joined(*back[0]), back_x, back_y], 4, (outs[-1], mark))
+    back2, back3 = add_up([back[0][1], x_far, y_far], 2, (outs[-1],))
+    last = Slices(grads[3:], 1, slots)
+    grad_down, mark = down_grads(me, hidden, last, count - 1, count, (grad_down,), (back2,))
+    back0, back1 = add_up([back[0][0], x_near, y_near], 2, (mark,))
     back3 = swap(back3, 6, "ep")
     back2 = swap(back2, 4, "ep")
     back1 = swap(back1, 2, "ep")
@@ -746,8 +758,10 @@
     )
     mixture = spread_rows(weighted, outs, layout, slots)
     backs = [back0, back1, back2, back3]
-    other = arrange(backs, [[(piece, slots, slots) for piece in range(4)]], (mark,))
-    backs.append(swap(other, 1, "ep"))
+    far_odd = [[(0, slots, slots), (1, slots, slots), (0, 0, two)]]
+    backs.append(swap(arrange((back2, back3), far_odd, (mark,)), 1, "ep"))
+    backs.append(swap(arrange((back0, back1), [far_odd[0][:2]], (mark,)), 1, "ep"))
+    layout = [(0, 0), (5, 0), (1, 0), (5, 1), (2, 0), (4, 0), (3, 0), (4, 1)]
     grad_tokens = spread_rows(plain, backs, layout, slots)
     return mixture, grad_tokens, grad_gate[None], grad_up[None], grad_down[None]
 

time: 103 us -> 100 us (0.971)
  starting transfers between devices: 49.1 us -> 46.7 us
  waiting for transfers between devices: 16 us -> 14.3 us
  Pallas kernels: 36.8 us -> 38 us
    ppermute x34 -> x38, starting transfers between devices: 49.1 us -> 46.7 us  [swap(): return lax.ppermute(array, axis, [(i, i ^ distance) for i in range(size)])]
    ppermute x34 -> x38, waiting for transfers between devices: 16 us -> 14.3 us  [swap(): return lax.ppermute(array, axis, [(i, i ^ distance) for i in range(size)])]
    pallas_call x26 -> x30, Pallas kernels: 36.8 us -> 38 us  [run_kernel(): pl.pallas_call(run, name=name, in_specs=[*[ANYWHERE] * len(later), *specs...]
  transfers between devices with their start and end apart: 34 -> 38, of which waited for: 13 -> 11; matrix products, arithmetic and copies ran while one was open for 0% -> 0% of each run, Pallas kernels for 31% -> 34%
where the time goes in v5:
time: 100 us
  starting transfers between devices  46.7 us (47%)
  Pallas kernels  38 us (38%)
  waiting for transfers between devices  14.3 us (14%)
  between operations  1.15 us (1%)
    ppermute x38, starting transfers between devices, swap(): return lax.ppermute(array, axis, [(i, i ^ distance) for i in range(size)])  46.7 us
    pallas_call x30, Pallas kernels, run_kernel(): pl.pallas_call(run, name=name, in_specs=[*[ANYWHERE] * len(later), *specs...  38 us
    ppermute x38, waiting for transfers between devices, swap(): return lax.ppermute(array, axis, [(i, i ^ distance) for i in range(size)])  14.3 us
  transfers between devices with their start and end apart: 38, of which 11 were waited for; matrix products, arithmetic and copies ran while one was open for 0% of the time, Pallas kernels for 34%

profile of v5, /device:TPU:1, one launch (start us, length us, event | category | flops | bytes accessed | tf_op | source)
XLA Modules:
  0.0 100.3 jit_solution(11832725396845420843)
XLA Ops:
  0.6 2.6 %pick_slots.1 = (bf16[32,1792]{1,0:T(8,128)(2,1)S(1)}, bf16[32,1792]{1,0:T(8,128)(2,1)S(1)}, bf16[32,1792]{1,0:T(8,128)(2,1)S(1)}, bf16[32,1792]{1,0:T(8,128)(2,...) custom-call(s32[1]{0:T(128)} %bitcast.refs_0_, ...), custom_call_target="tpu_custom_call" | custom-call | flops 1024 | bytes 1024 | tf_op jit(solution)/shard_map/pick_slots/pallas_call | solution.py:34
  3.2 0.1 collective-permute-start
  3.3 2.8 %collective-permute-start.1 = (bf16[32,1792]{1,0:T(8,128)(2,1)S(1)}, bf16[32,1792]{1,0:T(8,128)(2,1)S(1)}, u32[]{:S(2)}, u32[]{:S(2)}) collective-permute-start(bf16[32,1792]{1,0:T(8,128)(2,1)S(1)} %get-tuple-element.61), channel_id=1, source_target_pairs={{0,2},{1,3},{2,0},{3,1},{4,6},{5,7},{6,4},{7,5},{8,10},{9,11},{10,... | collective-permute-start | bytes 344072 | tf_op jit(solution)/shard_map/ppermute | solution.py:645
  6.1 2.7 %collective-permute-start.6 = (bf16[32,1792]{1,0:T(8,128)(2,1)S(1)}, bf16[32,1792]{1,0:T(8,128)(2,1)S(1)}, u32[]{:S(2)}, u32[]{:S(2)}) collective-permute-start(bf16[32,1792]{1,0:T(8,128)(2,1)S(1)} %get-tuple-element.66), channel_id=1, source_target_pairs={{0,4},{1,5},{2,6},{3,7},{4,0},{5,1},{6,2},{7,3},{8,12},{9,13},{10,... | collective-permute-start | bytes 344072 | tf_op jit(solution)/shard_map/ppermute | solution.py:645
  8.8 3.2 %load_weight.3.refs_0_.refs_6_.refs_4_.refs_2_ = bf16[4,1792,512]{2,1,0:T(8,128)(2,1)S(1)} custom-call(bf16[32,1792]{1,0:T(8,128)(2,1)S(1)} %get-tuple-element.59.refs_0_.refs_1_, s32[1]{0:T(128)} %bitcast.2.refs_1_, bf16[7168,512]{1,0:T(8,128)(2,1)} %bitcast.9), custom_call_target="tpu_custom_call" | custom-call | flops 1024 | bytes 1024 | tf_op jit(solution)/shard_map/load_weight/pallas_call | solution.py:34
  12.0 1.1 %collective-permute-start.7 = (bf16[32,1792]{1,0:T(8,128)(2,1)S(1)}, bf16[32,1792]{1,0:T(8,128)(2,1)S(1)}, u32[]{:S(2)}, u32[]{:S(2)}) collective-permute-start(bf16[32,1792]{1,0:T(8,128)(2,1)S(1)} %get-tuple-element.67), channel_id=1, source_target_pairs={{0,6},{1,7},{2,4},{3,5},{4,2},{5,3},{6,0},{7,1},{8,14},{9,15},{10,... | collective-permute-start | bytes 344072 | tf_op jit(solution)/shard_map/ppermute | solution.py:645
  13.2 1.3 %collective-permute-done.2 = bf16[32,1792]{1,0:T(8,128)(2,1)S(1)} collective-permute-done((bf16[32,1792]{1,0:T(8,128)(2,1)S(1)}, bf16[32,1792]{1,0:T(8,128)(2,1)S(1)}, u32[]{:S(2)}, u32[]{:S(2)}) %collective-permute-start.2) | collective-permute-done | bytes 114720 | tf_op jit(solution)/shard_map/ppermute | solution.py:645
  14.5 1.4 %collective-permute-start.3 = (bf16[128,1792]{1,0:T(8,128)(2,1)S(1)}, bf16[128,1792]{1,0:T(8,128)(2,1)S(1)}, u32[]{:S(2)}, u32[]{:S(2)}) collective-permute-start(bf16[128,1792]{1,0:T(8,128)(2,1)S(1)} %pad_maximum_fusion.refs_0_.refs_1_.refs_3_.refs_4_), channel_id=1, source_target_pairs={{0,8},{8,0},{16,24},{24,16},{1,9},{9,1},{17,25},{25,17},{2,10},{10... | collective-permute-start | bytes 1376264 | tf_op jit(solution)/shard_map/ppermute | solution.py:645
  15.9 1.2 %collective-permute-start.5 = (bf16[128,1792]{1,0:T(8,128)(2,1)S(1)}, bf16[128,1792]{1,0:T(8,128)(2,1)S(1)}, u32[]{:S(2)}, u32[]{:S(2)}) collective-permute-start(bf16[128,1792]{1,0:T(8,128)(2,1)S(1)} %pad_maximum_fusion.refs_0_.refs_1_.refs_3_.refs_4_), channel_id=1, source_target_pairs={{0,16},{8,24},{16,0},{24,8},{1,17},{9,25},{17,1},{25,9},{2,18},{10... | collective-permute-start | bytes 1376264 | tf_op jit(solution)/shard_map/ppermute | solution.py:645
  17.2 1.7 %collective-permute-done.7.refs_4_ = bf16[32,1792]{1,0:T(8,128)(2,1)S(1)} collective-permute-done((bf16[32,1792]{1,0:T(8,128)(2,1)S(1)}, bf16[32,1792]{1,0:T(8,128)(2,1)S(1)}, u32[]{:S(2)}, u32[]{:S(2)}) %collective-permute-start.7) | collective-permute-done | bytes 114720 | tf_op jit(solution)/shard_map/ppermute | solution.py:645
  18.9 1.1 %collective-permute-start.8 = (bf16[96,1792]{1,0:T(8,128)(2,1)S(1)}, bf16[96,1792]{1,0:T(8,128)(2,1)S(1)}, u32[]{:S(2)}, u32[]{:S(2)}) collective-permute-start(bf16[96,1792]{1,0:T(8,128)(2,1)S(1)} %pad_maximum_fusion.2), channel_id=1, source_target_pairs={{0,1},{1,0},{2,3},{3,2},{4,5},{5,4},{6,7},{7,6},{8,9},{9,8},{10,11... | collective-permute-start | bytes 1032200 | tf_op jit(solution)/shard_map/ppermute | solution.py:645
  20.0 3.0 %collective-permute-start.12 = (bf16[32,1792]{1,0:T(8,128)(2,1)S(1)}, bf16[32,1792]{1,0:T(8,128)(2,1)S(1)}, u32[]{:S(2)}, u32[]{:S(2)}) collective-permute-start(bf16[32,1792]{1,0:T(8,128)(2,1)S(1)} %get-tuple-element.71), channel_id=1, source_target_pairs={{0,4},{1,5},{2,6},{3,7},{4,0},{5,1},{6,2},{7,3},{8,12},{9,13},{10,... | collective-permute-start | bytes 344072 | tf_op jit(solution)/shard_map/ppermute | solution.py:645
  22.9 1.8 %collective-permute-start.13 = (bf16[32,1792]{1,0:T(8,128)(2,1)S(1)}, bf16[32,1792]{1,0:T(8,128)(2,1)S(1)}, u32[]{:S(2)}, u32[]{:S(2)}) collective-permute-start(bf16[32,1792]{1,0:T(8,128)(2,1)S(1)} %get-tuple-element.72), channel_id=1, source_target_pairs={{0,6},{1,7},{2,4},{3,5},{4,2},{5,3},{6,0},{7,1},{8,14},{9,15},{10,... | collective-permute-start | bytes 344072 | tf_op jit(solution)/shard_map/ppermute | solution.py:645
  24.7 3.2 %load_weight.4.refs_0_.refs_2_.refs_7_.refs_5_.refs_3_ = bf16[4,1792,512]{2,1,0:T(8,128)(2,1)S(1)} custom-call(bf16[128,1792]{1,0:T(8,128)(2,1)S(1)} %pad_maximum_fusion.refs_0_.refs_1_.refs_3_.refs_4_, s32[1]{0:T(128)} %bitcast.2.refs_1_, bf16[7168,512]{1,0:T(8,128)(2,1)} %bitcast.10), custom_call_target="tpu_custom_call" | custom-call | flops 1024 | bytes 1024 | tf_op jit(solution)/shard_map/load_weight/pallas_call | solution.py:34
  27.9 1.3 %collective-permute-start.10 = (bf16[64,1792]{1,0:T(8,128)(2,1)S(1)}, bf16[64,1792]{1,0:T(8,128)(2,1)S(1)}, u32[]{:S(2)}, u32[]{:S(2)}) collective-permute-start(bf16[64,1792]{1,0:T(8,128)(2,1)S(1)} %arrange.12.refs_1_.refs_5_), channel_id=1, source_target_pairs={{0,16},{8,24},{16,0},{24,8},{1,17},{9,25},{17,1},{25,9},{2,18},{10... | collective-permute-start | bytes 688136 | tf_op jit(solution)/shard_map/ppermute | solution.py:645
  29.3 1.2 %collective-permute-start.9 = (bf16[64,1792]{1,0:T(8,128)(2,1)S(1)}, bf16[64,1792]{1,0:T(8,128)(2,1)S(1)}, u32[]{:S(2)}, u32[]{:S(2)}) collective-permute-start(bf16[64,1792]{1,0:T(8,128)(2,1)S(1)} %arrange.12.refs_1_.refs_5_), channel_id=1, source_target_pairs={{0,8},{8,0},{16,24},{24,16},{1,9},{9,1},{17,25},{25,17},{2,10},{10... | collective-permute-start | bytes 688136 | tf_op jit(solution)/shard_map/ppermute | solution.py:645
  30.5 0.8 collective-permute-done.12.refs_0_
  31.3 1.0 collective-permute-start.14
  32.3 1.3 %collective-permute-start.4 = (bf16[64,1792]{1,0:T(8,128)(2,1)S(1)}, bf16[64,1792]{1,0:T(8,128)(2,1)S(1)}, u32[]{:S(2)}, u32[]{:S(2)}) collective-permute-start(bf16[64,1792]{1,0:T(8,128)(2,1)S(1)} %arrange.11), channel_id=1, source_target_pairs={{0,16},{8,24},{16,0},{24,8},{1,17},{9,25},{17,1},{25,9},{2,18},{10... | collective-permute-start | bytes 688136 | tf_op jit(solution)/shard_map/ppermute | solution.py:645
  33.6 0.6 collective-permute-done.10.refs_1_.refs_5_.refs_9_
  34.2 0.9 collective-permute-done.9.refs_0_.refs_3_.refs_7_
  35.2 1.6 %collective-permute-start.11 = (bf16[64,1792]{1,0:T(8,128)(2,1)S(1)}, bf16[64,1792]{1,0:T(8,128)(2,1)S(1)}, u32[]{:S(2)}, u32[]{:S(2)}) collective-permute-start(bf16[64,1792]{1,0:T(8,128)(2,1)S(1)} %arrange.13), channel_id=1, source_target_pairs={{0,8},{8,0},{16,24},{24,16},{1,9},{9,1},{17,25},{25,17},{2,10},{10... | collective-permute-start | bytes 688136 | tf_op jit(solution)/shard_map/ppermute | solution.py:645
  36.9 0.4 collective-permute-start.16
  37.3 3.2 %load_weight.5.refs_0_.refs_6_.refs_7_.refs_8_ = bf16[4,512,1792]{2,1,0:T(8,128)(2,1)S(1)} custom-call(bf16[4,1792,512]{2,1,0:T(8,128)(2,1)S(1)} %load_weight.4.refs_0_.refs_2_.refs_7_.refs_5_.refs_3_, s32[1]{0:T(128)} %bitcast.2.refs_1_, bf16[512,7168]{1,0:T(8,128)(2,1)} %bitcast.11), custom_call_target="tpu_custom_call" | custom-call | flops 1024 | bytes 1024 | tf_op jit(solution)/shard_map/load_weight/pallas_call | solution.py:34
  40.5 1.6 %partial_products.2 = (f32[128,512]{1,0:T(8,128)S(1)}, f32[128,512]{1,0:T(8,128)S(1)}) custom-call(bf16[128,1792]{1,0:T(8,128)(2,1)S(1)} %pad_maximum_fusion.refs_0_.refs_1_.refs_3_.refs_4_, bf16[64,1792]{1,0:T(8,128)(2,1)S(1)} %arrange.12.refs_1_.refs_5_, bf16[128,1792]{1,0:T(8,128)(2,1)S(1)} %collective-permute-done.3.refs_0_.refs_2_.refs_3_.refs_5_.refs_6_, ...), custom_call_target="tpu_custom_call" | custom-call | flops 1024 | bytes 1024 | tf_op jit(solution)/shard_map/partial_products/pallas_call | solution.py:34
  42.1 1.8 %forward_terms.1 = (bf16[128,512]{1,0:T(8,128)(2,1)S(1)}, f32[128,512]{1,0:T(8,128)S(1)}, f32[128,512]{1,0:T(8,128)S(1)}, bf16[64,1792]{1,0:T(8,128)(2,1)S(1)}, ...) custom-call(bf16[64,1792]{1,0:T(8,128)(2,1)S(1)} %collective-permute, ...), custom_call_target="tpu_custom_call" | custom-call | flops 1024 | bytes 1024 | tf_op jit(solution)/shard_map/forward_terms/pallas_call | solution.py:34
  43.9 1.2 %collective-permute-start.17 = (bf16[64,1792]{1,0:T(8,128)(2,1)S(1)}, bf16[64,1792]{1,0:T(8,128)(2,1)S(1)}, u32[]{:S(2)}, u32[]{:S(2)}) collective-permute-start(bf16[64,1792]{1,0:T(8,128)(2,1)S(1)} %get-tuple-element.78), channel_id=1, source_target_pairs={{0,16},{8,24},{16,0},{24,8},{1,17},{9,25},{17,1},{25,9},{2,18},{10... | collective-permute-start | bytes 688136 | tf_op jit(solution)/shard_map/ppermute | solution.py:645
  45.1 1.4 %collective-permute-start.18 = (bf16[64,1792]{1,0:T(8,128)(2,1)S(1)}, bf16[64,1792]{1,0:T(8,128)(2,1)S(1)}, u32[]{:S(2)}, u32[]{:S(2)}) collective-permute-start(bf16[64,1792]{1,0:T(8,128)(2,1)S(1)} %get-tuple-element.79), channel_id=1, source_target_pairs={{0,8},{8,0},{16,24},{24,16},{1,9},{9,1},{17,25},{25,17},{2,10},{10... | collective-permute-start | bytes 688136 | tf_op jit(solution)/shard_map/ppermute | solution.py:645
  46.5 0.2 collective-permute-start.19
  46.7 0.4 collective-permute-start.20
  47.0 1.9 %partial_products.3.refs_0_.refs_3_ = f32[128,512]{1,0:T(8,128)S(1)} custom-call(bf16[128,512]{1,0:T(8,128)(2,1)S(1)} %get-tuple-element.70.refs_0_.refs_2_, bf16[128,1792]{1,0:T(8,128)(2,1)S(1)} %pad_maximum_fusion.refs_0_.refs_1_.refs_3_.refs_4_, bf16[64,1792]{1,0:T(8,128)(2,1)S(1)} %arrange.15.refs_2_.refs_4_, ...), custom_call_target="tpu_custom_call" | custom-call | flops 1024 | bytes 1024 | tf_op jit(solution)/shard_map/partial_products/pallas_call | solution.py:34
  48.9 3.1 %down_grads.2 = (bf16[512,7168]{1,0:T(8,128)(2,1)}, f32[8,128]{1,0:T(8,128)S(1)}) custom-call(f32[128,512]{1,0:T(8,128)S(1)} %partial_products.3.refs_0_.refs_3_, s32[1]{0:T(128)} %bitcast.2.refs_1_, bf16[128,512]{1,0:T(8,128)(2,1)S(1)} %get-tuple-element.70.refs_0_.refs_2_, bf16[128,1792]{1,0:T(8,128)(2,1)S(1)} %pad_maximum_fusion.refs_0_.refs_1_.refs_3_.refs_4_, ...), custom_call_target="tpu_custom_call" | custom-call | flops 1024 | bytes 1024 | tf_op jit(solution)/shard_map/down_grads/pallas_call | solution.py:34
  52.1 0.1 merge.1
  52.2 1.5 %collective-permute-start.21 = (bf16[128,1792]{1,0:T(8,128)(2,1)S(1)}, bf16[128,1792]{1,0:T(8,128)(2,1)S(1)}, u32[]{:S(2)}, u32[]{:S(2)}) collective-permute-start(bf16[128,1792]{1,0:T(8,128)(2,1)S(1)} %get-tuple-element.80.refs_0_), channel_id=1, source_target_pairs={{0,8},{8,0},{16,24},{24,16},{1,9},{9,1},{17,25},{25,17},{2,10},{10... | collective-permute-start | bytes 1376264 | tf_op jit(solution)/shard_map/ppermute | solution.py:645
  53.6 1.1 %collective-permute-start.22 = (bf16[128,1792]{1,0:T(8,128)(2,1)S(1)}, bf16[128,1792]{1,0:T(8,128)(2,1)S(1)}, u32[]{:S(2)}, u32[]{:S(2)}) collective-permute-start(bf16[128,1792]{1,0:T(8,128)(2,1)S(1)} %get-tuple-element.88), channel_id=1, source_target_pairs={{0,16},{8,24},{16,0},{24,8},{1,17},{9,25},{17,1},{25,9},{2,18},{10... | collective-permute-start | bytes 1376264 | tf_op jit(solution)/shard_map/ppermute | solution.py:645
  54.8 2.0 %backward_terms.1 = (bf16[128,512]{1,0:T(8,128)(2,1)S(1)}, bf16[128,512]{1,0:T(8,128)(2,1)S(1)}, bf16[64,1792]{1,0:T(8,128)(2,1)S(1)}, bf16[64,1792]{1,0:T(8,128)(2,1)S(1)}) custom-call(bf16[128,1792]{1,0:T(8,128)(2,1)S(1)} %get-tuple-element.80.refs_0_, bf16[64,1792]{1,0:T(8,128)(2,1)S(1)} %collective-permute-done.19.refs_1_.refs_4_, ...), custom_call_target="tpu_custom_call" | custom-call | flops 1024 | bytes 1024 | tf_op jit(solution)/shard_map/backward_terms/pallas_call | solution.py:34
  56.7 0.8 collective-permute-start.28
  57.6 3.6 %backward_rest.1 = (bf16[64,1792]{1,0:T(8,128)(2,1)S(1)}, bf16[64,1792]{1,0:T(8,128)(2,1)S(1)}, bf16[64,1792]{1,0:T(8,128)(2,1)S(1)}, bf16[64,1792]{1,0:T(8,128)...) custom-call(bf16[128,512]{1,0:T(8,128)(2,1)S(1)} %get-tuple-element.83.refs_0_.refs_2_, ...), custom_call_target="tpu_custom_call" | custom-call | flops 1024 | bytes 1024 | tf_op jit(solution)/shard_map/backward_rest/pallas_call | solution.py:34
  61.2 3.6 %collective-permute-done.21.refs_2_ = bf16[128,1792]{1,0:T(8,128)(2,1)S(1)} collective-permute-done((bf16[128,1792]{1,0:T(8,128)(2,1)S(1)}, bf16[128,1792]{1,0:T(8,128)(2,1)S(1)}, u32[]{:S(2)}, u32[]{:S(2)}) %collective-permute-start.21) | collective-permute-done | bytes 458784 | tf_op jit(solution)/shard_map/ppermute | solution.py:645
  64.9 0.2 add_up.3
  65.0 1.8 %collective-permute-start.23 = (bf16[32,1792]{1,0:T(8,128)(2,1)S(1)}, bf16[32,1792]{1,0:T(8,128)(2,1)S(1)}, u32[]{:S(2)}, u32[]{:S(2)}) collective-permute-start(bf16[32,1792]{1,0:T(8,128)(2,1)S(1)} %get-tuple-element.90), channel_id=1, source_target_pairs={{0,2},{1,3},{2,0},{3,1},{4,6},{5,7},{6,4},{7,5},{8,10},{9,11},{10,... | collective-permute-start | bytes 344072 | tf_op jit(solution)/shard_map/ppermute | solution.py:645
  66.8 1.9 %collective-permute-start.24 = (bf16[32,1792]{1,0:T(8,128)(2,1)S(1)}, bf16[32,1792]{1,0:T(8,128)(2,1)S(1)}, u32[]{:S(2)}, u32[]{:S(2)}) collective-permute-start(bf16[32,1792]{1,0:T(8,128)(2,1)S(1)} %get-tuple-element.91), channel_id=1, source_target_pairs={{0,4},{1,5},{2,6},{3,7},{4,0},{5,1},{6,2},{7,3},{8,12},{9,13},{10,... | collective-permute-start | bytes 344072 | tf_op jit(solution)/shard_map/ppermute | solution.py:645
  68.7 0.3 collective-permute-start.25
  68.9 0.8 collective-permute-done.28.refs_2_
  69.8 1.4 %collective-permute-start.27 = (bf16[64,1792]{1,0:T(8,128)(2,1)S(1)}, bf16[64,1792]{1,0:T(8,128)(2,1)S(1)}, u32[]{:S(2)}, u32[]{:S(2)}) collective-permute-start(bf16[64,1792]{1,0:T(8,128)(2,1)S(1)} %get-tuple-element.95), channel_id=1, source_target_pairs={{0,8},{8,0},{16,24},{24,16},{1,9},{9,1},{17,25},{25,17},{2,10},{10... | collective-permute-start | bytes 688136 | tf_op jit(solution)/shard_map/ppermute | solution.py:645
  71.2 0.1 add_pairs.1
  71.3 0.5 collective-permute-start.30
  71.8 0.8 collective-permute-done.24.refs_3_
  72.6 1.7 %collective-permute-done.25.refs_4_ = bf16[32,1792]{1,0:T(8,128)(2,1)S(1)} collective-permute-done((bf16[32,1792]{1,0:T(8,128)(2,1)S(1)}, bf16[32,1792]{1,0:T(8,128)(2,1)S(1)}, u32[]{:S(2)}, u32[]{:S(2)}) %collective-permute-start.25) | collective-permute-done | bytes 114720 | tf_op jit(solution)/shard_map/ppermute | solution.py:645
  74.3 7.3 %collective-permute-start.26 = (bf16[64,1792]{1,0:T(8,128)(2,1)S(1)}, bf16[64,1792]{1,0:T(8,128)(2,1)S(1)}, u32[]{:S(2)}, u32[]{:S(2)}) collective-permute-start(bf16[64,1792]{1,0:T(8,128)(2,1)S(1)} %pad_maximum_fusion.3), channel_id=1, source_target_pairs={{0,1},{1,0},{2,3},{3,2},{4,5},{5,4},{6,7},{7,6},{8,9},{9,8},{10,11... | collective-permute-start | bytes 688136 | tf_op jit(solution)/shard_map/ppermute | solution.py:645
  81.6 0.3 collective-permute-start.32
  81.9 0.4 collective-permute-start.31
  82.3 0.4 collective-permute-done.26.refs_5_.refs_0_
  82.8 1.2 %collective-permute-start.34 = (bf16[32,1792]{1,0:T(8,128)(2,1)S(1)}, bf16[32,1792]{1,0:T(8,128)(2,1)S(1)}, u32[]{:S(2)}, u32[]{:S(2)}) collective-permute-start(bf16[32,1792]{1,0:T(8,128)(2,1)S(1)} %get-tuple-element.101.refs_0_), channel_id=1, source_target_pairs={{0,4},{1,5},{2,6},{3,7},{4,0},{5,1},{6,2},{7,3},{8,12},{9,13},{10,... | collective-permute-start | bytes 344072 | tf_op jit(solution)/shard_map/ppermute | solution.py:645
  84.0 1.3 %collective-permute-start.35 = (bf16[32,1792]{1,0:T(8,128)(2,1)S(1)}, bf16[32,1792]{1,0:T(8,128)(2,1)S(1)}, u32[]{:S(2)}, u32[]{:S(2)}) collective-permute-start(bf16[32,1792]{1,0:T(8,128)(2,1)S(1)} %get-tuple-element.108), channel_id=1, source_target_pairs={{0,6},{1,7},{2,4},{3,5},{4,2},{5,3},{6,0},{7,1},{8,14},{9,15},{10,... | collective-permute-start | bytes 344072 | tf_op jit(solution)/shard_map/ppermute | solution.py:645
  85.3 1.9 %down_grads.3 = (bf16[512,7168]{1,0:T(8,128)(2,1)}, f32[8,128]{1,0:T(8,128)S(1)}) custom-call(bf16[32,1792]{1,0:T(8,128)(2,1)S(1)} %get-tuple-element.101.refs_0_, s32[1]{0:T(128)} %bitcast.2.refs_1_, bf16[128,512]{1,0:T(8,128)(2,1)S(1)} %get-tuple-element.70.refs_0_.refs_2_, ...), custom_call_target="tpu_custom_call", output_to_operand_aliasing={{0}: (3, {})} | custom-call | flops 1024 | bytes 1024 | tf_op jit(solution)/shard_map/down_grads/pallas_call | solution.py:34
  87.2 1.6 %collective-permute-done.32.refs_3_ = bf16[64,1792]{1,0:T(8,128)(2,1)S(1)} collective-permute-done((bf16[64,1792]{1,0:T(8,128)(2,1)S(1)}, bf16[64,1792]{1,0:T(8,128)(2,1)S(1)}, u32[]{:S(2)}, u32[]{:S(2)}) %collective-permute-start.32) | collective-permute-done | bytes 229408 | tf_op jit(solution)/shard_map/ppermute | solution.py:645
  88.8 0.1 add_up.5
  89.0 6.0 %weight_grads.1 = (bf16[7168,512]{1,0:T(8,128)(2,1)}, bf16[7168,512]{1,0:T(8,128)(2,1)}, f32[8,128]{1,0:T(8,128)S(1)}) custom-call(bf16[32,1792]{1,0:T(8,128)(2,1)S(1)} %get-tuple-element.106.refs_0_.refs_1_, s32[1]{0:T(128)} %bitcast.2.refs_1_, bf16[128,512]{1,0:T(8,128)(2,1)S(1)} %get-tuple-element.83.refs_0_.refs_2_, ...), custom_call_target="tpu_custom_call" | custom-call | flops 1024 | bytes 1024 | tf_op jit(solution)/shard_map/weight_grads/pallas_call | solution.py:34
  95.0 1.2 %collective-permute-start.36 = (bf16[64,1792]{1,0:T(8,128)(2,1)S(1)}, bf16[64,1792]{1,0:T(8,128)(2,1)S(1)}, u32[]{:S(2)}, u32[]{:S(2)}) collective-permute-start(bf16[64,1792]{1,0:T(8,128)(2,1)S(1)} %arrange.18), channel_id=1, source_target_pairs={{0,1},{1,0},{2,3},{3,2},{4,5},{5,4},{6,7},{7,6},{8,9},{9,8},{10,11... | collective-permute-start | bytes 688136 | tf_op jit(solution)/shard_map/ppermute | solution.py:645
  96.2 0.5 collective-permute-start.37
  96.8 0.2 spread_matrices.1
  97.0 1.6 %spread_rows.2 = bf16[512,1792]{1,0:T(8,128)(2,1)} custom-call(bf16[512,256]{1,0:T(8,128)(2,1)S(1)} %get-tuple-element.65.refs_0_, bf16[32,1792]{1,0:T(8,128)(2,1)S(1)} %get-tuple-element.89.refs_1_.refs_0_, bf16[32,1792]{1,0:T(8,128)(2,1)S(1)} %collective-permute-done.23.refs_2_, bf16[32,1792]{1,0:T(8,128)(2,1)S(1)} %collective-permute-done.24.refs_3_, ...), custom_call_target="tpu_custom_call" | custom-call | flops 1024 | bytes 1024 | tf_op jit(solution)/shard_map/spread_rows/pallas_call | solution.py:34
  98.6 1.5 %spread_rows.3 = bf16[512,1792]{1,0:T(8,128)(2,1)} custom-call(bf16[512,128]{1,0:T(8,128)(2,1)S(1)} %get-tuple-element.93.refs_0_, bf16[32,1792]{1,0:T(8,128)(2,1)S(1)} %get-tuple-element.106.refs_0_.refs_1_, bf16[32,1792]{1,0:T(8,128)(2,1)S(1)} %collective-permute-done.33.refs_2_, bf16[32,1792]{1,0:T(8,128)(2,1)S(1)} %collective-permute-done.34.refs_1_.refs_3_, ...), custom_call_target="tpu_custom_call" | custom-call | flops 1024 | bytes 1024 | tf_op jit(solution)/shard_map/spread_rows/pallas_call | solution.py:34
  (52 shorter events, 0.6 us)
Async XLA Ops:
  3.2 9.9 %collective-permute-start = (bf16[32,1792]{1,0:T(8,128)(2,1)S(1)}, bf16[32,1792]{1,0:T(8,128)(2,1)S(1)}, u32[]{:S(2)}, u32[]{:S(2)}) collective-permute-start(bf16[32,1792]{1,0:T(8,128)(2,1)S(1)} %get-tuple-element.60), channel_id=1, source_target_pairs={{0,1},{1,0},{2,3},{3,2},{4,5},{5,4},{6,7},{7,6},{8,9},{9,8},{10,11... | collective-permute-start | bytes 344072 | tf_op jit(solution)/shard_map/ppermute | solution.py:645
  3.3 9.8 %collective-permute-start.1 = (bf16[32,1792]{1,0:T(8,128)(2,1)S(1)}, bf16[32,1792]{1,0:T(8,128)(2,1)S(1)}, u32[]{:S(2)}, u32[]{:S(2)}) collective-permute-start(bf16[32,1792]{1,0:T(8,128)(2,1)S(1)} %get-tuple-element.61), channel_id=1, source_target_pairs={{0,2},{1,3},{2,0},{3,1},{4,6},{5,7},{6,4},{7,5},{8,10},{9,11},{10,... | collective-permute-start | bytes 344072 | tf_op jit(solution)/shard_map/ppermute | solution.py:645
  6.1 8.3 %collective-permute-start.2 = (bf16[32,1792]{1,0:T(8,128)(2,1)S(1)}, bf16[32,1792]{1,0:T(8,128)(2,1)S(1)}, u32[]{:S(2)}, u32[]{:S(2)}) collective-permute-start(bf16[32,1792]{1,0:T(8,128)(2,1)S(1)} %get-tuple-element.62), channel_id=1, source_target_pairs={{0,3},{1,2},{2,1},{3,0},{4,7},{5,6},{6,5},{7,4},{8,11},{9,10},{10,... | collective-permute-start | bytes 344072 | tf_op jit(solution)/shard_map/ppermute | solution.py:645
  6.1 11.0 %collective-permute-start.6 = (bf16[32,1792]{1,0:T(8,128)(2,1)S(1)}, bf16[32,1792]{1,0:T(8,128)(2,1)S(1)}, u32[]{:S(2)}, u32[]{:S(2)}) collective-permute-start(bf16[32,1792]{1,0:T(8,128)(2,1)S(1)} %get-tuple-element.66), channel_id=1, source_target_pairs={{0,4},{1,5},{2,6},{3,7},{4,0},{5,1},{6,2},{7,3},{8,12},{9,13},{10,... | collective-permute-start | bytes 344072 | tf_op jit(solution)/shard_map/ppermute | solution.py:645
  12.0 6.9 %collective-permute-start.7 = (bf16[32,1792]{1,0:T(8,128)(2,1)S(1)}, bf16[32,1792]{1,0:T(8,128)(2,1)S(1)}, u32[]{:S(2)}, u32[]{:S(2)}) collective-permute-start(bf16[32,1792]{1,0:T(8,128)(2,1)S(1)} %get-tuple-element.67), channel_id=1, source_target_pairs={{0,6},{1,7},{2,4},{3,5},{4,2},{5,3},{6,0},{7,1},{8,14},{9,15},{10,... | collective-permute-start | bytes 344072 | tf_op jit(solution)/shard_map/ppermute | solution.py:645
  14.5 13.4 %collective-permute-start.3 = (bf16[128,1792]{1,0:T(8,128)(2,1)S(1)}, bf16[128,1792]{1,0:T(8,128)(2,1)S(1)}, u32[]{:S(2)}, u32[]{:S(2)}) collective-permute-start(bf16[128,1792]{1,0:T(8,128)(2,1)S(1)} %pad_maximum_fusion.refs_0_.refs_1_.refs_3_.refs_4_), channel_id=1, source_target_pairs={{0,8},{8,0},{16,24},{24,16},{1,9},{9,1},{17,25},{25,17},{2,10},{10... | collective-permute-start | bytes 1376264 | tf_op jit(solution)/shard_map/ppermute | solution.py:645
  15.9 12.0 %collective-permute-start.5 = (bf16[128,1792]{1,0:T(8,128)(2,1)S(1)}, bf16[128,1792]{1,0:T(8,128)(2,1)S(1)}, u32[]{:S(2)}, u32[]{:S(2)}) collective-permute-start(bf16[128,1792]{1,0:T(8,128)(2,1)S(1)} %pad_maximum_fusion.refs_0_.refs_1_.refs_3_.refs_4_), channel_id=1, source_target_pairs={{0,16},{8,24},{16,0},{24,8},{1,17},{9,25},{17,1},{25,9},{2,18},{10... | collective-permute-start | bytes 1376264 | tf_op jit(solution)/shard_map/ppermute | solution.py:645
  18.9 9.0 %collective-permute-start.8 = (bf16[96,1792]{1,0:T(8,128)(2,1)S(1)}, bf16[96,1792]{1,0:T(8,128)(2,1)S(1)}, u32[]{:S(2)}, u32[]{:S(2)}) collective-permute-start(bf16[96,1792]{1,0:T(8,128)(2,1)S(1)} %pad_maximum_fusion.2), channel_id=1, source_target_pairs={{0,1},{1,0},{2,3},{3,2},{4,5},{5,4},{6,7},{7,6},{8,9},{9,8},{10,11... | collective-permute-start | bytes 1032200 | tf_op jit(solution)/shard_map/ppermute | solution.py:645
  20.0 11.3 %collective-permute-start.12 = (bf16[32,1792]{1,0:T(8,128)(2,1)S(1)}, bf16[32,1792]{1,0:T(8,128)(2,1)S(1)}, u32[]{:S(2)}, u32[]{:S(2)}) collective-permute-start(bf16[32,1792]{1,0:T(8,128)(2,1)S(1)} %get-tuple-element.71), channel_id=1, source_target_pairs={{0,4},{1,5},{2,6},{3,7},{4,0},{5,1},{6,2},{7,3},{8,12},{9,13},{10,... | collective-permute-start | bytes 344072 | tf_op jit(solution)/shard_map/ppermute | solution.py:645
  22.9 8.3 %collective-permute-start.13 = (bf16[32,1792]{1,0:T(8,128)(2,1)S(1)}, bf16[32,1792]{1,0:T(8,128)(2,1)S(1)}, u32[]{:S(2)}, u32[]{:S(2)}) collective-permute-start(bf16[32,1792]{1,0:T(8,128)(2,1)S(1)} %get-tuple-element.72), channel_id=1, source_target_pairs={{0,6},{1,7},{2,4},{3,5},{4,2},{5,3},{6,0},{7,1},{8,14},{9,15},{10,... | collective-permute-start | bytes 344072 | tf_op jit(solution)/shard_map/ppermute | solution.py:645
  27.9 6.3 %collective-permute-start.10 = (bf16[64,1792]{1,0:T(8,128)(2,1)S(1)}, bf16[64,1792]{1,0:T(8,128)(2,1)S(1)}, u32[]{:S(2)}, u32[]{:S(2)}) collective-permute-start(bf16[64,1792]{1,0:T(8,128)(2,1)S(1)} %arrange.12.refs_1_.refs_5_), channel_id=1, source_target_pairs={{0,16},{8,24},{16,0},{24,8},{1,17},{9,25},{17,1},{25,9},{2,18},{10... | collective-permute-start | bytes 688136 | tf_op jit(solution)/shard_map/ppermute | solution.py:645
  29.3 5.9 %collective-permute-start.9 = (bf16[64,1792]{1,0:T(8,128)(2,1)S(1)}, bf16[64,1792]{1,0:T(8,128)(2,1)S(1)}, u32[]{:S(2)}, u32[]{:S(2)}) collective-permute-start(bf16[64,1792]{1,0:T(8,128)(2,1)S(1)} %arrange.12.refs_1_.refs_5_), channel_id=1, source_target_pairs={{0,8},{8,0},{16,24},{24,16},{1,9},{9,1},{17,25},{25,17},{2,10},{10... | collective-permute-start | bytes 688136 | tf_op jit(solution)/shard_map/ppermute | solution.py:645
  31.3 5.5 %collective-permute-start.14 = (bf16[96,1792]{1,0:T(8,128)(2,1)S(1)}, bf16[96,1792]{1,0:T(8,128)(2,1)S(1)}, u32[]{:S(2)}, u32[]{:S(2)}) collective-permute-start(bf16[96,1792]{1,0:T(8,128)(2,1)S(1)} %arrange.14), channel_id=1, source_target_pairs={{0,1},{1,0},{2,3},{3,2},{4,5},{5,4},{6,7},{7,6},{8,9},{9,8},{10,11... | collective-permute-start | bytes 1032200 | tf_op jit(solution)/shard_map/ppermute | solution.py:645
  32.3 9.8 %collective-permute-start.4 = (bf16[64,1792]{1,0:T(8,128)(2,1)S(1)}, bf16[64,1792]{1,0:T(8,128)(2,1)S(1)}, u32[]{:S(2)}, u32[]{:S(2)}) collective-permute-start(bf16[64,1792]{1,0:T(8,128)(2,1)S(1)} %arrange.11), channel_id=1, source_target_pairs={{0,16},{8,24},{16,0},{24,8},{1,17},{9,25},{17,1},{25,9},{2,18},{10... | collective-permute-start | bytes 688136 | tf_op jit(solution)/shard_map/ppermute | solution.py:645
  35.2 6.9 %collective-permute-start.11 = (bf16[64,1792]{1,0:T(8,128)(2,1)S(1)}, bf16[64,1792]{1,0:T(8,128)(2,1)S(1)}, u32[]{:S(2)}, u32[]{:S(2)}) collective-permute-start(bf16[64,1792]{1,0:T(8,128)(2,1)S(1)} %arrange.13), channel_id=1, source_target_pairs={{0,8},{8,0},{16,24},{24,16},{1,9},{9,1},{17,25},{25,17},{2,10},{10... | collective-permute-start | bytes 688136 | tf_op jit(solution)/shard_map/ppermute | solution.py:645
  36.8 9.8 %collective-permute-start.15 = (bf16[64,1792]{1,0:T(8,128)(2,1)S(1)}, bf16[64,1792]{1,0:T(8,128)(2,1)S(1)}, u32[]{:S(2)}, u32[]{:S(2)}) collective-permute-start(bf16[64,1792]{1,0:T(8,128)(2,1)S(1)} %arrange.15.refs_2_.refs_4_), channel_id=1, source_target_pairs={{0,8},{8,0},{16,24},{24,16},{1,9},{9,1},{17,25},{25,17},{2,10},{10... | collective-permute-start | bytes 688136 | tf_op jit(solution)/shard_map/ppermute | solution.py:645
  36.9 9.7 %collective-permute-start.16 = (bf16[64,1792]{1,0:T(8,128)(2,1)S(1)}, bf16[64,1792]{1,0:T(8,128)(2,1)S(1)}, u32[]{:S(2)}, u32[]{:S(2)}) collective-permute-start(bf16[64,1792]{1,0:T(8,128)(2,1)S(1)} %arrange.15.refs_2_.refs_4_), channel_id=1, source_target_pairs={{0,16},{8,24},{16,0},{24,8},{1,17},{9,25},{17,1},{25,9},{2,18},{10... | collective-permute-start | bytes 688136 | tf_op jit(solution)/shard_map/ppermute | solution.py:645
  43.9 8.2 %collective-permute-start.17 = (bf16[64,1792]{1,0:T(8,128)(2,1)S(1)}, bf16[64,1792]{1,0:T(8,128)(2,1)S(1)}, u32[]{:S(2)}, u32[]{:S(2)}) collective-permute-start(bf16[64,1792]{1,0:T(8,128)(2,1)S(1)} %get-tuple-element.78), channel_id=1, source_target_pairs={{0,16},{8,24},{16,0},{24,8},{1,17},{9,25},{17,1},{25,9},{2,18},{10... | collective-permute-start | bytes 688136 | tf_op jit(solution)/shard_map/ppermute | solution.py:645
  45.1 7.0 %collective-permute-start.18 = (bf16[64,1792]{1,0:T(8,128)(2,1)S(1)}, bf16[64,1792]{1,0:T(8,128)(2,1)S(1)}, u32[]{:S(2)}, u32[]{:S(2)}) collective-permute-start(bf16[64,1792]{1,0:T(8,128)(2,1)S(1)} %get-tuple-element.79), channel_id=1, source_target_pairs={{0,8},{8,0},{16,24},{24,16},{1,9},{9,1},{17,25},{25,17},{2,10},{10... | collective-permute-start | bytes 688136 | tf_op jit(solution)/shard_map/ppermute | solution.py:645
  46.5 8.3 %collective-permute-start.19 = (bf16[64,1792]{1,0:T(8,128)(2,1)S(1)}, bf16[64,1792]{1,0:T(8,128)(2,1)S(1)}, u32[]{:S(2)}, u32[]{:S(2)}) collective-permute-start(bf16[64,1792]{1,0:T(8,128)(2,1)S(1)} %arrange.16), channel_id=1, source_target_pairs={{0,8},{8,0},{16,24},{24,16},{1,9},{9,1},{17,25},{25,17},{2,10},{10... | collective-permute-start | bytes 688136 | tf_op jit(solution)/shard_map/ppermute | solution.py:645
  46.7 8.1 %collective-permute-start.20 = (bf16[64,1792]{1,0:T(8,128)(2,1)S(1)}, bf16[64,1792]{1,0:T(8,128)(2,1)S(1)}, u32[]{:S(2)}, u32[]{:S(2)}) collective-permute-start(bf16[64,1792]{1,0:T(8,128)(2,1)S(1)} %arrange.17), channel_id=1, source_target_pairs={{0,16},{8,24},{16,0},{24,8},{1,17},{9,25},{17,1},{25,9},{2,18},{10... | collective-permute-start | bytes 688136 | tf_op jit(solution)/shard_map/ppermute | solution.py:645
  52.2 12.7 %collective-permute-start.21 = (bf16[128,1792]{1,0:T(8,128)(2,1)S(1)}, bf16[128,1792]{1,0:T(8,128)(2,1)S(1)}, u32[]{:S(2)}, u32[]{:S(2)}) collective-permute-start(bf16[128,1792]{1,0:T(8,128)(2,1)S(1)} %get-tuple-element.80.refs_0_), channel_id=1, source_target_pairs={{0,8},{8,0},{16,24},{24,16},{1,9},{9,1},{17,25},{25,17},{2,10},{10... | collective-permute-start | bytes 1376264 | tf_op jit(solution)/shard_map/ppermute | solution.py:645
  53.6 11.2 %collective-permute-start.22 = (bf16[128,1792]{1,0:T(8,128)(2,1)S(1)}, bf16[128,1792]{1,0:T(8,128)(2,1)S(1)}, u32[]{:S(2)}, u32[]{:S(2)}) collective-permute-start(bf16[128,1792]{1,0:T(8,128)(2,1)S(1)} %get-tuple-element.88), channel_id=1, source_target_pairs={{0,16},{8,24},{16,0},{24,8},{1,17},{9,25},{17,1},{25,9},{2,18},{10... | collective-permute-start | bytes 1376264 | tf_op jit(solution)/shard_map/ppermute | solution.py:645
  56.7 13.0 %collective-permute-start.28 = (bf16[64,1792]{1,0:T(8,128)(2,1)S(1)}, bf16[64,1792]{1,0:T(8,128)(2,1)S(1)}, u32[]{:S(2)}, u32[]{:S(2)}) collective-permute-start(bf16[64,1792]{1,0:T(8,128)(2,1)S(1)} %get-tuple-element.97), channel_id=1, source_target_pairs={{0,8},{8,0},{16,24},{24,16},{1,9},{9,1},{17,25},{25,17},{2,10},{10... | collective-permute-start | bytes 688136 | tf_op jit(solution)/shard_map/ppermute | solution.py:645
  57.5 13.6 %collective-permute-start.29 = (bf16[64,1792]{1,0:T(8,128)(2,1)S(1)}, bf16[64,1792]{1,0:T(8,128)(2,1)S(1)}, u32[]{:S(2)}, u32[]{:S(2)}) collective-permute-start(bf16[64,1792]{1,0:T(8,128)(2,1)S(1)} %get-tuple-element.99), channel_id=1, source_target_pairs={{0,16},{8,24},{16,0},{24,8},{1,17},{9,25},{17,1},{25,9},{2,18},{10... | collective-permute-start | bytes 688136 | tf_op jit(solution)/shard_map/ppermute | solution.py:645
  65.0 6.7 %collective-permute-start.23 = (bf16[32,1792]{1,0:T(8,128)(2,1)S(1)}, bf16[32,1792]{1,0:T(8,128)(2,1)S(1)}, u32[]{:S(2)}, u32[]{:S(2)}) collective-permute-start(bf16[32,1792]{1,0:T(8,128)(2,1)S(1)} %get-tuple-element.90), channel_id=1, source_target_pairs={{0,2},{1,3},{2,0},{3,1},{4,6},{5,7},{6,4},{7,5},{8,10},{9,11},{10,... | collective-permute-start | bytes 344072 | tf_op jit(solution)/shard_map/ppermute | solution.py:645
  66.8 5.8 %collective-permute-start.24 = (bf16[32,1792]{1,0:T(8,128)(2,1)S(1)}, bf16[32,1792]{1,0:T(8,128)(2,1)S(1)}, u32[]{:S(2)}, u32[]{:S(2)}) collective-permute-start(bf16[32,1792]{1,0:T(8,128)(2,1)S(1)} %get-tuple-element.91), channel_id=1, source_target_pairs={{0,4},{1,5},{2,6},{3,7},{4,0},{5,1},{6,2},{7,3},{8,12},{9,13},{10,... | collective-permute-start | bytes 344072 | tf_op jit(solution)/shard_map/ppermute | solution.py:645
  68.7 5.6 %collective-permute-start.25 = (bf16[32,1792]{1,0:T(8,128)(2,1)S(1)}, bf16[32,1792]{1,0:T(8,128)(2,1)S(1)}, u32[]{:S(2)}, u32[]{:S(2)}) collective-permute-start(bf16[32,1792]{1,0:T(8,128)(2,1)S(1)} %get-tuple-element.92), channel_id=1, source_target_pairs={{0,6},{1,7},{2,4},{3,5},{4,2},{5,3},{6,0},{7,1},{8,14},{9,15},{10,... | collective-permute-start | bytes 344072 | tf_op jit(solution)/shard_map/ppermute | solution.py:645
  69.8 12.5 %collective-permute-start.27 = (bf16[64,1792]{1,0:T(8,128)(2,1)S(1)}, bf16[64,1792]{1,0:T(8,128)(2,1)S(1)}, u32[]{:S(2)}, u32[]{:S(2)}) collective-permute-start(bf16[64,1792]{1,0:T(8,128)(2,1)S(1)} %get-tuple-element.95), channel_id=1, source_target_pairs={{0,8},{8,0},{16,24},{24,16},{1,9},{9,1},{17,25},{25,17},{2,10},{10... | collective-permute-start | bytes 688136 | tf_op jit(solution)/shard_map/ppermute | solution.py:645
  71.3 11.0 %collective-permute-start.30 = (bf16[64,1792]{1,0:T(8,128)(2,1)S(1)}, bf16[64,1792]{1,0:T(8,128)(2,1)S(1)}, u32[]{:S(2)}, u32[]{:S(2)}) collective-permute-start(bf16[64,1792]{1,0:T(8,128)(2,1)S(1)} %get-tuple-element.100), channel_id=1, source_target_pairs={{0,16},{8,24},{16,0},{24,8},{1,17},{9,25},{17,1},{25,9},{2,18},{10... | collective-permute-start | bytes 688136 | tf_op jit(solution)/shard_map/ppermute | solution.py:645
  74.3 8.4 %collective-permute-start.26 = (bf16[64,1792]{1,0:T(8,128)(2,1)S(1)}, bf16[64,1792]{1,0:T(8,128)(2,1)S(1)}, u32[]{:S(2)}, u32[]{:S(2)}) collective-permute-start(bf16[64,1792]{1,0:T(8,128)(2,1)S(1)} %pad_maximum_fusion.3), channel_id=1, source_target_pairs={{0,1},{1,0},{2,3},{3,2},{4,5},{5,4},{6,7},{7,6},{8,9},{9,8},{10,11... | collective-permute-start | bytes 688136 | tf_op jit(solution)/shard_map/ppermute | solution.py:645
  81.6 7.2 %collective-permute-start.32 = (bf16[64,1792]{1,0:T(8,128)(2,1)S(1)}, bf16[64,1792]{1,0:T(8,128)(2,1)S(1)}, u32[]{:S(2)}, u32[]{:S(2)}) collective-permute-start(bf16[64,1792]{1,0:T(8,128)(2,1)S(1)} %get-tuple-element.105), channel_id=1, source_target_pairs={{0,16},{8,24},{16,0},{24,8},{1,17},{9,25},{17,1},{25,9},{2,18},{10... | collective-permute-start | bytes 688136 | tf_op jit(solution)/shard_map/ppermute | solution.py:645
  81.9 6.9 %collective-permute-start.31 = (bf16[64,1792]{1,0:T(8,128)(2,1)S(1)}, bf16[64,1792]{1,0:T(8,128)(2,1)S(1)}, u32[]{:S(2)}, u32[]{:S(2)}) collective-permute-start(bf16[64,1792]{1,0:T(8,128)(2,1)S(1)} %get-tuple-element.104), channel_id=1, source_target_pairs={{0,8},{8,0},{16,24},{24,16},{1,9},{9,1},{17,25},{25,17},{2,10},{10... | collective-permute-start | bytes 688136 | tf_op jit(solution)/shard_map/ppermute | solution.py:645
  82.8 12.2 %collective-permute-start.34 = (bf16[32,1792]{1,0:T(8,128)(2,1)S(1)}, bf16[32,1792]{1,0:T(8,128)(2,1)S(1)}, u32[]{:S(2)}, u32[]{:S(2)}) collective-permute-start(bf16[32,1792]{1,0:T(8,128)(2,1)S(1)} %get-tuple-element.101.refs_0_), channel_id=1, source_target_pairs={{0,4},{1,5},{2,6},{3,7},{4,0},{5,1},{6,2},{7,3},{8,12},{9,13},{10,... | collective-permute-start | bytes 344072 | tf_op jit(solution)/shard_map/ppermute | solution.py:645
  84.0 10.9 %collective-permute-start.35 = (bf16[32,1792]{1,0:T(8,128)(2,1)S(1)}, bf16[32,1792]{1,0:T(8,128)(2,1)S(1)}, u32[]{:S(2)}, u32[]{:S(2)}) collective-permute-start(bf16[32,1792]{1,0:T(8,128)(2,1)S(1)} %get-tuple-element.108), channel_id=1, source_target_pairs={{0,6},{1,7},{2,4},{3,5},{4,2},{5,3},{6,0},{7,1},{8,14},{9,15},{10,... | collective-permute-start | bytes 344072 | tf_op jit(solution)/shard_map/ppermute | solution.py:645
  88.9 7.3 %collective-permute-start.33 = (bf16[32,1792]{1,0:T(8,128)(2,1)S(1)}, bf16[32,1792]{1,0:T(8,128)(2,1)S(1)}, u32[]{:S(2)}, u32[]{:S(2)}) collective-permute-start(bf16[32,1792]{1,0:T(8,128)(2,1)S(1)} %get-tuple-element.107), channel_id=1, source_target_pairs={{0,2},{1,3},{2,0},{3,1},{4,6},{5,7},{6,4},{7,5},{8,10},{9,11},{10,... | collective-permute-start | bytes 344072 | tf_op jit(solution)/shard_map/ppermute | solution.py:645
  95.0 3.6 %collective-permute-start.36 = (bf16[64,1792]{1,0:T(8,128)(2,1)S(1)}, bf16[64,1792]{1,0:T(8,128)(2,1)S(1)}, u32[]{:S(2)}, u32[]{:S(2)}) collective-permute-start(bf16[64,1792]{1,0:T(8,128)(2,1)S(1)} %arrange.18), channel_id=1, source_target_pairs={{0,1},{1,0},{2,3},{3,2},{4,5},{5,4},{6,7},{7,6},{8,9},{9,8},{10,11... | collective-permute-start | bytes 688136 | tf_op jit(solution)/shard_map/ppermute | solution.py:645
  96.2 2.4 %collective-permute-start.37 = (bf16[32,1792]{1,0:T(8,128)(2,1)S(1)}, bf16[32,1792]{1,0:T(8,128)(2,1)S(1)}, u32[]{:S(2)}, u32[]{:S(2)}) collective-permute-start(bf16[32,1792]{1,0:T(8,128)(2,1)S(1)} %arrange.19), channel_id=1, source_target_pairs={{0,1},{1,0},{2,3},{3,2},{4,5},{5,4},{6,7},{7,6},{8,9},{9,8},{10,11... | collective-permute-start | bytes 344072 | tf_op jit(solution)/shard_map/ppermute | solution.py:645

commit v6 on v5

--- a/solution.py
+++ b/solution.py
@@ -263,19 +263,19 @@
     )
 
 
-def add_pairs_body(*refs):
-    for first_ref, second_ref, out_ref in zip(refs[0:4:2], refs[1:4:2], refs[4:]):
-        total = first_ref[...].astype(jnp.float32) + second_ref[...].astype(jnp.float32)
-        out_ref[...] = total.astype(out_ref.dtype)
-
-
-def add_pairs(first, second, later=()):
-    return run_kernel(
-        add_pairs_body,
-        "add_pairs",
-        (*first, *second),
-        [IN_VMEM] * 4,
-        [like(*first[0].shape), like(*second[0].shape)],
+def near_body(first_ref, top_ref, second_ref, first_out, second_out):
+    total = first_ref[...].astype(jnp.float32) + top_ref[...].astype(jnp.float32)
+    first_out[...] = total.astype(first_out.dtype)
+    second_out[...] = second_ref[...]
+
+
+def near_pair(first, top, second, later=()):
+    return run_kernel(
+        near_body,
+        "near_pair",
+        (first, top, second),
+        [IN_VMEM] * 3,
+        [like(*first.shape)] * 2,
         [IN_VMEM] * 2,
         [],
         8,
@@ -736,20 +736,21 @@
     out2 = swap(out2, 4, "ep")
     out1 = swap(out1, 2, "ep")
 
-    y_far, x_near = add_pairs((back[2][1], bottom), (back[1][0], top), (out0,))
+    y_far = add_up([back[2][1], bottom], 1, (out0,))
+    x_near, y_near = near_pair(back[1][0], top, back[2][0], (y_far,))
     x_far = swap(back[1][1], 1, "fsdp")
     y_far = swap(y_far, 2, "fsdp")
     x_near = swap(x_near, 1, "fsdp")
-    y_near = swap(back[2][0], 2, "fsdp")
+    y_near = swap(y_near, 2, "fsdp")
     layout = []
     for step in range(experts // 2):
         layout += [(step, 0), (experts // 2, step)]
     outs = [out0, out1, out2, out3]
     outs.append(swap(joined(*[piece[slots:] for piece in outs]), 1, "ep"))
-    back2, back3 = add_up([back[0][1], x_far, y_far], 2, (outs[-1],))
+    back2, back3 = add_up([back[0][1], x_far, y_far], 2)
     last = Slices(grads[3:], 1, slots)
     grad_down, mark = down_grads(me, hidden, last, count - 1, count, (grad_down,), (back2,))
-    back0, back1 = add_up([back[0][0], x_near, y_near], 2, (mark,))
+    back0, back1 = add_up([back[0][0], x_near, y_near], 2, (mark, outs[-1]))
     back3 = swap(back3, 6, "ep")
     back2 = swap(back2, 4, "ep")
     back1 = swap(back1, 2, "ep")

time: 100 us -> 99 us (0.990)
  waiting for transfers between devices: 14.3 us -> 10.5 us
  starting transfers between devices: 46.7 us -> 48.4 us
    ppermute x38, waiting for transfers between devices: 14.3 us -> 10.5 us  [swap(): return lax.ppermute(array, axis, [(i, i ^ distance) for i in range(size)])]
    ppermute x38, starting transfers between devices: 46.7 us -> 48.4 us  [swap(): return lax.ppermute(array, axis, [(i, i ^ distance) for i in range(size)])]
    pallas_call x30 -> x31, Pallas kernels: 38 us -> 38 us  [run_kernel(): pl.pallas_call(run, name=name, in_specs=[*[ANYWHERE] * len(later), *specs...]
  transfers between devices with their start and end apart: 38 -> 38, of which waited for: 11 -> 8; matrix products, arithmetic and copies ran while one was open for 0% -> 0% of each run, Pallas kernels for 34% -> 34%
where the time goes in v6:
time: 99 us; the launch traced here: 98.4 us
  starting transfers between devices  48.4 us (49%)
  Pallas kernels  38 us (38%)
  waiting for transfers between devices  10.5 us (11%)
  between operations  1.38 us (1%)
    ppermute x38, starting transfers between devices, swap(): return lax.ppermute(array, axis, [(i, i ^ distance) for i in range(size)])  48.4 us
    pallas_call x31, Pallas kernels, run_kernel(): pl.pallas_call(run, name=name, in_specs=[*[ANYWHERE] * len(later), *specs...  38 us
    ppermute x38, waiting for transfers between devices, swap(): return lax.ppermute(array, axis, [(i, i ^ distance) for i in range(size)])  10.5 us
  transfers between devices with their start and end apart: 38, of which 8 were waited for; matrix products, arithmetic and copies ran while one was open for 0% of the time, Pallas kernels for 34%

profile of v6, /device:TPU:1, one launch (start us, length us, event | category | flops | bytes accessed | tf_op | source)
XLA Modules:
  0.0 98.4 jit_solution(17051296655907701458)
XLA Ops:
  0.6 2.6 %pick_slots.1 = (bf16[32,1792]{1,0:T(8,128)(2,1)S(1)}, bf16[32,1792]{1,0:T(8,128)(2,1)S(1)}, bf16[32,1792]{1,0:T(8,128)(2,1)S(1)}, bf16[32,1792]{1,0:T(8,128)(2,...) custom-call(s32[1]{0:T(128)} %bitcast.refs_0_, ...), custom_call_target="tpu_custom_call" | custom-call | flops 1024 | bytes 1024 | tf_op jit(solution)/shard_map/pick_slots/pallas_call | solution.py:34
  3.2 0.1 collective-permute-start
  3.3 2.8 %collective-permute-start.1 = (bf16[32,1792]{1,0:T(8,128)(2,1)S(1)}, bf16[32,1792]{1,0:T(8,128)(2,1)S(1)}, u32[]{:S(2)}, u32[]{:S(2)}) collective-permute-start(bf16[32,1792]{1,0:T(8,128)(2,1)S(1)} %get-tuple-element.61), channel_id=1, source_target_pairs={{0,2},{1,3},{2,0},{3,1},{4,6},{5,7},{6,4},{7,5},{8,10},{9,11},{10,... | collective-permute-start | bytes 344072 | tf_op jit(solution)/shard_map/ppermute | solution.py:645
  6.1 2.7 %collective-permute-start.6 = (bf16[32,1792]{1,0:T(8,128)(2,1)S(1)}, bf16[32,1792]{1,0:T(8,128)(2,1)S(1)}, u32[]{:S(2)}, u32[]{:S(2)}) collective-permute-start(bf16[32,1792]{1,0:T(8,128)(2,1)S(1)} %get-tuple-element.66), channel_id=1, source_target_pairs={{0,4},{1,5},{2,6},{3,7},{4,0},{5,1},{6,2},{7,3},{8,12},{9,13},{10,... | collective-permute-start | bytes 344072 | tf_op jit(solution)/shard_map/ppermute | solution.py:645
  8.8 3.2 %load_weight.3.refs_0_.refs_6_.refs_4_.refs_2_ = bf16[4,1792,512]{2,1,0:T(8,128)(2,1)S(1)} custom-call(bf16[32,1792]{1,0:T(8,128)(2,1)S(1)} %get-tuple-element.59.refs_0_.refs_1_, s32[1]{0:T(128)} %bitcast.2.refs_1_, bf16[7168,512]{1,0:T(8,128)(2,1)} %bitcast.9), custom_call_target="tpu_custom_call" | custom-call | flops 1024 | bytes 1024 | tf_op jit(solution)/shard_map/load_weight/pallas_call | solution.py:34
  12.0 1.1 %collective-permute-start.7 = (bf16[32,1792]{1,0:T(8,128)(2,1)S(1)}, bf16[32,1792]{1,0:T(8,128)(2,1)S(1)}, u32[]{:S(2)}, u32[]{:S(2)}) collective-permute-start(bf16[32,1792]{1,0:T(8,128)(2,1)S(1)} %get-tuple-element.67), channel_id=1, source_target_pairs={{0,6},{1,7},{2,4},{3,5},{4,2},{5,3},{6,0},{7,1},{8,14},{9,15},{10,... | collective-permute-start | bytes 344072 | tf_op jit(solution)/shard_map/ppermute | solution.py:645
  13.2 1.3 %collective-permute-done.2 = bf16[32,1792]{1,0:T(8,128)(2,1)S(1)} collective-permute-done((bf16[32,1792]{1,0:T(8,128)(2,1)S(1)}, bf16[32,1792]{1,0:T(8,128)(2,1)S(1)}, u32[]{:S(2)}, u32[]{:S(2)}) %collective-permute-start.2) | collective-permute-done | bytes 114720 | tf_op jit(solution)/shard_map/ppermute | solution.py:645
  14.5 1.4 %collective-permute-start.3 = (bf16[128,1792]{1,0:T(8,128)(2,1)S(1)}, bf16[128,1792]{1,0:T(8,128)(2,1)S(1)}, u32[]{:S(2)}, u32[]{:S(2)}) collective-permute-start(bf16[128,1792]{1,0:T(8,128)(2,1)S(1)} %pad_maximum_fusion.refs_0_.refs_1_.refs_3_.refs_4_), channel_id=1, source_target_pairs={{0,8},{8,0},{16,24},{24,16},{1,9},{9,1},{17,25},{25,17},{2,10},{10... | collective-permute-start | bytes 1376264 | tf_op jit(solution)/shard_map/ppermute | solution.py:645
  15.9 1.2 %collective-permute-start.5 = (bf16[128,1792]{1,0:T(8,128)(2,1)S(1)}, bf16[128,1792]{1,0:T(8,128)(2,1)S(1)}, u32[]{:S(2)}, u32[]{:S(2)}) collective-permute-start(bf16[128,1792]{1,0:T(8,128)(2,1)S(1)} %pad_maximum_fusion.refs_0_.refs_1_.refs_3_.refs_4_), channel_id=1, source_target_pairs={{0,16},{8,24},{16,0},{24,8},{1,17},{9,25},{17,1},{25,9},{2,18},{10... | collective-permute-start | bytes 1376264 | tf_op jit(solution)/shard_map/ppermute | solution.py:645
  17.2 1.7 %collective-permute-done.7.refs_4_ = bf16[32,1792]{1,0:T(8,128)(2,1)S(1)} collective-permute-done((bf16[32,1792]{1,0:T(8,128)(2,1)S(1)}, bf16[32,1792]{1,0:T(8,128)(2,1)S(1)}, u32[]{:S(2)}, u32[]{:S(2)}) %collective-permute-start.7) | collective-permute-done | bytes 114720 | tf_op jit(solution)/shard_map/ppermute | solution.py:645
  18.9 1.1 %collective-permute-start.8 = (bf16[96,1792]{1,0:T(8,128)(2,1)S(1)}, bf16[96,1792]{1,0:T(8,128)(2,1)S(1)}, u32[]{:S(2)}, u32[]{:S(2)}) collective-permute-start(bf16[96,1792]{1,0:T(8,128)(2,1)S(1)} %pad_maximum_fusion.2), channel_id=1, source_target_pairs={{0,1},{1,0},{2,3},{3,2},{4,5},{5,4},{6,7},{7,6},{8,9},{9,8},{10,11... | collective-permute-start | bytes 1032200 | tf_op jit(solution)/shard_map/ppermute | solution.py:645
  20.0 3.0 %collective-permute-start.12 = (bf16[32,1792]{1,0:T(8,128)(2,1)S(1)}, bf16[32,1792]{1,0:T(8,128)(2,1)S(1)}, u32[]{:S(2)}, u32[]{:S(2)}) collective-permute-start(bf16[32,1792]{1,0:T(8,128)(2,1)S(1)} %get-tuple-element.71), channel_id=1, source_target_pairs={{0,4},{1,5},{2,6},{3,7},{4,0},{5,1},{6,2},{7,3},{8,12},{9,13},{10,... | collective-permute-start | bytes 344072 | tf_op jit(solution)/shard_map/ppermute | solution.py:645
  22.9 1.8 %collective-permute-start.13 = (bf16[32,1792]{1,0:T(8,128)(2,1)S(1)}, bf16[32,1792]{1,0:T(8,128)(2,1)S(1)}, u32[]{:S(2)}, u32[]{:S(2)}) collective-permute-start(bf16[32,1792]{1,0:T(8,128)(2,1)S(1)} %get-tuple-element.72), channel_id=1, source_target_pairs={{0,6},{1,7},{2,4},{3,5},{4,2},{5,3},{6,0},{7,1},{8,14},{9,15},{10,... | collective-permute-start | bytes 344072 | tf_op jit(solution)/shard_map/ppermute | solution.py:645
  24.7 3.2 %load_weight.4.refs_0_.refs_2_.refs_7_.refs_5_.refs_3_ = bf16[4,1792,512]{2,1,0:T(8,128)(2,1)S(1)} custom-call(bf16[128,1792]{1,0:T(8,128)(2,1)S(1)} %pad_maximum_fusion.refs_0_.refs_1_.refs_3_.refs_4_, s32[1]{0:T(128)} %bitcast.2.refs_1_, bf16[7168,512]{1,0:T(8,128)(2,1)} %bitcast.10), custom_call_target="tpu_custom_call" | custom-call | flops 1024 | bytes 1024 | tf_op jit(solution)/shard_map/load_weight/pallas_call | solution.py:34
  27.9 1.3 %collective-permute-start.10 = (bf16[64,1792]{1,0:T(8,128)(2,1)S(1)}, bf16[64,1792]{1,0:T(8,128)(2,1)S(1)}, u32[]{:S(2)}, u32[]{:S(2)}) collective-permute-start(bf16[64,1792]{1,0:T(8,128)(2,1)S(1)} %arrange.12.refs_1_.refs_5_), channel_id=1, source_target_pairs={{0,16},{8,24},{16,0},{24,8},{1,17},{9,25},{17,1},{25,9},{2,18},{10... | collective-permute-start | bytes 688136 | tf_op jit(solution)/shard_map/ppermute | solution.py:645
  29.3 1.2 %collective-permute-start.9 = (bf16[64,1792]{1,0:T(8,128)(2,1)S(1)}, bf16[64,1792]{1,0:T(8,128)(2,1)S(1)}, u32[]{:S(2)}, u32[]{:S(2)}) collective-permute-start(bf16[64,1792]{1,0:T(8,128)(2,1)S(1)} %arrange.12.refs_1_.refs_5_), channel_id=1, source_target_pairs={{0,8},{8,0},{16,24},{24,16},{1,9},{9,1},{17,25},{25,17},{2,10},{10... | collective-permute-start | bytes 688136 | tf_op jit(solution)/shard_map/ppermute | solution.py:645
  30.5 0.8 collective-permute-done.12.refs_0_
  31.3 1.0 collective-permute-start.14
  32.3 1.3 %collective-permute-start.4 = (bf16[64,1792]{1,0:T(8,128)(2,1)S(1)}, bf16[64,1792]{1,0:T(8,128)(2,1)S(1)}, u32[]{:S(2)}, u32[]{:S(2)}) collective-permute-start(bf16[64,1792]{1,0:T(8,128)(2,1)S(1)} %arrange.11), channel_id=1, source_target_pairs={{0,16},{8,24},{16,0},{24,8},{1,17},{9,25},{17,1},{25,9},{2,18},{10... | collective-permute-start | bytes 688136 | tf_op jit(solution)/shard_map/ppermute | solution.py:645
  33.6 0.6 collective-permute-done.10.refs_1_.refs_5_.refs_9_
  34.2 0.9 collective-permute-done.9.refs_0_.refs_3_.refs_7_
  35.2 1.6 %collective-permute-start.11 = (bf16[64,1792]{1,0:T(8,128)(2,1)S(1)}, bf16[64,1792]{1,0:T(8,128)(2,1)S(1)}, u32[]{:S(2)}, u32[]{:S(2)}) collective-permute-start(bf16[64,1792]{1,0:T(8,128)(2,1)S(1)} %arrange.13), channel_id=1, source_target_pairs={{0,8},{8,0},{16,24},{24,16},{1,9},{9,1},{17,25},{25,17},{2,10},{10... | collective-permute-start | bytes 688136 | tf_op jit(solution)/shard_map/ppermute | solution.py:645
  36.8 0.1 collective-permute-start.15
  36.9 0.4 collective-permute-start.16
  37.3 3.2 %load_weight.5.refs_0_.refs_6_.refs_7_.refs_8_ = bf16[4,512,1792]{2,1,0:T(8,128)(2,1)S(1)} custom-call(bf16[4,1792,512]{2,1,0:T(8,128)(2,1)S(1)} %load_weight.4.refs_0_.refs_2_.refs_7_.refs_5_.refs_3_, s32[1]{0:T(128)} %bitcast.2.refs_1_, bf16[512,7168]{1,0:T(8,128)(2,1)} %bitcast.11), custom_call_target="tpu_custom_call" | custom-call | flops 1024 | bytes 1024 | tf_op jit(solution)/shard_map/load_weight/pallas_call | solution.py:34
  40.5 1.6 %partial_products.2 = (f32[128,512]{1,0:T(8,128)S(1)}, f32[128,512]{1,0:T(8,128)S(1)}) custom-call(bf16[128,1792]{1,0:T(8,128)(2,1)S(1)} %pad_maximum_fusion.refs_0_.refs_1_.refs_3_.refs_4_, bf16[64,1792]{1,0:T(8,128)(2,1)S(1)} %arrange.12.refs_1_.refs_5_, bf16[128,1792]{1,0:T(8,128)(2,1)S(1)} %collective-permute-done.3.refs_0_.refs_2_.refs_3_.refs_5_.refs_6_, ...), custom_call_target="tpu_custom_call" | custom-call | flops 1024 | bytes 1024 | tf_op jit(solution)/shard_map/partial_products/pallas_call | solution.py:34
  42.1 1.8 %forward_terms.1 = (bf16[128,512]{1,0:T(8,128)(2,1)S(1)}, f32[128,512]{1,0:T(8,128)S(1)}, f32[128,512]{1,0:T(8,128)S(1)}, bf16[64,1792]{1,0:T(8,128)(2,1)S(1)}, ...) custom-call(bf16[64,1792]{1,0:T(8,128)(2,1)S(1)} %collective-permute, ...), custom_call_target="tpu_custom_call" | custom-call | flops 1024 | bytes 1024 | tf_op jit(solution)/shard_map/forward_terms/pallas_call | solution.py:34
  43.8 1.2 %collective-permute-start.17 = (bf16[64,1792]{1,0:T(8,128)(2,1)S(1)}, bf16[64,1792]{1,0:T(8,128)(2,1)S(1)}, u32[]{:S(2)}, u32[]{:S(2)}) collective-permute-start(bf16[64,1792]{1,0:T(8,128)(2,1)S(1)} %get-tuple-element.78), channel_id=1, source_target_pairs={{0,16},{8,24},{16,0},{24,8},{1,17},{9,25},{17,1},{25,9},{2,18},{10... | collective-permute-start | bytes 688136 | tf_op jit(solution)/shard_map/ppermute | solution.py:645
  45.1 1.4 %collective-permute-start.18 = (bf16[64,1792]{1,0:T(8,128)(2,1)S(1)}, bf16[64,1792]{1,0:T(8,128)(2,1)S(1)}, u32[]{:S(2)}, u32[]{:S(2)}) collective-permute-start(bf16[64,1792]{1,0:T(8,128)(2,1)S(1)} %get-tuple-element.79), channel_id=1, source_target_pairs={{0,8},{8,0},{16,24},{24,16},{1,9},{9,1},{17,25},{25,17},{2,10},{10... | collective-permute-start | bytes 688136 | tf_op jit(solution)/shard_map/ppermute | solution.py:645
  46.5 0.2 collective-permute-start.19
  46.6 0.4 collective-permute-start.20
  47.0 1.9 %partial_products.3.refs_0_.refs_3_ = f32[128,512]{1,0:T(8,128)S(1)} custom-call(bf16[128,512]{1,0:T(8,128)(2,1)S(1)} %get-tuple-element.70.refs_0_.refs_2_, bf16[128,1792]{1,0:T(8,128)(2,1)S(1)} %pad_maximum_fusion.refs_0_.refs_1_.refs_3_.refs_4_, bf16[64,1792]{1,0:T(8,128)(2,1)S(1)} %arrange.15.refs_2_.refs_4_, ...), custom_call_target="tpu_custom_call" | custom-call | flops 1024 | bytes 1024 | tf_op jit(solution)/shard_map/partial_products/pallas_call | solution.py:34
  48.9 3.1 %down_grads.2 = (bf16[512,7168]{1,0:T(8,128)(2,1)}, f32[8,128]{1,0:T(8,128)S(1)}) custom-call(f32[128,512]{1,0:T(8,128)S(1)} %partial_products.3.refs_0_.refs_3_, s32[1]{0:T(128)} %bitcast.2.refs_1_, bf16[128,512]{1,0:T(8,128)(2,1)S(1)} %get-tuple-element.70.refs_0_.refs_2_, bf16[128,1792]{1,0:T(8,128)(2,1)S(1)} %pad_maximum_fusion.refs_0_.refs_1_.refs_3_.refs_4_, ...), custom_call_target="tpu_custom_call" | custom-call | flops 1024 | bytes 1024 | tf_op jit(solution)/shard_map/down_grads/pallas_call | solution.py:34
  52.0 0.1 merge.1
  52.2 1.5 %collective-permute-start.21 = (bf16[128,1792]{1,0:T(8,128)(2,1)S(1)}, bf16[128,1792]{1,0:T(8,128)(2,1)S(1)}, u32[]{:S(2)}, u32[]{:S(2)}) collective-permute-start(bf16[128,1792]{1,0:T(8,128)(2,1)S(1)} %get-tuple-element.80.refs_0_), channel_id=1, source_target_pairs={{0,8},{8,0},{16,24},{24,16},{1,9},{9,1},{17,25},{25,17},{2,10},{10... | collective-permute-start | bytes 1376264 | tf_op jit(solution)/shard_map/ppermute | solution.py:645
  53.6 1.1 %collective-permute-start.22 = (bf16[128,1792]{1,0:T(8,128)(2,1)S(1)}, bf16[128,1792]{1,0:T(8,128)(2,1)S(1)}, u32[]{:S(2)}, u32[]{:S(2)}) collective-permute-start(bf16[128,1792]{1,0:T(8,128)(2,1)S(1)} %get-tuple-element.88), channel_id=1, source_target_pairs={{0,16},{8,24},{16,0},{24,8},{1,17},{9,25},{17,1},{25,9},{2,18},{10... | collective-permute-start | bytes 1376264 | tf_op jit(solution)/shard_map/ppermute | solution.py:645
  54.8 2.0 %backward_terms.1 = (bf16[128,512]{1,0:T(8,128)(2,1)S(1)}, bf16[128,512]{1,0:T(8,128)(2,1)S(1)}, bf16[64,1792]{1,0:T(8,128)(2,1)S(1)}, bf16[64,1792]{1,0:T(8,128)(2,1)S(1)}) custom-call(bf16[128,1792]{1,0:T(8,128)(2,1)S(1)} %get-tuple-element.80.refs_0_, bf16[64,1792]{1,0:T(8,128)(2,1)S(1)} %collective-permute-done.19.refs_1_.refs_4_, ...), custom_call_target="tpu_custom_call" | custom-call | flops 1024 | bytes 1024 | tf_op jit(solution)/shard_map/backward_terms/pallas_call | solution.py:34
  56.7 0.8 collective-permute-start.28
  57.6 3.6 %backward_rest.1 = (bf16[64,1792]{1,0:T(8,128)(2,1)S(1)}, bf16[64,1792]{1,0:T(8,128)(2,1)S(1)}, bf16[64,1792]{1,0:T(8,128)(2,1)S(1)}, bf16[64,1792]{1,0:T(8,128)...) custom-call(bf16[128,512]{1,0:T(8,128)(2,1)S(1)} %get-tuple-element.83.refs_0_.refs_2_, ...), custom_call_target="tpu_custom_call" | custom-call | flops 1024 | bytes 1024 | tf_op jit(solution)/shard_map/backward_rest/pallas_call | solution.py:34
  61.3 3.6 %collective-permute-done.21.refs_2_ = bf16[128,1792]{1,0:T(8,128)(2,1)S(1)} collective-permute-done((bf16[128,1792]{1,0:T(8,128)(2,1)S(1)}, bf16[128,1792]{1,0:T(8,128)(2,1)S(1)}, u32[]{:S(2)}, u32[]{:S(2)}) %collective-permute-start.21) | collective-permute-done | bytes 458784 | tf_op jit(solution)/shard_map/ppermute | solution.py:645
  64.8 0.2 add_up.4
  65.0 1.8 %collective-permute-start.23 = (bf16[32,1792]{1,0:T(8,128)(2,1)S(1)}, bf16[32,1792]{1,0:T(8,128)(2,1)S(1)}, u32[]{:S(2)}, u32[]{:S(2)}) collective-permute-start(bf16[32,1792]{1,0:T(8,128)(2,1)S(1)} %get-tuple-element.90), channel_id=1, source_target_pairs={{0,2},{1,3},{2,0},{3,1},{4,6},{5,7},{6,4},{7,5},{8,10},{9,11},{10,... | collective-permute-start | bytes 344072 | tf_op jit(solution)/shard_map/ppermute | solution.py:645
  66.8 1.9 %collective-permute-start.24 = (bf16[32,1792]{1,0:T(8,128)(2,1)S(1)}, bf16[32,1792]{1,0:T(8,128)(2,1)S(1)}, u32[]{:S(2)}, u32[]{:S(2)}) collective-permute-start(bf16[32,1792]{1,0:T(8,128)(2,1)S(1)} %get-tuple-element.91), channel_id=1, source_target_pairs={{0,4},{1,5},{2,6},{3,7},{4,0},{5,1},{6,2},{7,3},{8,12},{9,13},{10,... | collective-permute-start | bytes 344072 | tf_op jit(solution)/shard_map/ppermute | solution.py:645
  68.7 0.2 collective-permute-start.25
  68.9 0.8 collective-permute-done.28.refs_2_
  69.8 1.4 %collective-permute-start.27 = (bf16[64,1792]{1,0:T(8,128)(2,1)S(1)}, bf16[64,1792]{1,0:T(8,128)(2,1)S(1)}, u32[]{:S(2)}, u32[]{:S(2)}) collective-permute-start(bf16[64,1792]{1,0:T(8,128)(2,1)S(1)} %get-tuple-element.95), channel_id=1, source_target_pairs={{0,8},{8,0},{16,24},{24,16},{1,9},{9,1},{17,25},{25,17},{2,10},{10... | collective-permute-start | bytes 688136 | tf_op jit(solution)/shard_map/ppermute | solution.py:645
  71.2 0.5 collective-permute-start.29
  71.7 0.1 near_pair.1
  71.8 0.1 collective-permute-start.31
  71.9 0.7 collective-permute-done.24.refs_3_
  72.6 2.1 %collective-permute-start.32 = (bf16[64,1792]{1,0:T(8,128)(2,1)S(1)}, bf16[64,1792]{1,0:T(8,128)(2,1)S(1)}, u32[]{:S(2)}, u32[]{:S(2)}) collective-permute-start(bf16[64,1792]{1,0:T(8,128)(2,1)S(1)} %get-tuple-element.105), channel_id=1, source_target_pairs={{0,16},{8,24},{16,0},{24,8},{1,17},{9,25},{17,1},{25,9},{2,18},{10... | collective-permute-start | bytes 688136 | tf_op jit(solution)/shard_map/ppermute | solution.py:645
  74.9 6.9 %collective-permute-start.26 = (bf16[64,1792]{1,0:T(8,128)(2,1)S(1)}, bf16[64,1792]{1,0:T(8,128)(2,1)S(1)}, u32[]{:S(2)}, u32[]{:S(2)}) collective-permute-start(bf16[64,1792]{1,0:T(8,128)(2,1)S(1)} %pad_maximum_fusion.3), channel_id=1, source_target_pairs={{0,1},{1,0},{2,3},{3,2},{4,5},{5,4},{6,7},{7,6},{8,9},{9,8},{10,11... | collective-permute-start | bytes 688136 | tf_op jit(solution)/shard_map/ppermute | solution.py:645
  81.8 0.1 add_up.6
  81.9 1.2 %collective-permute-start.34 = (bf16[32,1792]{1,0:T(8,128)(2,1)S(1)}, bf16[32,1792]{1,0:T(8,128)(2,1)S(1)}, u32[]{:S(2)}, u32[]{:S(2)}) collective-permute-start(bf16[32,1792]{1,0:T(8,128)(2,1)S(1)} %get-tuple-element.98.refs_0_), channel_id=1, source_target_pairs={{0,4},{1,5},{2,6},{3,7},{4,0},{5,1},{6,2},{7,3},{8,12},{9,13},{10,... | collective-permute-start | bytes 344072 | tf_op jit(solution)/shard_map/ppermute | solution.py:645
  83.1 0.3 collective-permute-start.35
  83.4 1.9 %down_grads.3 = (bf16[512,7168]{1,0:T(8,128)(2,1)}, f32[8,128]{1,0:T(8,128)S(1)}) custom-call(bf16[32,1792]{1,0:T(8,128)(2,1)S(1)} %get-tuple-element.98.refs_0_, s32[1]{0:T(128)} %bitcast.2.refs_1_, bf16[128,512]{1,0:T(8,128)(2,1)S(1)} %get-tuple-element.70.refs_0_.refs_2_, ...), custom_call_target="tpu_custom_call", output_to_operand_aliasing={{0}: (3, {})} | custom-call | flops 1024 | bytes 1024 | tf_op jit(solution)/shard_map/down_grads/pallas_call | solution.py:34
  85.3 0.1 add_up.7
  85.4 1.2 %collective-permute-start.33 = (bf16[32,1792]{1,0:T(8,128)(2,1)S(1)}, bf16[32,1792]{1,0:T(8,128)(2,1)S(1)}, u32[]{:S(2)}, u32[]{:S(2)}) collective-permute-start(bf16[32,1792]{1,0:T(8,128)(2,1)S(1)} %get-tuple-element.107), channel_id=1, source_target_pairs={{0,2},{1,3},{2,0},{3,1},{4,6},{5,7},{6,4},{7,5},{8,10},{9,11},{10,... | collective-permute-start | bytes 344072 | tf_op jit(solution)/shard_map/ppermute | solution.py:645
  86.7 6.0 %weight_grads.1 = (bf16[7168,512]{1,0:T(8,128)(2,1)}, bf16[7168,512]{1,0:T(8,128)(2,1)}, f32[8,128]{1,0:T(8,128)S(1)}) custom-call(bf16[32,1792]{1,0:T(8,128)(2,1)S(1)} %get-tuple-element.106.refs_0_.refs_1_, s32[1]{0:T(128)} %bitcast.2.refs_1_, bf16[128,512]{1,0:T(8,128)(2,1)S(1)} %get-tuple-element.83.refs_0_.refs_2_, ...), custom_call_target="tpu_custom_call" | custom-call | flops 1024 | bytes 1024 | tf_op jit(solution)/shard_map/weight_grads/pallas_call | solution.py:34
  92.7 2.0 %collective-permute-start.36 = (bf16[64,1792]{1,0:T(8,128)(2,1)S(1)}, bf16[64,1792]{1,0:T(8,128)(2,1)S(1)}, u32[]{:S(2)}, u32[]{:S(2)}) collective-permute-start(bf16[64,1792]{1,0:T(8,128)(2,1)S(1)} %arrange.18), channel_id=1, source_target_pairs={{0,1},{1,0},{2,3},{3,2},{4,5},{5,4},{6,7},{7,6},{8,9},{9,8},{10,11... | collective-permute-start | bytes 688136 | tf_op jit(solution)/shard_map/ppermute | solution.py:645
  94.7 0.1 collective-permute-start.37
  94.8 0.2 spread_matrices.1
  95.1 1.6 %spread_rows.2 = bf16[512,1792]{1,0:T(8,128)(2,1)} custom-call(bf16[512,256]{1,0:T(8,128)(2,1)S(1)} %get-tuple-element.65.refs_0_, bf16[32,1792]{1,0:T(8,128)(2,1)S(1)} %get-tuple-element.89.refs_1_.refs_0_, bf16[32,1792]{1,0:T(8,128)(2,1)S(1)} %collective-permute-done.23.refs_2_, bf16[32,1792]{1,0:T(8,128)(2,1)S(1)} %collective-permute-done.24.refs_3_, ...), custom_call_target="tpu_custom_call" | custom-call | flops 1024 | bytes 1024 | tf_op jit(solution)/shard_map/spread_rows/pallas_call | solution.py:34
  96.7 1.5 %spread_rows.3 = bf16[512,1792]{1,0:T(8,128)(2,1)} custom-call(bf16[512,128]{1,0:T(8,128)(2,1)S(1)} %get-tuple-element.93.refs_0_, bf16[32,1792]{1,0:T(8,128)(2,1)S(1)} %get-tuple-element.106.refs_0_.refs_1_, bf16[32,1792]{1,0:T(8,128)(2,1)S(1)} %collective-permute-done.33.refs_2_, bf16[32,1792]{1,0:T(8,128)(2,1)S(1)} %collective-permute-done.34.refs_1_.refs_3_, ...), custom_call_target="tpu_custom_call" | custom-call | flops 1024 | bytes 1024 | tf_op jit(solution)/shard_map/spread_rows/pallas_call | solution.py:34
  (53 shorter events, 0.5 us)
Async XLA Ops:
  3.2 9.9 %collective-permute-start = (bf16[32,1792]{1,0:T(8,128)(2,1)S(1)}, bf16[32,1792]{1,0:T(8,128)(2,1)S(1)}, u32[]{:S(2)}, u32[]{:S(2)}) collective-permute-start(bf16[32,1792]{1,0:T(8,128)(2,1)S(1)} %get-tuple-element.60), channel_id=1, source_target_pairs={{0,1},{1,0},{2,3},{3,2},{4,5},{5,4},{6,7},{7,6},{8,9},{9,8},{10,11... | collective-permute-start | bytes 344072 | tf_op jit(solution)/shard_map/ppermute | solution.py:645
  3.3 9.8 %collective-permute-start.1 = (bf16[32,1792]{1,0:T(8,128)(2,1)S(1)}, bf16[32,1792]{1,0:T(8,128)(2,1)S(1)}, u32[]{:S(2)}, u32[]{:S(2)}) collective-permute-start(bf16[32,1792]{1,0:T(8,128)(2,1)S(1)} %get-tuple-element.61), channel_id=1, source_target_pairs={{0,2},{1,3},{2,0},{3,1},{4,6},{5,7},{6,4},{7,5},{8,10},{9,11},{10,... | collective-permute-start | bytes 344072 | tf_op jit(solution)/shard_map/ppermute | solution.py:645
  6.1 8.3 %collective-permute-start.2 = (bf16[32,1792]{1,0:T(8,128)(2,1)S(1)}, bf16[32,1792]{1,0:T(8,128)(2,1)S(1)}, u32[]{:S(2)}, u32[]{:S(2)}) collective-permute-start(bf16[32,1792]{1,0:T(8,128)(2,1)S(1)} %get-tuple-element.62), channel_id=1, source_target_pairs={{0,3},{1,2},{2,1},{3,0},{4,7},{5,6},{6,5},{7,4},{8,11},{9,10},{10,... | collective-permute-start | bytes 344072 | tf_op jit(solution)/shard_map/ppermute | solution.py:645
  6.1 11.0 %collective-permute-start.6 = (bf16[32,1792]{1,0:T(8,128)(2,1)S(1)}, bf16[32,1792]{1,0:T(8,128)(2,1)S(1)}, u32[]{:S(2)}, u32[]{:S(2)}) collective-permute-start(bf16[32,1792]{1,0:T(8,128)(2,1)S(1)} %get-tuple-element.66), channel_id=1, source_target_pairs={{0,4},{1,5},{2,6},{3,7},{4,0},{5,1},{6,2},{7,3},{8,12},{9,13},{10,... | collective-permute-start | bytes 344072 | tf_op jit(solution)/shard_map/ppermute | solution.py:645
  12.0 6.9 %collective-permute-start.7 = (bf16[32,1792]{1,0:T(8,128)(2,1)S(1)}, bf16[32,1792]{1,0:T(8,128)(2,1)S(1)}, u32[]{:S(2)}, u32[]{:S(2)}) collective-permute-start(bf16[32,1792]{1,0:T(8,128)(2,1)S(1)} %get-tuple-element.67), channel_id=1, source_target_pairs={{0,6},{1,7},{2,4},{3,5},{4,2},{5,3},{6,0},{7,1},{8,14},{9,15},{10,... | collective-permute-start | bytes 344072 | tf_op jit(solution)/shard_map/ppermute | solution.py:645
  14.5 13.4 %collective-permute-start.3 = (bf16[128,1792]{1,0:T(8,128)(2,1)S(1)}, bf16[128,1792]{1,0:T(8,128)(2,1)S(1)}, u32[]{:S(2)}, u32[]{:S(2)}) collective-permute-start(bf16[128,1792]{1,0:T(8,128)(2,1)S(1)} %pad_maximum_fusion.refs_0_.refs_1_.refs_3_.refs_4_), channel_id=1, source_target_pairs={{0,8},{8,0},{16,24},{24,16},{1,9},{9,1},{17,25},{25,17},{2,10},{10... | collective-permute-start | bytes 1376264 | tf_op jit(solution)/shard_map/ppermute | solution.py:645
  15.9 12.0 %collective-permute-start.5 = (bf16[128,1792]{1,0:T(8,128)(2,1)S(1)}, bf16[128,1792]{1,0:T(8,128)(2,1)S(1)}, u32[]{:S(2)}, u32[]{:S(2)}) collective-permute-start(bf16[128,1792]{1,0:T(8,128)(2,1)S(1)} %pad_maximum_fusion.refs_0_.refs_1_.refs_3_.refs_4_), channel_id=1, source_target_pairs={{0,16},{8,24},{16,0},{24,8},{1,17},{9,25},{17,1},{25,9},{2,18},{10... | collective-permute-start | bytes 1376264 | tf_op jit(solution)/shard_map/ppermute | solution.py:645
  18.9 9.0 %collective-permute-start.8 = (bf16[96,1792]{1,0:T(8,128)(2,1)S(1)}, bf16[96,1792]{1,0:T(8,128)(2,1)S(1)}, u32[]{:S(2)}, u32[]{:S(2)}) collective-permute-start(bf16[96,1792]{1,0:T(8,128)(2,1)S(1)} %pad_maximum_fusion.2), channel_id=1, source_target_pairs={{0,1},{1,0},{2,3},{3,2},{4,5},{5,4},{6,7},{7,6},{8,9},{9,8},{10,11... | collective-permute-start | bytes 1032200 | tf_op jit(solution)/shard_map/ppermute | solution.py:645
  20.0 11.3 %collective-permute-start.12 = (bf16[32,1792]{1,0:T(8,128)(2,1)S(1)}, bf16[32,1792]{1,0:T(8,128)(2,1)S(1)}, u32[]{:S(2)}, u32[]{:S(2)}) collective-permute-start(bf16[32,1792]{1,0:T(8,128)(2,1)S(1)} %get-tuple-element.71), channel_id=1, source_target_pairs={{0,4},{1,5},{2,6},{3,7},{4,0},{5,1},{6,2},{7,3},{8,12},{9,13},{10,... | collective-permute-start | bytes 344072 | tf_op jit(solution)/shard_map/ppermute | solution.py:645
  22.9 8.3 %collective-permute-start.13 = (bf16[32,1792]{1,0:T(8,128)(2,1)S(1)}, bf16[32,1792]{1,0:T(8,128)(2,1)S(1)}, u32[]{:S(2)}, u32[]{:S(2)}) collective-permute-start(bf16[32,1792]{1,0:T(8,128)(2,1)S(1)} %get-tuple-element.72), channel_id=1, source_target_pairs={{0,6},{1,7},{2,4},{3,5},{4,2},{5,3},{6,0},{7,1},{8,14},{9,15},{10,... | collective-permute-start | bytes 344072 | tf_op jit(solution)/shard_map/ppermute | solution.py:645
  27.9 6.3 %collective-permute-start.10 = (bf16[64,1792]{1,0:T(8,128)(2,1)S(1)}, bf16[64,1792]{1,0:T(8,128)(2,1)S(1)}, u32[]{:S(2)}, u32[]{:S(2)}) collective-permute-start(bf16[64,1792]{1,0:T(8,128)(2,1)S(1)} %arrange.12.refs_1_.refs_5_), channel_id=1, source_target_pairs={{0,16},{8,24},{16,0},{24,8},{1,17},{9,25},{17,1},{25,9},{2,18},{10... | collective-permute-start | bytes 688136 | tf_op jit(solution)/shard_map/ppermute | solution.py:645
  29.3 5.9 %collective-permute-start.9 = (bf16[64,1792]{1,0:T(8,128)(2,1)S(1)}, bf16[64,1792]{1,0:T(8,128)(2,1)S(1)}, u32[]{:S(2)}, u32[]{:S(2)}) collective-permute-start(bf16[64,1792]{1,0:T(8,128)(2,1)S(1)} %arrange.12.refs_1_.refs_5_), channel_id=1, source_target_pairs={{0,8},{8,0},{16,24},{24,16},{1,9},{9,1},{17,25},{25,17},{2,10},{10... | collective-permute-start | bytes 688136 | tf_op jit(solution)/shard_map/ppermute | solution.py:645
  31.3 5.5 %collective-permute-start.14 = (bf16[96,1792]{1,0:T(8,128)(2,1)S(1)}, bf16[96,1792]{1,0:T(8,128)(2,1)S(1)}, u32[]{:S(2)}, u32[]{:S(2)}) collective-permute-start(bf16[96,1792]{1,0:T(8,128)(2,1)S(1)} %arrange.14), channel_id=1, source_target_pairs={{0,1},{1,0},{2,3},{3,2},{4,5},{5,4},{6,7},{7,6},{8,9},{9,8},{10,11... | collective-permute-start | bytes 1032200 | tf_op jit(solution)/shard_map/ppermute | solution.py:645
  32.3 9.8 %collective-permute-start.4 = (bf16[64,1792]{1,0:T(8,128)(2,1)S(1)}, bf16[64,1792]{1,0:T(8,128)(2,1)S(1)}, u32[]{:S(2)}, u32[]{:S(2)}) collective-permute-start(bf16[64,1792]{1,0:T(8,128)(2,1)S(1)} %arrange.11), channel_id=1, source_target_pairs={{0,16},{8,24},{16,0},{24,8},{1,17},{9,25},{17,1},{25,9},{2,18},{10... | collective-permute-start | bytes 688136 | tf_op jit(solution)/shard_map/ppermute | solution.py:645
  35.2 6.9 %collective-permute-start.11 = (bf16[64,1792]{1,0:T(8,128)(2,1)S(1)}, bf16[64,1792]{1,0:T(8,128)(2,1)S(1)}, u32[]{:S(2)}, u32[]{:S(2)}) collective-permute-start(bf16[64,1792]{1,0:T(8,128)(2,1)S(1)} %arrange.13), channel_id=1, source_target_pairs={{0,8},{8,0},{16,24},{24,16},{1,9},{9,1},{17,25},{25,17},{2,10},{10... | collective-permute-start | bytes 688136 | tf_op jit(solution)/shard_map/ppermute | solution.py:645
  36.8 9.8 %collective-permute-start.15 = (bf16[64,1792]{1,0:T(8,128)(2,1)S(1)}, bf16[64,1792]{1,0:T(8,128)(2,1)S(1)}, u32[]{:S(2)}, u32[]{:S(2)}) collective-permute-start(bf16[64,1792]{1,0:T(8,128)(2,1)S(1)} %arrange.15.refs_2_.refs_4_), channel_id=1, source_target_pairs={{0,8},{8,0},{16,24},{24,16},{1,9},{9,1},{17,25},{25,17},{2,10},{10... | collective-permute-start | bytes 688136 | tf_op jit(solution)/shard_map/ppermute | solution.py:645
  36.9 9.7 %collective-permute-start.16 = (bf16[64,1792]{1,0:T(8,128)(2,1)S(1)}, bf16[64,1792]{1,0:T(8,128)(2,1)S(1)}, u32[]{:S(2)}, u32[]{:S(2)}) collective-permute-start(bf16[64,1792]{1,0:T(8,128)(2,1)S(1)} %arrange.15.refs_2_.refs_4_), channel_id=1, source_target_pairs={{0,16},{8,24},{16,0},{24,8},{1,17},{9,25},{17,1},{25,9},{2,18},{10... | collective-permute-start | bytes 688136 | tf_op jit(solution)/shard_map/ppermute | solution.py:645
  43.8 8.2 %collective-permute-start.17 = (bf16[64,1792]{1,0:T(8,128)(2,1)S(1)}, bf16[64,1792]{1,0:T(8,128)(2,1)S(1)}, u32[]{:S(2)}, u32[]{:S(2)}) collective-permute-start(bf16[64,1792]{1,0:T(8,128)(2,1)S(1)} %get-tuple-element.78), channel_id=1, source_target_pairs={{0,16},{8,24},{16,0},{24,8},{1,17},{9,25},{17,1},{25,9},{2,18},{10... | collective-permute-start | bytes 688136 | tf_op jit(solution)/shard_map/ppermute | solution.py:645
  45.1 7.0 %collective-permute-start.18 = (bf16[64,1792]{1,0:T(8,128)(2,1)S(1)}, bf16[64,1792]{1,0:T(8,128)(2,1)S(1)}, u32[]{:S(2)}, u32[]{:S(2)}) collective-permute-start(bf16[64,1792]{1,0:T(8,128)(2,1)S(1)} %get-tuple-element.79), channel_id=1, source_target_pairs={{0,8},{8,0},{16,24},{24,16},{1,9},{9,1},{17,25},{25,17},{2,10},{10... | collective-permute-start | bytes 688136 | tf_op jit(solution)/shard_map/ppermute | solution.py:645
  46.5 8.3 %collective-permute-start.19 = (bf16[64,1792]{1,0:T(8,128)(2,1)S(1)}, bf16[64,1792]{1,0:T(8,128)(2,1)S(1)}, u32[]{:S(2)}, u32[]{:S(2)}) collective-permute-start(bf16[64,1792]{1,0:T(8,128)(2,1)S(1)} %arrange.16), channel_id=1, source_target_pairs={{0,8},{8,0},{16,24},{24,16},{1,9},{9,1},{17,25},{25,17},{2,10},{10... | collective-permute-start | bytes 688136 | tf_op jit(solution)/shard_map/ppermute | solution.py:645
  46.6 8.1 %collective-permute-start.20 = (bf16[64,1792]{1,0:T(8,128)(2,1)S(1)}, bf16[64,1792]{1,0:T(8,128)(2,1)S(1)}, u32[]{:S(2)}, u32[]{:S(2)}) collective-permute-start(bf16[64,1792]{1,0:T(8,128)(2,1)S(1)} %arrange.17), channel_id=1, source_target_pairs={{0,16},{8,24},{16,0},{24,8},{1,17},{9,25},{17,1},{25,9},{2,18},{10... | collective-permute-start | bytes 688136 | tf_op jit(solution)/shard_map/ppermute | solution.py:645
  52.2 12.7 %collective-permute-start.21 = (bf16[128,1792]{1,0:T(8,128)(2,1)S(1)}, bf16[128,1792]{1,0:T(8,128)(2,1)S(1)}, u32[]{:S(2)}, u32[]{:S(2)}) collective-permute-start(bf16[128,1792]{1,0:T(8,128)(2,1)S(1)} %get-tuple-element.80.refs_0_), channel_id=1, source_target_pairs={{0,8},{8,0},{16,24},{24,16},{1,9},{9,1},{17,25},{25,17},{2,10},{10... | collective-permute-start | bytes 1376264 | tf_op jit(solution)/shard_map/ppermute | solution.py:645
  53.6 11.2 %collective-permute-start.22 = (bf16[128,1792]{1,0:T(8,128)(2,1)S(1)}, bf16[128,1792]{1,0:T(8,128)(2,1)S(1)}, u32[]{:S(2)}, u32[]{:S(2)}) collective-permute-start(bf16[128,1792]{1,0:T(8,128)(2,1)S(1)} %get-tuple-element.88), channel_id=1, source_target_pairs={{0,16},{8,24},{16,0},{24,8},{1,17},{9,25},{17,1},{25,9},{2,18},{10... | collective-permute-start | bytes 1376264 | tf_op jit(solution)/shard_map/ppermute | solution.py:645
  56.7 13.0 %collective-permute-start.28 = (bf16[64,1792]{1,0:T(8,128)(2,1)S(1)}, bf16[64,1792]{1,0:T(8,128)(2,1)S(1)}, u32[]{:S(2)}, u32[]{:S(2)}) collective-permute-start(bf16[64,1792]{1,0:T(8,128)(2,1)S(1)} %get-tuple-element.97), channel_id=1, source_target_pairs={{0,8},{8,0},{16,24},{24,16},{1,9},{9,1},{17,25},{25,17},{2,10},{10... | collective-permute-start | bytes 688136 | tf_op jit(solution)/shard_map/ppermute | solution.py:645
  57.6 13.7 %collective-permute-start.30 = (bf16[64,1792]{1,0:T(8,128)(2,1)S(1)}, bf16[64,1792]{1,0:T(8,128)(2,1)S(1)}, u32[]{:S(2)}, u32[]{:S(2)}) collective-permute-start(bf16[64,1792]{1,0:T(8,128)(2,1)S(1)} %get-tuple-element.102), channel_id=1, source_target_pairs={{0,16},{8,24},{16,0},{24,8},{1,17},{9,25},{17,1},{25,9},{2,18},{10... | collective-permute-start | bytes 688136 | tf_op jit(solution)/shard_map/ppermute | solution.py:645
  65.0 6.8 %collective-permute-start.23 = (bf16[32,1792]{1,0:T(8,128)(2,1)S(1)}, bf16[32,1792]{1,0:T(8,128)(2,1)S(1)}, u32[]{:S(2)}, u32[]{:S(2)}) collective-permute-start(bf16[32,1792]{1,0:T(8,128)(2,1)S(1)} %get-tuple-element.90), channel_id=1, source_target_pairs={{0,2},{1,3},{2,0},{3,1},{4,6},{5,7},{6,4},{7,5},{8,10},{9,11},{10,... | collective-permute-start | bytes 344072 | tf_op jit(solution)/shard_map/ppermute | solution.py:645
  66.8 5.8 %collective-permute-start.24 = (bf16[32,1792]{1,0:T(8,128)(2,1)S(1)}, bf16[32,1792]{1,0:T(8,128)(2,1)S(1)}, u32[]{:S(2)}, u32[]{:S(2)}) collective-permute-start(bf16[32,1792]{1,0:T(8,128)(2,1)S(1)} %get-tuple-element.91), channel_id=1, source_target_pairs={{0,4},{1,5},{2,6},{3,7},{4,0},{5,1},{6,2},{7,3},{8,12},{9,13},{10,... | collective-permute-start | bytes 344072 | tf_op jit(solution)/shard_map/ppermute | solution.py:645
  68.7 5.9 %collective-permute-start.25 = (bf16[32,1792]{1,0:T(8,128)(2,1)S(1)}, bf16[32,1792]{1,0:T(8,128)(2,1)S(1)}, u32[]{:S(2)}, u32[]{:S(2)}) collective-permute-start(bf16[32,1792]{1,0:T(8,128)(2,1)S(1)} %get-tuple-element.92), channel_id=1, source_target_pairs={{0,6},{1,7},{2,4},{3,5},{4,2},{5,3},{6,0},{7,1},{8,14},{9,15},{10,... | collective-permute-start | bytes 344072 | tf_op jit(solution)/shard_map/ppermute | solution.py:645
  69.8 12.0 %collective-permute-start.27 = (bf16[64,1792]{1,0:T(8,128)(2,1)S(1)}, bf16[64,1792]{1,0:T(8,128)(2,1)S(1)}, u32[]{:S(2)}, u32[]{:S(2)}) collective-permute-start(bf16[64,1792]{1,0:T(8,128)(2,1)S(1)} %get-tuple-element.95), channel_id=1, source_target_pairs={{0,8},{8,0},{16,24},{24,16},{1,9},{9,1},{17,25},{25,17},{2,10},{10... | collective-permute-start | bytes 688136 | tf_op jit(solution)/shard_map/ppermute | solution.py:645
  71.2 10.6 %collective-permute-start.29 = (bf16[64,1792]{1,0:T(8,128)(2,1)S(1)}, bf16[64,1792]{1,0:T(8,128)(2,1)S(1)}, u32[]{:S(2)}, u32[]{:S(2)}) collective-permute-start(bf16[64,1792]{1,0:T(8,128)(2,1)S(1)} %add_up.5.refs_0_), channel_id=1, source_target_pairs={{0,16},{8,24},{16,0},{24,8},{1,17},{9,25},{17,1},{25,9},{2,18},{10... | collective-permute-start | bytes 688136 | tf_op jit(solution)/shard_map/ppermute | solution.py:645
  71.8 13.5 %collective-permute-start.31 = (bf16[64,1792]{1,0:T(8,128)(2,1)S(1)}, bf16[64,1792]{1,0:T(8,128)(2,1)S(1)}, u32[]{:S(2)}, u32[]{:S(2)}) collective-permute-start(bf16[64,1792]{1,0:T(8,128)(2,1)S(1)} %get-tuple-element.104), channel_id=1, source_target_pairs={{0,8},{8,0},{16,24},{24,16},{1,9},{9,1},{17,25},{25,17},{2,10},{10... | collective-permute-start | bytes 688136 | tf_op jit(solution)/shard_map/ppermute | solution.py:645
  72.6 12.8 %collective-permute-start.32 = (bf16[64,1792]{1,0:T(8,128)(2,1)S(1)}, bf16[64,1792]{1,0:T(8,128)(2,1)S(1)}, u32[]{:S(2)}, u32[]{:S(2)}) collective-permute-start(bf16[64,1792]{1,0:T(8,128)(2,1)S(1)} %get-tuple-element.105), channel_id=1, source_target_pairs={{0,16},{8,24},{16,0},{24,8},{1,17},{9,25},{17,1},{25,9},{2,18},{10... | collective-permute-start | bytes 688136 | tf_op jit(solution)/shard_map/ppermute | solution.py:645
  74.9 10.4 %collective-permute-start.26 = (bf16[64,1792]{1,0:T(8,128)(2,1)S(1)}, bf16[64,1792]{1,0:T(8,128)(2,1)S(1)}, u32[]{:S(2)}, u32[]{:S(2)}) collective-permute-start(bf16[64,1792]{1,0:T(8,128)(2,1)S(1)} %pad_maximum_fusion.3), channel_id=1, source_target_pairs={{0,1},{1,0},{2,3},{3,2},{4,5},{5,4},{6,7},{7,6},{8,9},{9,8},{10,11... | collective-permute-start | bytes 688136 | tf_op jit(solution)/shard_map/ppermute | solution.py:645
  81.9 10.8 %collective-permute-start.34 = (bf16[32,1792]{1,0:T(8,128)(2,1)S(1)}, bf16[32,1792]{1,0:T(8,128)(2,1)S(1)}, u32[]{:S(2)}, u32[]{:S(2)}) collective-permute-start(bf16[32,1792]{1,0:T(8,128)(2,1)S(1)} %get-tuple-element.98.refs_0_), channel_id=1, source_target_pairs={{0,4},{1,5},{2,6},{3,7},{4,0},{5,1},{6,2},{7,3},{8,12},{9,13},{10,... | collective-permute-start | bytes 344072 | tf_op jit(solution)/shard_map/ppermute | solution.py:645
  83.1 9.6 %collective-permute-start.35 = (bf16[32,1792]{1,0:T(8,128)(2,1)S(1)}, bf16[32,1792]{1,0:T(8,128)(2,1)S(1)}, u32[]{:S(2)}, u32[]{:S(2)}) collective-permute-start(bf16[32,1792]{1,0:T(8,128)(2,1)S(1)} %get-tuple-element.108), channel_id=1, source_target_pairs={{0,6},{1,7},{2,4},{3,5},{4,2},{5,3},{6,0},{7,1},{8,14},{9,15},{10,... | collective-permute-start | bytes 344072 | tf_op jit(solution)/shard_map/ppermute | solution.py:645
  85.4 9.3 %collective-permute-start.33 = (bf16[32,1792]{1,0:T(8,128)(2,1)S(1)}, bf16[32,1792]{1,0:T(8,128)(2,1)S(1)}, u32[]{:S(2)}, u32[]{:S(2)}) collective-permute-start(bf16[32,1792]{1,0:T(8,128)(2,1)S(1)} %get-tuple-element.107), channel_id=1, source_target_pairs={{0,2},{1,3},{2,0},{3,1},{4,6},{5,7},{6,4},{7,5},{8,10},{9,11},{10,... | collective-permute-start | bytes 344072 | tf_op jit(solution)/shard_map/ppermute | solution.py:645
  92.7 3.9 %collective-permute-start.36 = (bf16[64,1792]{1,0:T(8,128)(2,1)S(1)}, bf16[64,1792]{1,0:T(8,128)(2,1)S(1)}, u32[]{:S(2)}, u32[]{:S(2)}) collective-permute-start(bf16[64,1792]{1,0:T(8,128)(2,1)S(1)} %arrange.18), channel_id=1, source_target_pairs={{0,1},{1,0},{2,3},{3,2},{4,5},{5,4},{6,7},{7,6},{8,9},{9,8},{10,11... | collective-permute-start | bytes 688136 | tf_op jit(solution)/shard_map/ppermute | solution.py:645
  94.7 1.9 %collective-permute-start.37 = (bf16[32,1792]{1,0:T(8,128)(2,1)S(1)}, bf16[32,1792]{1,0:T(8,128)(2,1)S(1)}, u32[]{:S(2)}, u32[]{:S(2)}) collective-permute-start(bf16[32,1792]{1,0:T(8,128)(2,1)S(1)} %arrange.19), channel_id=1, source_target_pairs={{0,1},{1,0},{2,3},{3,2},{4,5},{5,4},{6,7},{7,6},{8,9},{9,8},{10,11... | collective-permute-start | bytes 344072 | tf_op jit(solution)/shard_map/ppermute | solution.py:645

commit v7 on v6

--- a/solution.py
+++ b/solution.py
@@ -76,27 +76,27 @@
     *outs, mask_ref, weights_ref = refs[:-6]
     counts_ref, chosen_ref, prob_ref, tokens_ref, cotangent_ref, sems = refs[-6:]
     experts, _, slots = chosen_ref.shape
-    pairs = (
-        (counts_hbm, counts_ref),
-        (chosen_hbm, chosen_ref),
-        (prob_hbm, prob_ref),
-        (tokens_hbm, tokens_ref),
-        (cotangent_hbm, cotangent_ref),
-    )
+    length = tokens_ref.shape[0]
+    halves = [pl.ds(first, length // 2) for first in (0, length // 2)]
+    pairs = [(counts_hbm, counts_ref), (chosen_hbm, chosen_ref), (prob_hbm, prob_ref)]
+    for source, target in ((tokens_hbm, tokens_ref), (cotangent_hbm, cotangent_ref)):
+        pairs += [(source.at[half], target.at[half]) for half in halves]
     copies = [pltpu.make_async_copy(*pair, sems.at[index]) for index, pair in enumerate(pairs)]
     for copy in copies:
         copy.start()
     for copy in copies[:3]:
         copy.wait()
     rows, weights = slot_columns(me_ref[0], chosen_ref, counts_ref, prob_ref)
-    length = tokens_ref.shape[0]
     place = lax.broadcasted_iota(jnp.int32, (rows.shape[0], length), 1).astype(jnp.float32)
     mask = (place == rows).astype(jnp.bfloat16)
     mask_ref[...] = mask
     weights_ref[...] = jnp.broadcast_to(weights, weights_ref.shape)
     for which, source_ref in enumerate((tokens_ref, cotangent_ref)):
-        copies[3 + which].wait()
-        value = jnp.dot(mask, source_ref[...], preferred_element_type=jnp.float32)
+        value = 0.0
+        for part, half in enumerate(halves):
+            copies[3 + 2 * which + part].wait()
+            columns = mask[:, part * (length // 2) : (part + 1) * (length // 2)]
+            value += jnp.dot(columns, source_ref[half, :], preferred_element_type=jnp.float32)
         if which:
             value = weights * value
         value = value.astype(jnp.bfloat16)
@@ -122,7 +122,7 @@
         [IN_VMEM] * (len(plan) + 2),
         [pltpu.SMEM(counts.shape, counts.dtype)]
         + [pltpu.VMEM(array.shape, array.dtype) for array in operands[1:]]
-        + [pltpu.SemaphoreType.DMA((5,))],
+        + [pltpu.SemaphoreType.DMA((7,))],
         16,
     )
 
@@ -158,20 +158,26 @@
     if spread_ref.shape[1] > values.shape[0]:
         values = jnp.concatenate([values, values], axis=0)
     parts = sems.shape[0]
-    size = block.shape[0] // parts
+    size = block.shape[1] // parts
     copies = []
     for part in range(parts):
-        rows = pl.ds(part * size, size)
-        total = jnp.dot(spread_ref[rows, :], values, preferred_element_type=jnp.float32)
-        block[rows, :] = total.astype(jnp.bfloat16)
-        copies.append(pltpu.make_async_copy(block.at[rows], out_hbm.at[rows], sems.at[part]))
+        columns = pl.ds(part * size, size)
+        total = jnp.dot(
+            spread_ref[...],
+            values[:, part * size : (part + 1) * size],
+            preferred_element_type=jnp.float32,
+        )
+        block[:, columns] = total.astype(jnp.bfloat16)
+        target = out_hbm.at[:, columns]
+        copies.append(pltpu.make_async_copy(block.at[:, columns], target, sems.at[part]))
         copies[-1].start()
     for copy in copies:
         copy.wait()
 
 
-def spread_rows(spread, pieces, layout, slots, later=(), mark=False, parts=4):
+def spread_rows(spread, pieces, layout, slots, later=(), mark=False):
     length, width = spread.shape[0], pieces[0].shape[1]
+    parts = width // 256 if width % 256 == 0 else 1
     return run_kernel(
         functools.partial(spread_body, layout, slots),
         "spread_rows",
@@ -501,30 +507,35 @@
     )
 
 
-def weight_grad_body(slices, me_ref, *refs):
+def weight_grad_body(slices, parts, me_ref, *refs):
     grad_refs, (gate_hbm, up_hbm, block, sems) = refs[:2], refs[-4:]
     _, count, width, units = block.shape
     grads = jnp.concatenate([ref[...] for ref in grad_refs], axis=1)
+    size = width // parts
     copies = []
     for index in range(count):
         rows = slices.read(refs[2:], index)
         start = pl.multiple_of((me_ref[0] ^ index) * width, width)
-        both = lax.dot_general(rows, grads, ROWS, preferred_element_type=jnp.float32)
-        both = both.astype(jnp.bfloat16)
-        for which, out_ref in enumerate((gate_hbm, up_hbm)):
-            block[which, index] = both[:, which * units : (which + 1) * units]
-            target = out_ref.at[pl.ds(start, width), :]
-            sem = sems.at[2 * index + which]
-            copies.append(pltpu.make_async_copy(block.at[which, index], target, sem))
-            copies[-1].start()
+        for part in range(parts):
+            columns = rows[:, part * size : (part + 1) * size]
+            both = lax.dot_general(columns, grads, ROWS, preferred_element_type=jnp.float32)
+            both = both.astype(jnp.bfloat16)
+            for which, out_ref in enumerate((gate_hbm, up_hbm)):
+                source = block.at[which, index, pl.ds(part * size, size), :]
+                source[...] = both[:, which * units : (which + 1) * units]
+                target = out_ref.at[pl.ds(start + part * size, size), :]
+                sem = sems.at[(index * parts + part) * 2 + which]
+                copies.append(pltpu.make_async_copy(source, target, sem))
+                copies[-1].start()
     for copy in copies:
         copy.wait()
 
 
 def weight_grads(me, slices, gate_grad, up_grad, later=()):
     count, width, units = slices.count, slices.width, gate_grad.shape[1]
-    return run_kernel(
-        functools.partial(weight_grad_body, slices),
+    parts = 2 if width % 256 == 0 else 1
+    return run_kernel(
+        functools.partial(weight_grad_body, slices, parts),
         "weight_grads",
         (me, gate_grad, up_grad, *slices.flat),
         [IN_SMEM] + [IN_VMEM] * (2 + len(slices.flat)),
@@ -532,7 +543,7 @@
         [ANYWHERE] * 2,
         [
             pltpu.VMEM((2, count, width, units), jnp.bfloat16),
-            pltpu.SemaphoreType.DMA((2 * count,)),
+            pltpu.SemaphoreType.DMA((2 * count * parts,)),
         ],
         20,
         later,
@@ -687,7 +698,7 @@
     near = joined(arrange((own,), [[(0, 0, two)]], (gate,)), core, even1, odd1)
     near_x = swap(near, 1, "fsdp")
     near_y = swap(near, 2, "fsdp")
-    odd = swap(joined(token2[slots:], token3[slots:], token2, token3), 1, "ep")
+    odd = swap(joined(token2[slots:], token3[slots:], token2), 1, "ep")
     ends = [(0, 0, slots), (2, 0, slots), (1, 0, slots), (2, slots, slots)]
     up = load_weight(me, up_weight[0], True, count, (near,))
     far = arrange((token2, token3, odd), [ends], (near_x, near_y, up))

time: 99 us -> 98.7 us (level)
  transfers between devices with their start and end apart: 38 -> 38, of which waited for: 8 -> 9; matrix products, arithmetic and copies ran while one was open for 0% -> 0% of each run, Pallas kernels for 34% -> 34%
where the time goes in v7:
time: 98.7 us; the launch traced here: 98.1 us
  starting transfers between devices  47.8 us (48%)
  Pallas kernels  37.8 us (38%)
  waiting for transfers between devices  11.2 us (11%)
  between operations  1.18 us (1%)
    ppermute x38, starting transfers between devices, swap(): return lax.ppermute(array, axis, [(i, i ^ distance) for i in range(size)])  47.8 us
    pallas_call x31, Pallas kernels, run_kernel(): pl.pallas_call(run, name=name, in_specs=[*[ANYWHERE] * len(later), *specs...  37.8 us
    ppermute x38, waiting for transfers between devices, swap(): return lax.ppermute(array, axis, [(i, i ^ distance) for i in range(size)])  11.2 us
  transfers between devices with their start and end apart: 38, of which 9 were waited for; matrix products, arithmetic and copies ran while one was open for 0% of the time, Pallas kernels for 34%

profile of v7, /device:TPU:1, one launch (start us, length us, event | category | flops | bytes accessed | tf_op | source)
XLA Modules:
  0.0 98.1 jit_solution(12090954784314635212)
XLA Ops:
  0.6 2.6 %pick_slots.1 = (bf16[32,1792]{1,0:T(8,128)(2,1)S(1)}, bf16[32,1792]{1,0:T(8,128)(2,1)S(1)}, bf16[32,1792]{1,0:T(8,128)(2,1)S(1)}, bf16[32,1792]{1,0:T(8,128)(2,...) custom-call(s32[1]{0:T(128)} %bitcast.refs_0_, ...), custom_call_target="tpu_custom_call" | custom-call | flops 1024 | bytes 1024 | tf_op jit(solution)/shard_map/pick_slots/pallas_call | solution.py:34
  3.2 0.1 collective-permute-start
  3.3 2.8 %collective-permute-start.1 = (bf16[32,1792]{1,0:T(8,128)(2,1)S(1)}, bf16[32,1792]{1,0:T(8,128)(2,1)S(1)}, u32[]{:S(2)}, u32[]{:S(2)}) collective-permute-start(bf16[32,1792]{1,0:T(8,128)(2,1)S(1)} %get-tuple-element.61), channel_id=1, source_target_pairs={{0,2},{1,3},{2,0},{3,1},{4,6},{5,7},{6,4},{7,5},{8,10},{9,11},{10,... | collective-permute-start | bytes 344072 | tf_op jit(solution)/shard_map/ppermute | solution.py:656
  6.1 2.7 %collective-permute-start.6 = (bf16[32,1792]{1,0:T(8,128)(2,1)S(1)}, bf16[32,1792]{1,0:T(8,128)(2,1)S(1)}, u32[]{:S(2)}, u32[]{:S(2)}) collective-permute-start(bf16[32,1792]{1,0:T(8,128)(2,1)S(1)} %get-tuple-element.66), channel_id=1, source_target_pairs={{0,4},{1,5},{2,6},{3,7},{4,0},{5,1},{6,2},{7,3},{8,12},{9,13},{10,... | collective-permute-start | bytes 344072 | tf_op jit(solution)/shard_map/ppermute | solution.py:656
  8.8 3.2 %load_weight.3.refs_0_.refs_6_.refs_4_.refs_2_ = bf16[4,1792,512]{2,1,0:T(8,128)(2,1)S(1)} custom-call(bf16[32,1792]{1,0:T(8,128)(2,1)S(1)} %get-tuple-element.59.refs_0_.refs_1_, s32[1]{0:T(128)} %bitcast.2.refs_1_, bf16[7168,512]{1,0:T(8,128)(2,1)} %bitcast.9), custom_call_target="tpu_custom_call" | custom-call | flops 1024 | bytes 1024 | tf_op jit(solution)/shard_map/load_weight/pallas_call | solution.py:34
  12.0 1.1 %collective-permute-start.7 = (bf16[32,1792]{1,0:T(8,128)(2,1)S(1)}, bf16[32,1792]{1,0:T(8,128)(2,1)S(1)}, u32[]{:S(2)}, u32[]{:S(2)}) collective-permute-start(bf16[32,1792]{1,0:T(8,128)(2,1)S(1)} %get-tuple-element.67), channel_id=1, source_target_pairs={{0,6},{1,7},{2,4},{3,5},{4,2},{5,3},{6,0},{7,1},{8,14},{9,15},{10,... | collective-permute-start | bytes 344072 | tf_op jit(solution)/shard_map/ppermute | solution.py:656
  13.2 1.3 %collective-permute-done.2 = bf16[32,1792]{1,0:T(8,128)(2,1)S(1)} collective-permute-done((bf16[32,1792]{1,0:T(8,128)(2,1)S(1)}, bf16[32,1792]{1,0:T(8,128)(2,1)S(1)}, u32[]{:S(2)}, u32[]{:S(2)}) %collective-permute-start.2) | collective-permute-done | bytes 114720 | tf_op jit(solution)/shard_map/ppermute | solution.py:656
  14.5 1.4 %collective-permute-start.3 = (bf16[128,1792]{1,0:T(8,128)(2,1)S(1)}, bf16[128,1792]{1,0:T(8,128)(2,1)S(1)}, u32[]{:S(2)}, u32[]{:S(2)}) collective-permute-start(bf16[128,1792]{1,0:T(8,128)(2,1)S(1)} %pad_maximum_fusion.refs_0_.refs_1_.refs_3_.refs_4_), channel_id=1, source_target_pairs={{0,8},{8,0},{16,24},{24,16},{1,9},{9,1},{17,25},{25,17},{2,10},{10... | collective-permute-start | bytes 1376264 | tf_op jit(solution)/shard_map/ppermute | solution.py:656
  15.9 1.2 %collective-permute-start.5 = (bf16[128,1792]{1,0:T(8,128)(2,1)S(1)}, bf16[128,1792]{1,0:T(8,128)(2,1)S(1)}, u32[]{:S(2)}, u32[]{:S(2)}) collective-permute-start(bf16[128,1792]{1,0:T(8,128)(2,1)S(1)} %pad_maximum_fusion.refs_0_.refs_1_.refs_3_.refs_4_), channel_id=1, source_target_pairs={{0,16},{8,24},{16,0},{24,8},{1,17},{9,25},{17,1},{25,9},{2,18},{10... | collective-permute-start | bytes 1376264 | tf_op jit(solution)/shard_map/ppermute | solution.py:656
  17.1 1.7 %collective-permute-done.7.refs_4_ = bf16[32,1792]{1,0:T(8,128)(2,1)S(1)} collective-permute-done((bf16[32,1792]{1,0:T(8,128)(2,1)S(1)}, bf16[32,1792]{1,0:T(8,128)(2,1)S(1)}, u32[]{:S(2)}, u32[]{:S(2)}) %collective-permute-start.7) | collective-permute-done | bytes 114720 | tf_op jit(solution)/shard_map/ppermute | solution.py:656
  18.9 1.1 %collective-permute-start.8 = (bf16[64,1792]{1,0:T(8,128)(2,1)S(1)}, bf16[64,1792]{1,0:T(8,128)(2,1)S(1)}, u32[]{:S(2)}, u32[]{:S(2)}) collective-permute-start(bf16[64,1792]{1,0:T(8,128)(2,1)S(1)} %pad_maximum_fusion.2), channel_id=1, source_target_pairs={{0,1},{1,0},{2,3},{3,2},{4,5},{5,4},{6,7},{7,6},{8,9},{9,8},{10,11... | collective-permute-start | bytes 688136 | tf_op jit(solution)/shard_map/ppermute | solution.py:656
  19.9 2.9 %collective-permute-start.12 = (bf16[32,1792]{1,0:T(8,128)(2,1)S(1)}, bf16[32,1792]{1,0:T(8,128)(2,1)S(1)}, u32[]{:S(2)}, u32[]{:S(2)}) collective-permute-start(bf16[32,1792]{1,0:T(8,128)(2,1)S(1)} %get-tuple-element.71), channel_id=1, source_target_pairs={{0,4},{1,5},{2,6},{3,7},{4,0},{5,1},{6,2},{7,3},{8,12},{9,13},{10,... | collective-permute-start | bytes 344072 | tf_op jit(solution)/shard_map/ppermute | solution.py:656
  22.9 1.8 %collective-permute-start.13 = (bf16[32,1792]{1,0:T(8,128)(2,1)S(1)}, bf16[32,1792]{1,0:T(8,128)(2,1)S(1)}, u32[]{:S(2)}, u32[]{:S(2)}) collective-permute-start(bf16[32,1792]{1,0:T(8,128)(2,1)S(1)} %get-tuple-element.72), channel_id=1, source_target_pairs={{0,6},{1,7},{2,4},{3,5},{4,2},{5,3},{6,0},{7,1},{8,14},{9,15},{10,... | collective-permute-start | bytes 344072 | tf_op jit(solution)/shard_map/ppermute | solution.py:656
  24.7 3.2 %load_weight.4.refs_0_.refs_2_.refs_7_.refs_5_.refs_3_ = bf16[4,1792,512]{2,1,0:T(8,128)(2,1)S(1)} custom-call(bf16[128,1792]{1,0:T(8,128)(2,1)S(1)} %pad_maximum_fusion.refs_0_.refs_1_.refs_3_.refs_4_, s32[1]{0:T(128)} %bitcast.2.refs_1_, bf16[7168,512]{1,0:T(8,128)(2,1)} %bitcast.10), custom_call_target="tpu_custom_call" | custom-call | flops 1024 | bytes 1024 | tf_op jit(solution)/shard_map/load_weight/pallas_call | solution.py:34
  27.9 1.3 %collective-permute-start.10 = (bf16[64,1792]{1,0:T(8,128)(2,1)S(1)}, bf16[64,1792]{1,0:T(8,128)(2,1)S(1)}, u32[]{:S(2)}, u32[]{:S(2)}) collective-permute-start(bf16[64,1792]{1,0:T(8,128)(2,1)S(1)} %arrange.12.refs_1_.refs_5_), channel_id=1, source_target_pairs={{0,16},{8,24},{16,0},{24,8},{1,17},{9,25},{17,1},{25,9},{2,18},{10... | collective-permute-start | bytes 688136 | tf_op jit(solution)/shard_map/ppermute | solution.py:656
  29.2 1.2 %collective-permute-start.9 = (bf16[64,1792]{1,0:T(8,128)(2,1)S(1)}, bf16[64,1792]{1,0:T(8,128)(2,1)S(1)}, u32[]{:S(2)}, u32[]{:S(2)}) collective-permute-start(bf16[64,1792]{1,0:T(8,128)(2,1)S(1)} %arrange.12.refs_1_.refs_5_), channel_id=1, source_target_pairs={{0,8},{8,0},{16,24},{24,16},{1,9},{9,1},{17,25},{25,17},{2,10},{10... | collective-permute-start | bytes 688136 | tf_op jit(solution)/shard_map/ppermute | solution.py:656
  30.4 0.8 collective-permute-done.12.refs_0_
  31.3 1.0 %collective-permute-start.14 = (bf16[96,1792]{1,0:T(8,128)(2,1)S(1)}, bf16[96,1792]{1,0:T(8,128)(2,1)S(1)}, u32[]{:S(2)}, u32[]{:S(2)}) collective-permute-start(bf16[96,1792]{1,0:T(8,128)(2,1)S(1)} %arrange.14), channel_id=1, source_target_pairs={{0,1},{1,0},{2,3},{3,2},{4,5},{5,4},{6,7},{7,6},{8,9},{9,8},{10,11... | collective-permute-start | bytes 1032200 | tf_op jit(solution)/shard_map/ppermute | solution.py:656
  32.3 1.3 %collective-permute-start.4 = (bf16[64,1792]{1,0:T(8,128)(2,1)S(1)}, bf16[64,1792]{1,0:T(8,128)(2,1)S(1)}, u32[]{:S(2)}, u32[]{:S(2)}) collective-permute-start(bf16[64,1792]{1,0:T(8,128)(2,1)S(1)} %arrange.11), channel_id=1, source_target_pairs={{0,16},{8,24},{16,0},{24,8},{1,17},{9,25},{17,1},{25,9},{2,18},{10... | collective-permute-start | bytes 688136 | tf_op jit(solution)/shard_map/ppermute | solution.py:656
  33.6 0.6 collective-permute-done.10.refs_1_.refs_5_.refs_9_
  34.2 0.9 collective-permute-done.9.refs_0_.refs_3_.refs_7_
  35.2 1.6 %collective-permute-start.11 = (bf16[64,1792]{1,0:T(8,128)(2,1)S(1)}, bf16[64,1792]{1,0:T(8,128)(2,1)S(1)}, u32[]{:S(2)}, u32[]{:S(2)}) collective-permute-start(bf16[64,1792]{1,0:T(8,128)(2,1)S(1)} %arrange.13), channel_id=1, source_target_pairs={{0,8},{8,0},{16,24},{24,16},{1,9},{9,1},{17,25},{25,17},{2,10},{10... | collective-permute-start | bytes 688136 | tf_op jit(solution)/shard_map/ppermute | solution.py:656
  36.8 0.1 collective-permute-start.15
  36.8 0.4 collective-permute-start.16
  37.2 3.2 %load_weight.5.refs_0_.refs_6_.refs_7_.refs_8_ = bf16[4,512,1792]{2,1,0:T(8,128)(2,1)S(1)} custom-call(bf16[4,1792,512]{2,1,0:T(8,128)(2,1)S(1)} %load_weight.4.refs_0_.refs_2_.refs_7_.refs_5_.refs_3_, s32[1]{0:T(128)} %bitcast.2.refs_1_, bf16[512,7168]{1,0:T(8,128)(2,1)} %bitcast.11), custom_call_target="tpu_custom_call" | custom-call | flops 1024 | bytes 1024 | tf_op jit(solution)/shard_map/load_weight/pallas_call | solution.py:34
  40.4 1.6 %partial_products.2 = (f32[128,512]{1,0:T(8,128)S(1)}, f32[128,512]{1,0:T(8,128)S(1)}) custom-call(bf16[128,1792]{1,0:T(8,128)(2,1)S(1)} %pad_maximum_fusion.refs_0_.refs_1_.refs_3_.refs_4_, bf16[64,1792]{1,0:T(8,128)(2,1)S(1)} %arrange.12.refs_1_.refs_5_, bf16[128,1792]{1,0:T(8,128)(2,1)S(1)} %collective-permute-done.3.refs_0_.refs_2_.refs_3_.refs_5_.refs_6_, ...), custom_call_target="tpu_custom_call" | custom-call | flops 1024 | bytes 1024 | tf_op jit(solution)/shard_map/partial_products/pallas_call | solution.py:34
  42.0 1.8 %forward_terms.1 = (bf16[128,512]{1,0:T(8,128)(2,1)S(1)}, f32[128,512]{1,0:T(8,128)S(1)}, f32[128,512]{1,0:T(8,128)S(1)}, bf16[64,1792]{1,0:T(8,128)(2,1)S(1)}, ...) custom-call(bf16[64,1792]{1,0:T(8,128)(2,1)S(1)} %collective-permute, ...), custom_call_target="tpu_custom_call" | custom-call | flops 1024 | bytes 1024 | tf_op jit(solution)/shard_map/forward_terms/pallas_call | solution.py:34
  43.8 1.2 %collective-permute-start.17 = (bf16[64,1792]{1,0:T(8,128)(2,1)S(1)}, bf16[64,1792]{1,0:T(8,128)(2,1)S(1)}, u32[]{:S(2)}, u32[]{:S(2)}) collective-permute-start(bf16[64,1792]{1,0:T(8,128)(2,1)S(1)} %get-tuple-element.78), channel_id=1, source_target_pairs={{0,16},{8,24},{16,0},{24,8},{1,17},{9,25},{17,1},{25,9},{2,18},{10... | collective-permute-start | bytes 688136 | tf_op jit(solution)/shard_map/ppermute | solution.py:656
  45.0 1.4 %collective-permute-start.18 = (bf16[64,1792]{1,0:T(8,128)(2,1)S(1)}, bf16[64,1792]{1,0:T(8,128)(2,1)S(1)}, u32[]{:S(2)}, u32[]{:S(2)}) collective-permute-start(bf16[64,1792]{1,0:T(8,128)(2,1)S(1)} %get-tuple-element.79), channel_id=1, source_target_pairs={{0,8},{8,0},{16,24},{24,16},{1,9},{9,1},{17,25},{25,17},{2,10},{10... | collective-permute-start | bytes 688136 | tf_op jit(solution)/shard_map/ppermute | solution.py:656
  46.4 0.1 collective-permute-start.19
  46.6 0.4 collective-permute-start.20
  47.0 1.9 %partial_products.3.refs_0_.refs_3_ = f32[128,512]{1,0:T(8,128)S(1)} custom-call(bf16[128,512]{1,0:T(8,128)(2,1)S(1)} %get-tuple-element.70.refs_0_.refs_2_, bf16[128,1792]{1,0:T(8,128)(2,1)S(1)} %pad_maximum_fusion.refs_0_.refs_1_.refs_3_.refs_4_, bf16[64,1792]{1,0:T(8,128)(2,1)S(1)} %arrange.15.refs_2_.refs_4_, ...), custom_call_target="tpu_custom_call" | custom-call | flops 1024 | bytes 1024 | tf_op jit(solution)/shard_map/partial_products/pallas_call | solution.py:34
  48.9 3.1 %down_grads.2 = (bf16[512,7168]{1,0:T(8,128)(2,1)}, f32[8,128]{1,0:T(8,128)S(1)}) custom-call(f32[128,512]{1,0:T(8,128)S(1)} %partial_products.3.refs_0_.refs_3_, s32[1]{0:T(128)} %bitcast.2.refs_1_, bf16[128,512]{1,0:T(8,128)(2,1)S(1)} %get-tuple-element.70.refs_0_.refs_2_, bf16[128,1792]{1,0:T(8,128)(2,1)S(1)} %pad_maximum_fusion.refs_0_.refs_1_.refs_3_.refs_4_, ...), custom_call_target="tpu_custom_call" | custom-call | flops 1024 | bytes 1024 | tf_op jit(solution)/shard_map/down_grads/pallas_call | solution.py:34
  52.0 0.1 merge.1
  52.1 1.4 %collective-permute-start.21 = (bf16[128,1792]{1,0:T(8,128)(2,1)S(1)}, bf16[128,1792]{1,0:T(8,128)(2,1)S(1)}, u32[]{:S(2)}, u32[]{:S(2)}) collective-permute-start(bf16[128,1792]{1,0:T(8,128)(2,1)S(1)} %get-tuple-element.80.refs_0_), channel_id=1, source_target_pairs={{0,8},{8,0},{16,24},{24,16},{1,9},{9,1},{17,25},{25,17},{2,10},{10... | collective-permute-start | bytes 1376264 | tf_op jit(solution)/shard_map/ppermute | solution.py:656
  53.6 1.2 %collective-permute-start.22 = (bf16[128,1792]{1,0:T(8,128)(2,1)S(1)}, bf16[128,1792]{1,0:T(8,128)(2,1)S(1)}, u32[]{:S(2)}, u32[]{:S(2)}) collective-permute-start(bf16[128,1792]{1,0:T(8,128)(2,1)S(1)} %get-tuple-element.88), channel_id=1, source_target_pairs={{0,16},{8,24},{16,0},{24,8},{1,17},{9,25},{17,1},{25,9},{2,18},{10... | collective-permute-start | bytes 1376264 | tf_op jit(solution)/shard_map/ppermute | solution.py:656
  54.7 2.0 %backward_terms.1 = (bf16[128,512]{1,0:T(8,128)(2,1)S(1)}, bf16[128,512]{1,0:T(8,128)(2,1)S(1)}, bf16[64,1792]{1,0:T(8,128)(2,1)S(1)}, bf16[64,1792]{1,0:T(8,128)(2,1)S(1)}) custom-call(bf16[128,1792]{1,0:T(8,128)(2,1)S(1)} %get-tuple-element.80.refs_0_, bf16[64,1792]{1,0:T(8,128)(2,1)S(1)} %collective-permute-done.19.refs_1_.refs_4_, ...), custom_call_target="tpu_custom_call" | custom-call | flops 1024 | bytes 1024 | tf_op jit(solution)/shard_map/backward_terms/pallas_call | solution.py:34
  56.7 0.8 collective-permute-start.28
  57.6 3.6 %backward_rest.1 = (bf16[64,1792]{1,0:T(8,128)(2,1)S(1)}, bf16[64,1792]{1,0:T(8,128)(2,1)S(1)}, bf16[64,1792]{1,0:T(8,128)(2,1)S(1)}, bf16[64,1792]{1,0:T(8,128)...) custom-call(bf16[128,512]{1,0:T(8,128)(2,1)S(1)} %get-tuple-element.83.refs_0_.refs_2_, ...), custom_call_target="tpu_custom_call" | custom-call | flops 1024 | bytes 1024 | tf_op jit(solution)/shard_map/backward_rest/pallas_call | solution.py:34
  61.2 3.6 %collective-permute-done.21.refs_2_ = bf16[128,1792]{1,0:T(8,128)(2,1)S(1)} collective-permute-done((bf16[128,1792]{1,0:T(8,128)(2,1)S(1)}, bf16[128,1792]{1,0:T(8,128)(2,1)S(1)}, u32[]{:S(2)}, u32[]{:S(2)}) %collective-permute-start.21) | collective-permute-done | bytes 458784 | tf_op jit(solution)/shard_map/ppermute | solution.py:656
  64.8 0.2 add_up.4
  65.0 1.8 %collective-permute-start.23 = (bf16[32,1792]{1,0:T(8,128)(2,1)S(1)}, bf16[32,1792]{1,0:T(8,128)(2,1)S(1)}, u32[]{:S(2)}, u32[]{:S(2)}) collective-permute-start(bf16[32,1792]{1,0:T(8,128)(2,1)S(1)} %get-tuple-element.90), channel_id=1, source_target_pairs={{0,2},{1,3},{2,0},{3,1},{4,6},{5,7},{6,4},{7,5},{8,10},{9,11},{10,... | collective-permute-start | bytes 344072 | tf_op jit(solution)/shard_map/ppermute | solution.py:656
  66.8 1.9 %collective-permute-start.24 = (bf16[32,1792]{1,0:T(8,128)(2,1)S(1)}, bf16[32,1792]{1,0:T(8,128)(2,1)S(1)}, u32[]{:S(2)}, u32[]{:S(2)}) collective-permute-start(bf16[32,1792]{1,0:T(8,128)(2,1)S(1)} %get-tuple-element.91), channel_id=1, source_target_pairs={{0,4},{1,5},{2,6},{3,7},{4,0},{5,1},{6,2},{7,3},{8,12},{9,13},{10,... | collective-permute-start | bytes 344072 | tf_op jit(solution)/shard_map/ppermute | solution.py:656
  68.6 0.3 collective-permute-start.25
  68.9 0.8 collective-permute-done.28.refs_2_
  69.7 1.4 %collective-permute-start.27 = (bf16[64,1792]{1,0:T(8,128)(2,1)S(1)}, bf16[64,1792]{1,0:T(8,128)(2,1)S(1)}, u32[]{:S(2)}, u32[]{:S(2)}) collective-permute-start(bf16[64,1792]{1,0:T(8,128)(2,1)S(1)} %get-tuple-element.95), channel_id=1, source_target_pairs={{0,8},{8,0},{16,24},{24,16},{1,9},{9,1},{17,25},{25,17},{2,10},{10... | collective-permute-start | bytes 688136 | tf_op jit(solution)/shard_map/ppermute | solution.py:656
  71.2 0.5 collective-permute-start.29
  71.8 0.3 collective-permute-start.31
  72.0 0.5 collective-permute-done.24.refs_3_
  72.5 0.8 collective-permute-start.32
  73.4 0.9 collective-permute-done.25.refs_4_
  74.3 7.3 %collective-permute-start.26 = (bf16[64,1792]{1,0:T(8,128)(2,1)S(1)}, bf16[64,1792]{1,0:T(8,128)(2,1)S(1)}, u32[]{:S(2)}, u32[]{:S(2)}) collective-permute-start(bf16[64,1792]{1,0:T(8,128)(2,1)S(1)} %pad_maximum_fusion.3), channel_id=1, source_target_pairs={{0,1},{1,0},{2,3},{3,2},{4,5},{5,4},{6,7},{7,6},{8,9},{9,8},{10,11... | collective-permute-start | bytes 688136 | tf_op jit(solution)/shard_map/ppermute | solution.py:656
  81.6 0.1 add_up.6
  81.7 1.2 %collective-permute-start.34 = (bf16[32,1792]{1,0:T(8,128)(2,1)S(1)}, bf16[32,1792]{1,0:T(8,128)(2,1)S(1)}, u32[]{:S(2)}, u32[]{:S(2)}) collective-permute-start(bf16[32,1792]{1,0:T(8,128)(2,1)S(1)} %get-tuple-element.98.refs_0_), channel_id=1, source_target_pairs={{0,4},{1,5},{2,6},{3,7},{4,0},{5,1},{6,2},{7,3},{8,12},{9,13},{10,... | collective-permute-start | bytes 344072 | tf_op jit(solution)/shard_map/ppermute | solution.py:656
  82.9 0.5 collective-permute-start.35
  83.4 1.9 %down_grads.3 = (bf16[512,7168]{1,0:T(8,128)(2,1)}, f32[8,128]{1,0:T(8,128)S(1)}) custom-call(bf16[32,1792]{1,0:T(8,128)(2,1)S(1)} %get-tuple-element.98.refs_0_, s32[1]{0:T(128)} %bitcast.2.refs_1_, bf16[128,512]{1,0:T(8,128)(2,1)S(1)} %get-tuple-element.70.refs_0_.refs_2_, ...), custom_call_target="tpu_custom_call", output_to_operand_aliasing={{0}: (3, {})} | custom-call | flops 1024 | bytes 1024 | tf_op jit(solution)/shard_map/down_grads/pallas_call | solution.py:34
  85.3 0.1 add_up.7
  85.4 1.1 %collective-permute-start.33 = (bf16[32,1792]{1,0:T(8,128)(2,1)S(1)}, bf16[32,1792]{1,0:T(8,128)(2,1)S(1)}, u32[]{:S(2)}, u32[]{:S(2)}) collective-permute-start(bf16[32,1792]{1,0:T(8,128)(2,1)S(1)} %get-tuple-element.107), channel_id=1, source_target_pairs={{0,2},{1,3},{2,0},{3,1},{4,6},{5,7},{6,4},{7,5},{8,10},{9,11},{10,... | collective-permute-start | bytes 344072 | tf_op jit(solution)/shard_map/ppermute | solution.py:656
  86.5 5.8 %weight_grads.1 = (bf16[7168,512]{1,0:T(8,128)(2,1)}, bf16[7168,512]{1,0:T(8,128)(2,1)}, f32[8,128]{1,0:T(8,128)S(1)}) custom-call(bf16[32,1792]{1,0:T(8,128)(2,1)S(1)} %get-tuple-element.106.refs_0_.refs_1_, s32[1]{0:T(128)} %bitcast.2.refs_1_, bf16[128,512]{1,0:T(8,128)(2,1)S(1)} %get-tuple-element.83.refs_0_.refs_2_, ...), custom_call_target="tpu_custom_call" | custom-call | flops 1024 | bytes 1024 | tf_op jit(solution)/shard_map/weight_grads/pallas_call | solution.py:34
  92.3 2.2 %collective-permute-start.36 = (bf16[64,1792]{1,0:T(8,128)(2,1)S(1)}, bf16[64,1792]{1,0:T(8,128)(2,1)S(1)}, u32[]{:S(2)}, u32[]{:S(2)}) collective-permute-start(bf16[64,1792]{1,0:T(8,128)(2,1)S(1)} %arrange.18), channel_id=1, source_target_pairs={{0,1},{1,0},{2,3},{3,2},{4,5},{5,4},{6,7},{7,6},{8,9},{9,8},{10,11... | collective-permute-start | bytes 688136 | tf_op jit(solution)/shard_map/ppermute | solution.py:656
  94.5 0.1 collective-permute-start.37
  94.6 0.2 spread_matrices.1
  94.8 1.6 %spread_rows.2 = bf16[512,1792]{1,0:T(8,128)(2,1)} custom-call(bf16[512,256]{1,0:T(8,128)(2,1)S(1)} %get-tuple-element.65.refs_0_, bf16[32,1792]{1,0:T(8,128)(2,1)S(1)} %get-tuple-element.89.refs_1_.refs_0_, bf16[32,1792]{1,0:T(8,128)(2,1)S(1)} %collective-permute-done.23.refs_2_, bf16[32,1792]{1,0:T(8,128)(2,1)S(1)} %collective-permute-done.24.refs_3_, ...), custom_call_target="tpu_custom_call" | custom-call | flops 1024 | bytes 1024 | tf_op jit(solution)/shard_map/spread_rows/pallas_call | solution.py:34
  96.4 1.6 %spread_rows.3 = bf16[512,1792]{1,0:T(8,128)(2,1)} custom-call(bf16[512,128]{1,0:T(8,128)(2,1)S(1)} %get-tuple-element.93.refs_0_, bf16[32,1792]{1,0:T(8,128)(2,1)S(1)} %get-tuple-element.106.refs_0_.refs_1_, bf16[32,1792]{1,0:T(8,128)(2,1)S(1)} %collective-permute-done.33.refs_2_, bf16[32,1792]{1,0:T(8,128)(2,1)S(1)} %collective-permute-done.34.refs_1_.refs_3_, ...), custom_call_target="tpu_custom_call" | custom-call | flops 1024 | bytes 1024 | tf_op jit(solution)/shard_map/spread_rows/pallas_call | solution.py:34
  (53 shorter events, 0.5 us)
Async XLA Ops:
  3.2 9.9 %collective-permute-start = (bf16[32,1792]{1,0:T(8,128)(2,1)S(1)}, bf16[32,1792]{1,0:T(8,128)(2,1)S(1)}, u32[]{:S(2)}, u32[]{:S(2)}) collective-permute-start(bf16[32,1792]{1,0:T(8,128)(2,1)S(1)} %get-tuple-element.60), channel_id=1, source_target_pairs={{0,1},{1,0},{2,3},{3,2},{4,5},{5,4},{6,7},{7,6},{8,9},{9,8},{10,11... | collective-permute-start | bytes 344072 | tf_op jit(solution)/shard_map/ppermute | solution.py:656
  3.3 9.8 %collective-permute-start.1 = (bf16[32,1792]{1,0:T(8,128)(2,1)S(1)}, bf16[32,1792]{1,0:T(8,128)(2,1)S(1)}, u32[]{:S(2)}, u32[]{:S(2)}) collective-permute-start(bf16[32,1792]{1,0:T(8,128)(2,1)S(1)} %get-tuple-element.61), channel_id=1, source_target_pairs={{0,2},{1,3},{2,0},{3,1},{4,6},{5,7},{6,4},{7,5},{8,10},{9,11},{10,... | collective-permute-start | bytes 344072 | tf_op jit(solution)/shard_map/ppermute | solution.py:656
  6.1 8.3 %collective-permute-start.2 = (bf16[32,1792]{1,0:T(8,128)(2,1)S(1)}, bf16[32,1792]{1,0:T(8,128)(2,1)S(1)}, u32[]{:S(2)}, u32[]{:S(2)}) collective-permute-start(bf16[32,1792]{1,0:T(8,128)(2,1)S(1)} %get-tuple-element.62), channel_id=1, source_target_pairs={{0,3},{1,2},{2,1},{3,0},{4,7},{5,6},{6,5},{7,4},{8,11},{9,10},{10,... | collective-permute-start | bytes 344072 | tf_op jit(solution)/shard_map/ppermute | solution.py:656
  6.1 11.0 %collective-permute-start.6 = (bf16[32,1792]{1,0:T(8,128)(2,1)S(1)}, bf16[32,1792]{1,0:T(8,128)(2,1)S(1)}, u32[]{:S(2)}, u32[]{:S(2)}) collective-permute-start(bf16[32,1792]{1,0:T(8,128)(2,1)S(1)} %get-tuple-element.66), channel_id=1, source_target_pairs={{0,4},{1,5},{2,6},{3,7},{4,0},{5,1},{6,2},{7,3},{8,12},{9,13},{10,... | collective-permute-start | bytes 344072 | tf_op jit(solution)/shard_map/ppermute | solution.py:656
  12.0 6.9 %collective-permute-start.7 = (bf16[32,1792]{1,0:T(8,128)(2,1)S(1)}, bf16[32,1792]{1,0:T(8,128)(2,1)S(1)}, u32[]{:S(2)}, u32[]{:S(2)}) collective-permute-start(bf16[32,1792]{1,0:T(8,128)(2,1)S(1)} %get-tuple-element.67), channel_id=1, source_target_pairs={{0,6},{1,7},{2,4},{3,5},{4,2},{5,3},{6,0},{7,1},{8,14},{9,15},{10,... | collective-permute-start | bytes 344072 | tf_op jit(solution)/shard_map/ppermute | solution.py:656
  14.5 13.4 %collective-permute-start.3 = (bf16[128,1792]{1,0:T(8,128)(2,1)S(1)}, bf16[128,1792]{1,0:T(8,128)(2,1)S(1)}, u32[]{:S(2)}, u32[]{:S(2)}) collective-permute-start(bf16[128,1792]{1,0:T(8,128)(2,1)S(1)} %pad_maximum_fusion.refs_0_.refs_1_.refs_3_.refs_4_), channel_id=1, source_target_pairs={{0,8},{8,0},{16,24},{24,16},{1,9},{9,1},{17,25},{25,17},{2,10},{10... | collective-permute-start | bytes 1376264 | tf_op jit(solution)/shard_map/ppermute | solution.py:656
  15.9 12.0 %collective-permute-start.5 = (bf16[128,1792]{1,0:T(8,128)(2,1)S(1)}, bf16[128,1792]{1,0:T(8,128)(2,1)S(1)}, u32[]{:S(2)}, u32[]{:S(2)}) collective-permute-start(bf16[128,1792]{1,0:T(8,128)(2,1)S(1)} %pad_maximum_fusion.refs_0_.refs_1_.refs_3_.refs_4_), channel_id=1, source_target_pairs={{0,16},{8,24},{16,0},{24,8},{1,17},{9,25},{17,1},{25,9},{2,18},{10... | collective-permute-start | bytes 1376264 | tf_op jit(solution)/shard_map/ppermute | solution.py:656
  18.9 9.0 %collective-permute-start.8 = (bf16[64,1792]{1,0:T(8,128)(2,1)S(1)}, bf16[64,1792]{1,0:T(8,128)(2,1)S(1)}, u32[]{:S(2)}, u32[]{:S(2)}) collective-permute-start(bf16[64,1792]{1,0:T(8,128)(2,1)S(1)} %pad_maximum_fusion.2), channel_id=1, source_target_pairs={{0,1},{1,0},{2,3},{3,2},{4,5},{5,4},{6,7},{7,6},{8,9},{9,8},{10,11... | collective-permute-start | bytes 688136 | tf_op jit(solution)/shard_map/ppermute | solution.py:656
  19.9 11.3 %collective-permute-start.12 = (bf16[32,1792]{1,0:T(8,128)(2,1)S(1)}, bf16[32,1792]{1,0:T(8,128)(2,1)S(1)}, u32[]{:S(2)}, u32[]{:S(2)}) collective-permute-start(bf16[32,1792]{1,0:T(8,128)(2,1)S(1)} %get-tuple-element.71), channel_id=1, source_target_pairs={{0,4},{1,5},{2,6},{3,7},{4,0},{5,1},{6,2},{7,3},{8,12},{9,13},{10,... | collective-permute-start | bytes 344072 | tf_op jit(solution)/shard_map/ppermute | solution.py:656
  22.9 8.3 %collective-permute-start.13 = (bf16[32,1792]{1,0:T(8,128)(2,1)S(1)}, bf16[32,1792]{1,0:T(8,128)(2,1)S(1)}, u32[]{:S(2)}, u32[]{:S(2)}) collective-permute-start(bf16[32,1792]{1,0:T(8,128)(2,1)S(1)} %get-tuple-element.72), channel_id=1, source_target_pairs={{0,6},{1,7},{2,4},{3,5},{4,2},{5,3},{6,0},{7,1},{8,14},{9,15},{10,... | collective-permute-start | bytes 344072 | tf_op jit(solution)/shard_map/ppermute | solution.py:656
  27.9 6.3 %collective-permute-start.10 = (bf16[64,1792]{1,0:T(8,128)(2,1)S(1)}, bf16[64,1792]{1,0:T(8,128)(2,1)S(1)}, u32[]{:S(2)}, u32[]{:S(2)}) collective-permute-start(bf16[64,1792]{1,0:T(8,128)(2,1)S(1)} %arrange.12.refs_1_.refs_5_), channel_id=1, source_target_pairs={{0,16},{8,24},{16,0},{24,8},{1,17},{9,25},{17,1},{25,9},{2,18},{10... | collective-permute-start | bytes 688136 | tf_op jit(solution)/shard_map/ppermute | solution.py:656
  29.2 5.9 %collective-permute-start.9 = (bf16[64,1792]{1,0:T(8,128)(2,1)S(1)}, bf16[64,1792]{1,0:T(8,128)(2,1)S(1)}, u32[]{:S(2)}, u32[]{:S(2)}) collective-permute-start(bf16[64,1792]{1,0:T(8,128)(2,1)S(1)} %arrange.12.refs_1_.refs_5_), channel_id=1, source_target_pairs={{0,8},{8,0},{16,24},{24,16},{1,9},{9,1},{17,25},{25,17},{2,10},{10... | collective-permute-start | bytes 688136 | tf_op jit(solution)/shard_map/ppermute | solution.py:656
  31.3 5.5 %collective-permute-start.14 = (bf16[96,1792]{1,0:T(8,128)(2,1)S(1)}, bf16[96,1792]{1,0:T(8,128)(2,1)S(1)}, u32[]{:S(2)}, u32[]{:S(2)}) collective-permute-start(bf16[96,1792]{1,0:T(8,128)(2,1)S(1)} %arrange.14), channel_id=1, source_target_pairs={{0,1},{1,0},{2,3},{3,2},{4,5},{5,4},{6,7},{7,6},{8,9},{9,8},{10,11... | collective-permute-start | bytes 1032200 | tf_op jit(solution)/shard_map/ppermute | solution.py:656
  32.3 9.8 %collective-permute-start.4 = (bf16[64,1792]{1,0:T(8,128)(2,1)S(1)}, bf16[64,1792]{1,0:T(8,128)(2,1)S(1)}, u32[]{:S(2)}, u32[]{:S(2)}) collective-permute-start(bf16[64,1792]{1,0:T(8,128)(2,1)S(1)} %arrange.11), channel_id=1, source_target_pairs={{0,16},{8,24},{16,0},{24,8},{1,17},{9,25},{17,1},{25,9},{2,18},{10... | collective-permute-start | bytes 688136 | tf_op jit(solution)/shard_map/ppermute | solution.py:656
  35.2 6.9 %collective-permute-start.11 = (bf16[64,1792]{1,0:T(8,128)(2,1)S(1)}, bf16[64,1792]{1,0:T(8,128)(2,1)S(1)}, u32[]{:S(2)}, u32[]{:S(2)}) collective-permute-start(bf16[64,1792]{1,0:T(8,128)(2,1)S(1)} %arrange.13), channel_id=1, source_target_pairs={{0,8},{8,0},{16,24},{24,16},{1,9},{9,1},{17,25},{25,17},{2,10},{10... | collective-permute-start | bytes 688136 | tf_op jit(solution)/shard_map/ppermute | solution.py:656
  36.8 9.8 %collective-permute-start.15 = (bf16[64,1792]{1,0:T(8,128)(2,1)S(1)}, bf16[64,1792]{1,0:T(8,128)(2,1)S(1)}, u32[]{:S(2)}, u32[]{:S(2)}) collective-permute-start(bf16[64,1792]{1,0:T(8,128)(2,1)S(1)} %arrange.15.refs_2_.refs_4_), channel_id=1, source_target_pairs={{0,8},{8,0},{16,24},{24,16},{1,9},{9,1},{17,25},{25,17},{2,10},{10... | collective-permute-start | bytes 688136 | tf_op jit(solution)/shard_map/ppermute | solution.py:656
  36.8 9.7 %collective-permute-start.16 = (bf16[64,1792]{1,0:T(8,128)(2,1)S(1)}, bf16[64,1792]{1,0:T(8,128)(2,1)S(1)}, u32[]{:S(2)}, u32[]{:S(2)}) collective-permute-start(bf16[64,1792]{1,0:T(8,128)(2,1)S(1)} %arrange.15.refs_2_.refs_4_), channel_id=1, source_target_pairs={{0,16},{8,24},{16,0},{24,8},{1,17},{9,25},{17,1},{25,9},{2,18},{10... | collective-permute-start | bytes 688136 | tf_op jit(solution)/shard_map/ppermute | solution.py:656
  43.8 8.2 %collective-permute-start.17 = (bf16[64,1792]{1,0:T(8,128)(2,1)S(1)}, bf16[64,1792]{1,0:T(8,128)(2,1)S(1)}, u32[]{:S(2)}, u32[]{:S(2)}) collective-permute-start(bf16[64,1792]{1,0:T(8,128)(2,1)S(1)} %get-tuple-element.78), channel_id=1, source_target_pairs={{0,16},{8,24},{16,0},{24,8},{1,17},{9,25},{17,1},{25,9},{2,18},{10... | collective-permute-start | bytes 688136 | tf_op jit(solution)/shard_map/ppermute | solution.py:656
  45.0 7.0 %collective-permute-start.18 = (bf16[64,1792]{1,0:T(8,128)(2,1)S(1)}, bf16[64,1792]{1,0:T(8,128)(2,1)S(1)}, u32[]{:S(2)}, u32[]{:S(2)}) collective-permute-start(bf16[64,1792]{1,0:T(8,128)(2,1)S(1)} %get-tuple-element.79), channel_id=1, source_target_pairs={{0,8},{8,0},{16,24},{24,16},{1,9},{9,1},{17,25},{25,17},{2,10},{10... | collective-permute-start | bytes 688136 | tf_op jit(solution)/shard_map/ppermute | solution.py:656
  46.4 8.3 %collective-permute-start.19 = (bf16[64,1792]{1,0:T(8,128)(2,1)S(1)}, bf16[64,1792]{1,0:T(8,128)(2,1)S(1)}, u32[]{:S(2)}, u32[]{:S(2)}) collective-permute-start(bf16[64,1792]{1,0:T(8,128)(2,1)S(1)} %arrange.16), channel_id=1, source_target_pairs={{0,8},{8,0},{16,24},{24,16},{1,9},{9,1},{17,25},{25,17},{2,10},{10... | collective-permute-start | bytes 688136 | tf_op jit(solution)/shard_map/ppermute | solution.py:656
  46.6 8.1 %collective-permute-start.20 = (bf16[64,1792]{1,0:T(8,128)(2,1)S(1)}, bf16[64,1792]{1,0:T(8,128)(2,1)S(1)}, u32[]{:S(2)}, u32[]{:S(2)}) collective-permute-start(bf16[64,1792]{1,0:T(8,128)(2,1)S(1)} %arrange.17), channel_id=1, source_target_pairs={{0,16},{8,24},{16,0},{24,8},{1,17},{9,25},{17,1},{25,9},{2,18},{10... | collective-permute-start | bytes 688136 | tf_op jit(solution)/shard_map/ppermute | solution.py:656
  52.1 12.7 %collective-permute-start.21 = (bf16[128,1792]{1,0:T(8,128)(2,1)S(1)}, bf16[128,1792]{1,0:T(8,128)(2,1)S(1)}, u32[]{:S(2)}, u32[]{:S(2)}) collective-permute-start(bf16[128,1792]{1,0:T(8,128)(2,1)S(1)} %get-tuple-element.80.refs_0_), channel_id=1, source_target_pairs={{0,8},{8,0},{16,24},{24,16},{1,9},{9,1},{17,25},{25,17},{2,10},{10... | collective-permute-start | bytes 1376264 | tf_op jit(solution)/shard_map/ppermute | solution.py:656
  53.6 11.2 %collective-permute-start.22 = (bf16[128,1792]{1,0:T(8,128)(2,1)S(1)}, bf16[128,1792]{1,0:T(8,128)(2,1)S(1)}, u32[]{:S(2)}, u32[]{:S(2)}) collective-permute-start(bf16[128,1792]{1,0:T(8,128)(2,1)S(1)} %get-tuple-element.88), channel_id=1, source_target_pairs={{0,16},{8,24},{16,0},{24,8},{1,17},{9,25},{17,1},{25,9},{2,18},{10... | collective-permute-start | bytes 1376264 | tf_op jit(solution)/shard_map/ppermute | solution.py:656
  56.7 13.0 %collective-permute-start.28 = (bf16[64,1792]{1,0:T(8,128)(2,1)S(1)}, bf16[64,1792]{1,0:T(8,128)(2,1)S(1)}, u32[]{:S(2)}, u32[]{:S(2)}) collective-permute-start(bf16[64,1792]{1,0:T(8,128)(2,1)S(1)} %get-tuple-element.97), channel_id=1, source_target_pairs={{0,8},{8,0},{16,24},{24,16},{1,9},{9,1},{17,25},{25,17},{2,10},{10... | collective-permute-start | bytes 688136 | tf_op jit(solution)/shard_map/ppermute | solution.py:656
  57.5 13.7 %collective-permute-start.30 = (bf16[64,1792]{1,0:T(8,128)(2,1)S(1)}, bf16[64,1792]{1,0:T(8,128)(2,1)S(1)}, u32[]{:S(2)}, u32[]{:S(2)}) collective-permute-start(bf16[64,1792]{1,0:T(8,128)(2,1)S(1)} %get-tuple-element.102), channel_id=1, source_target_pairs={{0,16},{8,24},{16,0},{24,8},{1,17},{9,25},{17,1},{25,9},{2,18},{10... | collective-permute-start | bytes 688136 | tf_op jit(solution)/shard_map/ppermute | solution.py:656
  65.0 6.8 %collective-permute-start.23 = (bf16[32,1792]{1,0:T(8,128)(2,1)S(1)}, bf16[32,1792]{1,0:T(8,128)(2,1)S(1)}, u32[]{:S(2)}, u32[]{:S(2)}) collective-permute-start(bf16[32,1792]{1,0:T(8,128)(2,1)S(1)} %get-tuple-element.90), channel_id=1, source_target_pairs={{0,2},{1,3},{2,0},{3,1},{4,6},{5,7},{6,4},{7,5},{8,10},{9,11},{10,... | collective-permute-start | bytes 344072 | tf_op jit(solution)/shard_map/ppermute | solution.py:656
  66.8 5.8 %collective-permute-start.24 = (bf16[32,1792]{1,0:T(8,128)(2,1)S(1)}, bf16[32,1792]{1,0:T(8,128)(2,1)S(1)}, u32[]{:S(2)}, u32[]{:S(2)}) collective-permute-start(bf16[32,1792]{1,0:T(8,128)(2,1)S(1)} %get-tuple-element.91), channel_id=1, source_target_pairs={{0,4},{1,5},{2,6},{3,7},{4,0},{5,1},{6,2},{7,3},{8,12},{9,13},{10,... | collective-permute-start | bytes 344072 | tf_op jit(solution)/shard_map/ppermute | solution.py:656
  68.6 5.6 %collective-permute-start.25 = (bf16[32,1792]{1,0:T(8,128)(2,1)S(1)}, bf16[32,1792]{1,0:T(8,128)(2,1)S(1)}, u32[]{:S(2)}, u32[]{:S(2)}) collective-permute-start(bf16[32,1792]{1,0:T(8,128)(2,1)S(1)} %get-tuple-element.92), channel_id=1, source_target_pairs={{0,6},{1,7},{2,4},{3,5},{4,2},{5,3},{6,0},{7,1},{8,14},{9,15},{10,... | collective-permute-start | bytes 344072 | tf_op jit(solution)/shard_map/ppermute | solution.py:656
  69.7 11.8 %collective-permute-start.27 = (bf16[64,1792]{1,0:T(8,128)(2,1)S(1)}, bf16[64,1792]{1,0:T(8,128)(2,1)S(1)}, u32[]{:S(2)}, u32[]{:S(2)}) collective-permute-start(bf16[64,1792]{1,0:T(8,128)(2,1)S(1)} %get-tuple-element.95), channel_id=1, source_target_pairs={{0,8},{8,0},{16,24},{24,16},{1,9},{9,1},{17,25},{25,17},{2,10},{10... | collective-permute-start | bytes 688136 | tf_op jit(solution)/shard_map/ppermute | solution.py:656
  71.2 10.4 %collective-permute-start.29 = (bf16[64,1792]{1,0:T(8,128)(2,1)S(1)}, bf16[64,1792]{1,0:T(8,128)(2,1)S(1)}, u32[]{:S(2)}, u32[]{:S(2)}) collective-permute-start(bf16[64,1792]{1,0:T(8,128)(2,1)S(1)} %add_up.5.refs_0_), channel_id=1, source_target_pairs={{0,16},{8,24},{16,0},{24,8},{1,17},{9,25},{17,1},{25,9},{2,18},{10... | collective-permute-start | bytes 688136 | tf_op jit(solution)/shard_map/ppermute | solution.py:656
  71.8 13.5 %collective-permute-start.31 = (bf16[64,1792]{1,0:T(8,128)(2,1)S(1)}, bf16[64,1792]{1,0:T(8,128)(2,1)S(1)}, u32[]{:S(2)}, u32[]{:S(2)}) collective-permute-start(bf16[64,1792]{1,0:T(8,128)(2,1)S(1)} %get-tuple-element.104), channel_id=1, source_target_pairs={{0,8},{8,0},{16,24},{24,16},{1,9},{9,1},{17,25},{25,17},{2,10},{10... | collective-permute-start | bytes 688136 | tf_op jit(solution)/shard_map/ppermute | solution.py:656
  72.5 12.8 %collective-permute-start.32 = (bf16[64,1792]{1,0:T(8,128)(2,1)S(1)}, bf16[64,1792]{1,0:T(8,128)(2,1)S(1)}, u32[]{:S(2)}, u32[]{:S(2)}) collective-permute-start(bf16[64,1792]{1,0:T(8,128)(2,1)S(1)} %get-tuple-element.105), channel_id=1, source_target_pairs={{0,16},{8,24},{16,0},{24,8},{1,17},{9,25},{17,1},{25,9},{2,18},{10... | collective-permute-start | bytes 688136 | tf_op jit(solution)/shard_map/ppermute | solution.py:656
  74.3 11.0 %collective-permute-start.26 = (bf16[64,1792]{1,0:T(8,128)(2,1)S(1)}, bf16[64,1792]{1,0:T(8,128)(2,1)S(1)}, u32[]{:S(2)}, u32[]{:S(2)}) collective-permute-start(bf16[64,1792]{1,0:T(8,128)(2,1)S(1)} %pad_maximum_fusion.3), channel_id=1, source_target_pairs={{0,1},{1,0},{2,3},{3,2},{4,5},{5,4},{6,7},{7,6},{8,9},{9,8},{10,11... | collective-permute-start | bytes 688136 | tf_op jit(solution)/shard_map/ppermute | solution.py:656
  81.7 10.6 %collective-permute-start.34 = (bf16[32,1792]{1,0:T(8,128)(2,1)S(1)}, bf16[32,1792]{1,0:T(8,128)(2,1)S(1)}, u32[]{:S(2)}, u32[]{:S(2)}) collective-permute-start(bf16[32,1792]{1,0:T(8,128)(2,1)S(1)} %get-tuple-element.98.refs_0_), channel_id=1, source_target_pairs={{0,4},{1,5},{2,6},{3,7},{4,0},{5,1},{6,2},{7,3},{8,12},{9,13},{10,... | collective-permute-start | bytes 344072 | tf_op jit(solution)/shard_map/ppermute | solution.py:656
  82.9 9.3 %collective-permute-start.35 = (bf16[32,1792]{1,0:T(8,128)(2,1)S(1)}, bf16[32,1792]{1,0:T(8,128)(2,1)S(1)}, u32[]{:S(2)}, u32[]{:S(2)}) collective-permute-start(bf16[32,1792]{1,0:T(8,128)(2,1)S(1)} %get-tuple-element.108), channel_id=1, source_target_pairs={{0,6},{1,7},{2,4},{3,5},{4,2},{5,3},{6,0},{7,1},{8,14},{9,15},{10,... | collective-permute-start | bytes 344072 | tf_op jit(solution)/shard_map/ppermute | solution.py:656
  85.4 9.1 %collective-permute-start.33 = (bf16[32,1792]{1,0:T(8,128)(2,1)S(1)}, bf16[32,1792]{1,0:T(8,128)(2,1)S(1)}, u32[]{:S(2)}, u32[]{:S(2)}) collective-permute-start(bf16[32,1792]{1,0:T(8,128)(2,1)S(1)} %get-tuple-element.107), channel_id=1, source_target_pairs={{0,2},{1,3},{2,0},{3,1},{4,6},{5,7},{6,4},{7,5},{8,10},{9,11},{10,... | collective-permute-start | bytes 344072 | tf_op jit(solution)/shard_map/ppermute | solution.py:656
  92.3 4.1 %collective-permute-start.36 = (bf16[64,1792]{1,0:T(8,128)(2,1)S(1)}, bf16[64,1792]{1,0:T(8,128)(2,1)S(1)}, u32[]{:S(2)}, u32[]{:S(2)}) collective-permute-start(bf16[64,1792]{1,0:T(8,128)(2,1)S(1)} %arrange.18), channel_id=1, source_target_pairs={{0,1},{1,0},{2,3},{3,2},{4,5},{5,4},{6,7},{7,6},{8,9},{9,8},{10,11... | collective-permute-start | bytes 688136 | tf_op jit(solution)/shard_map/ppermute | solution.py:656
  94.5 1.9 %collective-permute-start.37 = (bf16[32,1792]{1,0:T(8,128)(2,1)S(1)}, bf16[32,1792]{1,0:T(8,128)(2,1)S(1)}, u32[]{:S(2)}, u32[]{:S(2)}) collective-permute-start(bf16[32,1792]{1,0:T(8,128)(2,1)S(1)} %arrange.19), channel_id=1, source_target_pairs={{0,1},{1,0},{2,3},{3,2},{4,5},{5,4},{6,7},{7,6},{8,9},{9,8},{10,11... | collective-permute-start | bytes 344072 | tf_op jit(solution)/shard_map/ppermute | solution.py:656

commit v8 on v7

--- a/solution.py
+++ b/solution.py
@@ -170,7 +170,7 @@
         block[:, columns] = total.astype(jnp.bfloat16)
         target = out_hbm.at[:, columns]
         copies.append(pltpu.make_async_copy(block.at[:, columns], target, sems.at[part]))
-        copies[-1].start()
+        copies[-1].start(priority=len(copies) % 2)
     for copy in copies:
         copy.wait()
 
@@ -199,7 +199,7 @@
         part = pl.ds(pl.multiple_of((me_ref[0] ^ index) * width, width), width)
         source = source_ref.at[part, :] if by_rows else source_ref.at[:, part]
         copies.append(pltpu.make_async_copy(source, target_ref.at[index], sems.at[index]))
-        copies[-1].start()
+        copies[-1].start(priority=len(copies) % 2)
     for copy in copies:
         copy.wait()
 
@@ -482,7 +482,7 @@
         first = pl.multiple_of((me_ref[0] ^ (start + index)) * width, width)
         target = out_ref.at[:, pl.ds(first, width)]
         copies.append(pltpu.make_async_copy(block.at[index], target, sems.at[index]))
-        copies[-1].start()
+        copies[-1].start(priority=len(copies) % 2)
     for copy in copies:
         copy.wait()
 
@@ -526,7 +526,7 @@
                 target = out_ref.at[pl.ds(start + part * size, size), :]
                 sem = sems.at[(index * parts + part) * 2 + which]
                 copies.append(pltpu.make_async_copy(source, target, sem))
-                copies[-1].start()
+                copies[-1].start(priority=len(copies) % 2)
     for copy in copies:
         copy.wait()
 

time: 98.7 us -> 98.7 us (level)
  no operation moved by 1% of the time
where the time goes in v8:
time: 98.7 us; the launch traced here: 98.1 us
  starting transfers between devices  47.8 us (48%)
  Pallas kernels  37.8 us (38%)
  waiting for transfers between devices  11.3 us (11%)
  between operations  1.18 us (1%)
    ppermute x38, starting transfers between devices, swap(): return lax.ppermute(array, axis, [(i, i ^ distance) for i in range(size)])  47.8 us
    pallas_call x31, Pallas kernels, run_kernel(): pl.pallas_call(run, name=name, in_specs=[*[ANYWHERE] * len(later), *specs...  37.8 us
    ppermute x38, waiting for transfers between devices, swap(): return lax.ppermute(array, axis, [(i, i ^ distance) for i in range(size)])  11.3 us
  transfers between devices with their start and end apart: 38, of which 9 were waited for; matrix products, arithmetic and copies ran while one was open for 0% of the time, Pallas kernels for 34%

profile of v8, /device:TPU:1, one launch (start us, length us, event | category | flops | bytes accessed | tf_op | source)
XLA Modules:
  0.0 98.1 jit_solution(14035635292218283981)
XLA Ops:
  0.6 2.6 %pick_slots.1 = (bf16[32,1792]{1,0:T(8,128)(2,1)S(1)}, bf16[32,1792]{1,0:T(8,128)(2,1)S(1)}, bf16[32,1792]{1,0:T(8,128)(2,1)S(1)}, bf16[32,1792]{1,0:T(8,128)(2,...) custom-call(s32[1]{0:T(128)} %bitcast.refs_0_, ...), custom_call_target="tpu_custom_call" | custom-call | flops 1024 | bytes 1024 | tf_op jit(solution)/shard_map/pick_slots/pallas_call | solution.py:34
  3.2 0.1 collective-permute-start
  3.3 2.8 %collective-permute-start.1 = (bf16[32,1792]{1,0:T(8,128)(2,1)S(1)}, bf16[32,1792]{1,0:T(8,128)(2,1)S(1)}, u32[]{:S(2)}, u32[]{:S(2)}) collective-permute-start(bf16[32,1792]{1,0:T(8,128)(2,1)S(1)} %get-tuple-element.61), channel_id=1, source_target_pairs={{0,2},{1,3},{2,0},{3,1},{4,6},{5,7},{6,4},{7,5},{8,10},{9,11},{10,... | collective-permute-start | bytes 344072 | tf_op jit(solution)/shard_map/ppermute | solution.py:656
  6.1 2.7 %collective-permute-start.6 = (bf16[32,1792]{1,0:T(8,128)(2,1)S(1)}, bf16[32,1792]{1,0:T(8,128)(2,1)S(1)}, u32[]{:S(2)}, u32[]{:S(2)}) collective-permute-start(bf16[32,1792]{1,0:T(8,128)(2,1)S(1)} %get-tuple-element.66), channel_id=1, source_target_pairs={{0,4},{1,5},{2,6},{3,7},{4,0},{5,1},{6,2},{7,3},{8,12},{9,13},{10,... | collective-permute-start | bytes 344072 | tf_op jit(solution)/shard_map/ppermute | solution.py:656
  8.8 3.2 %load_weight.3.refs_0_.refs_6_.refs_4_.refs_2_ = bf16[4,1792,512]{2,1,0:T(8,128)(2,1)S(1)} custom-call(bf16[32,1792]{1,0:T(8,128)(2,1)S(1)} %get-tuple-element.59.refs_0_.refs_1_, s32[1]{0:T(128)} %bitcast.2.refs_1_, bf16[7168,512]{1,0:T(8,128)(2,1)} %bitcast.9), custom_call_target="tpu_custom_call" | custom-call | flops 1024 | bytes 1024 | tf_op jit(solution)/shard_map/load_weight/pallas_call | solution.py:34
  12.0 1.1 %collective-permute-start.7 = (bf16[32,1792]{1,0:T(8,128)(2,1)S(1)}, bf16[32,1792]{1,0:T(8,128)(2,1)S(1)}, u32[]{:S(2)}, u32[]{:S(2)}) collective-permute-start(bf16[32,1792]{1,0:T(8,128)(2,1)S(1)} %get-tuple-element.67), channel_id=1, source_target_pairs={{0,6},{1,7},{2,4},{3,5},{4,2},{5,3},{6,0},{7,1},{8,14},{9,15},{10,... | collective-permute-start | bytes 344072 | tf_op jit(solution)/shard_map/ppermute | solution.py:656
  13.2 1.3 %collective-permute-done.2 = bf16[32,1792]{1,0:T(8,128)(2,1)S(1)} collective-permute-done((bf16[32,1792]{1,0:T(8,128)(2,1)S(1)}, bf16[32,1792]{1,0:T(8,128)(2,1)S(1)}, u32[]{:S(2)}, u32[]{:S(2)}) %collective-permute-start.2) | collective-permute-done | bytes 114720 | tf_op jit(solution)/shard_map/ppermute | solution.py:656
  14.5 1.4 %collective-permute-start.3 = (bf16[128,1792]{1,0:T(8,128)(2,1)S(1)}, bf16[128,1792]{1,0:T(8,128)(2,1)S(1)}, u32[]{:S(2)}, u32[]{:S(2)}) collective-permute-start(bf16[128,1792]{1,0:T(8,128)(2,1)S(1)} %pad_maximum_fusion.refs_0_.refs_1_.refs_3_.refs_4_), channel_id=1, source_target_pairs={{0,8},{8,0},{16,24},{24,16},{1,9},{9,1},{17,25},{25,17},{2,10},{10... | collective-permute-start | bytes 1376264 | tf_op jit(solution)/shard_map/ppermute | solution.py:656
  15.9 1.2 %collective-permute-start.5 = (bf16[128,1792]{1,0:T(8,128)(2,1)S(1)}, bf16[128,1792]{1,0:T(8,128)(2,1)S(1)}, u32[]{:S(2)}, u32[]{:S(2)}) collective-permute-start(bf16[128,1792]{1,0:T(8,128)(2,1)S(1)} %pad_maximum_fusion.refs_0_.refs_1_.refs_3_.refs_4_), channel_id=1, source_target_pairs={{0,16},{8,24},{16,0},{24,8},{1,17},{9,25},{17,1},{25,9},{2,18},{10... | collective-permute-start | bytes 1376264 | tf_op jit(solution)/shard_map/ppermute | solution.py:656
  17.1 1.7 %collective-permute-done.7.refs_4_ = bf16[32,1792]{1,0:T(8,128)(2,1)S(1)} collective-permute-done((bf16[32,1792]{1,0:T(8,128)(2,1)S(1)}, bf16[32,1792]{1,0:T(8,128)(2,1)S(1)}, u32[]{:S(2)}, u32[]{:S(2)}) %collective-permute-start.7) | collective-permute-done | bytes 114720 | tf_op jit(solution)/shard_map/ppermute | solution.py:656
  18.9 1.1 %collective-permute-start.8 = (bf16[64,1792]{1,0:T(8,128)(2,1)S(1)}, bf16[64,1792]{1,0:T(8,128)(2,1)S(1)}, u32[]{:S(2)}, u32[]{:S(2)}) collective-permute-start(bf16[64,1792]{1,0:T(8,128)(2,1)S(1)} %pad_maximum_fusion.2), channel_id=1, source_target_pairs={{0,1},{1,0},{2,3},{3,2},{4,5},{5,4},{6,7},{7,6},{8,9},{9,8},{10,11... | collective-permute-start | bytes 688136 | tf_op jit(solution)/shard_map/ppermute | solution.py:656
  19.9 2.9 %collective-permute-start.12 = (bf16[32,1792]{1,0:T(8,128)(2,1)S(1)}, bf16[32,1792]{1,0:T(8,128)(2,1)S(1)}, u32[]{:S(2)}, u32[]{:S(2)}) collective-permute-start(bf16[32,1792]{1,0:T(8,128)(2,1)S(1)} %get-tuple-element.71), channel_id=1, source_target_pairs={{0,4},{1,5},{2,6},{3,7},{4,0},{5,1},{6,2},{7,3},{8,12},{9,13},{10,... | collective-permute-start | bytes 344072 | tf_op jit(solution)/shard_map/ppermute | solution.py:656
  22.9 1.8 %collective-permute-start.13 = (bf16[32,1792]{1,0:T(8,128)(2,1)S(1)}, bf16[32,1792]{1,0:T(8,128)(2,1)S(1)}, u32[]{:S(2)}, u32[]{:S(2)}) collective-permute-start(bf16[32,1792]{1,0:T(8,128)(2,1)S(1)} %get-tuple-element.72), channel_id=1, source_target_pairs={{0,6},{1,7},{2,4},{3,5},{4,2},{5,3},{6,0},{7,1},{8,14},{9,15},{10,... | collective-permute-start | bytes 344072 | tf_op jit(solution)/shard_map/ppermute | solution.py:656
  24.7 3.2 %load_weight.4.refs_0_.refs_2_.refs_7_.refs_5_.refs_3_ = bf16[4,1792,512]{2,1,0:T(8,128)(2,1)S(1)} custom-call(bf16[128,1792]{1,0:T(8,128)(2,1)S(1)} %pad_maximum_fusion.refs_0_.refs_1_.refs_3_.refs_4_, s32[1]{0:T(128)} %bitcast.2.refs_1_, bf16[7168,512]{1,0:T(8,128)(2,1)} %bitcast.10), custom_call_target="tpu_custom_call" | custom-call | flops 1024 | bytes 1024 | tf_op jit(solution)/shard_map/load_weight/pallas_call | solution.py:34
  27.9 1.3 %collective-permute-start.10 = (bf16[64,1792]{1,0:T(8,128)(2,1)S(1)}, bf16[64,1792]{1,0:T(8,128)(2,1)S(1)}, u32[]{:S(2)}, u32[]{:S(2)}) collective-permute-start(bf16[64,1792]{1,0:T(8,128)(2,1)S(1)} %arrange.12.refs_1_.refs_5_), channel_id=1, source_target_pairs={{0,16},{8,24},{16,0},{24,8},{1,17},{9,25},{17,1},{25,9},{2,18},{10... | collective-permute-start | bytes 688136 | tf_op jit(solution)/shard_map/ppermute | solution.py:656
  29.2 1.2 %collective-permute-start.9 = (bf16[64,1792]{1,0:T(8,128)(2,1)S(1)}, bf16[64,1792]{1,0:T(8,128)(2,1)S(1)}, u32[]{:S(2)}, u32[]{:S(2)}) collective-permute-start(bf16[64,1792]{1,0:T(8,128)(2,1)S(1)} %arrange.12.refs_1_.refs_5_), channel_id=1, source_target_pairs={{0,8},{8,0},{16,24},{24,16},{1,9},{9,1},{17,25},{25,17},{2,10},{10... | collective-permute-start | bytes 688136 | tf_op jit(solution)/shard_map/ppermute | solution.py:656
  30.4 0.8 collective-permute-done.12.refs_0_
  31.3 1.0 %collective-permute-start.14 = (bf16[96,1792]{1,0:T(8,128)(2,1)S(1)}, bf16[96,1792]{1,0:T(8,128)(2,1)S(1)}, u32[]{:S(2)}, u32[]{:S(2)}) collective-permute-start(bf16[96,1792]{1,0:T(8,128)(2,1)S(1)} %arrange.14), channel_id=1, source_target_pairs={{0,1},{1,0},{2,3},{3,2},{4,5},{5,4},{6,7},{7,6},{8,9},{9,8},{10,11... | collective-permute-start | bytes 1032200 | tf_op jit(solution)/shard_map/ppermute | solution.py:656
  32.3 1.3 %collective-permute-start.4 = (bf16[64,1792]{1,0:T(8,128)(2,1)S(1)}, bf16[64,1792]{1,0:T(8,128)(2,1)S(1)}, u32[]{:S(2)}, u32[]{:S(2)}) collective-permute-start(bf16[64,1792]{1,0:T(8,128)(2,1)S(1)} %arrange.11), channel_id=1, source_target_pairs={{0,16},{8,24},{16,0},{24,8},{1,17},{9,25},{17,1},{25,9},{2,18},{10... | collective-permute-start | bytes 688136 | tf_op jit(solution)/shard_map/ppermute | solution.py:656
  33.6 0.6 collective-permute-done.10.refs_1_.refs_5_.refs_9_
  34.2 0.9 collective-permute-done.9.refs_0_.refs_3_.refs_7_
  35.2 1.6 %collective-permute-start.11 = (bf16[64,1792]{1,0:T(8,128)(2,1)S(1)}, bf16[64,1792]{1,0:T(8,128)(2,1)S(1)}, u32[]{:S(2)}, u32[]{:S(2)}) collective-permute-start(bf16[64,1792]{1,0:T(8,128)(2,1)S(1)} %arrange.13), channel_id=1, source_target_pairs={{0,8},{8,0},{16,24},{24,16},{1,9},{9,1},{17,25},{25,17},{2,10},{10... | collective-permute-start | bytes 688136 | tf_op jit(solution)/shard_map/ppermute | solution.py:656
  36.8 0.1 collective-permute-start.15
  36.9 0.4 collective-permute-start.16
  37.2 3.2 %load_weight.5.refs_0_.refs_6_.refs_7_.refs_8_ = bf16[4,512,1792]{2,1,0:T(8,128)(2,1)S(1)} custom-call(bf16[4,1792,512]{2,1,0:T(8,128)(2,1)S(1)} %load_weight.4.refs_0_.refs_2_.refs_7_.refs_5_.refs_3_, s32[1]{0:T(128)} %bitcast.2.refs_1_, bf16[512,7168]{1,0:T(8,128)(2,1)} %bitcast.11), custom_call_target="tpu_custom_call" | custom-call | flops 1024 | bytes 1024 | tf_op jit(solution)/shard_map/load_weight/pallas_call | solution.py:34
  40.4 1.6 %partial_products.2 = (f32[128,512]{1,0:T(8,128)S(1)}, f32[128,512]{1,0:T(8,128)S(1)}) custom-call(bf16[128,1792]{1,0:T(8,128)(2,1)S(1)} %pad_maximum_fusion.refs_0_.refs_1_.refs_3_.refs_4_, bf16[64,1792]{1,0:T(8,128)(2,1)S(1)} %arrange.12.refs_1_.refs_5_, bf16[128,1792]{1,0:T(8,128)(2,1)S(1)} %collective-permute-done.3.refs_0_.refs_2_.refs_3_.refs_5_.refs_6_, ...), custom_call_target="tpu_custom_call" | custom-call | flops 1024 | bytes 1024 | tf_op jit(solution)/shard_map/partial_products/pallas_call | solution.py:34
  42.0 1.8 %forward_terms.1 = (bf16[128,512]{1,0:T(8,128)(2,1)S(1)}, f32[128,512]{1,0:T(8,128)S(1)}, f32[128,512]{1,0:T(8,128)S(1)}, bf16[64,1792]{1,0:T(8,128)(2,1)S(1)}, ...) custom-call(bf16[64,1792]{1,0:T(8,128)(2,1)S(1)} %collective-permute, ...), custom_call_target="tpu_custom_call" | custom-call | flops 1024 | bytes 1024 | tf_op jit(solution)/shard_map/forward_terms/pallas_call | solution.py:34
  43.8 1.2 %collective-permute-start.17 = (bf16[64,1792]{1,0:T(8,128)(2,1)S(1)}, bf16[64,1792]{1,0:T(8,128)(2,1)S(1)}, u32[]{:S(2)}, u32[]{:S(2)}) collective-permute-start(bf16[64,1792]{1,0:T(8,128)(2,1)S(1)} %get-tuple-element.78), channel_id=1, source_target_pairs={{0,16},{8,24},{16,0},{24,8},{1,17},{9,25},{17,1},{25,9},{2,18},{10... | collective-permute-start | bytes 688136 | tf_op jit(solution)/shard_map/ppermute | solution.py:656
  45.0 1.4 %collective-permute-start.18 = (bf16[64,1792]{1,0:T(8,128)(2,1)S(1)}, bf16[64,1792]{1,0:T(8,128)(2,1)S(1)}, u32[]{:S(2)}, u32[]{:S(2)}) collective-permute-start(bf16[64,1792]{1,0:T(8,128)(2,1)S(1)} %get-tuple-element.79), channel_id=1, source_target_pairs={{0,8},{8,0},{16,24},{24,16},{1,9},{9,1},{17,25},{25,17},{2,10},{10... | collective-permute-start | bytes 688136 | tf_op jit(solution)/shard_map/ppermute | solution.py:656
  46.4 0.1 collective-permute-start.19
  46.6 0.4 collective-permute-start.20
  47.0 1.9 %partial_products.3.refs_0_.refs_3_ = f32[128,512]{1,0:T(8,128)S(1)} custom-call(bf16[128,512]{1,0:T(8,128)(2,1)S(1)} %get-tuple-element.70.refs_0_.refs_2_, bf16[128,1792]{1,0:T(8,128)(2,1)S(1)} %pad_maximum_fusion.refs_0_.refs_1_.refs_3_.refs_4_, bf16[64,1792]{1,0:T(8,128)(2,1)S(1)} %arrange.15.refs_2_.refs_4_, ...), custom_call_target="tpu_custom_call" | custom-call | flops 1024 | bytes 1024 | tf_op jit(solution)/shard_map/partial_products/pallas_call | solution.py:34
  48.9 3.1 %down_grads.2 = (bf16[512,7168]{1,0:T(8,128)(2,1)}, f32[8,128]{1,0:T(8,128)S(1)}) custom-call(f32[128,512]{1,0:T(8,128)S(1)} %partial_products.3.refs_0_.refs_3_, s32[1]{0:T(128)} %bitcast.2.refs_1_, bf16[128,512]{1,0:T(8,128)(2,1)S(1)} %get-tuple-element.70.refs_0_.refs_2_, bf16[128,1792]{1,0:T(8,128)(2,1)S(1)} %pad_maximum_fusion.refs_0_.refs_1_.refs_3_.refs_4_, ...), custom_call_target="tpu_custom_call" | custom-call | flops 1024 | bytes 1024 | tf_op jit(solution)/shard_map/down_grads/pallas_call | solution.py:34
  52.0 0.1 merge.1
  52.2 1.5 %collective-permute-start.21 = (bf16[128,1792]{1,0:T(8,128)(2,1)S(1)}, bf16[128,1792]{1,0:T(8,128)(2,1)S(1)}, u32[]{:S(2)}, u32[]{:S(2)}) collective-permute-start(bf16[128,1792]{1,0:T(8,128)(2,1)S(1)} %get-tuple-element.80.refs_0_), channel_id=1, source_target_pairs={{0,8},{8,0},{16,24},{24,16},{1,9},{9,1},{17,25},{25,17},{2,10},{10... | collective-permute-start | bytes 1376264 | tf_op jit(solution)/shard_map/ppermute | solution.py:656
  53.6 1.1 %collective-permute-start.22 = (bf16[128,1792]{1,0:T(8,128)(2,1)S(1)}, bf16[128,1792]{1,0:T(8,128)(2,1)S(1)}, u32[]{:S(2)}, u32[]{:S(2)}) collective-permute-start(bf16[128,1792]{1,0:T(8,128)(2,1)S(1)} %get-tuple-element.88), channel_id=1, source_target_pairs={{0,16},{8,24},{16,0},{24,8},{1,17},{9,25},{17,1},{25,9},{2,18},{10... | collective-permute-start | bytes 1376264 | tf_op jit(solution)/shard_map/ppermute | solution.py:656
  54.8 2.0 %backward_terms.1 = (bf16[128,512]{1,0:T(8,128)(2,1)S(1)}, bf16[128,512]{1,0:T(8,128)(2,1)S(1)}, bf16[64,1792]{1,0:T(8,128)(2,1)S(1)}, bf16[64,1792]{1,0:T(8,128)(2,1)S(1)}) custom-call(bf16[128,1792]{1,0:T(8,128)(2,1)S(1)} %get-tuple-element.80.refs_0_, bf16[64,1792]{1,0:T(8,128)(2,1)S(1)} %collective-permute-done.19.refs_1_.refs_4_, ...), custom_call_target="tpu_custom_call" | custom-call | flops 1024 | bytes 1024 | tf_op jit(solution)/shard_map/backward_terms/pallas_call | solution.py:34
  56.7 0.8 collective-permute-start.28
  57.6 3.6 %backward_rest.1 = (bf16[64,1792]{1,0:T(8,128)(2,1)S(1)}, bf16[64,1792]{1,0:T(8,128)(2,1)S(1)}, bf16[64,1792]{1,0:T(8,128)(2,1)S(1)}, bf16[64,1792]{1,0:T(8,128)...) custom-call(bf16[128,512]{1,0:T(8,128)(2,1)S(1)} %get-tuple-element.83.refs_0_.refs_2_, ...), custom_call_target="tpu_custom_call" | custom-call | flops 1024 | bytes 1024 | tf_op jit(solution)/shard_map/backward_rest/pallas_call | solution.py:34
  61.2 3.6 %collective-permute-done.21.refs_2_ = bf16[128,1792]{1,0:T(8,128)(2,1)S(1)} collective-permute-done((bf16[128,1792]{1,0:T(8,128)(2,1)S(1)}, bf16[128,1792]{1,0:T(8,128)(2,1)S(1)}, u32[]{:S(2)}, u32[]{:S(2)}) %collective-permute-start.21) | collective-permute-done | bytes 458784 | tf_op jit(solution)/shard_map/ppermute | solution.py:656
  64.8 0.2 add_up.4
  65.0 1.8 %collective-permute-start.23 = (bf16[32,1792]{1,0:T(8,128)(2,1)S(1)}, bf16[32,1792]{1,0:T(8,128)(2,1)S(1)}, u32[]{:S(2)}, u32[]{:S(2)}) collective-permute-start(bf16[32,1792]{1,0:T(8,128)(2,1)S(1)} %get-tuple-element.90), channel_id=1, source_target_pairs={{0,2},{1,3},{2,0},{3,1},{4,6},{5,7},{6,4},{7,5},{8,10},{9,11},{10,... | collective-permute-start | bytes 344072 | tf_op jit(solution)/shard_map/ppermute | solution.py:656
  66.8 1.9 %collective-permute-start.24 = (bf16[32,1792]{1,0:T(8,128)(2,1)S(1)}, bf16[32,1792]{1,0:T(8,128)(2,1)S(1)}, u32[]{:S(2)}, u32[]{:S(2)}) collective-permute-start(bf16[32,1792]{1,0:T(8,128)(2,1)S(1)} %get-tuple-element.91), channel_id=1, source_target_pairs={{0,4},{1,5},{2,6},{3,7},{4,0},{5,1},{6,2},{7,3},{8,12},{9,13},{10,... | collective-permute-start | bytes 344072 | tf_op jit(solution)/shard_map/ppermute | solution.py:656
  68.6 0.3 collective-permute-start.25
  68.9 0.8 collective-permute-done.28.refs_2_
  69.7 1.4 %collective-permute-start.27 = (bf16[64,1792]{1,0:T(8,128)(2,1)S(1)}, bf16[64,1792]{1,0:T(8,128)(2,1)S(1)}, u32[]{:S(2)}, u32[]{:S(2)}) collective-permute-start(bf16[64,1792]{1,0:T(8,128)(2,1)S(1)} %get-tuple-element.95), channel_id=1, source_target_pairs={{0,8},{8,0},{16,24},{24,16},{1,9},{9,1},{17,25},{25,17},{2,10},{10... | collective-permute-start | bytes 688136 | tf_op jit(solution)/shard_map/ppermute | solution.py:656
  71.2 0.5 collective-permute-start.29
  71.8 0.3 collective-permute-start.31
  72.0 0.5 collective-permute-done.24.refs_3_
  72.5 0.8 collective-permute-start.32
  73.4 0.9 collective-permute-done.25.refs_4_
  74.3 7.3 %collective-permute-start.26 = (bf16[64,1792]{1,0:T(8,128)(2,1)S(1)}, bf16[64,1792]{1,0:T(8,128)(2,1)S(1)}, u32[]{:S(2)}, u32[]{:S(2)}) collective-permute-start(bf16[64,1792]{1,0:T(8,128)(2,1)S(1)} %pad_maximum_fusion.3), channel_id=1, source_target_pairs={{0,1},{1,0},{2,3},{3,2},{4,5},{5,4},{6,7},{7,6},{8,9},{9,8},{10,11... | collective-permute-start | bytes 688136 | tf_op jit(solution)/shard_map/ppermute | solution.py:656
  81.6 0.1 add_up.6
  81.7 1.2 %collective-permute-start.34 = (bf16[32,1792]{1,0:T(8,128)(2,1)S(1)}, bf16[32,1792]{1,0:T(8,128)(2,1)S(1)}, u32[]{:S(2)}, u32[]{:S(2)}) collective-permute-start(bf16[32,1792]{1,0:T(8,128)(2,1)S(1)} %get-tuple-element.98.refs_0_), channel_id=1, source_target_pairs={{0,4},{1,5},{2,6},{3,7},{4,0},{5,1},{6,2},{7,3},{8,12},{9,13},{10,... | collective-permute-start | bytes 344072 | tf_op jit(solution)/shard_map/ppermute | solution.py:656
  82.9 0.5 collective-permute-start.35
  83.4 1.9 %down_grads.3 = (bf16[512,7168]{1,0:T(8,128)(2,1)}, f32[8,128]{1,0:T(8,128)S(1)}) custom-call(bf16[32,1792]{1,0:T(8,128)(2,1)S(1)} %get-tuple-element.98.refs_0_, s32[1]{0:T(128)} %bitcast.2.refs_1_, bf16[128,512]{1,0:T(8,128)(2,1)S(1)} %get-tuple-element.70.refs_0_.refs_2_, ...), custom_call_target="tpu_custom_call", output_to_operand_aliasing={{0}: (3, {})} | custom-call | flops 1024 | bytes 1024 | tf_op jit(solution)/shard_map/down_grads/pallas_call | solution.py:34
  85.3 0.1 add_up.7
  85.4 1.1 %collective-permute-start.33 = (bf16[32,1792]{1,0:T(8,128)(2,1)S(1)}, bf16[32,1792]{1,0:T(8,128)(2,1)S(1)}, u32[]{:S(2)}, u32[]{:S(2)}) collective-permute-start(bf16[32,1792]{1,0:T(8,128)(2,1)S(1)} %get-tuple-element.107), channel_id=1, source_target_pairs={{0,2},{1,3},{2,0},{3,1},{4,6},{5,7},{6,4},{7,5},{8,10},{9,11},{10,... | collective-permute-start | bytes 344072 | tf_op jit(solution)/shard_map/ppermute | solution.py:656
  86.5 5.8 %weight_grads.1 = (bf16[7168,512]{1,0:T(8,128)(2,1)}, bf16[7168,512]{1,0:T(8,128)(2,1)}, f32[8,128]{1,0:T(8,128)S(1)}) custom-call(bf16[32,1792]{1,0:T(8,128)(2,1)S(1)} %get-tuple-element.106.refs_0_.refs_1_, s32[1]{0:T(128)} %bitcast.2.refs_1_, bf16[128,512]{1,0:T(8,128)(2,1)S(1)} %get-tuple-element.83.refs_0_.refs_2_, ...), custom_call_target="tpu_custom_call" | custom-call | flops 1024 | bytes 1024 | tf_op jit(solution)/shard_map/weight_grads/pallas_call | solution.py:34
  92.3 2.2 %collective-permute-start.36 = (bf16[64,1792]{1,0:T(8,128)(2,1)S(1)}, bf16[64,1792]{1,0:T(8,128)(2,1)S(1)}, u32[]{:S(2)}, u32[]{:S(2)}) collective-permute-start(bf16[64,1792]{1,0:T(8,128)(2,1)S(1)} %arrange.18), channel_id=1, source_target_pairs={{0,1},{1,0},{2,3},{3,2},{4,5},{5,4},{6,7},{7,6},{8,9},{9,8},{10,11... | collective-permute-start | bytes 688136 | tf_op jit(solution)/shard_map/ppermute | solution.py:656
  94.5 0.1 collective-permute-start.37
  94.6 0.2 spread_matrices.1
  94.8 1.6 %spread_rows.2 = bf16[512,1792]{1,0:T(8,128)(2,1)} custom-call(bf16[512,256]{1,0:T(8,128)(2,1)S(1)} %get-tuple-element.65.refs_0_, bf16[32,1792]{1,0:T(8,128)(2,1)S(1)} %get-tuple-element.89.refs_1_.refs_0_, bf16[32,1792]{1,0:T(8,128)(2,1)S(1)} %collective-permute-done.23.refs_2_, bf16[32,1792]{1,0:T(8,128)(2,1)S(1)} %collective-permute-done.24.refs_3_, ...), custom_call_target="tpu_custom_call" | custom-call | flops 1024 | bytes 1024 | tf_op jit(solution)/shard_map/spread_rows/pallas_call | solution.py:34
  96.4 1.5 %spread_rows.3 = bf16[512,1792]{1,0:T(8,128)(2,1)} custom-call(bf16[512,128]{1,0:T(8,128)(2,1)S(1)} %get-tuple-element.93.refs_0_, bf16[32,1792]{1,0:T(8,128)(2,1)S(1)} %get-tuple-element.106.refs_0_.refs_1_, bf16[32,1792]{1,0:T(8,128)(2,1)S(1)} %collective-permute-done.33.refs_2_, bf16[32,1792]{1,0:T(8,128)(2,1)S(1)} %collective-permute-done.34.refs_1_.refs_3_, ...), custom_call_target="tpu_custom_call" | custom-call | flops 1024 | bytes 1024 | tf_op jit(solution)/shard_map/spread_rows/pallas_call | solution.py:34
  (53 shorter events, 0.5 us)
Async XLA Ops:
  3.2 9.9 %collective-permute-start = (bf16[32,1792]{1,0:T(8,128)(2,1)S(1)}, bf16[32,1792]{1,0:T(8,128)(2,1)S(1)}, u32[]{:S(2)}, u32[]{:S(2)}) collective-permute-start(bf16[32,1792]{1,0:T(8,128)(2,1)S(1)} %get-tuple-element.60), channel_id=1, source_target_pairs={{0,1},{1,0},{2,3},{3,2},{4,5},{5,4},{6,7},{7,6},{8,9},{9,8},{10,11... | collective-permute-start | bytes 344072 | tf_op jit(solution)/shard_map/ppermute | solution.py:656
  3.3 9.8 %collective-permute-start.1 = (bf16[32,1792]{1,0:T(8,128)(2,1)S(1)}, bf16[32,1792]{1,0:T(8,128)(2,1)S(1)}, u32[]{:S(2)}, u32[]{:S(2)}) collective-permute-start(bf16[32,1792]{1,0:T(8,128)(2,1)S(1)} %get-tuple-element.61), channel_id=1, source_target_pairs={{0,2},{1,3},{2,0},{3,1},{4,6},{5,7},{6,4},{7,5},{8,10},{9,11},{10,... | collective-permute-start | bytes 344072 | tf_op jit(solution)/shard_map/ppermute | solution.py:656
  6.1 8.3 %collective-permute-start.2 = (bf16[32,1792]{1,0:T(8,128)(2,1)S(1)}, bf16[32,1792]{1,0:T(8,128)(2,1)S(1)}, u32[]{:S(2)}, u32[]{:S(2)}) collective-permute-start(bf16[32,1792]{1,0:T(8,128)(2,1)S(1)} %get-tuple-element.62), channel_id=1, source_target_pairs={{0,3},{1,2},{2,1},{3,0},{4,7},{5,6},{6,5},{7,4},{8,11},{9,10},{10,... | collective-permute-start | bytes 344072 | tf_op jit(solution)/shard_map/ppermute | solution.py:656
  6.1 11.0 %collective-permute-start.6 = (bf16[32,1792]{1,0:T(8,128)(2,1)S(1)}, bf16[32,1792]{1,0:T(8,128)(2,1)S(1)}, u32[]{:S(2)}, u32[]{:S(2)}) collective-permute-start(bf16[32,1792]{1,0:T(8,128)(2,1)S(1)} %get-tuple-element.66), channel_id=1, source_target_pairs={{0,4},{1,5},{2,6},{3,7},{4,0},{5,1},{6,2},{7,3},{8,12},{9,13},{10,... | collective-permute-start | bytes 344072 | tf_op jit(solution)/shard_map/ppermute | solution.py:656
  12.0 6.9 %collective-permute-start.7 = (bf16[32,1792]{1,0:T(8,128)(2,1)S(1)}, bf16[32,1792]{1,0:T(8,128)(2,1)S(1)}, u32[]{:S(2)}, u32[]{:S(2)}) collective-permute-start(bf16[32,1792]{1,0:T(8,128)(2,1)S(1)} %get-tuple-element.67), channel_id=1, source_target_pairs={{0,6},{1,7},{2,4},{3,5},{4,2},{5,3},{6,0},{7,1},{8,14},{9,15},{10,... | collective-permute-start | bytes 344072 | tf_op jit(solution)/shard_map/ppermute | solution.py:656
  14.5 13.4 %collective-permute-start.3 = (bf16[128,1792]{1,0:T(8,128)(2,1)S(1)}, bf16[128,1792]{1,0:T(8,128)(2,1)S(1)}, u32[]{:S(2)}, u32[]{:S(2)}) collective-permute-start(bf16[128,1792]{1,0:T(8,128)(2,1)S(1)} %pad_maximum_fusion.refs_0_.refs_1_.refs_3_.refs_4_), channel_id=1, source_target_pairs={{0,8},{8,0},{16,24},{24,16},{1,9},{9,1},{17,25},{25,17},{2,10},{10... | collective-permute-start | bytes 1376264 | tf_op jit(solution)/shard_map/ppermute | solution.py:656
  15.9 12.0 %collective-permute-start.5 = (bf16[128,1792]{1,0:T(8,128)(2,1)S(1)}, bf16[128,1792]{1,0:T(8,128)(2,1)S(1)}, u32[]{:S(2)}, u32[]{:S(2)}) collective-permute-start(bf16[128,1792]{1,0:T(8,128)(2,1)S(1)} %pad_maximum_fusion.refs_0_.refs_1_.refs_3_.refs_4_), channel_id=1, source_target_pairs={{0,16},{8,24},{16,0},{24,8},{1,17},{9,25},{17,1},{25,9},{2,18},{10... | collective-permute-start | bytes 1376264 | tf_op jit(solution)/shard_map/ppermute | solution.py:656
  18.9 9.0 %collective-permute-start.8 = (bf16[64,1792]{1,0:T(8,128)(2,1)S(1)}, bf16[64,1792]{1,0:T(8,128)(2,1)S(1)}, u32[]{:S(2)}, u32[]{:S(2)}) collective-permute-start(bf16[64,1792]{1,0:T(8,128)(2,1)S(1)} %pad_maximum_fusion.2), channel_id=1, source_target_pairs={{0,1},{1,0},{2,3},{3,2},{4,5},{5,4},{6,7},{7,6},{8,9},{9,8},{10,11... | collective-permute-start | bytes 688136 | tf_op jit(solution)/shard_map/ppermute | solution.py:656
  19.9 11.3 %collective-permute-start.12 = (bf16[32,1792]{1,0:T(8,128)(2,1)S(1)}, bf16[32,1792]{1,0:T(8,128)(2,1)S(1)}, u32[]{:S(2)}, u32[]{:S(2)}) collective-permute-start(bf16[32,1792]{1,0:T(8,128)(2,1)S(1)} %get-tuple-element.71), channel_id=1, source_target_pairs={{0,4},{1,5},{2,6},{3,7},{4,0},{5,1},{6,2},{7,3},{8,12},{9,13},{10,... | collective-permute-start | bytes 344072 | tf_op jit(solution)/shard_map/ppermute | solution.py:656
  22.9 8.3 %collective-permute-start.13 = (bf16[32,1792]{1,0:T(8,128)(2,1)S(1)}, bf16[32,1792]{1,0:T(8,128)(2,1)S(1)}, u32[]{:S(2)}, u32[]{:S(2)}) collective-permute-start(bf16[32,1792]{1,0:T(8,128)(2,1)S(1)} %get-tuple-element.72), channel_id=1, source_target_pairs={{0,6},{1,7},{2,4},{3,5},{4,2},{5,3},{6,0},{7,1},{8,14},{9,15},{10,... | collective-permute-start | bytes 344072 | tf_op jit(solution)/shard_map/ppermute | solution.py:656
  27.9 6.3 %collective-permute-start.10 = (bf16[64,1792]{1,0:T(8,128)(2,1)S(1)}, bf16[64,1792]{1,0:T(8,128)(2,1)S(1)}, u32[]{:S(2)}, u32[]{:S(2)}) collective-permute-start(bf16[64,1792]{1,0:T(8,128)(2,1)S(1)} %arrange.12.refs_1_.refs_5_), channel_id=1, source_target_pairs={{0,16},{8,24},{16,0},{24,8},{1,17},{9,25},{17,1},{25,9},{2,18},{10... | collective-permute-start | bytes 688136 | tf_op jit(solution)/shard_map/ppermute | solution.py:656
  29.2 5.9 %collective-permute-start.9 = (bf16[64,1792]{1,0:T(8,128)(2,1)S(1)}, bf16[64,1792]{1,0:T(8,128)(2,1)S(1)}, u32[]{:S(2)}, u32[]{:S(2)}) collective-permute-start(bf16[64,1792]{1,0:T(8,128)(2,1)S(1)} %arrange.12.refs_1_.refs_5_), channel_id=1, source_target_pairs={{0,8},{8,0},{16,24},{24,16},{1,9},{9,1},{17,25},{25,17},{2,10},{10... | collective-permute-start | bytes 688136 | tf_op jit(solution)/shard_map/ppermute | solution.py:656
  31.3 5.5 %collective-permute-start.14 = (bf16[96,1792]{1,0:T(8,128)(2,1)S(1)}, bf16[96,1792]{1,0:T(8,128)(2,1)S(1)}, u32[]{:S(2)}, u32[]{:S(2)}) collective-permute-start(bf16[96,1792]{1,0:T(8,128)(2,1)S(1)} %arrange.14), channel_id=1, source_target_pairs={{0,1},{1,0},{2,3},{3,2},{4,5},{5,4},{6,7},{7,6},{8,9},{9,8},{10,11... | collective-permute-start | bytes 1032200 | tf_op jit(solution)/shard_map/ppermute | solution.py:656
  32.3 9.8 %collective-permute-start.4 = (bf16[64,1792]{1,0:T(8,128)(2,1)S(1)}, bf16[64,1792]{1,0:T(8,128)(2,1)S(1)}, u32[]{:S(2)}, u32[]{:S(2)}) collective-permute-start(bf16[64,1792]{1,0:T(8,128)(2,1)S(1)} %arrange.11), channel_id=1, source_target_pairs={{0,16},{8,24},{16,0},{24,8},{1,17},{9,25},{17,1},{25,9},{2,18},{10... | collective-permute-start | bytes 688136 | tf_op jit(solution)/shard_map/ppermute | solution.py:656
  35.2 6.9 %collective-permute-start.11 = (bf16[64,1792]{1,0:T(8,128)(2,1)S(1)}, bf16[64,1792]{1,0:T(8,128)(2,1)S(1)}, u32[]{:S(2)}, u32[]{:S(2)}) collective-permute-start(bf16[64,1792]{1,0:T(8,128)(2,1)S(1)} %arrange.13), channel_id=1, source_target_pairs={{0,8},{8,0},{16,24},{24,16},{1,9},{9,1},{17,25},{25,17},{2,10},{10... | collective-permute-start | bytes 688136 | tf_op jit(solution)/shard_map/ppermute | solution.py:656
  36.8 9.8 %collective-permute-start.15 = (bf16[64,1792]{1,0:T(8,128)(2,1)S(1)}, bf16[64,1792]{1,0:T(8,128)(2,1)S(1)}, u32[]{:S(2)}, u32[]{:S(2)}) collective-permute-start(bf16[64,1792]{1,0:T(8,128)(2,1)S(1)} %arrange.15.refs_2_.refs_4_), channel_id=1, source_target_pairs={{0,8},{8,0},{16,24},{24,16},{1,9},{9,1},{17,25},{25,17},{2,10},{10... | collective-permute-start | bytes 688136 | tf_op jit(solution)/shard_map/ppermute | solution.py:656
  36.9 9.7 %collective-permute-start.16 = (bf16[64,1792]{1,0:T(8,128)(2,1)S(1)}, bf16[64,1792]{1,0:T(8,128)(2,1)S(1)}, u32[]{:S(2)}, u32[]{:S(2)}) collective-permute-start(bf16[64,1792]{1,0:T(8,128)(2,1)S(1)} %arrange.15.refs_2_.refs_4_), channel_id=1, source_target_pairs={{0,16},{8,24},{16,0},{24,8},{1,17},{9,25},{17,1},{25,9},{2,18},{10... | collective-permute-start | bytes 688136 | tf_op jit(solution)/shard_map/ppermute | solution.py:656
  43.8 8.2 %collective-permute-start.17 = (bf16[64,1792]{1,0:T(8,128)(2,1)S(1)}, bf16[64,1792]{1,0:T(8,128)(2,1)S(1)}, u32[]{:S(2)}, u32[]{:S(2)}) collective-permute-start(bf16[64,1792]{1,0:T(8,128)(2,1)S(1)} %get-tuple-element.78), channel_id=1, source_target_pairs={{0,16},{8,24},{16,0},{24,8},{1,17},{9,25},{17,1},{25,9},{2,18},{10... | collective-permute-start | bytes 688136 | tf_op jit(solution)/shard_map/ppermute | solution.py:656
  45.0 7.0 %collective-permute-start.18 = (bf16[64,1792]{1,0:T(8,128)(2,1)S(1)}, bf16[64,1792]{1,0:T(8,128)(2,1)S(1)}, u32[]{:S(2)}, u32[]{:S(2)}) collective-permute-start(bf16[64,1792]{1,0:T(8,128)(2,1)S(1)} %get-tuple-element.79), channel_id=1, source_target_pairs={{0,8},{8,0},{16,24},{24,16},{1,9},{9,1},{17,25},{25,17},{2,10},{10... | collective-permute-start | bytes 688136 | tf_op jit(solution)/shard_map/ppermute | solution.py:656
  46.4 8.3 %collective-permute-start.19 = (bf16[64,1792]{1,0:T(8,128)(2,1)S(1)}, bf16[64,1792]{1,0:T(8,128)(2,1)S(1)}, u32[]{:S(2)}, u32[]{:S(2)}) collective-permute-start(bf16[64,1792]{1,0:T(8,128)(2,1)S(1)} %arrange.16), channel_id=1, source_target_pairs={{0,8},{8,0},{16,24},{24,16},{1,9},{9,1},{17,25},{25,17},{2,10},{10... | collective-permute-start | bytes 688136 | tf_op jit(solution)/shard_map/ppermute | solution.py:656
  46.6 8.1 %collective-permute-start.20 = (bf16[64,1792]{1,0:T(8,128)(2,1)S(1)}, bf16[64,1792]{1,0:T(8,128)(2,1)S(1)}, u32[]{:S(2)}, u32[]{:S(2)}) collective-permute-start(bf16[64,1792]{1,0:T(8,128)(2,1)S(1)} %arrange.17), channel_id=1, source_target_pairs={{0,16},{8,24},{16,0},{24,8},{1,17},{9,25},{17,1},{25,9},{2,18},{10... | collective-permute-start | bytes 688136 | tf_op jit(solution)/shard_map/ppermute | solution.py:656
  52.2 12.7 %collective-permute-start.21 = (bf16[128,1792]{1,0:T(8,128)(2,1)S(1)}, bf16[128,1792]{1,0:T(8,128)(2,1)S(1)}, u32[]{:S(2)}, u32[]{:S(2)}) collective-permute-start(bf16[128,1792]{1,0:T(8,128)(2,1)S(1)} %get-tuple-element.80.refs_0_), channel_id=1, source_target_pairs={{0,8},{8,0},{16,24},{24,16},{1,9},{9,1},{17,25},{25,17},{2,10},{10... | collective-permute-start | bytes 1376264 | tf_op jit(solution)/shard_map/ppermute | solution.py:656
  53.6 11.2 %collective-permute-start.22 = (bf16[128,1792]{1,0:T(8,128)(2,1)S(1)}, bf16[128,1792]{1,0:T(8,128)(2,1)S(1)}, u32[]{:S(2)}, u32[]{:S(2)}) collective-permute-start(bf16[128,1792]{1,0:T(8,128)(2,1)S(1)} %get-tuple-element.88), channel_id=1, source_target_pairs={{0,16},{8,24},{16,0},{24,8},{1,17},{9,25},{17,1},{25,9},{2,18},{10... | collective-permute-start | bytes 1376264 | tf_op jit(solution)/shard_map/ppermute | solution.py:656
  56.7 13.0 %collective-permute-start.28 = (bf16[64,1792]{1,0:T(8,128)(2,1)S(1)}, bf16[64,1792]{1,0:T(8,128)(2,1)S(1)}, u32[]{:S(2)}, u32[]{:S(2)}) collective-permute-start(bf16[64,1792]{1,0:T(8,128)(2,1)S(1)} %get-tuple-element.97), channel_id=1, source_target_pairs={{0,8},{8,0},{16,24},{24,16},{1,9},{9,1},{17,25},{25,17},{2,10},{10... | collective-permute-start | bytes 688136 | tf_op jit(solution)/shard_map/ppermute | solution.py:656
  57.5 13.7 %collective-permute-start.30 = (bf16[64,1792]{1,0:T(8,128)(2,1)S(1)}, bf16[64,1792]{1,0:T(8,128)(2,1)S(1)}, u32[]{:S(2)}, u32[]{:S(2)}) collective-permute-start(bf16[64,1792]{1,0:T(8,128)(2,1)S(1)} %get-tuple-element.102), channel_id=1, source_target_pairs={{0,16},{8,24},{16,0},{24,8},{1,17},{9,25},{17,1},{25,9},{2,18},{10... | collective-permute-start | bytes 688136 | tf_op jit(solution)/shard_map/ppermute | solution.py:656
  65.0 6.8 %collective-permute-start.23 = (bf16[32,1792]{1,0:T(8,128)(2,1)S(1)}, bf16[32,1792]{1,0:T(8,128)(2,1)S(1)}, u32[]{:S(2)}, u32[]{:S(2)}) collective-permute-start(bf16[32,1792]{1,0:T(8,128)(2,1)S(1)} %get-tuple-element.90), channel_id=1, source_target_pairs={{0,2},{1,3},{2,0},{3,1},{4,6},{5,7},{6,4},{7,5},{8,10},{9,11},{10,... | collective-permute-start | bytes 344072 | tf_op jit(solution)/shard_map/ppermute | solution.py:656
  66.8 5.8 %collective-permute-start.24 = (bf16[32,1792]{1,0:T(8,128)(2,1)S(1)}, bf16[32,1792]{1,0:T(8,128)(2,1)S(1)}, u32[]{:S(2)}, u32[]{:S(2)}) collective-permute-start(bf16[32,1792]{1,0:T(8,128)(2,1)S(1)} %get-tuple-element.91), channel_id=1, source_target_pairs={{0,4},{1,5},{2,6},{3,7},{4,0},{5,1},{6,2},{7,3},{8,12},{9,13},{10,... | collective-permute-start | bytes 344072 | tf_op jit(solution)/shard_map/ppermute | solution.py:656
  68.6 5.6 %collective-permute-start.25 = (bf16[32,1792]{1,0:T(8,128)(2,1)S(1)}, bf16[32,1792]{1,0:T(8,128)(2,1)S(1)}, u32[]{:S(2)}, u32[]{:S(2)}) collective-permute-start(bf16[32,1792]{1,0:T(8,128)(2,1)S(1)} %get-tuple-element.92), channel_id=1, source_target_pairs={{0,6},{1,7},{2,4},{3,5},{4,2},{5,3},{6,0},{7,1},{8,14},{9,15},{10,... | collective-permute-start | bytes 344072 | tf_op jit(solution)/shard_map/ppermute | solution.py:656
  69.7 11.8 %collective-permute-start.27 = (bf16[64,1792]{1,0:T(8,128)(2,1)S(1)}, bf16[64,1792]{1,0:T(8,128)(2,1)S(1)}, u32[]{:S(2)}, u32[]{:S(2)}) collective-permute-start(bf16[64,1792]{1,0:T(8,128)(2,1)S(1)} %get-tuple-element.95), channel_id=1, source_target_pairs={{0,8},{8,0},{16,24},{24,16},{1,9},{9,1},{17,25},{25,17},{2,10},{10... | collective-permute-start | bytes 688136 | tf_op jit(solution)/shard_map/ppermute | solution.py:656
  71.2 10.4 %collective-permute-start.29 = (bf16[64,1792]{1,0:T(8,128)(2,1)S(1)}, bf16[64,1792]{1,0:T(8,128)(2,1)S(1)}, u32[]{:S(2)}, u32[]{:S(2)}) collective-permute-start(bf16[64,1792]{1,0:T(8,128)(2,1)S(1)} %add_up.5.refs_0_), channel_id=1, source_target_pairs={{0,16},{8,24},{16,0},{24,8},{1,17},{9,25},{17,1},{25,9},{2,18},{10... | collective-permute-start | bytes 688136 | tf_op jit(solution)/shard_map/ppermute | solution.py:656
  71.8 13.5 %collective-permute-start.31 = (bf16[64,1792]{1,0:T(8,128)(2,1)S(1)}, bf16[64,1792]{1,0:T(8,128)(2,1)S(1)}, u32[]{:S(2)}, u32[]{:S(2)}) collective-permute-start(bf16[64,1792]{1,0:T(8,128)(2,1)S(1)} %get-tuple-element.104), channel_id=1, source_target_pairs={{0,8},{8,0},{16,24},{24,16},{1,9},{9,1},{17,25},{25,17},{2,10},{10... | collective-permute-start | bytes 688136 | tf_op jit(solution)/shard_map/ppermute | solution.py:656
  72.5 12.8 %collective-permute-start.32 = (bf16[64,1792]{1,0:T(8,128)(2,1)S(1)}, bf16[64,1792]{1,0:T(8,128)(2,1)S(1)}, u32[]{:S(2)}, u32[]{:S(2)}) collective-permute-start(bf16[64,1792]{1,0:T(8,128)(2,1)S(1)} %get-tuple-element.105), channel_id=1, source_target_pairs={{0,16},{8,24},{16,0},{24,8},{1,17},{9,25},{17,1},{25,9},{2,18},{10... | collective-permute-start | bytes 688136 | tf_op jit(solution)/shard_map/ppermute | solution.py:656
  74.3 11.0 %collective-permute-start.26 = (bf16[64,1792]{1,0:T(8,128)(2,1)S(1)}, bf16[64,1792]{1,0:T(8,128)(2,1)S(1)}, u32[]{:S(2)}, u32[]{:S(2)}) collective-permute-start(bf16[64,1792]{1,0:T(8,128)(2,1)S(1)} %pad_maximum_fusion.3), channel_id=1, source_target_pairs={{0,1},{1,0},{2,3},{3,2},{4,5},{5,4},{6,7},{7,6},{8,9},{9,8},{10,11... | collective-permute-start | bytes 688136 | tf_op jit(solution)/shard_map/ppermute | solution.py:656
  81.7 10.6 %collective-permute-start.34 = (bf16[32,1792]{1,0:T(8,128)(2,1)S(1)}, bf16[32,1792]{1,0:T(8,128)(2,1)S(1)}, u32[]{:S(2)}, u32[]{:S(2)}) collective-permute-start(bf16[32,1792]{1,0:T(8,128)(2,1)S(1)} %get-tuple-element.98.refs_0_), channel_id=1, source_target_pairs={{0,4},{1,5},{2,6},{3,7},{4,0},{5,1},{6,2},{7,3},{8,12},{9,13},{10,... | collective-permute-start | bytes 344072 | tf_op jit(solution)/shard_map/ppermute | solution.py:656
  82.9 9.3 %collective-permute-start.35 = (bf16[32,1792]{1,0:T(8,128)(2,1)S(1)}, bf16[32,1792]{1,0:T(8,128)(2,1)S(1)}, u32[]{:S(2)}, u32[]{:S(2)}) collective-permute-start(bf16[32,1792]{1,0:T(8,128)(2,1)S(1)} %get-tuple-element.108), channel_id=1, source_target_pairs={{0,6},{1,7},{2,4},{3,5},{4,2},{5,3},{6,0},{7,1},{8,14},{9,15},{10,... | collective-permute-start | bytes 344072 | tf_op jit(solution)/shard_map/ppermute | solution.py:656
  85.4 9.1 %collective-permute-start.33 = (bf16[32,1792]{1,0:T(8,128)(2,1)S(1)}, bf16[32,1792]{1,0:T(8,128)(2,1)S(1)}, u32[]{:S(2)}, u32[]{:S(2)}) collective-permute-start(bf16[32,1792]{1,0:T(8,128)(2,1)S(1)} %get-tuple-element.107), channel_id=1, source_target_pairs={{0,2},{1,3},{2,0},{3,1},{4,6},{5,7},{6,4},{7,5},{8,10},{9,11},{10,... | collective-permute-start | bytes 344072 | tf_op jit(solution)/shard_map/ppermute | solution.py:656
  92.3 4.1 %collective-permute-start.36 = (bf16[64,1792]{1,0:T(8,128)(2,1)S(1)}, bf16[64,1792]{1,0:T(8,128)(2,1)S(1)}, u32[]{:S(2)}, u32[]{:S(2)}) collective-permute-start(bf16[64,1792]{1,0:T(8,128)(2,1)S(1)} %arrange.18), channel_id=1, source_target_pairs={{0,1},{1,0},{2,3},{3,2},{4,5},{5,4},{6,7},{7,6},{8,9},{9,8},{10,11... | collective-permute-start | bytes 688136 | tf_op jit(solution)/shard_map/ppermute | solution.py:656
  94.5 1.9 %collective-permute-start.37 = (bf16[32,1792]{1,0:T(8,128)(2,1)S(1)}, bf16[32,1792]{1,0:T(8,128)(2,1)S(1)}, u32[]{:S(2)}, u32[]{:S(2)}) collective-permute-start(bf16[32,1792]{1,0:T(8,128)(2,1)S(1)} %arrange.19), channel_id=1, source_target_pairs={{0,1},{1,0},{2,3},{3,2},{4,5},{5,4},{6,7},{7,6},{8,9},{9,8},{10,11... | collective-permute-start | bytes 344072 | tf_op jit(solution)/shard_map/ppermute | solution.py:656
